TPU v7x, 32 devices: a whole 2x2x4 slice. The times are simulated.
32 devices in a mesh: dp: 8 (over y, x, core), tensor: 4 (over z).
Axes of the slice: x: 2, y: 2, z: 4, core: 2. Of those that a mesh axis runs over, the one named last changes fastest.
Arguments:
- tokens: bfloat16 [4096, 8192], P('dp', 'tensor'), may hold values from -6 to 6
- row_adapter_index: int32 [4096, 1], P('dp'), may hold values from 0 to 63; in each aligned block of 512 rows (0 to 511, 512 to 1023, ...) at most 16 rows name the same one
- adapter_storage_slot: int32 [64], replicated, may hold values from 0 to 63, each once
- key_value_base_weight: bfloat16 [8192, 2, 1024], P('tensor'), may hold values from -0.09375 to 0.09375
- adapter_down_weight: bfloat16 [64, 8192, 128], P('dp', 'tensor'), may hold values from -0.0625 to 0.0625
- adapter_up_weight: bfloat16 [64, 2, 64, 1024], P('dp', None, None, 'tensor'), may hold values from -0.75 to 0.75
Outputs:
- key_value: bfloat16 [4096, 2, 1024], P('dp', None, 'tensor')
Inputs may be any that keep to these rules, and one draw needn't show every extreme that they name: `row_adapter_index`: within the rows of one index of dp no adapter is named by more than 16 rows, a bound that some block reaches. `adapter_storage_slot`: A permutation of the slots.
All inputs are finite; a program needn't handle non-finite values.
Results may differ from a plain program's by a relative error of at most 0.0034.
Values may be sent and summed in bfloat16 or wider, within the bound.
No kernel may reach another device: no remote copies, remote signals or barrier semaphores. Data moves between devices by JAX's collectives and lax.ppermute only.
A program may use at most 64 MiB of HBM per device.

v0:
```python
import jax
import jax.numpy as jnp
from jax import lax
from jax.sharding import PartitionSpec as P

adapter_scale = 0.5


def per_device(
    tokens,
    row_adapter_index,
    adapter_storage_slot,
    key_value_base_weight,
    adapter_down_weight,
    adapter_up_weight,
):
    row_count, shard_width = tokens.shape
    local_adapter_slots = adapter_down_weight.shape[0]
    groups = lax.axis_size("dp")
    experts = local_adapter_slots * groups
    capacity = max(2, 2 * row_count // experts)
    doubled_rank = adapter_down_weight.shape[2]
    adapter_of = row_adapter_index[:, 0]
    columns = lax.broadcasted_iota(jnp.int32, (row_count, experts), 1)
    onehot = (adapter_of[:, None] == columns).astype(jnp.int32)
    earlier = jnp.cumsum(onehot, axis=0) - onehot
    position = jnp.sum(earlier * onehot, axis=1)
    storage_device = jnp.sum(onehot * adapter_storage_slot[None, :], axis=1)
    target = storage_device * capacity + position
    outbox = jnp.zeros((experts * capacity, shard_width), tokens.dtype).at[target].set(tokens)
    outbox = outbox.reshape(groups, local_adapter_slots, capacity, shard_width)
    partials = jnp.einsum(
        "rd,djn->rjn", tokens, key_value_base_weight, preferred_element_type=jnp.float32
    )
    base = lax.psum_scatter(partials, "tensor", scatter_dimension=2, tiled=True)
    pieces_sum = jnp.einsum(
        "sekd,edr->sekr",
        lax.all_to_all(outbox, "dp", split_axis=0, concat_axis=0, tiled=True),
        adapter_down_weight,
        preferred_element_type=jnp.float32,
    )
    reduced_rows = lax.psum(pieces_sum, "tensor").astype(jnp.bfloat16)
    dims_now = reduced_rows.shape
    reduced_rows = reduced_rows.reshape(dims_now[0], dims_now[1], dims_now[2], 2, doubled_rank // 2)
    adapter_delta = jnp.einsum(
        "upgtl,ptlz->upgtz", reduced_rows, adapter_up_weight, preferred_element_type=jnp.float32
    )
    adapter_delta = (adapter_scale * adapter_delta).astype(jnp.bfloat16)
    returned = lax.all_to_all(adapter_delta, "dp", split_axis=0, concat_axis=0, tiled=True)
    returned_flat = returned.reshape(experts * capacity, 2, returned.shape[-1])
    update_rows = returned_flat[target]
    return (base + update_rows.astype(jnp.float32)).astype(jnp.bfloat16)


def solution(mesh):
    placed = (
        P("dp", "tensor"),
        P("dp", None),
        P(),
        P("tensor", None, None),
        P("dp", "tensor", None),
        P("dp", None, None, "tensor"),
    )
    return jax.shard_map(
        per_device, mesh=mesh, in_specs=placed, out_specs=P("dp", None, "tensor"), check_vma=False
    )
```

profile of v0, /device:TPU:0, one launch (start us, length us, event | category | flops | bytes accessed | tf_op | source)
XLA Modules:
  0.0 153.6 jit_solution(836014396838935869)
XLA Ops:
  6.5 0.0 copy-start
  6.5 0.0 reduce-scatter.2.cloned.1.call-start
  6.5 10.6 %fusion = f32[512,2,1024]{2,0,1:T(8,128)} fusion(bf16[2048,2,1024]{2,1,0:T(2,128)(2,1)} %param.9, bf16[512,2048]{1,0:T(8,128)(2,1)} %param.6), kind=kOutput, calls=%fused_computation.2 | convolution fusion | flops 4294967296 | bytes 14680064 | tf_op jit(solution)/shard_map/rd,djn->rjn/dot_general | solution.py:32
  17.1 0.0 copy-start.1
  17.2 0.0 copy-start.2
  17.2 0.0 reduce-scatter.2.cloned.1.call-update
  17.2 0.7 copy-done.1
  17.8 1.2 reduce-window.6
  19.1 0.2 slice_reduce_fusion
  19.3 0.0 copy-done.2
  19.3 0.1 select_reduce_fusion
  19.5 7.5 %scatter_custom_fusion = bf16[1024,2048]{1,0:T(8,128)(2,1)} fusion(s32[512]{0:T(512)S(1)} %bitcast.52, bf16[512,2048]{1,0:T(8,128)(2,1)} %param.6, bf16[]{:T(256)} %constant.5.clone.1), kind=kCustom, calls=%fused_computation.9 | custom fusion | bytes 4194816 | tf_op jit(solution)/shard_map/scatter | solution.py:30
  27.0 0.0 copy-start.3
  27.0 54.3 %all_to_all.10 = bf16[8,8,16,2048]{3,2,1,0:T(8,128)(2,1)S(1)} all-to-all(bf16[8,8,16,2048]{3,2,1,0:T(8,128)(2,1)} %bitcast.48), channel_id=1, replica_groups=mesh['dp'=8,'tensor'=4] {'dp'}, dimensions={0} | all-to-all | bytes 8388608 | tf_op jit(solution)/shard_map/all_to_all | solution.py:38
  81.2 0.0 copy-done.3
  81.2 1.2 fusion.9
  82.5 36.3 %all-reduce.1 = bf16[8,8,16,128]{3,2,0,1:T(8,128)(2,1)S(1)} all-reduce(f32[8,8,16,128]{3,2,0,1:T(8,128)S(1)} %fusion.9), channel_id=1, replica_groups=mesh['dp'=8,'tensor'=4] {'tensor'}, use_global_device_ids=true, to_apply=%region_6.7 | all-reduce | flops 131072 | bytes 786432 | tf_op jit(solution)/shard_map/psum | solution.py:42
  118.8 0.2 reshape.52
  119.0 0.0 copy-done
  119.0 0.4 fusion.8
  119.5 1.1 copy.22
  120.6 4.3 %all-to-all-start.1 = ((bf16[8,8,16,2,256]{4,2,3,1,0:T(8,128)(2,1)}), bf16[8,8,16,2,256]{4,2,3,1,0:T(8,128)(2,1)S(1)}, u32[]{:S(2)}, u32[]{:S(2)}) async-start(bf16[8,8,16,2,256]{4,2,3,1,0:T(8,128)(2,1)} %copy.22), calls=%async_computation.2 | async-start | bytes 2097152 | tf_op jit(solution)/shard_map/all_to_all | solution.py:49
  124.9 15.4 %all-to-all-done.1 = bf16[8,8,16,2,256]{4,2,3,1,0:T(8,128)(2,1)S(1)} async-done(((bf16[8,8,16,2,256]{4,2,3,1,0:T(8,128)(2,1)}), bf16[8,8,16,2,256]{4,2,3,1,0:T(8,128)(2,1)S(1)}, u32[]{:S(2)}, u32[]{:S(2)}) %all-to-all-start.1) | async-done | bytes 1048608 | tf_op jit(solution)/shard_map/all_to_all | solution.py:49
  140.3 0.1 copy.23
  140.4 1.1 copy.24
  141.5 2.6 %gather_fusion = bf16[512,2,256]{2,1,0:T(2,128)(2,1)S(1)} fusion(bf16[1024,2,256]{2,1,0:T(2,128)(2,1)S(1)} %copy.24, s32[1024]{0:T(1024)S(1)} %pad_clamp_fusion), kind=kCustom, calls=%fused_computation | custom fusion | bytes 1050624 | tf_op jit(solution)/shard_map/gather | solution.py:51
  144.1 0.0 reduce-scatter.2.cloned.1.call-done
  144.1 1.4 add_convert_fusion
  145.4 1.3 copy.26
  (6 shorter events, 0.1 us)
Async XLA Ops:
  6.5 112.5 %copy-start = (bf16[8,2,64,256]{3,2,1,0:T(8,128)(2,1)S(1)}, bf16[8,2,64,256]{3,2,1,0:T(8,128)(2,1)}, u32[]{:S(2)}) copy-start(bf16[8,2,64,256]{3,2,1,0:T(8,128)(2,1)} %param.11) | copy-start | bytes 1572868
  6.5 137.5 %reduce-scatter.2.cloned.1.call-start = ((), (), s32[]{:S(2)}) async-start(), calls=%async_computation.3 | async-start | bytes 5242880 | tf_op jit(solution)/shard_map/reduce_scatter | solution.py:35
  17.1 0.7 copy-start.1
  17.2 2.2 %copy-start.2 = (s32[64]{0:T(128)S(1)}, s32[64]{0:T(128)}, u32[]{:S(2)}) copy-start(s32[64]{0:T(128)} %param.8) | copy-start | bytes 772
  27.0 54.3 %copy-start.3 = (bf16[8,2048,128]{2,1,0:T(8,128)(2,1)S(1)}, bf16[8,2048,128]{2,1,0:T(8,128)(2,1)}, u32[]{:S(2)}) copy-start(bf16[8,2048,128]{2,1,0:T(8,128)(2,1)} %param.10) | copy-start | bytes 12582916
  120.6 19.7 %all-to-all-start.1 = ((bf16[8,8,16,2,256]{4,2,3,1,0:T(8,128)(2,1)}), bf16[8,8,16,2,256]{4,2,3,1,0:T(8,128)(2,1)S(1)}, u32[]{:S(2)}, u32[]{:S(2)}) async-start(bf16[8,8,16,2,256]{4,2,3,1,0:T(8,128)(2,1)} %copy.22), calls=%async_computation.2 | async-start | bytes 2097152 | tf_op jit(solution)/shard_map/all_to_all | solution.py:49
Sparse Core Ops, SparseCore 0:
  17.3 85.9 reduce-scatter.1
where the time goes:
time: 154 us
  blocking collectives  90.6 us (59%)
  waiting for transfers between devices  15.4 us (10%)
  local copies, waits for them, and re-layouts  14.8 us (10%)
  between operations  13.5 us (9%)
  matrix products  12.3 us (8%)
  starting transfers between devices  4.28 us (3%)
  other arithmetic  2.77 us (2%)
    all_to_all x1, blocking collectives, per_device(): lax.all_to_all(outbox, 'dp', split_axis=0, concat_axis=0, tiled=True)  54.3 us
    psum x1, blocking collectives, per_device(): reduced_rows = lax.psum(pieces_sum, 'tensor').astype(jnp.bfloat16)  36.3 us
    all_to_all x1, waiting for transfers between devices, per_device(): lax.all_to_all(adapter_delta, 'dp', split_axis=0, concat_axis=0, tiled=True)  15.4 us
    dot_general x1, matrix products, per_device(): jnp.einsum('rd,djn->rjn', tokens, key_value_base_weight, preferred_elemen...  10.6 us
    scatter x1, local copies, waits for them, and re-layouts, per_device(): jnp.zeros((experts * capacity, shard_width), tokens.dtype).at[target]  7.47 us
    all_to_all x1, starting transfers between devices, per_device(): lax.all_to_all(adapter_delta, 'dp', split_axis=0, concat_axis=0, tiled=True)  4.27 us
  transfers between devices with their start and end apart: 2, of which 1 were waited for; matrix products, arithmetic and copies ran while one was open for 10% of the time, Pallas kernels for 0%

commit v1 on v0

v1 whole, which is shorter than its diff:
```python
import functools

import jax
import jax.numpy as jnp
from jax import lax
from jax.experimental import pallas as pl
from jax.experimental.pallas import tpu as pltpu
from jax.sharding import PartitionSpec as P

adapter_scale = 0.5
BF = jnp.bfloat16
F32 = jnp.float32
VMEM_LIMIT = 48 * 1024 * 1024


def round_up(value, unit):
    return (value + unit - 1) // unit * unit


def dot(a, b, contract=((1,), (0,))):
    return lax.dot_general(a, b, (contract, ((), ())), preferred_element_type=F32)


def pack_kernel(shape, place_ref, adapter_ref, slot_ref, tokens_ref, *refs):
    sizes, first_rows, chip_slots, flag_lane = shape
    messages = len(sizes)
    outs, spread_ref, pick = refs[:messages], refs[messages], refs[messages + 1]
    rows, width = tokens_ref.shape
    experts = slot_ref.shape[1]
    offsets = [sum(round_up(s, 128) for s in sizes[:m]) for m in range(messages)]

    @pl.when(pl.program_id(0) == 0)
    def _():
        named = (lax.broadcasted_iota(jnp.int32, (experts, rows), 0) == adapter_ref[...]).astype(BF)
        slots = jnp.broadcast_to(slot_ref[...].astype(F32), (16, experts)).astype(BF)
        slot = dot(slots, named)[0:1, :].astype(jnp.int32)
        shift = (slot // chip_slots) ^ place_ref[0]
        within = (slot % chip_slots + 1).astype(F32)
        lanes = round_up(messages, 16)
        goes = lax.broadcasted_iota(jnp.int32, (lanes, rows), 0) == shift
        earlier = lax.broadcasted_iota(jnp.int32, (rows, rows), 0) < lax.broadcasted_iota(jnp.int32, (rows, rows), 1)
        goes_f = goes.astype(F32)
        rank = dot(goes_f.astype(BF), earlier.astype(F32).astype(BF))
        position = jnp.sum(rank * goes_f, axis=0, keepdims=True).astype(jnp.int32)
        counts = jnp.sum(goes_f, axis=1, keepdims=True)
        sub = lax.broadcasted_iota(jnp.int32, (lanes, 1), 0)
        limit = jnp.zeros((lanes, 1), F32)
        for m in range(messages):
            limit = jnp.where(sub == m, F32(first_rows[m] + sizes[m] - 1), limit)
        over = jnp.max(jnp.where((sub < messages) & (counts > limit), 1.0, 0.0), axis=0, keepdims=True)
        within8 = jnp.broadcast_to(within, (16, rows)).astype(BF)
        for m in range(messages):
            padded = round_up(sizes[m], 128)
            target = lax.broadcasted_iota(jnp.int32, (padded, rows), 0)
            hit = (target + first_rows[m] == position) & (shift == m) & (target < sizes[m] - 1)
            chosen = hit.astype(F32).astype(BF)
            pick[offsets[m]:offsets[m] + padded, :] = chosen
            spread_ref[:, offsets[m]:offsets[m] + padded] = hit.astype(F32).T.astype(BF)
            places = dot(within8, chosen, ((1,), (1,)))[0:1, :]
            if padded < width:
                places = jnp.concatenate([places, jnp.zeros((1, width - padded), F32)], axis=1)
            lane = lax.broadcasted_iota(jnp.int32, (1, width), 1)
            places = jnp.where(lane == flag_lane, over, places)
            body = dot(chosen, tokens_ref[...])[:sizes[m], :]
            row = lax.broadcasted_iota(jnp.int32, (sizes[m], 1), 0)
            outs[m][...] = jnp.where(row == sizes[m] - 1, places, body).astype(BF)

    @pl.when(pl.program_id(0) > 0)
    def _():
        for m in range(messages):
            outs[m][...] = dot(pick[offsets[m]:offsets[m] + sizes[m], :], tokens_ref[...]).astype(BF)


def pack(chip, adapters, slots, tokens, sizes, first_rows, chip_slots, steps=4):
    rows, width = tokens.shape
    block = width // steps
    spread = sum(round_up(s, 128) for s in sizes)
    return pl.pallas_call(
        functools.partial(pack_kernel, (sizes, first_rows, chip_slots, block - 1)),
        grid=(steps,),
        in_specs=[
            pl.BlockSpec(memory_space=pltpu.SMEM),
            pl.BlockSpec((1, rows), lambda i: (0, 0)),
            pl.BlockSpec((1, slots.shape[1]), lambda i: (0, 0)),
            pl.BlockSpec((rows, block), lambda i: (0, i)),
        ],
        out_specs=[pl.BlockSpec((s, block), lambda i: (0, i)) for s in sizes]
        + [pl.BlockSpec((rows, spread), lambda i: (0, 0))],
        out_shape=[jax.ShapeDtypeStruct((s, width), BF) for s in sizes] + [jax.ShapeDtypeStruct((rows, spread), BF)],
        scratch_shapes=[pltpu.VMEM((spread, rows), BF)],
        compiler_params=pltpu.CompilerParams(vmem_limit_bytes=VMEM_LIMIT),
        name="pack_rows",
    )(chip, adapters, slots, tokens)


def shrink_kernel(count, flag_lane, core_ref, *refs):
    messages, (mine, sibling), (out, place_out, flag_out) = refs[:count], refs[count:count + 2], refs[count + 2:count + 5]
    total, places = refs[count + 5:]
    step = pl.program_id(0)
    local = 2 * pl.num_programs(0)
    sizes = [m.shape[0] for m in messages]

    @pl.when(step == 0)
    def _():
        flag = jnp.zeros((1, 1), F32)
        start = 0
        for m, size in zip(messages, sizes):
            padded = round_up(size, 128)
            tail = m[size - 16:size, 0:padded].astype(F32)[15:16, :]
            same = lax.broadcasted_iota(jnp.int32, (size, padded), 0) == lax.broadcasted_iota(jnp.int32, (size, padded), 1)
            column = jnp.sum(jnp.where(same, tail, 0.0), axis=1, keepdims=True)
            places[start:start + size, :] = jnp.broadcast_to(column, (size, 128))
            block = m[size - 16:size, flag_lane - 127:flag_lane + 1].astype(F32)[15:16, :]
            last = lax.broadcasted_iota(jnp.int32, (1, 128), 1) == 127
            flag = jnp.maximum(flag, jnp.max(jnp.where(last, block, 0.0), axis=1, keepdims=True))
            start += size
        place_out[...] = places[...].astype(BF)
        flag_out[...] = jnp.broadcast_to(flag, (8, 128))
        total[...] = jnp.zeros_like(total)

    rows = messages[0][...] if count == 1 else jnp.concatenate([m[...] for m in messages], axis=0)
    place = places[...]
    core = core_ref[0]
    for weights, side in ((mine, core), (sibling, 1 - core)):
        product = dot(rows, jnp.concatenate([weights[0], weights[1]], axis=1))
        first = (side * local + 2 * step + 1).astype(F32)
        total[...] += jnp.where(place == first, product[:, :128], 0.0) + jnp.where(
            place == first + 1.0, product[:, 128:], 0.0
        )

    @pl.when(step == pl.num_programs(0) - 1)
    def _():
        out[...] = total[...].astype(BF)


def shrink(core, messages, mine, sibling, flag_lane):
    local, width, both = mine.shape
    rows = sum(m.shape[0] for m in messages)
    whole = [pl.BlockSpec(m.shape, lambda i: (0, 0)) for m in messages]
    pair = pl.BlockSpec((2, width, both), lambda i: (i, 0, 0))
    keep = pl.BlockSpec((rows, both), lambda i: (0, 0))
    return pl.pallas_call(
        functools.partial(shrink_kernel, len(messages), flag_lane),
        grid=(local // 2,),
        in_specs=[pl.BlockSpec(memory_space=pltpu.SMEM)] + whole + [pair, pair],
        out_specs=[keep, keep, pl.BlockSpec((8, 128), lambda i: (0, 0))],
        out_shape=[
            jax.ShapeDtypeStruct((rows, both), BF),
            jax.ShapeDtypeStruct((rows, both), BF),
            jax.ShapeDtypeStruct((8, 128), F32),
        ],
        scratch_shapes=[pltpu.VMEM((rows, both), F32), pltpu.VMEM((rows, both), F32)],
        compiler_params=pltpu.CompilerParams(vmem_limit_bytes=VMEM_LIMIT),
        name="shrink_rows",
    )(core, *messages, mine, sibling)


def grow_kernel(shares, sizes, core_ref, *refs):
    parts, place_ref, mine, sibling = refs[:shares], refs[shares], refs[shares + 1], refs[shares + 2]
    outs = refs[shares + 3:]
    summed = parts[0][...].astype(F32)
    for part in parts[1:]:
        summed = summed + part[...].astype(F32)
    shrunk = summed.astype(BF).astype(F32)
    place = place_ref[...].astype(F32)
    local, _, rank, columns = mine.shape
    core = core_ref[0]
    low = lax.broadcasted_iota(jnp.int32, shrunk.shape, 1) < rank
    turned = pltpu.roll(shrunk, rank, 1)
    result = []
    for j in range(2):
        twice = jnp.where(low, shrunk, turned) if j == 0 else jnp.where(low, turned, shrunk)
        total = None
        for weights, side in ((mine, core), (sibling, 1 - core)):
            left = []
            for e in range(0, local, 2):
                first = (side * local + e + 1).astype(F32)
                wanted = jnp.where(low, first, first + 1.0)
                left.append(jnp.where(place == wanted, twice, 0.0).astype(BF))
            right = weights[:, j].reshape(local * rank, columns)
            product = dot(jnp.concatenate(left, axis=1), right)
            total = product if total is None else total + product
        result.append((adapter_scale * total).astype(BF))
    start = 0
    for out, size in zip(outs, sizes):
        out[:, :columns] = result[0][start:start + size, :]
        out[:, columns:] = result[1][start:start + size, :]
        start += size


def grow(core, parts, place, mine, sibling, sizes):
    columns = mine.shape[3]
    vmem = pl.BlockSpec(memory_space=pltpu.VMEM)
    return pl.pallas_call(
        functools.partial(grow_kernel, len(parts), sizes),
        in_specs=[pl.BlockSpec(memory_space=pltpu.SMEM)] + [vmem] * (len(parts) + 3),
        out_specs=[vmem] * len(sizes),
        out_shape=[jax.ShapeDtypeStruct((s, 2 * columns), BF) for s in sizes],
        compiler_params=pltpu.CompilerParams(vmem_limit_bytes=VMEM_LIMIT),
        name="grow_rows",
    )(core, *parts, place, mine, sibling)


def place_kernel(sizes, spread_ref, *refs):
    updates, out = refs[:-1], refs[-1]
    total = None
    start = 0
    for update, size in zip(updates, sizes):
        padded = round_up(size, 128)
        rows = update[...]
        if padded > size:
            rows = jnp.concatenate([rows, jnp.zeros((padded - size, rows.shape[1]), rows.dtype)], axis=0)
        product = dot(spread_ref[:, start:start + padded], rows)
        total = product if total is None else total + product
        start += padded
    out[...] = total


def place_rows(spread, updates):
    sizes = tuple(u.shape[0] for u in updates)
    vmem = pl.BlockSpec(memory_space=pltpu.VMEM)
    return pl.pallas_call(
        functools.partial(place_kernel, sizes),
        in_specs=[vmem] * (len(updates) + 1),
        out_specs=vmem,
        out_shape=jax.ShapeDtypeStruct((spread.shape[0], updates[0].shape[1]), F32),
        compiler_params=pltpu.CompilerParams(vmem_limit_bytes=VMEM_LIMIT),
        name="place_rows",
    )(spread, *updates)


def exchange(array, axis, shift):
    size = lax.axis_size(axis)
    return lax.ppermute(array, axis, [(i, i ^ shift) for i in range(size)])


def after(array, *others):
    return lax.optimization_barrier((array,) + others)[0]


def bits(value):
    return bin(value).count("1")


def per_device(
    tokens,
    row_adapter_index,
    adapter_storage_slot,
    key_value_base_weight,
    adapter_down_weight,
    adapter_up_weight,
):
    row_count, width = tokens.shape
    local = adapter_down_weight.shape[0]
    groups = lax.axis_size("dp")
    blocks = lax.axis_size("tensor")
    experts = local * groups
    chips = groups // 2
    capacity = max(2, 2 * row_count // experts)
    chip_slots = 2 * local
    full = chip_slots * capacity

    me = lax.axis_index("dp").astype(jnp.int32)
    chip, core = (me // 2).reshape(1), (me % 2).reshape(1)
    adapters = row_adapter_index.reshape(1, row_count)
    slots = adapter_storage_slot.reshape(1, experts)
    flag_lane = width // 4 - 1

    down_sibling = exchange(adapter_down_weight, "dp", 1)
    up_sibling = exchange(adapter_up_weight, "dp", 1)

    near = [m for m in range(chips) if bits(m) <= 1]
    far = [m for m in range(chips) if bits(m) > 1]

    def update_of(sizes, first_rows, meanwhile):
        packed = pack(chip, adapters, slots, tokens, sizes, first_rows, chip_slots)
        sent, spread = list(packed[:-1]), packed[-1]
        arrived, returned = {0: sent[0]}, {}
        for m in near[1:]:
            arrived[m] = exchange(sent[m], "dp", 2 * m)
        held = meanwhile(sent)
        for m in far:
            arrived[m] = exchange(after(sent[m], held) if held is not None else sent[m], "dp", 2 * m)
        for part in (near, far):
            if not part:
                continue
            group = [arrived[m] for m in part]
            share, place, flag = shrink(core, group, adapter_down_weight, down_sibling, flag_lane)
            shares = [share] + [exchange(share, "tensor", t) for t in range(1, blocks)]
            grown = grow(core, shares, place, adapter_up_weight, up_sibling, tuple(sizes[m] for m in part))
            for m, update in zip(part, grown):
                returned[m] = update if m == 0 else exchange(update, "dp", 2 * m)
        return place_rows(spread, [returned[m] for m in range(chips)])

    base = []

    def base_part(j):
        partial = dot(tokens, key_value_base_weight[:, j, :])
        return partial.reshape(row_count, blocks, partial.shape[1] // blocks)

    def reduce_part(partial):
        t = lax.axis_index("tensor")
        step = 1
        while step < blocks:
            halves = partial.reshape(row_count, partial.shape[1] // 2, 2, partial.shape[2])
            bit = (t // step) % 2
            send = lax.dynamic_index_in_dim(halves, 1 - bit, 2, keepdims=False).astype(BF)
            keep = lax.dynamic_index_in_dim(halves, bit, 2, keepdims=False)
            partial = keep + exchange(send, "tensor", step).astype(F32)
            step *= 2
        return partial[:, 0, :]

    def meanwhile(sent):
        parts = [base_part(j) for j in range(2)]
        base.extend(reduce_part(p) for p in parts)
        return parts[1]

    message = round_up(full + 1, 16)
    update = update_of((message,) * chips, (0,) * chips, meanwhile)
    summed = jnp.stack(base, axis=1) + update.reshape(row_count, 2, update.shape[1] // 2)
    return summed.astype(BF)


def solution(mesh):
    placed = (
        P("dp", "tensor"),
        P("dp", None),
        P(),
        P("tensor", None, None),
        P("dp", "tensor", None),
        P("dp", None, None, "tensor"),
    )
    return jax.shard_map(
        per_device, mesh=mesh, in_specs=placed, out_specs=P("dp", None, "tensor"), check_vma=False
    )
```

time: 154 us -> 164 us (1.065)
  blocking collectives: 90.6 us -> 0 us
  local copies, waits for them, and re-layouts: 14.8 us -> 72.4 us
  Pallas kernels: 0 us -> 27.1 us
  starting transfers between devices: 4.28 us -> 29.3 us
  between operations: 13.5 us -> 0.17 us
  other arithmetic: 2.77 us -> 4.85 us
    all_to_all x1 -> x0, blocking collectives: 54.3 us -> none  [per_device(): lax.all_to_all(outbox, 'dp', split_axis=0, concat_axis=0, tiled=True)]
    dot_general x0 -> x2, local copies, waits for them, and re-layouts: none -> 40.1 us  [dot(): lax.dot_general(a, b, (contract, ((), ())), preferred_element_type=F32)]
    psum x1 -> x0, blocking collectives: 36.3 us -> none  [per_device(): reduced_rows = lax.psum(pieces_sum, 'tensor').astype(jnp.bfloat16)]
    ppermute x0 -> x18, starting transfers between devices: none -> 29.3 us  [exchange(): return lax.ppermute(array, axis, [(i, i ^ shift) for i in range(size)])]
    pallas_call x0 -> x6, Pallas kernels: none -> 27.1 us  [the longest x2 16.8 us: shrink(): pl.pallas_call(functools.partial(shrink_kernel, len(messages), flag_lane)...]
    slice x1, local copies, waits for them, and re-layouts: 0.23 us -> 17.8 us  [base_part(): partial = dot(tokens, key_value_base_weight[:, j, :])]
    ppermute x0 -> x18, waiting for transfers between devices: none -> 16.9 us  [exchange(): return lax.ppermute(array, axis, [(i, i ^ shift) for i in range(size)])]
    all_to_all x1 -> x0, waiting for transfers between devices: 15.4 us -> none  [per_device(): lax.all_to_all(adapter_delta, 'dp', split_axis=0, concat_axis=0, tiled=True)]
  transfers between devices with their start and end apart: 2 -> 18, of which waited for: 1 -> 4; matrix products, arithmetic and copies ran while one was open for 10% -> 49% of each run, Pallas kernels for 0% -> 12%
where the time goes in v1:
time: 164 us; the launch traced here: 162 us
  local copies, waits for them, and re-layouts  72.4 us (44%)
  starting transfers between devices  29.3 us (18%)
  Pallas kernels  27.1 us (17%)
  waiting for transfers between devices  16.9 us (10%)
  matrix products  11.7 us (7%)
  other arithmetic  4.85 us (3%)
    dot_general x2, local copies, waits for them, and re-layouts, dot(): lax.dot_general(a, b, (contract, ((), ())), preferred_element_type=F32)  40.1 us
    ppermute x18, starting transfers between devices, exchange(): return lax.ppermute(array, axis, [(i, i ^ shift) for i in range(size)])  29.3 us
    slice x1, local copies, waits for them, and re-layouts, base_part(): partial = dot(tokens, key_value_base_weight[:, j, :])  17.8 us
    ppermute x18, waiting for transfers between devices, exchange(): return lax.ppermute(array, axis, [(i, i ^ shift) for i in range(size)])  16.9 us
    pallas_call x2, Pallas kernels, shrink(): pl.pallas_call(functools.partial(shrink_kernel, len(messages), flag_lane)...  16.8 us
    dot_general x2, matrix products, dot(): lax.dot_general(a, b, (contract, ((), ())), preferred_element_type=F32)  11.7 us
    unnamed x40, local copies, waits for them, and re-layouts  8.64 us
    pallas_call x1, Pallas kernels, pack(): pl.pallas_call(functools.partial(pack_kernel, (sizes, first_rows, chip_sl...  6.44 us
  transfers between devices with their start and end apart: 18, of which 4 were waited for; matrix products, arithmetic and copies ran while one was open for 49% of the time, Pallas kernels for 12%

profile of v1, /device:TPU:0, one launch (start us, length us, event | category | flops | bytes accessed | tf_op | source)
XLA Modules:
  0.0 162.4 jit_solution(176046918431153320)
XLA Ops:
  1.3 6.4 %pack_rows.1 = (bf16[272,2048]{1,0:T(8,128)(2,1)S(1)}, bf16[272,2048]{1,0:T(8,128)(2,1)}, bf16[272,2048]{1,0:T(8,128)(2,1)}, bf16[272,2048]{1,0:T(8,128)(2,1)S(1)}, bf16[512,1536]{1,0:T(8,128)(2,1)S(1)}) custom-call(s32[1]{0:T(128)} %bitcast.13.place_ref, s32[1,512]{1,0:T(1,128)S(1)} %bitcast.43, s32[1,64]{1,0:T(1,128)S(1)} %bitcast.44, ...), custom_call_target="tpu_custom_call" | custom-call | tf_op jit(solution)/shard_map/pack_rows/pallas_call | solution.py:78
  7.8 3.9 %collective-permute-start.13 = (bf16[272,2048]{1,0:T(8,128)(2,1)S(1)}, bf16[272,2048]{1,0:T(8,128)(2,1)}, u32[]{:S(2)}, u32[]{:S(2)}) collective-permute-start(bf16[272,2048]{1,0:T(8,128)(2,1)S(1)} %get-tuple-element.26), channel_id=1, source_target_pairs={{0,24},{4,28},{8,16},{12,20},{16,8},{20,12},{24,0},{28,4},{1,25},{... | collective-permute-start | bytes 3342344 | tf_op jit(solution)/shard_map/ppermute | solution.py:234
  11.7 17.8 %fusion.7 = (bf16[2048,1,1024]{2,1,0:T(2,128)(2,1)}, bf16[2048,1,1024]{2,1,0:T(2,128)(2,1)}) fusion(bf16[2048,2,1024]{2,1,0:T(2,128)(2,1)} %param.9), kind=kLoop, calls=%fused_computation.16 | loop fusion | bytes 16777216 | tf_op jit(solution)/shard_map/slice | solution.py:298
  29.5 20.1 %copy.24 = bf16[2048,1,1024]{0,2,1:T(8,128)(2,1)} copy(bf16[2048,1,1024]{2,1,0:T(2,128)(2,1)} %get-tuple-element.29) | data formatting | bytes 8388608 | tf_op jit(solution)/shard_map/dot_general | solution.py:21
  49.6 6.5 %fusion.2 = f32[512,2,2,256]{3,0,2,1:T(8,128)} fusion(bf16[2,2,256,2048]{3,2,1,0:T(8,128)(2,1)} %bitcast.45, bf16[512,2048]{1,0:T(8,128)(2,1)} %tokens_ref.1), kind=kOutput, calls=%fused_computation.2 | convolution fusion | flops 2147483648 | bytes 8388608 | tf_op jit(solution)/shard_map/dot_general | solution.py:21
  56.1 2.1 %fusion.5 = bf16[512,2,256]{2,0,1:T(8,128)(2,1)} fusion(f32[512,2,2,256]{3,0,2,1:T(8,128)} %fusion.2, s32[]{:T(128)S(6)} %select_n.49), kind=kLoop, calls=%fused_computation.10 | loop fusion | bytes 1048580 | tf_op jit(solution)/shard_map/convert_element_type | solution.py:307
  58.2 1.6 collective-permute-start
  60.8 20.1 %copy.23 = bf16[2048,1,1024]{0,2,1:T(8,128)(2,1)} copy(bf16[2048,1,1024]{2,1,0:T(2,128)(2,1)} %get-tuple-element.30) | data formatting | bytes 8388608 | tf_op jit(solution)/shard_map/dot_general | solution.py:21
  80.8 5.2 %fusion = f32[512,2,2,256]{3,0,2,1:T(8,128)S(1)} fusion(bf16[2,2,256,2048]{3,2,1,0:T(8,128)(2,1)} %bitcast.46, bf16[512,2048]{1,0:T(8,128)(2,1)} %tokens_ref.1), kind=kOutput, calls=%fused_computation | convolution fusion | flops 2147483648 | bytes 8388608 | tf_op jit(solution)/shard_map/dot_general | solution.py:21
  86.1 0.9 fusion.6
  87.6 1.5 bitcast_add_fusion.2
  89.1 2.6 %copy-done = bf16[8,2048,128]{2,1,0:T(8,128)(2,1)S(1)} copy-done((bf16[8,2048,128]{2,1,0:T(8,128)(2,1)S(1)}, bf16[8,2048,128]{2,1,0:T(8,128)(2,1)}, u32[]{:S(2)}) %copy-start) | copy-done | bytes 4194328
  91.7 6.0 %shrink_rows.3 = (bf16[272,128]{1,0:T(8,128)(2,1)S(1)}, bf16[272,128]{1,0:T(8,128)(2,1)S(1)}, f32[8,128]{1,0:T(8,128)}) custom-call(s32[1]{0:T(128)} %bitcast.16.core_ref, bf16[272,2048]{1,0:T(8,128)(2,1)} %collective-permute-done.13.refs_0_, bf16[8,2048,128]{2,1,0:T(8,128)(2,1)S(1)} %copy-done, bf16[8,2048,128]{2,1,0:T(8,128)(2,1)} %collective-permute-done.6.refs_4_.refs_2_), custom_call_target="tpu_custom_call" | custom-call | tf_op jit(solution)/shard_map/shrink_rows/pallas_call | solution.py:142
  97.7 1.6 collective-permute-start.14
  100.0 2.6 %collective-permute-start.1 = (bf16[512,1,256]{2,0,1:T(8,128)(2,1)}, bf16[512,1,256]{2,0,1:T(8,128)(2,1)}, u32[]{:S(2)}, u32[]{:S(2)}) collective-permute-start(bf16[512,1,256]{2,0,1:T(8,128)(2,1)} %dynamic-slice_convert_fusion.2), channel_id=1, source_target_pairs={{0,2},{1,3},{2,0},{3,1},{4,6},{5,7},{6,4},{7,5},{8,10},{9,11},{10,... | collective-permute-start | bytes 786440 | tf_op jit(solution)/shard_map/ppermute | solution.py:234
  103.0 10.8 %shrink_rows.2 = (bf16[816,128]{1,0:T(8,128)(2,1)S(1)}, bf16[816,128]{1,0:T(8,128)(2,1)S(1)}, f32[8,128]{1,0:T(8,128)}) custom-call(s32[1]{0:T(128)} %bitcast.16.core_ref, bf16[272,2048]{1,0:T(8,128)(2,1)S(1)} %copy-done.3, bf16[272,2048]{1,0:T(8,128)(2,1)} %collective-permute-done.4.refs_1_, bf16[272,2048]{1,0:T(8,128)(2,1)} %collective-permute-done.5.refs_2_, ...), custom_call_target="tpu_custom_call" | custom-call | tf_op jit(solution)/shard_map/shrink_rows/pallas_call | solution.py:142
  114.3 2.6 %collective-permute-start.8 = (bf16[816,128]{1,0:T(8,128)(2,1)S(1)}, bf16[816,128]{1,0:T(8,128)(2,1)S(1)}, u32[]{:S(2)}, u32[]{:S(2)}) collective-permute-start(bf16[816,128]{1,0:T(8,128)(2,1)S(1)} %get-tuple-element.21.refs_0_), channel_id=1, source_target_pairs={{0,2},{1,3},{2,0},{3,1},{4,6},{5,7},{6,4},{7,5},{8,10},{9,11},{10,... | collective-permute-start | bytes 626696 | tf_op jit(solution)/shard_map/ppermute | solution.py:234
  116.9 1.3 collective-permute-start.9
  118.3 1.2 bitcast_add_fusion.1
  119.5 2.5 %collective-permute-start.16 = (bf16[272,128]{1,0:T(8,128)(2,1)S(1)}, bf16[272,128]{1,0:T(8,128)(2,1)S(1)}, u32[]{:S(2)}, u32[]{:S(2)}) collective-permute-start(bf16[272,128]{1,0:T(8,128)(2,1)S(1)} %get-tuple-element.27.refs_0_), channel_id=1, source_target_pairs={{0,3},{1,2},{2,1},{3,0},{4,7},{5,6},{6,5},{7,4},{8,11},{9,10},{10,... | collective-permute-start | bytes 208904 | tf_op jit(solution)/shard_map/ppermute | solution.py:234
  122.8 10.4 %collective-permute-done.16.refs_3_ = bf16[272,128]{1,0:T(8,128)(2,1)S(1)} collective-permute-done((bf16[272,128]{1,0:T(8,128)(2,1)S(1)}, bf16[272,128]{1,0:T(8,128)(2,1)S(1)}, u32[]{:S(2)}, u32[]{:S(2)}) %collective-permute-start.16) | collective-permute-done | bytes 69664 | tf_op jit(solution)/shard_map/ppermute | solution.py:234
  133.8 7.6 %collective-permute-start.3 = (bf16[512,1,256]{2,0,1:T(8,128)(2,1)}, bf16[512,1,256]{2,0,1:T(8,128)(2,1)}, u32[]{:S(2)}, u32[]{:S(2)}) collective-permute-start(bf16[512,1,256]{2,0,1:T(8,128)(2,1)} %dynamic-slice_convert_fusion.1), channel_id=1, source_target_pairs={{0,2},{1,3},{2,0},{3,1},{4,6},{5,7},{6,4},{7,5},{8,10},{9,11},{10,... | collective-permute-start | bytes 786440 | tf_op jit(solution)/shard_map/ppermute | solution.py:234
  142.3 0.9 copy-done.7
  143.1 0.9 copy-done.9
  145.4 2.5 %collective-permute-start.17 = (bf16[272,512]{1,0:T(8,128)(2,1)S(1)}, bf16[272,512]{1,0:T(8,128)(2,1)S(1)}, u32[]{:S(2)}, u32[]{:S(2)}) collective-permute-start(bf16[272,512]{1,0:T(8,128)(2,1)S(1)} %grow_rows.3), channel_id=1, source_target_pairs={{0,24},{4,28},{8,16},{12,20},{16,8},{20,12},{24,0},{28,4},{1,25},{... | collective-permute-start | bytes 835592 | tf_op jit(solution)/shard_map/ppermute | solution.py:234
  148.0 2.0 %grow_rows.2 = (bf16[272,512]{1,0:T(8,128)(2,1)S(1)}, bf16[272,512]{1,0:T(8,128)(2,1)S(1)}, bf16[272,512]{1,0:T(8,128)(2,1)S(1)}) custom-call(s32[1]{0:T(128)} %bitcast.16.core_ref, bf16[816,128]{1,0:T(8,128)(2,1)S(1)} %get-tuple-element.21.refs_0_, bf16[816,128]{1,0:T(8,128)(2,1)S(1)} %collective-permute-done.7.refs_1_, ...), custom_call_target="tpu_custom_call" | custom-call | tf_op jit(solution)/shard_map/grow_rows/pallas_call | solution.py:194
  151.1 1.0 convert_add_fusion.1
  152.7 1.0 convert_add_fusion
  153.7 2.3 %collective-permute-done.17.refs_3_ = bf16[272,512]{1,0:T(8,128)(2,1)S(1)} collective-permute-done((bf16[272,512]{1,0:T(8,128)(2,1)S(1)}, bf16[272,512]{1,0:T(8,128)(2,1)S(1)}, u32[]{:S(2)}, u32[]{:S(2)}) %collective-permute-start.17) | collective-permute-done | bytes 278560 | tf_op jit(solution)/shard_map/ppermute | solution.py:234
  156.0 3.6 %collective-permute-done.11.refs_1_ = bf16[272,512]{1,0:T(8,128)(2,1)S(1)} collective-permute-done((bf16[272,512]{1,0:T(8,128)(2,1)S(1)}, bf16[272,512]{1,0:T(8,128)(2,1)S(1)}, u32[]{:S(2)}, u32[]{:S(2)}) %collective-permute-start.11) | collective-permute-done | bytes 278560 | tf_op jit(solution)/shard_map/ppermute | solution.py:234
  159.6 1.2 place_rows.1
  161.0 1.3 copy.18
  (65 shorter events, 10.1 us)
Async XLA Ops:
  7.8 21.7 %copy-start.2 = (bf16[272,2048]{1,0:T(8,128)(2,1)}, bf16[272,2048]{1,0:T(8,128)(2,1)S(1)}, u32[]{:S(2)}) copy-start(bf16[272,2048]{1,0:T(8,128)(2,1)S(1)} %get-tuple-element.18.refs_0_) | copy-start | bytes 3342340
  7.8 79.3 %collective-permute-start.13 = (bf16[272,2048]{1,0:T(8,128)(2,1)S(1)}, bf16[272,2048]{1,0:T(8,128)(2,1)}, u32[]{:S(2)}, u32[]{:S(2)}) collective-permute-start(bf16[272,2048]{1,0:T(8,128)(2,1)S(1)} %get-tuple-element.26), channel_id=1, source_target_pairs={{0,24},{4,28},{8,16},{12,20},{16,8},{20,12},{24,0},{28,4},{1,25},{... | collective-permute-start | bytes 3342344 | tf_op jit(solution)/shard_map/ppermute | solution.py:234
  11.7 77.4 %collective-permute-start.6 = (bf16[8,2048,128]{2,1,0:T(8,128)(2,1)}, bf16[8,2048,128]{2,1,0:T(8,128)(2,1)}, u32[]{:S(2)}, u32[]{:S(2)}) collective-permute-start(bf16[8,2048,128]{2,1,0:T(8,128)(2,1)} %refs_1_.1), channel_id=1, source_target_pairs={{0,4},{4,0},{8,12},{12,8},{16,20},{20,16},{24,28},{28,24},{1,5},{5... | collective-permute-start | bytes 12582920 | tf_op jit(solution)/shard_map/ppermute | solution.py:234
  58.2 28.8 %collective-permute-start = (bf16[512,2,256]{2,0,1:T(8,128)(2,1)}, bf16[512,2,256]{2,0,1:T(8,128)(2,1)}, u32[]{:S(2)}, u32[]{:S(2)}) collective-permute-start(bf16[512,2,256]{2,0,1:T(8,128)(2,1)} %fusion.5), channel_id=1, source_target_pairs={{0,1},{1,0},{2,3},{3,2},{4,5},{5,4},{6,7},{7,6},{8,9},{9,8},{10,11... | collective-permute-start | bytes 1572872 | tf_op jit(solution)/shard_map/ppermute | solution.py:234
  59.7 40.3 %collective-permute-start.4 = (bf16[272,2048]{1,0:T(8,128)(2,1)}, bf16[272,2048]{1,0:T(8,128)(2,1)}, u32[]{:S(2)}, u32[]{:S(2)}) collective-permute-start(bf16[272,2048]{1,0:T(8,128)(2,1)} %get-tuple-element.19), channel_id=1, source_target_pairs={{0,8},{4,12},{8,0},{12,4},{16,24},{20,28},{24,16},{28,20},{1,9},{5... | collective-permute-start | bytes 3342344 | tf_op jit(solution)/shard_map/ppermute | solution.py:234
  60.3 42.4 %collective-permute-start.5 = (bf16[272,2048]{1,0:T(8,128)(2,1)}, bf16[272,2048]{1,0:T(8,128)(2,1)}, u32[]{:S(2)}, u32[]{:S(2)}) collective-permute-start(bf16[272,2048]{1,0:T(8,128)(2,1)} %get-tuple-element.20), channel_id=1, source_target_pairs={{0,16},{4,20},{8,24},{12,28},{16,0},{20,4},{24,8},{28,12},{1,17},{... | collective-permute-start | bytes 3342344 | tf_op jit(solution)/shard_map/ppermute | solution.py:234
  80.8 6.8 %copy-start.1 = (bf16[8,2,64,256]{3,2,1,0:T(8,128)(2,1)S(1)}, bf16[8,2,64,256]{3,2,1,0:T(8,128)(2,1)}, u32[]{:S(2)}) copy-start(bf16[8,2,64,256]{3,2,1,0:T(8,128)(2,1)} %refs_5_.3) | copy-start | bytes 1572868
  86.1 1.5 copy-start.18
  87.0 26.8 %collective-permute-start.2 = (bf16[512,2,256]{2,0,1:T(8,128)(2,1)}, bf16[512,2,256]{2,0,1:T(8,128)(2,1)}, u32[]{:S(2)}, u32[]{:S(2)}) collective-permute-start(bf16[512,2,256]{2,0,1:T(8,128)(2,1)} %fusion.6), channel_id=1, source_target_pairs={{0,1},{1,0},{2,3},{3,2},{4,5},{5,4},{6,7},{7,6},{8,9},{9,8},{10,11... | collective-permute-start | bytes 1572872 | tf_op jit(solution)/shard_map/ppermute | solution.py:234
  87.6 26.7 %collective-permute-start.10 = (bf16[8,2,64,256]{3,2,1,0:T(8,128)(2,1)S(1)}, bf16[8,2,64,256]{3,2,1,0:T(8,128)(2,1)S(1)}, u32[]{:S(2)}, u32[]{:S(2)}) collective-permute-start(bf16[8,2,64,256]{3,2,1,0:T(8,128)(2,1)S(1)} %copy-done.1), channel_id=1, source_target_pairs={{0,4},{4,0},{8,12},{12,8},{16,20},{20,16},{24,28},{28,24},{1,5},{5... | collective-permute-start | bytes 1572872 | tf_op jit(solution)/shard_map/ppermute | solution.py:234
  89.1 10.2 %copy-start.14 = (f32[512,2,256]{2,0,1:T(8,128)}, f32[512,2,256]{2,0,1:T(8,128)S(1)}, u32[]{:S(2)}) copy-start(f32[512,2,256]{2,0,1:T(8,128)S(1)} %bitcast_add_fusion.2) | copy-start | bytes 3145732
  89.1 2.6 %copy-start = (bf16[8,2048,128]{2,1,0:T(8,128)(2,1)S(1)}, bf16[8,2048,128]{2,1,0:T(8,128)(2,1)}, u32[]{:S(2)}) copy-start(bf16[8,2048,128]{2,1,0:T(8,128)(2,1)} %refs_1_.1) | copy-start | bytes 12582916
  91.7 11.3 %copy-start.3 = (bf16[272,2048]{1,0:T(8,128)(2,1)S(1)}, bf16[272,2048]{1,0:T(8,128)(2,1)}, u32[]{:S(2)}) copy-start(bf16[272,2048]{1,0:T(8,128)(2,1)} %copy-done.2) | copy-start | bytes 3342340
  97.7 16.1 %copy-start.4 = (bf16[272,128]{1,0:T(8,128)(2,1)}, bf16[272,128]{1,0:T(8,128)(2,1)S(1)}, u32[]{:S(2)}) copy-start(bf16[272,128]{1,0:T(8,128)(2,1)S(1)} %get-tuple-element.28.refs_4_) | copy-start | bytes 208900
  97.7 19.2 %collective-permute-start.14 = (bf16[272,128]{1,0:T(8,128)(2,1)S(1)}, bf16[272,128]{1,0:T(8,128)(2,1)S(1)}, u32[]{:S(2)}, u32[]{:S(2)}) collective-permute-start(bf16[272,128]{1,0:T(8,128)(2,1)S(1)} %get-tuple-element.27.refs_0_), channel_id=1, source_target_pairs={{0,1},{1,0},{2,3},{3,2},{4,5},{5,4},{6,7},{7,6},{8,9},{9,8},{10,11... | collective-permute-start | bytes 208904 | tf_op jit(solution)/shard_map/ppermute | solution.py:234
  100.0 51.1 %collective-permute-start.1 = (bf16[512,1,256]{2,0,1:T(8,128)(2,1)}, bf16[512,1,256]{2,0,1:T(8,128)(2,1)}, u32[]{:S(2)}, u32[]{:S(2)}) collective-permute-start(bf16[512,1,256]{2,0,1:T(8,128)(2,1)} %dynamic-slice_convert_fusion.2), channel_id=1, source_target_pairs={{0,2},{1,3},{2,0},{3,1},{4,6},{5,7},{6,4},{7,5},{8,10},{9,11},{10,... | collective-permute-start | bytes 786440 | tf_op jit(solution)/shard_map/ppermute | solution.py:234
  102.6 16.8 %collective-permute-start.15 = (bf16[272,128]{1,0:T(8,128)(2,1)S(1)}, bf16[272,128]{1,0:T(8,128)(2,1)S(1)}, u32[]{:S(2)}, u32[]{:S(2)}) collective-permute-start(bf16[272,128]{1,0:T(8,128)(2,1)S(1)} %get-tuple-element.27.refs_0_), channel_id=1, source_target_pairs={{0,2},{1,3},{2,0},{3,1},{4,6},{5,7},{6,4},{7,5},{8,10},{9,11},{10,... | collective-permute-start | bytes 208904 | tf_op jit(solution)/shard_map/ppermute | solution.py:234
  103.0 15.3 %copy-start.19 = (f32[512,2,2,256]{3,0,2,1:T(8,128)S(1)}, f32[512,2,2,256]{3,0,2,1:T(8,128)}, u32[]{:S(2)}) copy-start(f32[512,2,2,256]{3,0,2,1:T(8,128)} %copy-done.18) | copy-start | bytes 6291460
  113.8 31.6 %collective-permute-start.7 = (bf16[816,128]{1,0:T(8,128)(2,1)S(1)}, bf16[816,128]{1,0:T(8,128)(2,1)S(1)}, u32[]{:S(2)}, u32[]{:S(2)}) collective-permute-start(bf16[816,128]{1,0:T(8,128)(2,1)S(1)} %get-tuple-element.21.refs_0_), channel_id=1, source_target_pairs={{0,1},{1,0},{2,3},{3,2},{4,5},{5,4},{6,7},{7,6},{8,9},{9,8},{10,11... | collective-permute-start | bytes 626696 | tf_op jit(solution)/shard_map/ppermute | solution.py:234
  114.3 33.6 %collective-permute-start.8 = (bf16[816,128]{1,0:T(8,128)(2,1)S(1)}, bf16[816,128]{1,0:T(8,128)(2,1)S(1)}, u32[]{:S(2)}, u32[]{:S(2)}) collective-permute-start(bf16[816,128]{1,0:T(8,128)(2,1)S(1)} %get-tuple-element.21.refs_0_), channel_id=1, source_target_pairs={{0,2},{1,3},{2,0},{3,1},{4,6},{5,7},{6,4},{7,5},{8,10},{9,11},{10,... | collective-permute-start | bytes 626696 | tf_op jit(solution)/shard_map/ppermute | solution.py:234
  116.9 16.2 %copy-start.6 = (bf16[272,128]{1,0:T(8,128)(2,1)}, bf16[272,128]{1,0:T(8,128)(2,1)S(1)}, u32[]{:S(2)}) copy-start(bf16[272,128]{1,0:T(8,128)(2,1)S(1)} %collective-permute-done.14.refs_1_) | copy-start | bytes 208900
  116.9 31.0 %collective-permute-start.9 = (bf16[816,128]{1,0:T(8,128)(2,1)S(1)}, bf16[816,128]{1,0:T(8,128)(2,1)}, u32[]{:S(2)}, u32[]{:S(2)}) collective-permute-start(bf16[816,128]{1,0:T(8,128)(2,1)S(1)} %get-tuple-element.21.refs_0_), channel_id=1, source_target_pairs={{0,3},{1,2},{2,1},{3,0},{4,7},{5,6},{6,5},{7,4},{8,11},{9,10},{10,... | collective-permute-start | bytes 626696 | tf_op jit(solution)/shard_map/ppermute | solution.py:234
  119.4 13.7 %copy-start.16 = (f32[512,2,256]{2,0,1:T(8,128)}, f32[512,2,256]{2,0,1:T(8,128)S(1)}, u32[]{:S(2)}) copy-start(f32[512,2,256]{2,0,1:T(8,128)S(1)} %bitcast_add_fusion.1) | copy-start | bytes 3145732
  119.5 13.7 %copy-start.8 = (bf16[272,128]{1,0:T(8,128)(2,1)}, bf16[272,128]{1,0:T(8,128)(2,1)S(1)}, u32[]{:S(2)}) copy-start(bf16[272,128]{1,0:T(8,128)(2,1)S(1)} %collective-permute-done.15.refs_2_) | copy-start | bytes 208900
  119.5 13.6 %collective-permute-start.16 = (bf16[272,128]{1,0:T(8,128)(2,1)S(1)}, bf16[272,128]{1,0:T(8,128)(2,1)S(1)}, u32[]{:S(2)}, u32[]{:S(2)}) collective-permute-start(bf16[272,128]{1,0:T(8,128)(2,1)S(1)} %get-tuple-element.27.refs_0_), channel_id=1, source_target_pairs={{0,3},{1,2},{2,1},{3,0},{4,7},{5,6},{6,5},{7,4},{8,11},{9,10},{10,... | collective-permute-start | bytes 208904 | tf_op jit(solution)/shard_map/ppermute | solution.py:234
  133.8 18.9 %collective-permute-start.3 = (bf16[512,1,256]{2,0,1:T(8,128)(2,1)}, bf16[512,1,256]{2,0,1:T(8,128)(2,1)}, u32[]{:S(2)}, u32[]{:S(2)}) collective-permute-start(bf16[512,1,256]{2,0,1:T(8,128)(2,1)} %dynamic-slice_convert_fusion.1), channel_id=1, source_target_pairs={{0,2},{1,3},{2,0},{3,1},{4,6},{5,7},{6,4},{7,5},{8,10},{9,11},{10,... | collective-permute-start | bytes 786440 | tf_op jit(solution)/shard_map/ppermute | solution.py:234
  141.4 0.9 copy-start.5
  144.9 6.2 %copy-start.15 = (f32[512,2,256]{2,0,1:T(8,128)S(1)}, f32[512,2,256]{2,0,1:T(8,128)}, u32[]{:S(2)}) copy-start(f32[512,2,256]{2,0,1:T(8,128)} %copy-done.14) | copy-start | bytes 3145732
  145.4 7.3 %copy-start.17 = (f32[512,2,256]{2,0,1:T(8,128)S(1)}, f32[512,2,256]{2,0,1:T(8,128)}, u32[]{:S(2)}) copy-start(f32[512,2,256]{2,0,1:T(8,128)} %copy-done.16) | copy-start | bytes 3145732
  145.4 10.6 %collective-permute-start.17 = (bf16[272,512]{1,0:T(8,128)(2,1)S(1)}, bf16[272,512]{1,0:T(8,128)(2,1)S(1)}, u32[]{:S(2)}, u32[]{:S(2)}) collective-permute-start(bf16[272,512]{1,0:T(8,128)(2,1)S(1)} %grow_rows.3), channel_id=1, source_target_pairs={{0,24},{4,28},{8,16},{12,20},{16,8},{20,12},{24,0},{28,4},{1,25},{... | collective-permute-start | bytes 835592 | tf_op jit(solution)/shard_map/ppermute | solution.py:234
  150.0 9.6 %collective-permute-start.11 = (bf16[272,512]{1,0:T(8,128)(2,1)S(1)}, bf16[272,512]{1,0:T(8,128)(2,1)S(1)}, u32[]{:S(2)}, u32[]{:S(2)}) collective-permute-start(bf16[272,512]{1,0:T(8,128)(2,1)S(1)} %get-tuple-element.24), channel_id=1, source_target_pairs={{0,8},{4,12},{8,0},{12,4},{16,24},{20,28},{24,16},{28,20},{1,9},{5... | collective-permute-start | bytes 835592 | tf_op jit(solution)/shard_map/ppermute | solution.py:234
  150.6 9.0 %collective-permute-start.12 = (bf16[272,512]{1,0:T(8,128)(2,1)S(1)}, bf16[272,512]{1,0:T(8,128)(2,1)S(1)}, u32[]{:S(2)}, u32[]{:S(2)}) collective-permute-start(bf16[272,512]{1,0:T(8,128)(2,1)S(1)} %get-tuple-element.25), channel_id=1, source_target_pairs={{0,16},{4,20},{8,24},{12,28},{16,0},{20,4},{24,8},{28,12},{1,17},{... | collective-permute-start | bytes 835592 | tf_op jit(solution)/shard_map/ppermute | solution.py:234
  (6 other events, 4.6 us)

commit v2 on v1

--- a/solution.py
+++ b/solution.py
@@ -201,32 +201,90 @@
     )(core, *parts, place, mine, sibling)
 
 
-def place_kernel(sizes, spread_ref, *refs):
+def block_kernel(steps, count, block_ref, tokens_ref, weight_ref, *refs):
+    arrived, out, total = refs[:count], refs[count], refs[count + 1]
+    step = pl.program_id(0)
+    weight = jnp.swapaxes(weight_ref[...], 0, 1)
+    columns = weight.shape[2]
+
+    @pl.when(step == 0)
+    def _():
+        start = jnp.zeros(total.shape, F32)
+        for one in arrived:
+            start = start + one[...].astype(F32)
+        total[...] = start
+
+    for j in range(2):
+        total[:, j * columns:(j + 1) * columns] += dot(tokens_ref[...], weight[j])
+
+    @pl.when(step == steps - 1)
+    def _():
+        out[...] = total[...].astype(out.dtype)
+
+
+def base_block(block, tokens, weight, columns, arrived, dtype, steps=4):
+    rows, width = tokens.shape
+    if columns % 128:
+        part = lax.dynamic_slice_in_dim(weight, block[0] * columns, columns, 2)
+        total = dot(tokens, part.reshape(width, 2 * columns))
+        for one in arrived:
+            total = total + one.astype(F32)
+        return total.astype(dtype)
+    deep = width // steps
+    keep = pl.BlockSpec((rows, 2 * columns), lambda i, b: (0, 0))
+    return pl.pallas_call(
+        functools.partial(block_kernel, steps, len(arrived)),
+        grid_spec=pltpu.PrefetchScalarGridSpec(
+            num_scalar_prefetch=1,
+            grid=(steps,),
+            in_specs=[
+                pl.BlockSpec((rows, deep), lambda i, b: (0, i)),
+                pl.BlockSpec((deep, 2, columns), lambda i, b: (i, 0, b[0])),
+            ]
+            + [keep] * len(arrived),
+            out_specs=keep,
+            scratch_shapes=[pltpu.VMEM((rows, 2 * columns), F32)],
+        ),
+        out_shape=jax.ShapeDtypeStruct((rows, 2 * columns), dtype),
+        compiler_params=pltpu.CompilerParams(vmem_limit_bytes=VMEM_LIMIT),
+        name="base_block",
+    )(block, tokens, weight, *arrived)
+
+
+def finish_kernel(sizes, base_ref, spread_ref, *refs):
     updates, out = refs[:-1], refs[-1]
-    total = None
+    total = base_ref[...]
+    update_rows = jnp.zeros(total.shape, F32)
     start = 0
     for update, size in zip(updates, sizes):
         padded = round_up(size, 128)
         rows = update[...]
         if padded > size:
             rows = jnp.concatenate([rows, jnp.zeros((padded - size, rows.shape[1]), rows.dtype)], axis=0)
-        product = dot(spread_ref[:, start:start + padded], rows)
-        total = product if total is None else total + product
+        update_rows = update_rows + dot(spread_ref[:, start:start + padded], rows)
         start += padded
-    out[...] = total
-
-
-def place_rows(spread, updates):
+    total = total + update_rows
+    columns = out.shape[2]
+    if columns % 128:
+        out[:, 0, :] = total[:, :columns].astype(BF)
+        out[:, 1, :] = total[:, columns:].astype(BF)
+    else:
+        both = jnp.stack([total[:, :columns], total[:, columns:]], axis=0).astype(BF)
+        out[...] = jnp.swapaxes(both, 0, 1)
+
+
+def finish(base, spread, updates):
     sizes = tuple(u.shape[0] for u in updates)
+    rows, both = base.shape
     vmem = pl.BlockSpec(memory_space=pltpu.VMEM)
     return pl.pallas_call(
-        functools.partial(place_kernel, sizes),
-        in_specs=[vmem] * (len(updates) + 1),
+        functools.partial(finish_kernel, sizes),
+        in_specs=[vmem] * (len(updates) + 2),
         out_specs=vmem,
-        out_shape=jax.ShapeDtypeStruct((spread.shape[0], updates[0].shape[1]), F32),
-        compiler_params=pltpu.CompilerParams(vmem_limit_bytes=VMEM_LIMIT),
-        name="place_rows",
-    )(spread, *updates)
+        out_shape=jax.ShapeDtypeStruct((rows, 2, both // 2), BF),
+        compiler_params=pltpu.CompilerParams(vmem_limit_bytes=VMEM_LIMIT),
+        name="finish_rows",
+    )(base, spread, *updates)
 
 
 def exchange(array, axis, shift):
@@ -271,54 +329,46 @@
 
     near = [m for m in range(chips) if bits(m) <= 1]
     far = [m for m in range(chips) if bits(m) > 1]
-
-    def update_of(sizes, first_rows, meanwhile):
-        packed = pack(chip, adapters, slots, tokens, sizes, first_rows, chip_slots)
-        sent, spread = list(packed[:-1]), packed[-1]
-        arrived, returned = {0: sent[0]}, {}
-        for m in near[1:]:
-            arrived[m] = exchange(sent[m], "dp", 2 * m)
-        held = meanwhile(sent)
-        for m in far:
-            arrived[m] = exchange(after(sent[m], held) if held is not None else sent[m], "dp", 2 * m)
-        for part in (near, far):
-            if not part:
-                continue
-            group = [arrived[m] for m in part]
-            share, place, flag = shrink(core, group, adapter_down_weight, down_sibling, flag_lane)
-            shares = [share] + [exchange(share, "tensor", t) for t in range(1, blocks)]
-            grown = grow(core, shares, place, adapter_up_weight, up_sibling, tuple(sizes[m] for m in part))
-            for m, update in zip(part, grown):
-                returned[m] = update if m == 0 else exchange(update, "dp", 2 * m)
-        return place_rows(spread, [returned[m] for m in range(chips)])
-
-    base = []
-
-    def base_part(j):
-        partial = dot(tokens, key_value_base_weight[:, j, :])
-        return partial.reshape(row_count, blocks, partial.shape[1] // blocks)
-
-    def reduce_part(partial):
-        t = lax.axis_index("tensor")
-        step = 1
-        while step < blocks:
-            halves = partial.reshape(row_count, partial.shape[1] // 2, 2, partial.shape[2])
-            bit = (t // step) % 2
-            send = lax.dynamic_index_in_dim(halves, 1 - bit, 2, keepdims=False).astype(BF)
-            keep = lax.dynamic_index_in_dim(halves, bit, 2, keepdims=False)
-            partial = keep + exchange(send, "tensor", step).astype(F32)
-            step *= 2
-        return partial[:, 0, :]
-
-    def meanwhile(sent):
-        parts = [base_part(j) for j in range(2)]
-        base.extend(reduce_part(p) for p in parts)
-        return parts[1]
-
     message = round_up(full + 1, 16)
-    update = update_of((message,) * chips, (0,) * chips, meanwhile)
-    summed = jnp.stack(base, axis=1) + update.reshape(row_count, 2, update.shape[1] // 2)
-    return summed.astype(BF)
+    sizes, first_rows = (message,) * chips, (0,) * chips
+
+    packed = pack(chip, adapters, slots, tokens, sizes, first_rows, chip_slots)
+    sent, spread = list(packed[:-1]), packed[-1]
+    arrived, returned = {0: sent[0]}, {}
+    for m in near[1:]:
+        arrived[m] = exchange(sent[m], "dp", 2 * m)
+
+    columns = key_value_base_weight.shape[2] // blocks
+    t = lax.axis_index("tensor").astype(jnp.int32)
+    came = {}
+
+    def summands(r):
+        return [came[key] for key in sorted(came) if key[1] == r]
+
+    def base_of(r, dtype):
+        return base_block((t ^ r).reshape(1), tokens, key_value_base_weight, columns, summands(r), dtype)
+
+    order = sorted(range(1, blocks), key=lambda r: (r & -r, -r))
+    for r in order:
+        low = r & -r
+        if r == 2:
+            for m in far:
+                arrived[m] = exchange(after(sent[m], came_last), "dp", 2 * m)
+        part = base_of(r, BF)
+        came_last = part
+        came[(low, r ^ low)] = exchange(part, "tensor", low)
+
+    for part in (near, far):
+        if not part:
+            continue
+        group = [arrived[m] for m in part]
+        share, place, flag = shrink(core, group, adapter_down_weight, down_sibling, flag_lane)
+        shares = [share] + [exchange(share, "tensor", z) for z in range(1, blocks)]
+        grown = grow(core, shares, place, adapter_up_weight, up_sibling, tuple(sizes[m] for m in part))
+        for m, update in zip(part, grown):
+            returned[m] = update if m == 0 else exchange(update, "dp", 2 * m)
+    base = base_of(0, F32)
+    return finish(base, spread, [returned[m] for m in range(chips)])
 
 
 def solution(mesh):

time: 164 us -> 126 us (0.77)
  the two profiles are of different devices: /device:TPU:0 before, /device:TPU:8 now
where the time goes in v2:
time: 126 us
  waiting for transfers between devices  51.7 us (41%)
  Pallas kernels  47 us (37%)
  starting transfers between devices  19.9 us (16%)
  local copies, waits for them, and re-layouts  6.84 us (5%)
    ppermute x17, waiting for transfers between devices, exchange(): return lax.ppermute(array, axis, [(i, i ^ shift) for i in range(size)])  51.7 us
    ppermute x17, starting transfers between devices, exchange(): return lax.ppermute(array, axis, [(i, i ^ shift) for i in range(size)])  19.9 us
    pallas_call x4, Pallas kernels, base_block(): pl.pallas_call(functools.partial(block_kernel, steps, len(arrived)), grid...  19.8 us
    pallas_call x2, Pallas kernels, shrink(): pl.pallas_call(functools.partial(shrink_kernel, len(messages), flag_lane)...  16.5 us
    unnamed x24, local copies, waits for them, and re-layouts  6.84 us
    pallas_call x1, Pallas kernels, pack(): pl.pallas_call(functools.partial(pack_kernel, (sizes, first_rows, chip_sl...  6.76 us
  transfers between devices with their start and end apart: 17, of which 8 were waited for; matrix products, arithmetic and copies ran while one was open for 0% of the time, Pallas kernels for 36%

profile of v2, /device:TPU:8, one launch (start us, length us, event | category | flops | bytes accessed | tf_op | source)
XLA Modules:
  0.0 125.6 jit_solution(6355071677893946089)
XLA Ops:
  0.0 1.6 %copy-done = bf16[512,2048]{1,0:T(8,128)(2,1)S(1)} copy-done((bf16[512,2048]{1,0:T(8,128)(2,1)S(1)}, bf16[512,2048]{1,0:T(8,128)(2,1)}, u32[]{:S(2)}) %copy-start) | copy-done | bytes 2097176
  1.6 4.7 %base_block.4 = bf16[512,512]{1,0:T(8,128)(2,1)S(1)} custom-call(s32[1]{0:T(128)} %bitcast.1.block_ref, bf16[512,2048]{1,0:T(8,128)(2,1)S(1)} %copy-done, bf16[2048,2,1024]{2,1,0:T(2,128)(2,1)} %weight_ref.7), custom_call_target="tpu_custom_call" | custom-call | tf_op jit(solution)/shard_map/base_block/pallas_call | solution.py:235
  6.3 0.8 copy-done.8
  7.1 6.8 %pack_rows.1 = (bf16[272,2048]{1,0:T(8,128)(2,1)S(1)}, bf16[272,2048]{1,0:T(8,128)(2,1)}, bf16[272,2048]{1,0:T(8,128)(2,1)}, bf16[272,2048]{1,0:T(8,128)(2,1)}, bf16[512,1536]{1,0:T(8,128)(2,1)S(1)}) custom-call(s32[1]{0:T(128)} %bitcast.4.place_ref, s32[1,512]{1,0:T(1,128)S(1)} %bitcast.8, s32[1,64]{1,0:T(1,128)S(1)} %bitcast.9, bf16[512,2048]{1,0:T(8,128)(2,1)} %tokens_ref.9), custom_call_target="tpu_custom_call" | custom-call | tf_op jit(solution)/shard_map/pack_rows/pallas_call | solution.py:78
  13.9 1.2 copy-done.4
  15.0 1.1 copy-done.6
  16.1 2.4 %collective-permute-start.12 = (bf16[272,2048]{1,0:T(8,128)(2,1)}, bf16[272,2048]{1,0:T(8,128)(2,1)}, u32[]{:S(2)}, u32[]{:S(2)}) collective-permute-start(bf16[272,2048]{1,0:T(8,128)(2,1)} %get-tuple-element.28), channel_id=1, source_target_pairs={{0,24},{4,28},{8,16},{12,20},{16,8},{20,12},{24,0},{28,4},{1,25},{... | collective-permute-start | bytes 3342344 | tf_op jit(solution)/shard_map/ppermute | solution.py:292
  19.6 5.4 %base_block.5 = bf16[512,512]{1,0:T(8,128)(2,1)} custom-call(s32[1]{0:T(128)} %bitcast.3.block_ref, bf16[512,2048]{1,0:T(8,128)(2,1)S(1)} %copy-done.1, bf16[2048,2,1024]{2,1,0:T(2,128)(2,1)} %weight_ref.7), custom_call_target="tpu_custom_call" | custom-call | tf_op jit(solution)/shard_map/base_block/pallas_call | solution.py:235
  25.0 19.7 %collective-permute-done.12.refs_0_ = bf16[272,2048]{1,0:T(8,128)(2,1)} collective-permute-done((bf16[272,2048]{1,0:T(8,128)(2,1)}, bf16[272,2048]{1,0:T(8,128)(2,1)}, u32[]{:S(2)}, u32[]{:S(2)}) %collective-permute-start.12) | collective-permute-done | bytes 1114144 | tf_op jit(solution)/shard_map/ppermute | solution.py:292
  44.8 2.2 %copy-done.2 = bf16[8,2048,128]{2,1,0:T(8,128)(2,1)S(1)} copy-done((bf16[8,2048,128]{2,1,0:T(8,128)(2,1)S(1)}, bf16[8,2048,128]{2,1,0:T(8,128)(2,1)}, u32[]{:S(2)}) %copy-start.2) | copy-done | bytes 4194328
  47.0 5.9 %shrink_rows.3 = (bf16[272,128]{1,0:T(8,128)(2,1)S(1)}, bf16[272,128]{1,0:T(8,128)(2,1)S(1)}, f32[8,128]{1,0:T(8,128)}) custom-call(s32[1]{0:T(128)} %bitcast.7.core_ref, bf16[272,2048]{1,0:T(8,128)(2,1)} %collective-permute-done.12.refs_0_, bf16[8,2048,128]{2,1,0:T(8,128)(2,1)S(1)} %copy-done.2, bf16[8,2048,128]{2,1,0:T(8,128)(2,1)} %collective-permute-done.5.refs_4_.refs_2_), custom_call_target="tpu_custom_call" | custom-call | tf_op jit(solution)/shard_map/shrink_rows/pallas_call | solution.py:142
  52.8 2.0 %collective-permute-start.13 = (bf16[272,128]{1,0:T(8,128)(2,1)S(1)}, bf16[272,128]{1,0:T(8,128)(2,1)S(1)}, u32[]{:S(2)}, u32[]{:S(2)}) collective-permute-start(bf16[272,128]{1,0:T(8,128)(2,1)S(1)} %get-tuple-element.29.refs_0_), channel_id=1, source_target_pairs={{0,1},{1,0},{2,3},{3,2},{4,5},{5,4},{6,7},{7,6},{8,9},{9,8},{10,11... | collective-permute-start | bytes 208904 | tf_op jit(solution)/shard_map/ppermute | solution.py:292
  54.8 2.6 %collective-permute-start.14 = (bf16[272,128]{1,0:T(8,128)(2,1)S(1)}, bf16[272,128]{1,0:T(8,128)(2,1)S(1)}, u32[]{:S(2)}, u32[]{:S(2)}) collective-permute-start(bf16[272,128]{1,0:T(8,128)(2,1)S(1)} %get-tuple-element.29.refs_0_), channel_id=1, source_target_pairs={{0,2},{1,3},{2,0},{3,1},{4,6},{5,7},{6,4},{7,5},{8,10},{9,11},{10,... | collective-permute-start | bytes 208904 | tf_op jit(solution)/shard_map/ppermute | solution.py:292
  57.4 2.3 %collective-permute-done.1.refs_0_ = bf16[512,512]{1,0:T(8,128)(2,1)} collective-permute-done((bf16[512,512]{1,0:T(8,128)(2,1)}, bf16[512,512]{1,0:T(8,128)(2,1)}, u32[]{:S(2)}, u32[]{:S(2)}) %collective-permute-start.1) | collective-permute-done | bytes 524320 | tf_op jit(solution)/shard_map/ppermute | solution.py:292
  59.7 1.7 %collective-permute-start.15 = (bf16[272,128]{1,0:T(8,128)(2,1)S(1)}, bf16[272,128]{1,0:T(8,128)(2,1)S(1)}, u32[]{:S(2)}, u32[]{:S(2)}) collective-permute-start(bf16[272,128]{1,0:T(8,128)(2,1)S(1)} %get-tuple-element.29.refs_0_), channel_id=1, source_target_pairs={{0,3},{1,2},{2,1},{3,0},{4,7},{5,6},{6,5},{7,4},{8,11},{9,10},{10,... | collective-permute-start | bytes 208904 | tf_op jit(solution)/shard_map/ppermute | solution.py:292
  61.4 4.9 %base_block.6 = bf16[512,512]{1,0:T(8,128)(2,1)S(1)} custom-call(s32[1]{0:T(128)} %bitcast.2.block_ref, bf16[512,2048]{1,0:T(8,128)(2,1)S(1)} %copy-done.1, bf16[2048,2,1024]{2,1,0:T(2,128)(2,1)} %weight_ref.7, bf16[512,512]{1,0:T(8,128)(2,1)} %collective-permute-done.1.refs_0_), custom_call_target="tpu_custom_call" | custom-call | tf_op jit(solution)/shard_map/base_block/pallas_call | solution.py:235
  66.3 2.0 %collective-permute-done.3.refs_1_ = bf16[272,2048]{1,0:T(8,128)(2,1)} collective-permute-done((bf16[272,2048]{1,0:T(8,128)(2,1)}, bf16[272,2048]{1,0:T(8,128)(2,1)}, u32[]{:S(2)}, u32[]{:S(2)}) %collective-permute-start.3) | collective-permute-done | bytes 1114144 | tf_op jit(solution)/shard_map/ppermute | solution.py:292
  68.3 0.8 collective-permute-start
  69.1 2.2 %collective-permute-start.2 = (bf16[512,512]{1,0:T(8,128)(2,1)S(1)}, bf16[512,512]{1,0:T(8,128)(2,1)S(1)}, u32[]{:S(2)}, u32[]{:S(2)}) collective-permute-start(bf16[512,512]{1,0:T(8,128)(2,1)S(1)} %base_block.6), channel_id=1, source_target_pairs={{0,2},{1,3},{2,0},{3,1},{4,6},{5,7},{6,4},{7,5},{8,10},{9,11},{10,... | collective-permute-start | bytes 1572872 | tf_op jit(solution)/shard_map/ppermute | solution.py:292
  71.3 10.7 %shrink_rows.2 = (bf16[816,128]{1,0:T(8,128)(2,1)S(1)}, bf16[816,128]{1,0:T(8,128)(2,1)S(1)}, f32[8,128]{1,0:T(8,128)}) custom-call(s32[1]{0:T(128)} %bitcast.7.core_ref, bf16[272,2048]{1,0:T(8,128)(2,1)S(1)} %copy-done.7, bf16[272,2048]{1,0:T(8,128)(2,1)} %collective-permute-done.3.refs_1_, bf16[272,2048]{1,0:T(8,128)(2,1)} %collective-permute-done.4.refs_2_, ...), custom_call_target="tpu_custom_call" | custom-call | tf_op jit(solution)/shard_map/shrink_rows/pallas_call | solution.py:142
  82.0 1.6 %collective-permute-start.6 = (bf16[816,128]{1,0:T(8,128)(2,1)S(1)}, bf16[816,128]{1,0:T(8,128)(2,1)S(1)}, u32[]{:S(2)}, u32[]{:S(2)}) collective-permute-start(bf16[816,128]{1,0:T(8,128)(2,1)S(1)} %get-tuple-element.22.refs_0_), channel_id=1, source_target_pairs={{0,1},{1,0},{2,3},{3,2},{4,5},{5,4},{6,7},{7,6},{8,9},{9,8},{10,11... | collective-permute-start | bytes 626696 | tf_op jit(solution)/shard_map/ppermute | solution.py:292
  83.9 1.6 %collective-permute-start.8 = (bf16[816,128]{1,0:T(8,128)(2,1)S(1)}, bf16[816,128]{1,0:T(8,128)(2,1)S(1)}, u32[]{:S(2)}, u32[]{:S(2)}) collective-permute-start(bf16[816,128]{1,0:T(8,128)(2,1)S(1)} %get-tuple-element.22.refs_0_), channel_id=1, source_target_pairs={{0,3},{1,2},{2,1},{3,0},{4,7},{5,6},{6,5},{7,4},{8,11},{9,10},{10,... | collective-permute-start | bytes 626696 | tf_op jit(solution)/shard_map/ppermute | solution.py:292
  86.0 13.9 %collective-permute-done.6.refs_1_ = bf16[816,128]{1,0:T(8,128)(2,1)S(1)} collective-permute-done((bf16[816,128]{1,0:T(8,128)(2,1)S(1)}, bf16[816,128]{1,0:T(8,128)(2,1)S(1)}, u32[]{:S(2)}, u32[]{:S(2)}) %collective-permute-start.6) | collective-permute-done | bytes 208928 | tf_op jit(solution)/shard_map/ppermute | solution.py:292
  99.9 1.4 %collective-permute-start.16 = (bf16[272,512]{1,0:T(8,128)(2,1)S(1)}, bf16[272,512]{1,0:T(8,128)(2,1)S(1)}, u32[]{:S(2)}, u32[]{:S(2)}) collective-permute-start(bf16[272,512]{1,0:T(8,128)(2,1)S(1)} %grow_rows.3), channel_id=1, source_target_pairs={{0,24},{4,28},{8,16},{12,20},{16,8},{20,12},{24,0},{28,4},{1,25},{... | collective-permute-start | bytes 835592 | tf_op jit(solution)/shard_map/ppermute | solution.py:292
  101.3 6.8 %collective-permute-done.7.refs_2_ = bf16[816,128]{1,0:T(8,128)(2,1)S(1)} collective-permute-done((bf16[816,128]{1,0:T(8,128)(2,1)S(1)}, bf16[816,128]{1,0:T(8,128)(2,1)S(1)}, u32[]{:S(2)}, u32[]{:S(2)}) %collective-permute-start.7) | collective-permute-done | bytes 208928 | tf_op jit(solution)/shard_map/ppermute | solution.py:292
  108.1 4.2 %collective-permute-done.8.refs_3_ = bf16[816,128]{1,0:T(8,128)(2,1)S(1)} collective-permute-done((bf16[816,128]{1,0:T(8,128)(2,1)S(1)}, bf16[816,128]{1,0:T(8,128)(2,1)S(1)}, u32[]{:S(2)}, u32[]{:S(2)}) %collective-permute-start.8) | collective-permute-done | bytes 208928 | tf_op jit(solution)/shard_map/ppermute | solution.py:292
  112.3 1.1 grow_rows.2
  113.3 1.5 %collective-permute-start.10 = (bf16[272,512]{1,0:T(8,128)(2,1)S(1)}, bf16[272,512]{1,0:T(8,128)(2,1)S(1)}, u32[]{:S(2)}, u32[]{:S(2)}) collective-permute-start(bf16[272,512]{1,0:T(8,128)(2,1)S(1)} %get-tuple-element.25), channel_id=1, source_target_pairs={{0,8},{4,12},{8,0},{12,4},{16,24},{20,28},{24,16},{28,20},{1,9},{5... | collective-permute-start | bytes 835592 | tf_op jit(solution)/shard_map/ppermute | solution.py:292
  115.5 4.8 %base_block.7.base_ref = f32[512,512]{1,0:T(8,128)S(1)} custom-call(s32[1]{0:T(128)} %bitcast.block_ref, bf16[512,2048]{1,0:T(8,128)(2,1)S(1)} %copy-done.1, bf16[2048,2,1024]{2,1,0:T(2,128)(2,1)} %weight_ref.7, bf16[512,512]{1,0:T(8,128)(2,1)S(1)} %collective-permute-done.refs_0_, bf16[512,512]{1,0:T(8,128)(2,1)S(1)} %collective-permute-done.2.refs_1_), custom_call_target="tpu_custom_call" | custom-call | tf_op jit(solution)/shard_map/base_block/pallas_call | solution.py:235
  120.4 1.7 %collective-permute-done.10.refs_1_ = bf16[272,512]{1,0:T(8,128)(2,1)S(1)} collective-permute-done((bf16[272,512]{1,0:T(8,128)(2,1)S(1)}, bf16[272,512]{1,0:T(8,128)(2,1)S(1)}, u32[]{:S(2)}, u32[]{:S(2)}) %collective-permute-start.10) | collective-permute-done | bytes 278560 | tf_op jit(solution)/shard_map/ppermute | solution.py:292
  122.0 1.2 collective-permute-done.11.refs_2_
  123.3 2.3 %finish_rows.1 = bf16[512,2,256]{2,1,0:T(2,128)(2,1)} custom-call(f32[512,512]{1,0:T(8,128)S(1)} %base_block.7.base_ref, bf16[512,1536]{1,0:T(8,128)(2,1)S(1)} %copy-done.5, bf16[272,512]{1,0:T(8,128)(2,1)S(1)} %get-tuple-element.24.refs_0_, bf16[272,512]{1,0:T(8,128)(2,1)S(1)} %collective-permute-done.10.refs_1_, ...), custom_call_target="tpu_custom_call" | custom-call | tf_op jit(solution)/shard_map/finish_rows/pallas_call | solution.py:280
  (36 shorter events, 2.6 us)
Async XLA Ops:
  0.0 44.8 %collective-permute-start.5 = (bf16[8,2048,128]{2,1,0:T(8,128)(2,1)}, bf16[8,2048,128]{2,1,0:T(8,128)(2,1)}, u32[]{:S(2)}, u32[]{:S(2)}) collective-permute-start(bf16[8,2048,128]{2,1,0:T(8,128)(2,1)} %refs_1_.1), channel_id=1, source_target_pairs={{0,4},{4,0},{8,12},{12,8},{16,20},{20,16},{24,28},{28,24},{1,5},{5... | collective-permute-start | bytes 12582920 | tf_op jit(solution)/shard_map/ppermute | solution.py:292
  0.0 1.6 %copy-start = (bf16[512,2048]{1,0:T(8,128)(2,1)S(1)}, bf16[512,2048]{1,0:T(8,128)(2,1)}, u32[]{:S(2)}) copy-start(bf16[512,2048]{1,0:T(8,128)(2,1)} %tokens_ref.9) | copy-start | bytes 6291460
  1.6 5.5 %copy-start.10 = (s32[512,1]{0,1:T(1,128)S(1)}, s32[512,1]{0,1:T(1,128)}, u32[]{:S(2)}) copy-start(s32[512,1]{0,1:T(1,128)} %param.7) | copy-start | bytes 6148
  1.6 5.5 %copy-start.11 = (s32[64]{0:T(128)S(1)}, s32[64]{0:T(128)}, u32[]{:S(2)}) copy-start(s32[64]{0:T(128)} %param.8) | copy-start | bytes 772
  1.6 18.0 %copy-start.3 = (bf16[8,2,64,256]{3,2,1,0:T(8,128)(2,1)S(1)}, bf16[8,2,64,256]{3,2,1,0:T(8,128)(2,1)}, u32[]{:S(2)}) copy-start(bf16[8,2,64,256]{3,2,1,0:T(8,128)(2,1)} %refs_5_.3) | copy-start | bytes 1572868
  6.3 0.8 copy-start.8
  7.1 12.5 %copy-start.1 = (bf16[512,2048]{1,0:T(8,128)(2,1)S(1)}, bf16[512,2048]{1,0:T(8,128)(2,1)}, u32[]{:S(2)}) copy-start(bf16[512,2048]{1,0:T(8,128)(2,1)} %tokens_ref.9) | copy-start | bytes 6291460
  13.9 1.2 copy-start.4
  15.0 1.1 copy-start.6
  16.1 28.6 %collective-permute-start.12 = (bf16[272,2048]{1,0:T(8,128)(2,1)}, bf16[272,2048]{1,0:T(8,128)(2,1)}, u32[]{:S(2)}, u32[]{:S(2)}) collective-permute-start(bf16[272,2048]{1,0:T(8,128)(2,1)} %get-tuple-element.28), channel_id=1, source_target_pairs={{0,24},{4,28},{8,16},{12,20},{16,8},{20,12},{24,0},{28,4},{1,25},{... | collective-permute-start | bytes 3342344 | tf_op jit(solution)/shard_map/ppermute | solution.py:292
  18.6 49.7 %collective-permute-start.3 = (bf16[272,2048]{1,0:T(8,128)(2,1)}, bf16[272,2048]{1,0:T(8,128)(2,1)}, u32[]{:S(2)}, u32[]{:S(2)}) collective-permute-start(bf16[272,2048]{1,0:T(8,128)(2,1)} %get-tuple-element.20), channel_id=1, source_target_pairs={{0,8},{4,12},{8,0},{12,4},{16,24},{20,28},{24,16},{28,20},{1,9},{5... | collective-permute-start | bytes 3342344 | tf_op jit(solution)/shard_map/ppermute | solution.py:292
  19.1 50.0 %collective-permute-start.4 = (bf16[272,2048]{1,0:T(8,128)(2,1)}, bf16[272,2048]{1,0:T(8,128)(2,1)}, u32[]{:S(2)}, u32[]{:S(2)}) collective-permute-start(bf16[272,2048]{1,0:T(8,128)(2,1)} %get-tuple-element.21), channel_id=1, source_target_pairs={{0,16},{4,20},{8,24},{12,28},{16,0},{20,4},{24,8},{28,12},{1,17},{... | collective-permute-start | bytes 3342344 | tf_op jit(solution)/shard_map/ppermute | solution.py:292
  19.6 35.2 %collective-permute-start.9 = (bf16[8,2,64,256]{3,2,1,0:T(8,128)(2,1)S(1)}, bf16[8,2,64,256]{3,2,1,0:T(8,128)(2,1)S(1)}, u32[]{:S(2)}, u32[]{:S(2)}) collective-permute-start(bf16[8,2,64,256]{3,2,1,0:T(8,128)(2,1)S(1)} %copy-done.3), channel_id=1, source_target_pairs={{0,4},{4,0},{8,12},{12,8},{16,20},{20,16},{24,28},{28,24},{1,5},{5... | collective-permute-start | bytes 1572872 | tf_op jit(solution)/shard_map/ppermute | solution.py:292
  44.7 15.0 %collective-permute-start.1 = (bf16[512,512]{1,0:T(8,128)(2,1)}, bf16[512,512]{1,0:T(8,128)(2,1)}, u32[]{:S(2)}, u32[]{:S(2)}) collective-permute-start(bf16[512,512]{1,0:T(8,128)(2,1)} %base_block.5), channel_id=1, source_target_pairs={{0,1},{1,0},{2,3},{3,2},{4,5},{5,4},{6,7},{7,6},{8,9},{9,8},{10,11... | collective-permute-start | bytes 1572872 | tf_op jit(solution)/shard_map/ppermute | solution.py:292
  44.8 2.2 %copy-start.2 = (bf16[8,2048,128]{2,1,0:T(8,128)(2,1)S(1)}, bf16[8,2048,128]{2,1,0:T(8,128)(2,1)}, u32[]{:S(2)}) copy-start(bf16[8,2048,128]{2,1,0:T(8,128)(2,1)} %refs_1_.1) | copy-start | bytes 12582916
  52.8 29.1 %collective-permute-start.13 = (bf16[272,128]{1,0:T(8,128)(2,1)S(1)}, bf16[272,128]{1,0:T(8,128)(2,1)S(1)}, u32[]{:S(2)}, u32[]{:S(2)}) collective-permute-start(bf16[272,128]{1,0:T(8,128)(2,1)S(1)} %get-tuple-element.29.refs_0_), channel_id=1, source_target_pairs={{0,1},{1,0},{2,3},{3,2},{4,5},{5,4},{6,7},{7,6},{8,9},{9,8},{10,11... | collective-permute-start | bytes 208904 | tf_op jit(solution)/shard_map/ppermute | solution.py:292
  54.8 28.7 %collective-permute-start.14 = (bf16[272,128]{1,0:T(8,128)(2,1)S(1)}, bf16[272,128]{1,0:T(8,128)(2,1)S(1)}, u32[]{:S(2)}, u32[]{:S(2)}) collective-permute-start(bf16[272,128]{1,0:T(8,128)(2,1)S(1)} %get-tuple-element.29.refs_0_), channel_id=1, source_target_pairs={{0,2},{1,3},{2,0},{3,1},{4,6},{5,7},{6,4},{7,5},{8,10},{9,11},{10,... | collective-permute-start | bytes 208904 | tf_op jit(solution)/shard_map/ppermute | solution.py:292
  59.7 24.2 %collective-permute-start.15 = (bf16[272,128]{1,0:T(8,128)(2,1)S(1)}, bf16[272,128]{1,0:T(8,128)(2,1)S(1)}, u32[]{:S(2)}, u32[]{:S(2)}) collective-permute-start(bf16[272,128]{1,0:T(8,128)(2,1)S(1)} %get-tuple-element.29.refs_0_), channel_id=1, source_target_pairs={{0,3},{1,2},{2,1},{3,0},{4,7},{5,6},{6,5},{7,4},{8,11},{9,10},{10,... | collective-permute-start | bytes 208904 | tf_op jit(solution)/shard_map/ppermute | solution.py:292
  61.4 6.9 %copy-start.9 = (bf16[512,512]{1,0:T(8,128)(2,1)S(1)}, bf16[512,512]{1,0:T(8,128)(2,1)}, u32[]{:S(2)}) copy-start(bf16[512,512]{1,0:T(8,128)(2,1)} %copy-done.8) | copy-start | bytes 1572868
  61.4 9.9 %copy-start.7 = (bf16[272,2048]{1,0:T(8,128)(2,1)S(1)}, bf16[272,2048]{1,0:T(8,128)(2,1)}, u32[]{:S(2)}) copy-start(bf16[272,2048]{1,0:T(8,128)(2,1)} %copy-done.6) | copy-start | bytes 3342340
  68.3 47.3 %collective-permute-start = (bf16[512,512]{1,0:T(8,128)(2,1)S(1)}, bf16[512,512]{1,0:T(8,128)(2,1)S(1)}, u32[]{:S(2)}, u32[]{:S(2)}) collective-permute-start(bf16[512,512]{1,0:T(8,128)(2,1)S(1)} %copy-done.9), channel_id=1, source_target_pairs={{0,1},{1,0},{2,3},{3,2},{4,5},{5,4},{6,7},{7,6},{8,9},{9,8},{10,11... | collective-permute-start | bytes 1572872 | tf_op jit(solution)/shard_map/ppermute | solution.py:292
  69.1 46.5 %collective-permute-start.2 = (bf16[512,512]{1,0:T(8,128)(2,1)S(1)}, bf16[512,512]{1,0:T(8,128)(2,1)S(1)}, u32[]{:S(2)}, u32[]{:S(2)}) collective-permute-start(bf16[512,512]{1,0:T(8,128)(2,1)S(1)} %base_block.6), channel_id=1, source_target_pairs={{0,2},{1,3},{2,0},{3,1},{4,6},{5,7},{6,4},{7,5},{8,10},{9,11},{10,... | collective-permute-start | bytes 1572872 | tf_op jit(solution)/shard_map/ppermute | solution.py:292
  82.0 17.9 %collective-permute-start.6 = (bf16[816,128]{1,0:T(8,128)(2,1)S(1)}, bf16[816,128]{1,0:T(8,128)(2,1)S(1)}, u32[]{:S(2)}, u32[]{:S(2)}) collective-permute-start(bf16[816,128]{1,0:T(8,128)(2,1)S(1)} %get-tuple-element.22.refs_0_), channel_id=1, source_target_pairs={{0,1},{1,0},{2,3},{3,2},{4,5},{5,4},{6,7},{7,6},{8,9},{9,8},{10,11... | collective-permute-start | bytes 626696 | tf_op jit(solution)/shard_map/ppermute | solution.py:292
  83.6 24.5 %collective-permute-start.7 = (bf16[816,128]{1,0:T(8,128)(2,1)S(1)}, bf16[816,128]{1,0:T(8,128)(2,1)S(1)}, u32[]{:S(2)}, u32[]{:S(2)}) collective-permute-start(bf16[816,128]{1,0:T(8,128)(2,1)S(1)} %get-tuple-element.22.refs_0_), channel_id=1, source_target_pairs={{0,2},{1,3},{2,0},{3,1},{4,6},{5,7},{6,4},{7,5},{8,10},{9,11},{10,... | collective-permute-start | bytes 626696 | tf_op jit(solution)/shard_map/ppermute | solution.py:292
  83.9 28.4 %collective-permute-start.8 = (bf16[816,128]{1,0:T(8,128)(2,1)S(1)}, bf16[816,128]{1,0:T(8,128)(2,1)S(1)}, u32[]{:S(2)}, u32[]{:S(2)}) collective-permute-start(bf16[816,128]{1,0:T(8,128)(2,1)S(1)} %get-tuple-element.22.refs_0_), channel_id=1, source_target_pairs={{0,3},{1,2},{2,1},{3,0},{4,7},{5,6},{6,5},{7,4},{8,11},{9,10},{10,... | collective-permute-start | bytes 626696 | tf_op jit(solution)/shard_map/ppermute | solution.py:292
  99.9 20.5 %collective-permute-start.16 = (bf16[272,512]{1,0:T(8,128)(2,1)S(1)}, bf16[272,512]{1,0:T(8,128)(2,1)S(1)}, u32[]{:S(2)}, u32[]{:S(2)}) collective-permute-start(bf16[272,512]{1,0:T(8,128)(2,1)S(1)} %grow_rows.3), channel_id=1, source_target_pairs={{0,24},{4,28},{8,16},{12,20},{16,8},{20,12},{24,0},{28,4},{1,25},{... | collective-permute-start | bytes 835592 | tf_op jit(solution)/shard_map/ppermute | solution.py:292
  113.3 8.7 %collective-permute-start.10 = (bf16[272,512]{1,0:T(8,128)(2,1)S(1)}, bf16[272,512]{1,0:T(8,128)(2,1)S(1)}, u32[]{:S(2)}, u32[]{:S(2)}) collective-permute-start(bf16[272,512]{1,0:T(8,128)(2,1)S(1)} %get-tuple-element.25), channel_id=1, source_target_pairs={{0,8},{4,12},{8,0},{12,4},{16,24},{20,28},{24,16},{28,20},{1,9},{5... | collective-permute-start | bytes 835592 | tf_op jit(solution)/shard_map/ppermute | solution.py:292
  114.9 8.4 %collective-permute-start.11 = (bf16[272,512]{1,0:T(8,128)(2,1)S(1)}, bf16[272,512]{1,0:T(8,128)(2,1)S(1)}, u32[]{:S(2)}, u32[]{:S(2)}) collective-permute-start(bf16[272,512]{1,0:T(8,128)(2,1)S(1)} %get-tuple-element.26), channel_id=1, source_target_pairs={{0,16},{4,20},{8,24},{12,28},{16,0},{20,4},{24,8},{28,12},{1,17},{... | collective-permute-start | bytes 835592 | tf_op jit(solution)/shard_map/ppermute | solution.py:292
  115.5 7.7 %copy-start.5 = (bf16[512,1536]{1,0:T(8,128)(2,1)S(1)}, bf16[512,1536]{1,0:T(8,128)(2,1)}, u32[]{:S(2)}) copy-start(bf16[512,1536]{1,0:T(8,128)(2,1)} %copy-done.4) | copy-start | bytes 4718596

commit v3 on v2

--- a/solution.py
+++ b/solution.py
@@ -10,7 +10,8 @@
 adapter_scale = 0.5
 BF = jnp.bfloat16
 F32 = jnp.float32
-VMEM_LIMIT = 48 * 1024 * 1024
+VMEM_LIMIT = 26 * 1024 * 1024
+COST = pl.CostEstimate(flops=1000, bytes_accessed=1000, transcendentals=0)
 
 
 def round_up(value, unit):
@@ -48,6 +49,8 @@
         for m in range(messages):
             limit = jnp.where(sub == m, F32(first_rows[m] + sizes[m] - 1), limit)
         over = jnp.max(jnp.where((sub < messages) & (counts > limit), 1.0, 0.0), axis=0, keepdims=True)
+        key = jnp.broadcast_to(position + shift * 65536, (8, rows))
+        key_column = key.astype(F32).T[:, 0:1].astype(jnp.int32)
         within8 = jnp.broadcast_to(within, (16, rows)).astype(BF)
         for m in range(messages):
             padded = round_up(sizes[m], 128)
@@ -55,7 +58,9 @@
             hit = (target + first_rows[m] == position) & (shift == m) & (target < sizes[m] - 1)
             chosen = hit.astype(F32).astype(BF)
             pick[offsets[m]:offsets[m] + padded, :] = chosen
-            spread_ref[:, offsets[m]:offsets[m] + padded] = hit.astype(F32).T.astype(BF)
+            lane_target = lax.broadcasted_iota(jnp.int32, (rows, padded), 1)
+            back = (lane_target == key_column - first_rows[m] - m * 65536) & (lane_target < sizes[m] - 1)
+            spread_ref[:, offsets[m]:offsets[m] + padded] = back.astype(F32).astype(BF)
             places = dot(within8, chosen, ((1,), (1,)))[0:1, :]
             if padded < width:
                 places = jnp.concatenate([places, jnp.zeros((1, width - padded), F32)], axis=1)
@@ -88,14 +93,17 @@
         + [pl.BlockSpec((rows, spread), lambda i: (0, 0))],
         out_shape=[jax.ShapeDtypeStruct((s, width), BF) for s in sizes] + [jax.ShapeDtypeStruct((rows, spread), BF)],
         scratch_shapes=[pltpu.VMEM((spread, rows), BF)],
+        cost_estimate=COST,
         compiler_params=pltpu.CompilerParams(vmem_limit_bytes=VMEM_LIMIT),
         name="pack_rows",
     )(chip, adapters, slots, tokens)
 
 
-def shrink_kernel(count, flag_lane, core_ref, *refs):
-    messages, (mine, sibling), (out, place_out, flag_out) = refs[:count], refs[count:count + 2], refs[count + 2:count + 5]
-    total, places = refs[count + 5:]
+def shrink_kernel(count, carried, flag_lane, core_ref, *refs):
+    messages, (mine, sibling) = refs[:count], refs[count:count + 2]
+    carry, refs = refs[count + 2:count + 2 + carried], refs[count + 2 + carried:]
+    out, place_out, flag_out, total, places = refs
+    kept = carry[0].shape[0] if carried else 0
     step = pl.program_id(0)
     local = 2 * pl.num_programs(0)
     sizes = [m.shape[0] for m in messages]
@@ -114,7 +122,11 @@
             last = lax.broadcasted_iota(jnp.int32, (1, 128), 1) == 127
             flag = jnp.maximum(flag, jnp.max(jnp.where(last, block, 0.0), axis=1, keepdims=True))
             start += size
-        place_out[...] = places[...].astype(BF)
+        place_out[kept:, :] = places[...].astype(BF)
+        if carried:
+            out[:kept, :] = carry[0][...]
+            place_out[:kept, :] = carry[1][...]
+            flag = jnp.maximum(flag, carry[2][0:1, 0:1])
         flag_out[...] = jnp.broadcast_to(flag, (8, 128))
         total[...] = jnp.zeros_like(total)
 
@@ -130,29 +142,32 @@
 
     @pl.when(step == pl.num_programs(0) - 1)
     def _():
-        out[...] = total[...].astype(BF)
-
-
-def shrink(core, messages, mine, sibling, flag_lane):
+        out[kept:, :] = total[...].astype(BF)
+
+
+def shrink(core, messages, mine, sibling, flag_lane, carry=()):
     local, width, both = mine.shape
     rows = sum(m.shape[0] for m in messages)
     whole = [pl.BlockSpec(m.shape, lambda i: (0, 0)) for m in messages]
     pair = pl.BlockSpec((2, width, both), lambda i: (i, 0, 0))
-    keep = pl.BlockSpec((rows, both), lambda i: (0, 0))
+    every = rows + (carry[0].shape[0] if carry else 0)
+    keep = pl.BlockSpec((every, both), lambda i: (0, 0))
+    whole_carry = [pl.BlockSpec(c.shape, lambda i: (0, 0)) for c in carry]
     return pl.pallas_call(
-        functools.partial(shrink_kernel, len(messages), flag_lane),
+        functools.partial(shrink_kernel, len(messages), len(carry), flag_lane),
         grid=(local // 2,),
-        in_specs=[pl.BlockSpec(memory_space=pltpu.SMEM)] + whole + [pair, pair],
+        in_specs=[pl.BlockSpec(memory_space=pltpu.SMEM)] + whole + [pair, pair] + whole_carry,
         out_specs=[keep, keep, pl.BlockSpec((8, 128), lambda i: (0, 0))],
         out_shape=[
-            jax.ShapeDtypeStruct((rows, both), BF),
-            jax.ShapeDtypeStruct((rows, both), BF),
+            jax.ShapeDtypeStruct((every, both), BF),
+            jax.ShapeDtypeStruct((every, both), BF),
             jax.ShapeDtypeStruct((8, 128), F32),
         ],
         scratch_shapes=[pltpu.VMEM((rows, both), F32), pltpu.VMEM((rows, both), F32)],
+        cost_estimate=COST,
         compiler_params=pltpu.CompilerParams(vmem_limit_bytes=VMEM_LIMIT),
         name="shrink_rows",
-    )(core, *messages, mine, sibling)
+    )(core, *messages, mine, sibling, *carry)
 
 
 def grow_kernel(shares, sizes, core_ref, *refs):
@@ -196,64 +211,67 @@
         in_specs=[pl.BlockSpec(memory_space=pltpu.SMEM)] + [vmem] * (len(parts) + 3),
         out_specs=[vmem] * len(sizes),
         out_shape=[jax.ShapeDtypeStruct((s, 2 * columns), BF) for s in sizes],
+        cost_estimate=COST,
         compiler_params=pltpu.CompilerParams(vmem_limit_bytes=VMEM_LIMIT),
         name="grow_rows",
     )(core, *parts, place, mine, sibling)
 
 
-def block_kernel(steps, count, block_ref, tokens_ref, weight_ref, *refs):
-    arrived, out, total = refs[:count], refs[count], refs[count + 1]
+def base_kernel(steps, blocks, place_ref, tokens_ref, weight_ref, *refs):
+    outs, total = refs[:blocks], refs[blocks]
     step = pl.program_id(0)
     weight = jnp.swapaxes(weight_ref[...], 0, 1)
-    columns = weight.shape[2]
-
-    @pl.when(step == 0)
-    def _():
-        start = jnp.zeros(total.shape, F32)
-        for one in arrived:
-            start = start + one[...].astype(F32)
-        total[...] = start
-
+    columns = total.shape[2] // blocks
     for j in range(2):
-        total[:, j * columns:(j + 1) * columns] += dot(tokens_ref[...], weight[j])
+        product = dot(tokens_ref[...], weight[j])
+
+        @pl.when(step == 0)
+        def _():
+            total[j] = product
+
+        @pl.when(step > 0)
+        def _():
+            total[j] += product
 
     @pl.when(step == steps - 1)
     def _():
-        out[...] = total[...].astype(out.dtype)
-
-
-def base_block(block, tokens, weight, columns, arrived, dtype, steps=4):
+        for r, out in enumerate(outs):
+            start = pl.multiple_of((place_ref[0] ^ r) * columns, columns)
+            for j in range(2):
+                out[:, j * columns:(j + 1) * columns] = total[j, :, pl.ds(start, columns)].astype(out.dtype)
+
+
+def base_parts(t, tokens, weight, blocks, steps=4):
     rows, width = tokens.shape
+    columns = weight.shape[2] // blocks
+    types = [BF if r % 2 else F32 for r in range(blocks)]
     if columns % 128:
-        part = lax.dynamic_slice_in_dim(weight, block[0] * columns, columns, 2)
-        total = dot(tokens, part.reshape(width, 2 * columns))
-        for one in arrived:
-            total = total + one.astype(F32)
-        return total.astype(dtype)
+        total = jnp.einsum("rd,djn->rjn", tokens, weight, preferred_element_type=F32)
+        cut = [lax.dynamic_slice_in_dim(total, (t ^ r) * columns, columns, 2) for r in range(blocks)]
+        return [c.reshape(rows, 2 * columns).astype(k) for c, k in zip(cut, types)]
     deep = width // steps
-    keep = pl.BlockSpec((rows, 2 * columns), lambda i, b: (0, 0))
     return pl.pallas_call(
-        functools.partial(block_kernel, steps, len(arrived)),
-        grid_spec=pltpu.PrefetchScalarGridSpec(
-            num_scalar_prefetch=1,
-            grid=(steps,),
-            in_specs=[
-                pl.BlockSpec((rows, deep), lambda i, b: (0, i)),
-                pl.BlockSpec((deep, 2, columns), lambda i, b: (i, 0, b[0])),
-            ]
-            + [keep] * len(arrived),
-            out_specs=keep,
-            scratch_shapes=[pltpu.VMEM((rows, 2 * columns), F32)],
-        ),
-        out_shape=jax.ShapeDtypeStruct((rows, 2 * columns), dtype),
+        functools.partial(base_kernel, steps, blocks),
+        grid=(steps,),
+        in_specs=[
+            pl.BlockSpec(memory_space=pltpu.SMEM),
+            pl.BlockSpec((rows, deep), lambda i: (0, i)),
+            pl.BlockSpec((deep, 2, weight.shape[2]), lambda i: (i, 0, 0)),
+        ],
+        out_specs=[pl.BlockSpec((rows, 2 * columns), lambda i: (0, 0))] * blocks,
+        out_shape=[jax.ShapeDtypeStruct((rows, 2 * columns), k) for k in types],
+        scratch_shapes=[pltpu.VMEM((2, rows, weight.shape[2]), F32)],
+        cost_estimate=COST,
         compiler_params=pltpu.CompilerParams(vmem_limit_bytes=VMEM_LIMIT),
-        name="base_block",
-    )(block, tokens, weight, *arrived)
-
-
-def finish_kernel(sizes, base_ref, spread_ref, *refs):
-    updates, out = refs[:-1], refs[-1]
-    total = base_ref[...]
+        name="base_parts",
+    )(t.reshape(1), tokens, weight)
+
+
+def finish_kernel(sizes, count, *refs):
+    bases, spread_ref, updates, out = refs[:count], refs[count], refs[count + 1:-1], refs[-1]
+    total = bases[0][...]
+    for base in bases[1:]:
+        total = total + base[...].astype(F32)
     update_rows = jnp.zeros(total.shape, F32)
     start = 0
     for update, size in zip(updates, sizes):
@@ -273,18 +291,19 @@
         out[...] = jnp.swapaxes(both, 0, 1)
 
 
-def finish(base, spread, updates):
+def finish(bases, spread, updates):
     sizes = tuple(u.shape[0] for u in updates)
-    rows, both = base.shape
+    rows, both = bases[0].shape
     vmem = pl.BlockSpec(memory_space=pltpu.VMEM)
     return pl.pallas_call(
-        functools.partial(finish_kernel, sizes),
-        in_specs=[vmem] * (len(updates) + 2),
+        functools.partial(finish_kernel, sizes, len(bases)),
+        in_specs=[vmem] * (len(bases) + 1 + len(updates)),
         out_specs=vmem,
         out_shape=jax.ShapeDtypeStruct((rows, 2, both // 2), BF),
+        cost_estimate=COST,
         compiler_params=pltpu.CompilerParams(vmem_limit_bytes=VMEM_LIMIT),
         name="finish_rows",
-    )(base, spread, *updates)
+    )(*bases, spread, *updates)
 
 
 def exchange(array, axis, shift):
@@ -325,7 +344,6 @@
     flag_lane = width // 4 - 1
 
     down_sibling = exchange(adapter_down_weight, "dp", 1)
-    up_sibling = exchange(adapter_up_weight, "dp", 1)
 
     near = [m for m in range(chips) if bits(m) <= 1]
     far = [m for m in range(chips) if bits(m) > 1]
@@ -338,37 +356,38 @@
     for m in near[1:]:
         arrived[m] = exchange(sent[m], "dp", 2 * m)
 
-    columns = key_value_base_weight.shape[2] // blocks
     t = lax.axis_index("tensor").astype(jnp.int32)
+    parts = base_parts(t, after(tokens, *sent), key_value_base_weight, blocks)
     came = {}
 
-    def summands(r):
+    def arrived_for(r):
         return [came[key] for key in sorted(came) if key[1] == r]
 
-    def base_of(r, dtype):
-        return base_block((t ^ r).reshape(1), tokens, key_value_base_weight, columns, summands(r), dtype)
-
-    order = sorted(range(1, blocks), key=lambda r: (r & -r, -r))
-    for r in order:
+    for m in far:
+        arrived[m] = exchange(after(sent[m], parts[0], down_sibling), "dp", 2 * m)
+    for r in sorted(range(1, blocks), key=lambda r: (r & -r, -r)):
         low = r & -r
-        if r == 2:
-            for m in far:
-                arrived[m] = exchange(after(sent[m], came_last), "dp", 2 * m)
-        part = base_of(r, BF)
-        came_last = part
-        came[(low, r ^ low)] = exchange(part, "tensor", low)
-
+        part = parts[r]
+        for one in arrived_for(r):
+            part = part + one.astype(F32)
+        came[(low, r ^ low)] = exchange(part.astype(BF), "tensor", low)
+
+    own = after(sent[0], came[(1, blocks - 2)])
+    carry = shrink(core, [own], adapter_down_weight, down_sibling, flag_lane)
+    up_sibling = exchange(after(adapter_up_weight, down_sibling), "dp", 1)
     for part in (near, far):
         if not part:
             continue
-        group = [arrived[m] for m in part]
-        share, place, flag = shrink(core, group, adapter_down_weight, down_sibling, flag_lane)
-        shares = [share] + [exchange(share, "tensor", z) for z in range(1, blocks)]
+        group = [arrived[m] for m in part if m]
+        share, place, flag = shrink(
+            core, group, adapter_down_weight, after(down_sibling, up_sibling), flag_lane, carry if part is near else ()
+        )
+        other = came[(1, 0)] if part is near else came[(blocks // 2, 0)]
+        shares = [after(share, other)] + [exchange(share, "tensor", z) for z in range(1, blocks)]
         grown = grow(core, shares, place, adapter_up_weight, up_sibling, tuple(sizes[m] for m in part))
         for m, update in zip(part, grown):
             returned[m] = update if m == 0 else exchange(update, "dp", 2 * m)
-    base = base_of(0, F32)
-    return finish(base, spread, [returned[m] for m in range(chips)])
+    return finish([parts[0]] + arrived_for(0), spread, [returned[m] for m in range(chips)])
 
 
 def solution(mesh):

time: 126 us -> 113 us (0.90)
  the two profiles are of different devices: /device:TPU:8 before, /device:TPU:0 now
where the time goes in v3:
time: 113 us; the launch traced here: 112 us
  Pallas kernels  38.1 us (34%)
  waiting for transfers between devices  36.1 us (32%)
  starting transfers between devices  25.2 us (22%)
  local copies, waits for them, and re-layouts  12 us (11%)
    ppermute x17, waiting for transfers between devices, exchange(): return lax.ppermute(array, axis, [(i, i ^ shift) for i in range(size)])  36.1 us
    ppermute x17, starting transfers between devices, exchange(): return lax.ppermute(array, axis, [(i, i ^ shift) for i in range(size)])  25.2 us
    pallas_call x3, Pallas kernels, shrink(): pl.pallas_call(functools.partial(shrink_kernel, len(messages), len(carry)...  18.7 us
    unnamed x28, local copies, waits for them, and re-layouts  12 us
    pallas_call x1, Pallas kernels, base_parts(): pl.pallas_call(functools.partial(base_kernel, steps, blocks), grid=(steps...  8.89 us
    pallas_call x1, Pallas kernels, pack(): pl.pallas_call(functools.partial(pack_kernel, (sizes, first_rows, chip_sl...  5.43 us
    pallas_call x1, Pallas kernels, finish(): pl.pallas_call(functools.partial(finish_kernel, sizes, len(bases)), in_sp...  3.45 us
  transfers between devices with their start and end apart: 17, of which 6 were waited for; matrix products, arithmetic and copies ran while one was open for 1% of the time, Pallas kernels for 31%

profile of v3, /device:TPU:0, one launch (start us, length us, event | category | flops | bytes accessed | tf_op | source)
XLA Modules:
  0.0 112.4 jit_solution(1568152443024445822)
XLA Ops:
  0.5 1.6 %copy-done.3 = bf16[512,2048]{1,0:T(8,128)(2,1)S(1)} copy-done((bf16[512,2048]{1,0:T(8,128)(2,1)S(1)}, bf16[512,2048]{1,0:T(8,128)(2,1)}, u32[]{:S(2)}) %copy-start.3) | copy-done | bytes 2097176
  2.0 0.7 copy-done.12
  3.4 5.4 %pack_rows.1 = (bf16[272,2048]{1,0:T(8,128)(2,1)S(1)}, bf16[272,2048]{1,0:T(8,128)(2,1)}, bf16[272,2048]{1,0:T(8,128)(2,1)}, bf16[272,2048]{1,0:T(8,128)(2,1)}, bf16[512,1536]{1,0:T(8,128)(2,1)S(1)}) custom-call(s32[1]{0:T(128)} %bitcast.1.place_ref, s32[1,512]{1,0:T(1,128)S(1)} %bitcast.5, s32[1,64]{1,0:T(1,128)S(1)} %bitcast.6, bf16[512,2048]{1,0:T(8,128)(2,1)S(1)} %copy-done.3), custom_call_target="tpu_custom_call" | custom-call | flops 1000 | bytes 1000 | tf_op jit(solution)/shard_map/pack_rows/pallas_call | solution.py:83
  8.8 1.2 %copy-done.6 = bf16[512,1536]{1,0:T(8,128)(2,1)} copy-done((bf16[512,1536]{1,0:T(8,128)(2,1)}, bf16[512,1536]{1,0:T(8,128)(2,1)S(1)}, u32[]{:S(2)}) %copy-start.6) | copy-done | bytes 1572888
  10.0 1.0 copy-done.8
  11.0 2.5 %collective-permute-start.3 = (bf16[272,2048]{1,0:T(8,128)(2,1)}, bf16[272,2048]{1,0:T(8,128)(2,1)}, u32[]{:S(2)}, u32[]{:S(2)}) collective-permute-start(bf16[272,2048]{1,0:T(8,128)(2,1)} %get-tuple-element.32), channel_id=1, source_target_pairs={{0,8},{4,12},{8,0},{12,4},{16,24},{20,28},{24,16},{28,20},{1,9},{5... | collective-permute-start | bytes 3342344 | tf_op jit(solution)/shard_map/ppermute | solution.py:311
  13.5 1.5 %collective-permute-start.4 = (bf16[272,2048]{1,0:T(8,128)(2,1)}, bf16[272,2048]{1,0:T(8,128)(2,1)}, u32[]{:S(2)}, u32[]{:S(2)}) collective-permute-start(bf16[272,2048]{1,0:T(8,128)(2,1)} %get-tuple-element.33), channel_id=1, source_target_pairs={{0,16},{4,20},{8,24},{12,28},{16,0},{20,4},{24,8},{28,12},{1,17},{... | collective-permute-start | bytes 3342344 | tf_op jit(solution)/shard_map/ppermute | solution.py:311
  15.0 3.4 %copy-done.2 = bf16[2048,2,1024]{2,1,0:T(2,128)(2,1)S(1)} copy-done((bf16[2048,2,1024]{2,1,0:T(2,128)(2,1)S(1)}, bf16[2048,2,1024]{2,1,0:T(2,128)(2,1)}, u32[]{:S(2)}) %copy-start.2) | copy-done | bytes 8388632
  18.4 8.9 %base_parts.1 = (f32[512,512]{1,0:T(8,128)S(1)}, bf16[512,512]{1,0:T(8,128)(2,1)}, f32[512,512]{1,0:T(8,128)S(1)}, bf16[512,512]{1,0:T(8,128)(2,1)S(1)}) custom-call(s32[1]{0:T(128)} %bitcast.place_ref, bf16[512,2048]{1,0:T(8,128)(2,1)S(1)} %copy-done.4, bf16[2048,2,1024]{2,1,0:T(2,128)(2,1)S(1)} %copy-done.2), custom_call_target="tpu_custom_call" | custom-call | flops 1000 | bytes 1000 | tf_op jit(solution)/shard_map/base_parts/pallas_call | solution.py:253
  27.3 1.6 %collective-permute-start.1 = (bf16[512,512]{1,0:T(8,128)(2,1)S(1)}, bf16[512,512]{1,0:T(8,128)(2,1)S(1)}, u32[]{:S(2)}, u32[]{:S(2)}) collective-permute-start(bf16[512,512]{1,0:T(8,128)(2,1)S(1)} %get-tuple-element.39), channel_id=1, source_target_pairs={{0,1},{1,0},{2,3},{3,2},{4,5},{5,4},{6,7},{7,6},{8,9},{9,8},{10,11... | collective-permute-start | bytes 1572872 | tf_op jit(solution)/shard_map/ppermute | solution.py:311
  29.4 11.7 %collective-permute-done.1 = bf16[512,512]{1,0:T(8,128)(2,1)S(1)} collective-permute-done((bf16[512,512]{1,0:T(8,128)(2,1)S(1)}, bf16[512,512]{1,0:T(8,128)(2,1)S(1)}, u32[]{:S(2)}, u32[]{:S(2)}) %collective-permute-start.1) | collective-permute-done | bytes 524320 | tf_op jit(solution)/shard_map/ppermute | solution.py:311
  41.1 1.6 %collective-permute-start = (bf16[512,512]{1,0:T(8,128)(2,1)}, bf16[512,512]{1,0:T(8,128)(2,1)S(1)}, u32[]{:S(2)}, u32[]{:S(2)}) collective-permute-start(bf16[512,512]{1,0:T(8,128)(2,1)} %get-tuple-element.37), channel_id=1, source_target_pairs={{0,1},{1,0},{2,3},{3,2},{4,5},{5,4},{6,7},{7,6},{8,9},{9,8},{10,11... | collective-permute-start | bytes 1572872 | tf_op jit(solution)/shard_map/ppermute | solution.py:311
  42.6 1.0 add_convert_fusion
  43.6 2.6 %collective-permute-start.2 = (bf16[512,512]{1,0:T(8,128)(2,1)}, bf16[512,512]{1,0:T(8,128)(2,1)}, u32[]{:S(2)}, u32[]{:S(2)}) collective-permute-start(bf16[512,512]{1,0:T(8,128)(2,1)} %add_convert_fusion), channel_id=1, source_target_pairs={{0,2},{1,3},{2,0},{3,1},{4,6},{5,7},{6,4},{7,5},{8,10},{9,11},{10,... | collective-permute-start | bytes 1572872 | tf_op jit(solution)/shard_map/ppermute | solution.py:311
  46.2 2.2 %copy-done = bf16[8,2048,128]{2,1,0:T(8,128)(2,1)S(1)} copy-done((bf16[8,2048,128]{2,1,0:T(8,128)(2,1)S(1)}, bf16[8,2048,128]{2,1,0:T(8,128)(2,1)}, u32[]{:S(2)}) %copy-start) | copy-done | bytes 4194328
  48.4 1.2 %copy-done.9 = bf16[272,2048]{1,0:T(8,128)(2,1)S(1)} copy-done((bf16[272,2048]{1,0:T(8,128)(2,1)S(1)}, bf16[272,2048]{1,0:T(8,128)(2,1)}, u32[]{:S(2)}) %copy-start.9) | copy-done | bytes 1114136
  49.7 5.1 %shrink_rows.3 = (bf16[272,128]{1,0:T(8,128)(2,1)S(1)}, bf16[272,128]{1,0:T(8,128)(2,1)S(1)}, f32[8,128]{1,0:T(8,128)S(1)}) custom-call(s32[1]{0:T(128)} %bitcast.4.core_ref, bf16[272,2048]{1,0:T(8,128)(2,1)S(1)} %copy-done.9, bf16[8,2048,128]{2,1,0:T(8,128)(2,1)S(1)} %copy-done, bf16[8,2048,128]{2,1,0:T(8,128)(2,1)} %collective-permute-done.5.refs_2_.refs_3_), custom_call_target="tpu_custom_call" | custom-call | flops 1000 | bytes 1000 | tf_op jit(solution)/shard_map/shrink_rows/pallas_call | solution.py:156
  54.8 9.6 %collective-permute-done.4.refs_1_ = bf16[272,2048]{1,0:T(8,128)(2,1)} collective-permute-done((bf16[272,2048]{1,0:T(8,128)(2,1)}, bf16[272,2048]{1,0:T(8,128)(2,1)}, u32[]{:S(2)}, u32[]{:S(2)}) %collective-permute-start.4) | collective-permute-done | bytes 1114144 | tf_op jit(solution)/shard_map/ppermute | solution.py:311
  64.4 8.1 %shrink_rows.4 = (bf16[816,128]{1,0:T(8,128)(2,1)S(1)}, bf16[816,128]{1,0:T(8,128)(2,1)S(1)}, f32[8,128]{1,0:T(8,128)}) custom-call(s32[1]{0:T(128)} %bitcast.4.core_ref, bf16[272,2048]{1,0:T(8,128)(2,1)} %collective-permute-done.3.refs_0_, bf16[272,2048]{1,0:T(8,128)(2,1)} %collective-permute-done.4.refs_1_, bf16[8,2048,128]{2,1,0:T(8,128)(2,1)S(1)} %copy-done.1, ...), custom_call_target="tpu_custom_call" | custom-call | flops 1000 | bytes 1000 | tf_op jit(solution)/shard_map/shrink_rows/pallas_call | solution.py:156
  72.4 1.6 %collective-permute-start.7 = (bf16[816,128]{1,0:T(8,128)(2,1)S(1)}, bf16[816,128]{1,0:T(8,128)(2,1)S(1)}, u32[]{:S(2)}, u32[]{:S(2)}) collective-permute-start(bf16[816,128]{1,0:T(8,128)(2,1)S(1)} %get-tuple-element.48.refs_0_), channel_id=1, source_target_pairs={{0,1},{1,0},{2,3},{3,2},{4,5},{5,4},{6,7},{7,6},{8,9},{9,8},{10,11... | collective-permute-start | bytes 626696 | tf_op jit(solution)/shard_map/ppermute | solution.py:311
  74.0 2.6 %collective-permute-start.8 = (bf16[816,128]{1,0:T(8,128)(2,1)S(1)}, bf16[816,128]{1,0:T(8,128)(2,1)S(1)}, u32[]{:S(2)}, u32[]{:S(2)}) collective-permute-start(bf16[816,128]{1,0:T(8,128)(2,1)S(1)} %get-tuple-element.48.refs_0_), channel_id=1, source_target_pairs={{0,2},{1,3},{2,0},{3,1},{4,6},{5,7},{6,4},{7,5},{8,10},{9,11},{10,... | collective-permute-start | bytes 626696 | tf_op jit(solution)/shard_map/ppermute | solution.py:311
  76.8 5.6 %shrink_rows.5 = (bf16[272,128]{1,0:T(8,128)(2,1)S(1)}, bf16[272,128]{1,0:T(8,128)(2,1)S(1)}, f32[8,128]{1,0:T(8,128)}) custom-call(s32[1]{0:T(128)} %bitcast.4.core_ref, bf16[272,2048]{1,0:T(8,128)(2,1)S(1)} %collective-permute-done.12.refs_0_, bf16[8,2048,128]{2,1,0:T(8,128)(2,1)S(1)} %copy-done.1, bf16[8,2048,128]{2,1,0:T(8,128)(2,1)} %collective-permute-done.5.refs_2_.refs_3_), custom_call_target="tpu_custom_call" | custom-call | flops 1000 | bytes 1000 | tf_op jit(solution)/shard_map/shrink_rows/pallas_call | solution.py:156
  82.4 0.7 collective-permute-start.13
  83.1 3.5 %collective-permute-start.14 = (bf16[272,128]{1,0:T(8,128)(2,1)S(1)}, bf16[272,128]{1,0:T(8,128)(2,1)S(1)}, u32[]{:S(2)}, u32[]{:S(2)}) collective-permute-start(bf16[272,128]{1,0:T(8,128)(2,1)S(1)} %get-tuple-element.55.refs_0_), channel_id=1, source_target_pairs={{0,2},{1,3},{2,0},{3,1},{4,6},{5,7},{6,4},{7,5},{8,10},{9,11},{10,... | collective-permute-start | bytes 208904 | tf_op jit(solution)/shard_map/ppermute | solution.py:311
  86.6 6.9 %collective-permute-done.8.refs_2_ = bf16[816,128]{1,0:T(8,128)(2,1)S(1)} collective-permute-done((bf16[816,128]{1,0:T(8,128)(2,1)S(1)}, bf16[816,128]{1,0:T(8,128)(2,1)S(1)}, u32[]{:S(2)}, u32[]{:S(2)}) %collective-permute-start.8) | collective-permute-done | bytes 208928 | tf_op jit(solution)/shard_map/ppermute | solution.py:311
  93.5 2.1 %collective-permute-start.15 = (bf16[272,128]{1,0:T(8,128)(2,1)S(1)}, bf16[272,128]{1,0:T(8,128)(2,1)S(1)}, u32[]{:S(2)}, u32[]{:S(2)}) collective-permute-start(bf16[272,128]{1,0:T(8,128)(2,1)S(1)} %get-tuple-element.55.refs_0_), channel_id=1, source_target_pairs={{0,3},{1,2},{2,1},{3,0},{4,7},{5,6},{6,5},{7,4},{8,11},{9,10},{10,... | collective-permute-start | bytes 208904 | tf_op jit(solution)/shard_map/ppermute | solution.py:311
  95.6 1.1 grow_rows.2
  96.8 2.6 %collective-permute-start.11 = (bf16[272,512]{1,0:T(8,128)(2,1)S(1)}, bf16[272,512]{1,0:T(8,128)(2,1)S(1)}, u32[]{:S(2)}, u32[]{:S(2)}) collective-permute-start(bf16[272,512]{1,0:T(8,128)(2,1)S(1)} %get-tuple-element.52), channel_id=1, source_target_pairs={{0,16},{4,20},{8,24},{12,28},{16,0},{20,4},{24,8},{28,12},{1,17},{... | collective-permute-start | bytes 835592 | tf_op jit(solution)/shard_map/ppermute | solution.py:311
  100.1 1.2 %collective-permute-start.16 = (bf16[272,512]{1,0:T(8,128)(2,1)S(1)}, bf16[272,512]{1,0:T(8,128)(2,1)S(1)}, u32[]{:S(2)}, u32[]{:S(2)}) collective-permute-start(bf16[272,512]{1,0:T(8,128)(2,1)S(1)} %grow_rows.3), channel_id=1, source_target_pairs={{0,24},{4,28},{8,16},{12,20},{16,8},{20,12},{24,0},{28,4},{1,25},{... | collective-permute-start | bytes 835592 | tf_op jit(solution)/shard_map/ppermute | solution.py:311
  101.4 4.8 %collective-permute-done.10.refs_5_ = bf16[272,512]{1,0:T(8,128)(2,1)S(1)} collective-permute-done((bf16[272,512]{1,0:T(8,128)(2,1)S(1)}, bf16[272,512]{1,0:T(8,128)(2,1)S(1)}, u32[]{:S(2)}, u32[]{:S(2)}) %collective-permute-start.10) | collective-permute-done | bytes 278560 | tf_op jit(solution)/shard_map/ppermute | solution.py:311
  106.2 2.7 %collective-permute-done.11.refs_6_ = bf16[272,512]{1,0:T(8,128)(2,1)S(1)} collective-permute-done((bf16[272,512]{1,0:T(8,128)(2,1)S(1)}, bf16[272,512]{1,0:T(8,128)(2,1)S(1)}, u32[]{:S(2)}, u32[]{:S(2)}) %collective-permute-start.11) | collective-permute-done | bytes 278560 | tf_op jit(solution)/shard_map/ppermute | solution.py:311
  108.9 3.5 %finish_rows.1 = bf16[512,2,256]{2,1,0:T(2,128)(2,1)} custom-call(f32[512,512]{1,0:T(8,128)S(1)} %copy-done.11, bf16[512,512]{1,0:T(8,128)(2,1)S(1)} %collective-permute-done.refs_1_, bf16[512,512]{1,0:T(8,128)(2,1)} %collective-permute-done.2.refs_2_, bf16[512,1536]{1,0:T(8,128)(2,1)S(1)} %copy-done.7, bf16[272,512]{1,0:T(8,128)(2,1)S(1)} %get-tuple-element.50.refs_4_, ...), custom_call_target="tpu_custom_call" | custom-call | flops 1000 | bytes 1000 | tf_op jit(solution)/shard_map/finish_rows/pallas_call | solution.py:298
  (39 shorter events, 2.7 us)
Async XLA Ops:
  0.0 28.9 %collective-permute-start.5 = (bf16[8,2048,128]{2,1,0:T(8,128)(2,1)}, bf16[8,2048,128]{2,1,0:T(8,128)(2,1)}, u32[]{:S(2)}, u32[]{:S(2)}) collective-permute-start(bf16[8,2048,128]{2,1,0:T(8,128)(2,1)} %refs_1_.3), channel_id=1, source_target_pairs={{0,4},{4,0},{8,12},{12,8},{16,20},{20,16},{24,28},{28,24},{1,5},{5... | collective-permute-start | bytes 12582920 | tf_op jit(solution)/shard_map/ppermute | solution.py:311
  0.5 1.6 %copy-start.3 = (bf16[512,2048]{1,0:T(8,128)(2,1)S(1)}, bf16[512,2048]{1,0:T(8,128)(2,1)}, u32[]{:S(2)}) copy-start(bf16[512,2048]{1,0:T(8,128)(2,1)} %tokens_ref.2) | copy-start | bytes 6291460
  2.0 0.7 copy-start.12
  2.7 0.7 copy-start.13
  3.4 11.6 %copy-start.4 = (bf16[512,2048]{1,0:T(8,128)(2,1)S(1)}, bf16[512,2048]{1,0:T(8,128)(2,1)}, u32[]{:S(2)}) copy-start(bf16[512,2048]{1,0:T(8,128)(2,1)} %tokens_ref.2) | copy-start | bytes 6291460
  8.8 1.2 %copy-start.6 = (bf16[512,1536]{1,0:T(8,128)(2,1)}, bf16[512,1536]{1,0:T(8,128)(2,1)S(1)}, u32[]{:S(2)}) copy-start(bf16[512,1536]{1,0:T(8,128)(2,1)S(1)} %get-tuple-element.40.refs_3_) | copy-start | bytes 4718596
  10.0 1.0 copy-start.8
  11.0 43.8 %collective-permute-start.3 = (bf16[272,2048]{1,0:T(8,128)(2,1)}, bf16[272,2048]{1,0:T(8,128)(2,1)}, u32[]{:S(2)}, u32[]{:S(2)}) collective-permute-start(bf16[272,2048]{1,0:T(8,128)(2,1)} %get-tuple-element.32), channel_id=1, source_target_pairs={{0,8},{4,12},{8,0},{12,4},{16,24},{20,28},{24,16},{28,20},{1,9},{5... | collective-permute-start | bytes 3342344 | tf_op jit(solution)/shard_map/ppermute | solution.py:311
  13.5 50.9 %collective-permute-start.4 = (bf16[272,2048]{1,0:T(8,128)(2,1)}, bf16[272,2048]{1,0:T(8,128)(2,1)}, u32[]{:S(2)}, u32[]{:S(2)}) collective-permute-start(bf16[272,2048]{1,0:T(8,128)(2,1)} %get-tuple-element.33), channel_id=1, source_target_pairs={{0,16},{4,20},{8,24},{12,28},{16,0},{20,4},{24,8},{28,12},{1,17},{... | collective-permute-start | bytes 3342344 | tf_op jit(solution)/shard_map/ppermute | solution.py:311
  15.0 3.4 %copy-start.2 = (bf16[2048,2,1024]{2,1,0:T(2,128)(2,1)S(1)}, bf16[2048,2,1024]{2,1,0:T(2,128)(2,1)}, u32[]{:S(2)}) copy-start(bf16[2048,2,1024]{2,1,0:T(2,128)(2,1)} %weight_ref.1) | copy-start | bytes 25165828
  18.4 11.0 %copy-start.5 = (bf16[8,2,64,256]{3,2,1,0:T(8,128)(2,1)S(1)}, bf16[8,2,64,256]{3,2,1,0:T(8,128)(2,1)}, u32[]{:S(2)}) copy-start(bf16[8,2,64,256]{3,2,1,0:T(8,128)(2,1)} %refs_5_.3) | copy-start | bytes 1572868
  27.3 16.3 %copy-start.10 = (f32[512,512]{1,0:T(8,128)}, f32[512,512]{1,0:T(8,128)S(1)}, u32[]{:S(2)}) copy-start(f32[512,512]{1,0:T(8,128)S(1)} %get-tuple-element.36.refs_0_) | copy-start | bytes 3145732
  27.3 13.8 %collective-permute-start.1 = (bf16[512,512]{1,0:T(8,128)(2,1)S(1)}, bf16[512,512]{1,0:T(8,128)(2,1)S(1)}, u32[]{:S(2)}, u32[]{:S(2)}) collective-permute-start(bf16[512,512]{1,0:T(8,128)(2,1)S(1)} %get-tuple-element.39), channel_id=1, source_target_pairs={{0,1},{1,0},{2,3},{3,2},{4,5},{5,4},{6,7},{7,6},{8,9},{9,8},{10,11... | collective-permute-start | bytes 1572872 | tf_op jit(solution)/shard_map/ppermute | solution.py:311
  28.9 47.7 %collective-permute-start.12 = (bf16[272,2048]{1,0:T(8,128)(2,1)}, bf16[272,2048]{1,0:T(8,128)(2,1)S(1)}, u32[]{:S(2)}, u32[]{:S(2)}) collective-permute-start(bf16[272,2048]{1,0:T(8,128)(2,1)} %get-tuple-element.53), channel_id=1, source_target_pairs={{0,24},{4,28},{8,16},{12,20},{16,8},{20,12},{24,0},{28,4},{1,25},{... | collective-permute-start | bytes 3342344 | tf_op jit(solution)/shard_map/ppermute | solution.py:311
  29.4 14.3 %collective-permute-start.6 = (bf16[8,2,64,256]{3,2,1,0:T(8,128)(2,1)S(1)}, bf16[8,2,64,256]{3,2,1,0:T(8,128)(2,1)S(1)}, u32[]{:S(2)}, u32[]{:S(2)}) collective-permute-start(bf16[8,2,64,256]{3,2,1,0:T(8,128)(2,1)S(1)} %copy-done.5), channel_id=1, source_target_pairs={{0,4},{4,0},{8,12},{12,8},{16,20},{20,16},{24,28},{28,24},{1,5},{5... | collective-permute-start | bytes 1572872 | tf_op jit(solution)/shard_map/ppermute | solution.py:311
  41.1 41.4 %collective-permute-start = (bf16[512,512]{1,0:T(8,128)(2,1)}, bf16[512,512]{1,0:T(8,128)(2,1)S(1)}, u32[]{:S(2)}, u32[]{:S(2)}) collective-permute-start(bf16[512,512]{1,0:T(8,128)(2,1)} %get-tuple-element.37), channel_id=1, source_target_pairs={{0,1},{1,0},{2,3},{3,2},{4,5},{5,4},{6,7},{7,6},{8,9},{9,8},{10,11... | collective-permute-start | bytes 1572872 | tf_op jit(solution)/shard_map/ppermute | solution.py:311
  43.6 53.2 %collective-permute-start.2 = (bf16[512,512]{1,0:T(8,128)(2,1)}, bf16[512,512]{1,0:T(8,128)(2,1)}, u32[]{:S(2)}, u32[]{:S(2)}) collective-permute-start(bf16[512,512]{1,0:T(8,128)(2,1)} %add_convert_fusion), channel_id=1, source_target_pairs={{0,2},{1,3},{2,0},{3,1},{4,6},{5,7},{6,4},{7,5},{8,10},{9,11},{10,... | collective-permute-start | bytes 1572872 | tf_op jit(solution)/shard_map/ppermute | solution.py:311
  46.2 2.2 %copy-start = (bf16[8,2048,128]{2,1,0:T(8,128)(2,1)S(1)}, bf16[8,2048,128]{2,1,0:T(8,128)(2,1)}, u32[]{:S(2)}) copy-start(bf16[8,2048,128]{2,1,0:T(8,128)(2,1)} %refs_1_.3) | copy-start | bytes 12582916
  48.4 1.2 %copy-start.9 = (bf16[272,2048]{1,0:T(8,128)(2,1)S(1)}, bf16[272,2048]{1,0:T(8,128)(2,1)}, u32[]{:S(2)}) copy-start(bf16[272,2048]{1,0:T(8,128)(2,1)} %copy-done.8) | copy-start | bytes 3342340
  49.7 14.7 %copy-start.1 = (bf16[8,2048,128]{2,1,0:T(8,128)(2,1)S(1)}, bf16[8,2048,128]{2,1,0:T(8,128)(2,1)}, u32[]{:S(2)}) copy-start(bf16[8,2048,128]{2,1,0:T(8,128)(2,1)} %refs_1_.3) | copy-start | bytes 12582916
  72.4 10.7 %collective-permute-start.7 = (bf16[816,128]{1,0:T(8,128)(2,1)S(1)}, bf16[816,128]{1,0:T(8,128)(2,1)S(1)}, u32[]{:S(2)}, u32[]{:S(2)}) collective-permute-start(bf16[816,128]{1,0:T(8,128)(2,1)S(1)} %get-tuple-element.48.refs_0_), channel_id=1, source_target_pairs={{0,1},{1,0},{2,3},{3,2},{4,5},{5,4},{6,7},{7,6},{8,9},{9,8},{10,11... | collective-permute-start | bytes 626696 | tf_op jit(solution)/shard_map/ppermute | solution.py:311
  74.0 19.5 %collective-permute-start.8 = (bf16[816,128]{1,0:T(8,128)(2,1)S(1)}, bf16[816,128]{1,0:T(8,128)(2,1)S(1)}, u32[]{:S(2)}, u32[]{:S(2)}) collective-permute-start(bf16[816,128]{1,0:T(8,128)(2,1)S(1)} %get-tuple-element.48.refs_0_), channel_id=1, source_target_pairs={{0,2},{1,3},{2,0},{3,1},{4,6},{5,7},{6,4},{7,5},{8,10},{9,11},{10,... | collective-permute-start | bytes 626696 | tf_op jit(solution)/shard_map/ppermute | solution.py:311
  76.6 19.0 %collective-permute-start.9 = (bf16[816,128]{1,0:T(8,128)(2,1)S(1)}, bf16[816,128]{1,0:T(8,128)(2,1)S(1)}, u32[]{:S(2)}, u32[]{:S(2)}) collective-permute-start(bf16[816,128]{1,0:T(8,128)(2,1)S(1)} %get-tuple-element.48.refs_0_), channel_id=1, source_target_pairs={{0,3},{1,2},{2,1},{3,0},{4,7},{5,6},{6,5},{7,4},{8,11},{9,10},{10,... | collective-permute-start | bytes 626696 | tf_op jit(solution)/shard_map/ppermute | solution.py:311
  82.4 17.0 %collective-permute-start.13 = (bf16[272,128]{1,0:T(8,128)(2,1)S(1)}, bf16[272,128]{1,0:T(8,128)(2,1)S(1)}, u32[]{:S(2)}, u32[]{:S(2)}) collective-permute-start(bf16[272,128]{1,0:T(8,128)(2,1)S(1)} %get-tuple-element.55.refs_0_), channel_id=1, source_target_pairs={{0,1},{1,0},{2,3},{3,2},{4,5},{5,4},{6,7},{7,6},{8,9},{9,8},{10,11... | collective-permute-start | bytes 208904 | tf_op jit(solution)/shard_map/ppermute | solution.py:311
  83.1 16.3 %collective-permute-start.14 = (bf16[272,128]{1,0:T(8,128)(2,1)S(1)}, bf16[272,128]{1,0:T(8,128)(2,1)S(1)}, u32[]{:S(2)}, u32[]{:S(2)}) collective-permute-start(bf16[272,128]{1,0:T(8,128)(2,1)S(1)} %get-tuple-element.55.refs_0_), channel_id=1, source_target_pairs={{0,2},{1,3},{2,0},{3,1},{4,6},{5,7},{6,4},{7,5},{8,10},{9,11},{10,... | collective-permute-start | bytes 208904 | tf_op jit(solution)/shard_map/ppermute | solution.py:311
  93.5 6.1 %collective-permute-start.15 = (bf16[272,128]{1,0:T(8,128)(2,1)S(1)}, bf16[272,128]{1,0:T(8,128)(2,1)S(1)}, u32[]{:S(2)}, u32[]{:S(2)}) collective-permute-start(bf16[272,128]{1,0:T(8,128)(2,1)S(1)} %get-tuple-element.55.refs_0_), channel_id=1, source_target_pairs={{0,3},{1,2},{2,1},{3,0},{4,7},{5,6},{6,5},{7,4},{8,11},{9,10},{10,... | collective-permute-start | bytes 208904 | tf_op jit(solution)/shard_map/ppermute | solution.py:311
  95.6 13.3 %copy-start.11 = (f32[512,512]{1,0:T(8,128)S(1)}, f32[512,512]{1,0:T(8,128)}, u32[]{:S(2)}) copy-start(f32[512,512]{1,0:T(8,128)} %copy-done.10) | copy-start | bytes 3145732
  96.7 12.2 %copy-start.7 = (bf16[512,1536]{1,0:T(8,128)(2,1)S(1)}, bf16[512,1536]{1,0:T(8,128)(2,1)}, u32[]{:S(2)}) copy-start(bf16[512,1536]{1,0:T(8,128)(2,1)} %copy-done.6) | copy-start | bytes 4718596
  96.7 9.5 %collective-permute-start.10 = (bf16[272,512]{1,0:T(8,128)(2,1)S(1)}, bf16[272,512]{1,0:T(8,128)(2,1)S(1)}, u32[]{:S(2)}, u32[]{:S(2)}) collective-permute-start(bf16[272,512]{1,0:T(8,128)(2,1)S(1)} %get-tuple-element.51), channel_id=1, source_target_pairs={{0,8},{4,12},{8,0},{12,4},{16,24},{20,28},{24,16},{28,20},{1,9},{5... | collective-permute-start | bytes 835592 | tf_op jit(solution)/shard_map/ppermute | solution.py:311
  96.8 12.1 %collective-permute-start.11 = (bf16[272,512]{1,0:T(8,128)(2,1)S(1)}, bf16[272,512]{1,0:T(8,128)(2,1)S(1)}, u32[]{:S(2)}, u32[]{:S(2)}) collective-permute-start(bf16[272,512]{1,0:T(8,128)(2,1)S(1)} %get-tuple-element.52), channel_id=1, source_target_pairs={{0,16},{4,20},{8,24},{12,28},{16,0},{20,4},{24,8},{28,12},{1,17},{... | collective-permute-start | bytes 835592 | tf_op jit(solution)/shard_map/ppermute | solution.py:311
  100.1 8.8 %collective-permute-start.16 = (bf16[272,512]{1,0:T(8,128)(2,1)S(1)}, bf16[272,512]{1,0:T(8,128)(2,1)S(1)}, u32[]{:S(2)}, u32[]{:S(2)}) collective-permute-start(bf16[272,512]{1,0:T(8,128)(2,1)S(1)} %grow_rows.3), channel_id=1, source_target_pairs={{0,24},{4,28},{8,16},{12,20},{16,8},{20,12},{24,0},{28,4},{1,25},{... | collective-permute-start | bytes 835592 | tf_op jit(solution)/shard_map/ppermute | solution.py:311

commit v4 on v3

--- a/solution.py
+++ b/solution.py
@@ -10,7 +10,7 @@
 adapter_scale = 0.5
 BF = jnp.bfloat16
 F32 = jnp.float32
-VMEM_LIMIT = 26 * 1024 * 1024
+VMEM_LIMIT = 60 * 1024 * 1024
 COST = pl.CostEstimate(flops=1000, bytes_accessed=1000, transcendentals=0)
 
 
@@ -268,19 +268,23 @@
 
 
 def finish_kernel(sizes, count, *refs):
-    bases, spread_ref, updates, out = refs[:count], refs[count], refs[count + 1:-1], refs[-1]
+    bases, spreads, out = refs[:count], refs[count:count + len(sizes)], refs[-1]
+    updates = refs[count + len(sizes):-1]
     total = bases[0][...]
     for base in bases[1:]:
         total = total + base[...].astype(F32)
     update_rows = jnp.zeros(total.shape, F32)
-    start = 0
-    for update, size in zip(updates, sizes):
-        padded = round_up(size, 128)
-        rows = update[...]
-        if padded > size:
-            rows = jnp.concatenate([rows, jnp.zeros((padded - size, rows.shape[1]), rows.dtype)], axis=0)
-        update_rows = update_rows + dot(spread_ref[:, start:start + padded], rows)
-        start += padded
+    done = 0
+    for spread, group in zip(spreads, sizes):
+        start = 0
+        for size in group:
+            padded = round_up(size, 128)
+            rows = updates[done][...]
+            if padded > size:
+                rows = jnp.concatenate([rows, jnp.zeros((padded - size, rows.shape[1]), rows.dtype)], axis=0)
+            update_rows = update_rows + dot(spread[:, start:start + padded], rows)
+            start += padded
+            done += 1
     total = total + update_rows
     columns = out.shape[2]
     if columns % 128:
@@ -291,19 +295,20 @@
         out[...] = jnp.swapaxes(both, 0, 1)
 
 
-def finish(bases, spread, updates):
-    sizes = tuple(u.shape[0] for u in updates)
+def finish(bases, spreads, groups):
+    sizes = tuple(tuple(u.shape[0] for u in group) for group in groups)
     rows, both = bases[0].shape
+    updates = [u for group in groups for u in group]
     vmem = pl.BlockSpec(memory_space=pltpu.VMEM)
     return pl.pallas_call(
         functools.partial(finish_kernel, sizes, len(bases)),
-        in_specs=[vmem] * (len(bases) + 1 + len(updates)),
+        in_specs=[vmem] * (len(bases) + len(spreads) + len(updates)),
         out_specs=vmem,
         out_shape=jax.ShapeDtypeStruct((rows, 2, both // 2), BF),
         cost_estimate=COST,
         compiler_params=pltpu.CompilerParams(vmem_limit_bytes=VMEM_LIMIT),
         name="finish_rows",
-    )(*bases, spread, *updates)
+    )(*bases, *spreads, *updates)
 
 
 def exchange(array, axis, shift):
@@ -347,8 +352,9 @@
 
     near = [m for m in range(chips) if bits(m) <= 1]
     far = [m for m in range(chips) if bits(m) > 1]
-    message = round_up(full + 1, 16)
-    sizes, first_rows = (message,) * chips, (0,) * chips
+    whole, message = round_up(full + 1, 16), round_up(full * 11 // 16, 16)
+    rest = round_up(full - message + 2, 16)
+    sizes, first_rows = (whole,) + (message,) * (chips - 1), (0,) * chips
 
     packed = pack(chip, adapters, slots, tokens, sizes, first_rows, chip_slots)
     sent, spread = list(packed[:-1]), packed[-1]
@@ -363,18 +369,21 @@
     def arrived_for(r):
         return [came[key] for key in sorted(came) if key[1] == r]
 
-    for m in far:
-        arrived[m] = exchange(after(sent[m], parts[0], down_sibling), "dp", 2 * m)
+    carry = shrink(core, [after(sent[0], parts[0])], adapter_down_weight, down_sibling, flag_lane)
+    up_sibling = exchange(after(adapter_up_weight, down_sibling), "dp", 1)
+    near_done = [arrived[m] for m in near[1:]] + [carry[0]]
     for r in sorted(range(1, blocks), key=lambda r: (r & -r, -r)):
         low = r & -r
         part = parts[r]
         for one in arrived_for(r):
             part = part + one.astype(F32)
+        if r == 1:
+            part = after(part, *near_done)
         came[(low, r ^ low)] = exchange(part.astype(BF), "tensor", low)
-
-    own = after(sent[0], came[(1, blocks - 2)])
-    carry = shrink(core, [own], adapter_down_weight, down_sibling, flag_lane)
-    up_sibling = exchange(after(adapter_up_weight, down_sibling), "dp", 1)
+    for m in far:
+        arrived[m] = exchange(after(sent[m], *near_done), "dp", 2 * m)
+
+    flags = []
     for part in (near, far):
         if not part:
             continue
@@ -382,12 +391,31 @@
         share, place, flag = shrink(
             core, group, adapter_down_weight, after(down_sibling, up_sibling), flag_lane, carry if part is near else ()
         )
+        flags.append(flag)
         other = came[(1, 0)] if part is near else came[(blocks // 2, 0)]
         shares = [after(share, other)] + [exchange(share, "tensor", z) for z in range(1, blocks)]
         grown = grow(core, shares, place, adapter_up_weight, up_sibling, tuple(sizes[m] for m in part))
         for m, update in zip(part, grown):
             returned[m] = update if m == 0 else exchange(update, "dp", 2 * m)
-    return finish([parts[0]] + arrived_for(0), spread, [returned[m] for m in range(chips)])
+    flag = functools.reduce(jnp.maximum, flags)
+    flag = jnp.maximum(flag, exchange(flag, "dp", 1))
+    bases = [parts[0]] + arrived_for(0)
+    updates = [returned[m] for m in range(chips)]
+
+    def as_is():
+        return finish(bases, [spread], [updates])
+
+    def second_round():
+        later_sizes, later_rows = (16,) + (rest,) * (chips - 1), (full,) + (message - 1,) * (chips - 1)
+        packed = pack(chip, adapters, slots, tokens, later_sizes, later_rows, chip_slots)
+        group = [packed[0]] + [exchange(packed[m], "dp", 2 * m) for m in range(1, chips)]
+        share, place, _ = shrink(core, group, adapter_down_weight, down_sibling, flag_lane)
+        shares = [share] + [exchange(share, "tensor", z) for z in range(1, blocks)]
+        grown = grow(core, shares, place, adapter_up_weight, up_sibling, later_sizes)
+        back = [grown[0]] + [exchange(grown[m], "dp", 2 * m) for m in range(1, chips)]
+        return finish(bases, [spread, packed[-1]], [updates, back])
+
+    return lax.cond(flag[0, 0] > 0.0, second_round, as_is)
 
 
 def solution(mesh):

time: 113 us -> 97.5 us (0.86)
  waiting for transfers between devices: 36.1 us -> 20.9 us
  local copies, waits for them, and re-layouts: 12 us -> 2.21 us
  Pallas kernels: 38.1 us -> 45.6 us
    ppermute x17 -> x18, waiting for transfers between devices: 36.1 us -> 20.9 us  [exchange(): return lax.ppermute(array, axis, [(i, i ^ shift) for i in range(size)])]
    unnamed x28 -> x20, local copies, waits for them, and re-layouts: 12 us -> 1.63 us
    pallas_call x2, Pallas kernels: 1.58 us -> 5.28 us  [grow(): pl.pallas_call(functools.partial(grow_kernel, len(parts), sizes), in_spec...]
    pallas_call x1, Pallas kernels: 8.89 us -> 11.3 us  [base_parts(): pl.pallas_call(functools.partial(base_kernel, steps, blocks), grid=(steps...]
    pallas_call x3, Pallas kernels: 18.7 us -> 20.1 us  [shrink(): pl.pallas_call(functools.partial(shrink_kernel, len(messages), len(carry)...]
    ppermute x17 -> x18, starting transfers between devices: 25.2 us -> 25.7 us  [exchange(): return lax.ppermute(array, axis, [(i, i ^ shift) for i in range(size)])]
  transfers between devices with their start and end apart: 17 -> 18, of which waited for: 6 -> 5; matrix products, arithmetic and copies ran while one was open for 1% -> 2% of each run, Pallas kernels for 31% -> 44%
where the time goes in v4:
time: 97.5 us; the launch traced here: 97.1 us
  Pallas kernels  45.6 us (47%)
  starting transfers between devices  25.7 us (26%)
  waiting for transfers between devices  20.9 us (21%)
  local copies, waits for them, and re-layouts  2.21 us (2%)
  other arithmetic  1.65 us (2%)
    ppermute x18, starting transfers between devices, exchange(): return lax.ppermute(array, axis, [(i, i ^ shift) for i in range(size)])  25.7 us
    ppermute x18, waiting for transfers between devices, exchange(): return lax.ppermute(array, axis, [(i, i ^ shift) for i in range(size)])  20.9 us
    pallas_call x3, Pallas kernels, shrink(): pl.pallas_call(functools.partial(shrink_kernel, len(messages), len(carry)...  20.1 us
    pallas_call x1, Pallas kernels, base_parts(): pl.pallas_call(functools.partial(base_kernel, steps, blocks), grid=(steps...  11.3 us
    pallas_call x1, Pallas kernels, pack(): pl.pallas_call(functools.partial(pack_kernel, (sizes, first_rows, chip_sl...  6.08 us
    pallas_call x2, Pallas kernels, grow(): pl.pallas_call(functools.partial(grow_kernel, len(parts), sizes), in_spec...  5.28 us
    pallas_call x1, Pallas kernels, finish(): pl.pallas_call(functools.partial(finish_kernel, sizes, len(bases)), in_sp...  2.86 us
  transfers between devices with their start and end apart: 18, of which 5 were waited for; matrix products, arithmetic and copies ran while one was open for 2% of the time, Pallas kernels for 44%

profile of v4, /device:TPU:0, one launch (start us, length us, event | category | flops | bytes accessed | tf_op | source)
XLA Modules:
  0.0 97.1 jit_solution(1858880764753167387)
XLA Ops:
  0.0 0.5 collective-permute-start.11
  0.5 6.1 %pack_rows.3 = (bf16[272,2048]{1,0:T(8,128)(2,1)}, bf16[176,2048]{1,0:T(8,128)(2,1)}, bf16[176,2048]{1,0:T(8,128)(2,1)}, bf16[176,2048]{1,0:T(8,128)(2,1)}, bf16[512,1152]{1,0:T(8,128)(2,1)S(1)}) custom-call(s32[1]{0:T(128)} %bitcast.1.place_ref, s32[1,512]{1,0:T(1,128)} %bitcast.6, s32[1,64]{1,0:T(1,128)} %bitcast.8, bf16[512,2048]{1,0:T(8,128)(2,1)} %tokens_ref.2), custom_call_target="tpu_custom_call" | custom-call | flops 1000 | bytes 1000 | tf_op jit(solution)/shard_map/pack_rows/pallas_call | solution.py:83
  6.5 2.5 %collective-permute-start.10 = (bf16[176,2048]{1,0:T(8,128)(2,1)}, bf16[176,2048]{1,0:T(8,128)(2,1)S(1)}, u32[]{:S(2)}, u32[]{:S(2)}) collective-permute-start(bf16[176,2048]{1,0:T(8,128)(2,1)} %get-tuple-element.124), channel_id=1, source_target_pairs={{0,16},{4,20},{8,24},{12,28},{16,0},{20,4},{24,8},{28,12},{1,17},{... | collective-permute-start | bytes 2162696 | tf_op jit(solution)/shard_map/ppermute | solution.py:316
  9.1 1.5 %collective-permute-start.9 = (bf16[176,2048]{1,0:T(8,128)(2,1)}, bf16[176,2048]{1,0:T(8,128)(2,1)}, u32[]{:S(2)}, u32[]{:S(2)}) collective-permute-start(bf16[176,2048]{1,0:T(8,128)(2,1)} %get-tuple-element.123), channel_id=1, source_target_pairs={{0,8},{4,12},{8,0},{12,4},{16,24},{20,28},{24,16},{28,20},{1,9},{5... | collective-permute-start | bytes 2162696 | tf_op jit(solution)/shard_map/ppermute | solution.py:316
  10.6 11.3 %base_parts.1 = (f32[512,512]{1,0:T(8,128)}, bf16[512,512]{1,0:T(8,128)(2,1)}, f32[512,512]{1,0:T(8,128)}, bf16[512,512]{1,0:T(8,128)(2,1)}) custom-call(s32[1]{0:T(128)} %bitcast.4.place_ref, bf16[512,2048]{1,0:T(8,128)(2,1)} %tokens_ref.2, bf16[2048,2,1024]{2,1,0:T(2,128)(2,1)} %weight_ref.1), custom_call_target="tpu_custom_call" | custom-call | flops 1000 | bytes 1000 | tf_op jit(solution)/shard_map/base_parts/pallas_call | solution.py:253
  21.9 1.6 %collective-permute-start.16 = (bf16[512,512]{1,0:T(8,128)(2,1)}, bf16[512,512]{1,0:T(8,128)(2,1)S(1)}, u32[]{:S(2)}, u32[]{:S(2)}) collective-permute-start(bf16[512,512]{1,0:T(8,128)(2,1)} %get-tuple-element.141), channel_id=1, source_target_pairs={{0,1},{1,0},{2,3},{3,2},{4,5},{5,4},{6,7},{7,6},{8,9},{9,8},{10,11... | collective-permute-start | bytes 1572872 | tf_op jit(solution)/shard_map/ppermute | solution.py:316
  23.5 6.8 %shrink_rows.5 = (bf16[272,128]{1,0:T(8,128)(2,1)}, bf16[272,128]{1,0:T(8,128)(2,1)}, f32[8,128]{1,0:T(8,128)}) custom-call(s32[1]{0:T(128)} %bitcast.core_ref, bf16[272,2048]{1,0:T(8,128)(2,1)} %get-tuple-element.131.refs_0_, bf16[8,2048,128]{2,1,0:T(8,128)(2,1)} %refs_1_.3, bf16[8,2048,128]{2,1,0:T(8,128)(2,1)} %collective-permute-done.11.refs_2_.refs_3_), custom_call_target="tpu_custom_call" | custom-call | flops 1000 | bytes 1000 | tf_op jit(solution)/shard_map/shrink_rows/pallas_call | solution.py:156
  30.3 0.5 collective-permute-start.13
  31.0 5.9 %collective-permute-done.16 = bf16[512,512]{1,0:T(8,128)(2,1)S(1)} collective-permute-done((bf16[512,512]{1,0:T(8,128)(2,1)}, bf16[512,512]{1,0:T(8,128)(2,1)S(1)}, u32[]{:S(2)}, u32[]{:S(2)}) %collective-permute-start.16) | collective-permute-done | bytes 524320 | tf_op jit(solution)/shard_map/ppermute | solution.py:316
  36.9 1.0 add_convert_fusion
  37.9 2.6 %collective-permute-start.17 = (bf16[512,512]{1,0:T(8,128)(2,1)}, bf16[512,512]{1,0:T(8,128)(2,1)}, u32[]{:S(2)}, u32[]{:S(2)}) collective-permute-start(bf16[512,512]{1,0:T(8,128)(2,1)} %add_convert_fusion), channel_id=1, source_target_pairs={{0,2},{1,3},{2,0},{3,1},{4,6},{5,7},{6,4},{7,5},{8,10},{9,11},{10,... | collective-permute-start | bytes 1572872 | tf_op jit(solution)/shard_map/ppermute | solution.py:316
  40.5 0.8 copy-done.2
  41.3 7.4 %shrink_rows.6 = (bf16[624,128]{1,0:T(8,128)(2,1)}, bf16[624,128]{1,0:T(8,128)(2,1)}, f32[8,128]{1,0:T(8,128)}) custom-call(s32[1]{0:T(128)} %bitcast.core_ref, bf16[176,2048]{1,0:T(8,128)(2,1)} %collective-permute-done.9.refs_0_, bf16[176,2048]{1,0:T(8,128)(2,1)} %copy-done.6, bf16[8,2048,128]{2,1,0:T(8,128)(2,1)} %refs_1_.3, ...), custom_call_target="tpu_custom_call" | custom-call | flops 1000 | bytes 1000 | tf_op jit(solution)/shard_map/shrink_rows/pallas_call | solution.py:156
  48.7 1.6 %collective-permute-start.18 = (bf16[624,128]{1,0:T(8,128)(2,1)}, bf16[624,128]{1,0:T(8,128)(2,1)S(1)}, u32[]{:S(2)}, u32[]{:S(2)}) collective-permute-start(bf16[624,128]{1,0:T(8,128)(2,1)} %get-tuple-element.144.refs_0_), channel_id=1, source_target_pairs={{0,1},{1,0},{2,3},{3,2},{4,5},{5,4},{6,7},{7,6},{8,9},{9,8},{10,11... | collective-permute-start | bytes 479240 | tf_op jit(solution)/shard_map/ppermute | solution.py:316
  50.7 2.5 %collective-permute-start.20 = (bf16[624,128]{1,0:T(8,128)(2,1)}, bf16[624,128]{1,0:T(8,128)(2,1)}, u32[]{:S(2)}, u32[]{:S(2)}) collective-permute-start(bf16[624,128]{1,0:T(8,128)(2,1)} %get-tuple-element.144.refs_0_), channel_id=1, source_target_pairs={{0,3},{1,2},{2,1},{3,0},{4,7},{5,6},{6,5},{7,4},{8,11},{9,10},{10,... | collective-permute-start | bytes 479240 | tf_op jit(solution)/shard_map/ppermute | solution.py:316
  53.1 5.9 %shrink_rows.7 = (bf16[176,128]{1,0:T(8,128)(2,1)}, bf16[176,128]{1,0:T(8,128)(2,1)}, f32[8,128]{1,0:T(8,128)}) custom-call(s32[1]{0:T(128)} %bitcast.core_ref, bf16[176,2048]{1,0:T(8,128)(2,1)} %collective-permute-done.13.refs_0_, bf16[8,2048,128]{2,1,0:T(8,128)(2,1)} %refs_1_.3, bf16[8,2048,128]{2,1,0:T(8,128)(2,1)} %collective-permute-done.11.refs_2_.refs_3_), custom_call_target="tpu_custom_call" | custom-call | flops 1000 | bytes 1000 | tf_op jit(solution)/shard_map/shrink_rows/pallas_call | solution.py:156
  59.1 0.7 collective-permute-start.23
  59.8 3.2 %collective-permute-done.18.refs_1_ = bf16[624,128]{1,0:T(8,128)(2,1)S(1)} collective-permute-done((bf16[624,128]{1,0:T(8,128)(2,1)}, bf16[624,128]{1,0:T(8,128)(2,1)S(1)}, u32[]{:S(2)}, u32[]{:S(2)}) %collective-permute-start.18) | collective-permute-done | bytes 159776 | tf_op jit(solution)/shard_map/ppermute | solution.py:316
  63.0 2.5 %collective-permute-start.24 = (bf16[176,128]{1,0:T(8,128)(2,1)}, bf16[176,128]{1,0:T(8,128)(2,1)}, u32[]{:S(2)}, u32[]{:S(2)}) collective-permute-start(bf16[176,128]{1,0:T(8,128)(2,1)} %get-tuple-element.150.refs_0_), channel_id=1, source_target_pairs={{0,2},{1,3},{2,0},{3,1},{4,6},{5,7},{6,4},{7,5},{8,10},{9,11},{10,... | collective-permute-start | bytes 135176 | tf_op jit(solution)/shard_map/ppermute | solution.py:316
  65.4 9.6 %collective-permute-done.19.refs_2_ = bf16[624,128]{1,0:T(8,128)(2,1)S(1)} collective-permute-done((bf16[624,128]{1,0:T(8,128)(2,1)}, bf16[624,128]{1,0:T(8,128)(2,1)S(1)}, u32[]{:S(2)}, u32[]{:S(2)}) %collective-permute-start.19) | collective-permute-done | bytes 159776 | tf_op jit(solution)/shard_map/ppermute | solution.py:316
  75.0 5.2 %collective-permute-start.25 = (bf16[176,128]{1,0:T(8,128)(2,1)}, bf16[176,128]{1,0:T(8,128)(2,1)}, u32[]{:S(2)}, u32[]{:S(2)}) collective-permute-start(bf16[176,128]{1,0:T(8,128)(2,1)} %get-tuple-element.150.refs_0_), channel_id=1, source_target_pairs={{0,3},{1,2},{2,1},{3,0},{4,7},{5,6},{6,5},{7,4},{8,11},{9,10},{10,... | collective-permute-start | bytes 135176 | tf_op jit(solution)/shard_map/ppermute | solution.py:316
  80.3 3.0 %grow_rows.4 = (bf16[272,512]{1,0:T(8,128)(2,1)S(1)}, bf16[176,512]{1,0:T(8,128)(2,1)}, bf16[176,512]{1,0:T(8,128)(2,1)}) custom-call(s32[1]{0:T(128)} %bitcast.core_ref, bf16[624,128]{1,0:T(8,128)(2,1)} %get-tuple-element.144.refs_0_, bf16[624,128]{1,0:T(8,128)(2,1)} %copy-done.11, bf16[624,128]{1,0:T(8,128)(2,1)} %copy-done.12, ...), custom_call_target="tpu_custom_call" | custom-call | flops 1000 | bytes 1000 | tf_op jit(solution)/shard_map/grow_rows/pallas_call | solution.py:209
  83.3 0.5 collective-permute-start.21
  84.2 2.3 %grow_rows.5 = bf16[176,512]{1,0:T(8,128)(2,1)} custom-call(s32[1]{0:T(128)} %bitcast.core_ref, bf16[176,128]{1,0:T(8,128)(2,1)} %get-tuple-element.150.refs_0_, bf16[176,128]{1,0:T(8,128)(2,1)} %collective-permute-done.23.refs_1_, bf16[176,128]{1,0:T(8,128)(2,1)} %collective-permute-done.24.refs_2_, bf16[176,128]{1,0:T(8,128)(2,1)} %collective-permute-done.25.refs_3_, ...), custom_call_target="tpu_custom_call" | custom-call | flops 1000 | bytes 1000 | tf_op jit(solution)/shard_map/grow_rows/pallas_call | solution.py:209
  86.5 2.5 %collective-permute-start.26 = (bf16[176,512]{1,0:T(8,128)(2,1)}, bf16[176,512]{1,0:T(8,128)(2,1)}, u32[]{:S(2)}, u32[]{:S(2)}) collective-permute-start(bf16[176,512]{1,0:T(8,128)(2,1)} %grow_rows.5), channel_id=1, source_target_pairs={{0,24},{4,28},{8,16},{12,20},{16,8},{20,12},{24,0},{28,4},{1,25},{... | collective-permute-start | bytes 540680 | tf_op jit(solution)/shard_map/ppermute | solution.py:316
  89.0 0.7 max.6
  89.7 1.2 %collective-permute-done.14 = f32[8,128]{1,0:T(8,128)S(1)} collective-permute-done((f32[8,128]{1,0:T(8,128)S(1)}, f32[8,128]{1,0:T(8,128)S(1)}, u32[]{:S(2)}, u32[]{:S(2)}) %collective-permute-start.14) | collective-permute-done | bytes 4128 | tf_op jit(solution)/shard_map/ppermute | solution.py:316
  90.9 0.6 slice.3
  92.2 1.1 %collective-permute-done.26 = bf16[176,512]{1,0:T(8,128)(2,1)} collective-permute-done((bf16[176,512]{1,0:T(8,128)(2,1)}, bf16[176,512]{1,0:T(8,128)(2,1)}, u32[]{:S(2)}, u32[]{:S(2)}) %collective-permute-start.26) | collective-permute-done | bytes 180256 | tf_op jit(solution)/shard_map/ppermute | solution.py:316
  93.2 3.1 %conditional.1 = (bf16[512,2,256]{2,1,0:T(2,128)(2,1)S(1)}) conditional(s32[]{:T(128)} %bitcast.5, (f32[512,512]{1,0:T(8,128)}, bf16[512,512]{1,0:T(8,128)(2,1)}, bf16[512,512]{1,0:T(8,128)(2,1)}, bf16[512,1152]{1,0:T(8,128)(2,1)S(1)}, bf16[272,512]{1,0:T(8,128)(2,1)S(1)}, /*index=5*/bf16[176,512]{1,0:T(8,128)(2,1)}, bf16[176,512]{1,0:T(8,128)(2,1)}, ...), branch_computations={%region_0.1_spmd, %region_1.2_spmd} | conditional | flops 4000 | bytes 19960388 | solution.py:418
  93.2 2.9 %finish_rows.2 = bf16[512,2,256]{2,1,0:T(2,128)(2,1)S(1)} custom-call(f32[512,512]{1,0:T(8,128)} %get-tuple-element.58.refs_0_, bf16[512,512]{1,0:T(8,128)(2,1)} %get-tuple-element.59.refs_1_, bf16[512,512]{1,0:T(8,128)(2,1)} %get-tuple-element.60.refs_2_, bf16[512,1152]{1,0:T(8,128)(2,1)S(1)} %get-tuple-element.61.refs_3_, ...), custom_call_target="tpu_custom_call" | custom-call | flops 1000 | bytes 1000 | tf_op jit(solution)/shard_map/cond/branch_0_fun/finish_rows/pallas_call | solution.py:303
  96.3 0.8 copy-done.7
  (37 shorter events, 1.0 us)
Async XLA Ops:
  0.0 23.5 %collective-permute-start.11 = (bf16[8,2048,128]{2,1,0:T(8,128)(2,1)}, bf16[8,2048,128]{2,1,0:T(8,128)(2,1)}, u32[]{:S(2)}, u32[]{:S(2)}) collective-permute-start(bf16[8,2048,128]{2,1,0:T(8,128)(2,1)} %refs_1_.3), channel_id=1, source_target_pairs={{0,4},{4,0},{8,12},{12,8},{16,20},{20,16},{24,28},{28,24},{1,5},{5... | collective-permute-start | bytes 12582920 | tf_op jit(solution)/shard_map/ppermute | solution.py:316
  6.5 23.7 %collective-permute-start.10 = (bf16[176,2048]{1,0:T(8,128)(2,1)}, bf16[176,2048]{1,0:T(8,128)(2,1)S(1)}, u32[]{:S(2)}, u32[]{:S(2)}) collective-permute-start(bf16[176,2048]{1,0:T(8,128)(2,1)} %get-tuple-element.124), channel_id=1, source_target_pairs={{0,16},{4,20},{8,24},{12,28},{16,0},{20,4},{24,8},{28,12},{1,17},{... | collective-permute-start | bytes 2162696 | tf_op jit(solution)/shard_map/ppermute | solution.py:316
  9.1 21.2 %collective-permute-start.9 = (bf16[176,2048]{1,0:T(8,128)(2,1)}, bf16[176,2048]{1,0:T(8,128)(2,1)}, u32[]{:S(2)}, u32[]{:S(2)}) collective-permute-start(bf16[176,2048]{1,0:T(8,128)(2,1)} %get-tuple-element.123), channel_id=1, source_target_pairs={{0,8},{4,12},{8,0},{12,4},{16,24},{20,28},{24,16},{28,20},{1,9},{5... | collective-permute-start | bytes 2162696 | tf_op jit(solution)/shard_map/ppermute | solution.py:316
  21.9 15.0 %collective-permute-start.16 = (bf16[512,512]{1,0:T(8,128)(2,1)}, bf16[512,512]{1,0:T(8,128)(2,1)S(1)}, u32[]{:S(2)}, u32[]{:S(2)}) collective-permute-start(bf16[512,512]{1,0:T(8,128)(2,1)} %get-tuple-element.141), channel_id=1, source_target_pairs={{0,1},{1,0},{2,3},{3,2},{4,5},{5,4},{6,7},{7,6},{8,9},{9,8},{10,11... | collective-permute-start | bytes 1572872 | tf_op jit(solution)/shard_map/ppermute | solution.py:316
  23.5 7.3 %copy-start.1 = (bf16[8,2,64,256]{3,2,1,0:T(8,128)(2,1)S(1)}, bf16[8,2,64,256]{3,2,1,0:T(8,128)(2,1)}, u32[]{:S(2)}) copy-start(bf16[8,2,64,256]{3,2,1,0:T(8,128)(2,1)} %refs_5_.3) | copy-start | bytes 1572868
  23.5 13.4 %copy-start.5 = (f32[512,512]{1,0:T(8,128)S(1)}, f32[512,512]{1,0:T(8,128)}, u32[]{:S(2)}) copy-start(f32[512,512]{1,0:T(8,128)} %get-tuple-element.140) | copy-start | bytes 3145732
  30.3 11.0 %copy-start.6 = (bf16[176,2048]{1,0:T(8,128)(2,1)}, bf16[176,2048]{1,0:T(8,128)(2,1)S(1)}, u32[]{:S(2)}) copy-start(bf16[176,2048]{1,0:T(8,128)(2,1)S(1)} %collective-permute-done.10.refs_1_) | copy-start | bytes 2162692
  30.3 20.4 %collective-permute-start.13 = (bf16[176,2048]{1,0:T(8,128)(2,1)}, bf16[176,2048]{1,0:T(8,128)(2,1)}, u32[]{:S(2)}, u32[]{:S(2)}) collective-permute-start(bf16[176,2048]{1,0:T(8,128)(2,1)} %get-tuple-element.136), channel_id=1, source_target_pairs={{0,24},{4,28},{8,16},{12,20},{16,8},{20,12},{24,0},{28,4},{1,25},{... | collective-permute-start | bytes 2162696 | tf_op jit(solution)/shard_map/ppermute | solution.py:316
  30.8 9.6 %collective-permute-start.12 = (bf16[8,2,64,256]{3,2,1,0:T(8,128)(2,1)S(1)}, bf16[8,2,64,256]{3,2,1,0:T(8,128)(2,1)S(1)}, u32[]{:S(2)}, u32[]{:S(2)}) collective-permute-start(bf16[8,2,64,256]{3,2,1,0:T(8,128)(2,1)S(1)} %copy-done.1), channel_id=1, source_target_pairs={{0,4},{4,0},{8,12},{12,8},{16,20},{20,16},{24,28},{28,24},{1,5},{5... | collective-permute-start | bytes 1572872 | tf_op jit(solution)/shard_map/ppermute | solution.py:316
  30.8 28.2 %collective-permute-start.15 = (bf16[512,512]{1,0:T(8,128)(2,1)}, bf16[512,512]{1,0:T(8,128)(2,1)}, u32[]{:S(2)}, u32[]{:S(2)}) collective-permute-start(bf16[512,512]{1,0:T(8,128)(2,1)} %get-tuple-element.139), channel_id=1, source_target_pairs={{0,1},{1,0},{2,3},{3,2},{4,5},{5,4},{6,7},{7,6},{8,9},{9,8},{10,11... | collective-permute-start | bytes 1572872 | tf_op jit(solution)/shard_map/ppermute | solution.py:316
  37.9 45.9 %collective-permute-start.17 = (bf16[512,512]{1,0:T(8,128)(2,1)}, bf16[512,512]{1,0:T(8,128)(2,1)}, u32[]{:S(2)}, u32[]{:S(2)}) collective-permute-start(bf16[512,512]{1,0:T(8,128)(2,1)} %add_convert_fusion), channel_id=1, source_target_pairs={{0,2},{1,3},{2,0},{3,1},{4,6},{5,7},{6,4},{7,5},{8,10},{9,11},{10,... | collective-permute-start | bytes 1572872 | tf_op jit(solution)/shard_map/ppermute | solution.py:316
  40.5 0.8 copy-start.2
  48.7 40.4 %copy-start.20 = (f32[8,128]{1,0:T(8,128)S(1)}, f32[8,128]{1,0:T(8,128)}, u32[]{:S(2)}) copy-start(f32[8,128]{1,0:T(8,128)} %get-tuple-element.135) | copy-start | bytes 12292
  48.7 44.6 %copy-start = (bf16[512,2048]{1,0:T(8,128)(2,1)S(1)}, bf16[512,2048]{1,0:T(8,128)(2,1)}, u32[]{:S(2)}) copy-start(bf16[512,2048]{1,0:T(8,128)(2,1)} %tokens_ref.2) | copy-start | bytes 6291460
  48.7 44.6 %copy-start.19 = (s32[512,1]{0,1:T(1,128)S(1)}, s32[512,1]{0,1:T(1,128)}, u32[]{:S(2)}) copy-start(s32[512,1]{0,1:T(1,128)} %param.9) | copy-start | bytes 6148
  48.7 14.3 %collective-permute-start.18 = (bf16[624,128]{1,0:T(8,128)(2,1)}, bf16[624,128]{1,0:T(8,128)(2,1)S(1)}, u32[]{:S(2)}, u32[]{:S(2)}) collective-permute-start(bf16[624,128]{1,0:T(8,128)(2,1)} %get-tuple-element.144.refs_0_), channel_id=1, source_target_pairs={{0,1},{1,0},{2,3},{3,2},{4,5},{5,4},{6,7},{7,6},{8,9},{9,8},{10,11... | collective-permute-start | bytes 479240 | tf_op jit(solution)/shard_map/ppermute | solution.py:316
  50.3 24.7 %collective-permute-start.19 = (bf16[624,128]{1,0:T(8,128)(2,1)}, bf16[624,128]{1,0:T(8,128)(2,1)S(1)}, u32[]{:S(2)}, u32[]{:S(2)}) collective-permute-start(bf16[624,128]{1,0:T(8,128)(2,1)} %get-tuple-element.144.refs_0_), channel_id=1, source_target_pairs={{0,2},{1,3},{2,0},{3,1},{4,6},{5,7},{6,4},{7,5},{8,10},{9,11},{10,... | collective-permute-start | bytes 479240 | tf_op jit(solution)/shard_map/ppermute | solution.py:316
  50.7 29.6 %collective-permute-start.20 = (bf16[624,128]{1,0:T(8,128)(2,1)}, bf16[624,128]{1,0:T(8,128)(2,1)}, u32[]{:S(2)}, u32[]{:S(2)}) collective-permute-start(bf16[624,128]{1,0:T(8,128)(2,1)} %get-tuple-element.144.refs_0_), channel_id=1, source_target_pairs={{0,3},{1,2},{2,1},{3,0},{4,7},{5,6},{6,5},{7,4},{8,11},{9,10},{10,... | collective-permute-start | bytes 479240 | tf_op jit(solution)/shard_map/ppermute | solution.py:316
  59.1 25.2 %collective-permute-start.23 = (bf16[176,128]{1,0:T(8,128)(2,1)}, bf16[176,128]{1,0:T(8,128)(2,1)}, u32[]{:S(2)}, u32[]{:S(2)}) collective-permute-start(bf16[176,128]{1,0:T(8,128)(2,1)} %get-tuple-element.150.refs_0_), channel_id=1, source_target_pairs={{0,1},{1,0},{2,3},{3,2},{4,5},{5,4},{6,7},{7,6},{8,9},{9,8},{10,11... | collective-permute-start | bytes 135176 | tf_op jit(solution)/shard_map/ppermute | solution.py:316
  63.0 17.3 %copy-start.11 = (bf16[624,128]{1,0:T(8,128)(2,1)}, bf16[624,128]{1,0:T(8,128)(2,1)S(1)}, u32[]{:S(2)}) copy-start(bf16[624,128]{1,0:T(8,128)(2,1)S(1)} %collective-permute-done.18.refs_1_) | copy-start | bytes 479236
  63.0 21.3 %collective-permute-start.24 = (bf16[176,128]{1,0:T(8,128)(2,1)}, bf16[176,128]{1,0:T(8,128)(2,1)}, u32[]{:S(2)}, u32[]{:S(2)}) collective-permute-start(bf16[176,128]{1,0:T(8,128)(2,1)} %get-tuple-element.150.refs_0_), channel_id=1, source_target_pairs={{0,2},{1,3},{2,0},{3,1},{4,6},{5,7},{6,4},{7,5},{8,10},{9,11},{10,... | collective-permute-start | bytes 135176 | tf_op jit(solution)/shard_map/ppermute | solution.py:316
  75.0 5.2 %copy-start.12 = (bf16[624,128]{1,0:T(8,128)(2,1)}, bf16[624,128]{1,0:T(8,128)(2,1)S(1)}, u32[]{:S(2)}) copy-start(bf16[624,128]{1,0:T(8,128)(2,1)S(1)} %collective-permute-done.19.refs_2_) | copy-start | bytes 479236
  75.0 9.2 %collective-permute-start.25 = (bf16[176,128]{1,0:T(8,128)(2,1)}, bf16[176,128]{1,0:T(8,128)(2,1)}, u32[]{:S(2)}, u32[]{:S(2)}) collective-permute-start(bf16[176,128]{1,0:T(8,128)(2,1)} %get-tuple-element.150.refs_0_), channel_id=1, source_target_pairs={{0,3},{1,2},{2,1},{3,0},{4,7},{5,6},{6,5},{7,4},{8,11},{9,10},{10,... | collective-permute-start | bytes 135176 | tf_op jit(solution)/shard_map/ppermute | solution.py:316
  83.3 8.9 %collective-permute-start.21 = (bf16[176,512]{1,0:T(8,128)(2,1)}, bf16[176,512]{1,0:T(8,128)(2,1)}, u32[]{:S(2)}, u32[]{:S(2)}) collective-permute-start(bf16[176,512]{1,0:T(8,128)(2,1)} %get-tuple-element.147), channel_id=1, source_target_pairs={{0,8},{4,12},{8,0},{12,4},{16,24},{20,28},{24,16},{28,20},{1,9},{5... | collective-permute-start | bytes 540680 | tf_op jit(solution)/shard_map/ppermute | solution.py:316
  83.8 8.4 %collective-permute-start.22 = (bf16[176,512]{1,0:T(8,128)(2,1)}, bf16[176,512]{1,0:T(8,128)(2,1)}, u32[]{:S(2)}, u32[]{:S(2)}) collective-permute-start(bf16[176,512]{1,0:T(8,128)(2,1)} %get-tuple-element.148), channel_id=1, source_target_pairs={{0,16},{4,20},{8,24},{12,28},{16,0},{20,4},{24,8},{28,12},{1,17},{... | collective-permute-start | bytes 540680 | tf_op jit(solution)/shard_map/ppermute | solution.py:316
  86.5 6.7 %collective-permute-start.26 = (bf16[176,512]{1,0:T(8,128)(2,1)}, bf16[176,512]{1,0:T(8,128)(2,1)}, u32[]{:S(2)}, u32[]{:S(2)}) collective-permute-start(bf16[176,512]{1,0:T(8,128)(2,1)} %grow_rows.5), channel_id=1, source_target_pairs={{0,24},{4,28},{8,16},{12,20},{16,8},{20,12},{24,0},{28,4},{1,25},{... | collective-permute-start | bytes 540680 | tf_op jit(solution)/shard_map/ppermute | solution.py:316
  89.7 1.2 %collective-permute-start.14 = (f32[8,128]{1,0:T(8,128)S(1)}, f32[8,128]{1,0:T(8,128)S(1)}, u32[]{:S(2)}, u32[]{:S(2)}) collective-permute-start(f32[8,128]{1,0:T(8,128)S(1)} %max.6), channel_id=1, source_target_pairs={{0,4},{4,0},{8,12},{12,8},{16,20},{20,16},{24,28},{28,24},{1,5},{5... | collective-permute-start | bytes 12296 | tf_op jit(solution)/shard_map/ppermute | solution.py:316
  96.3 0.8 copy-start.7

commit v5 on v4

--- a/solution.py
+++ b/solution.py
@@ -10,7 +10,8 @@
 adapter_scale = 0.5
 BF = jnp.bfloat16
 F32 = jnp.float32
-VMEM_LIMIT = 60 * 1024 * 1024
+VMEM_LIMIT = 28 * 1024 * 1024
+VMEM_MOST = 57 * 1024 * 1024
 COST = pl.CostEstimate(flops=1000, bytes_accessed=1000, transcendentals=0)
 
 
@@ -164,7 +165,9 @@
             jax.ShapeDtypeStruct((8, 128), F32),
         ],
         scratch_shapes=[pltpu.VMEM((rows, both), F32), pltpu.VMEM((rows, both), F32)],
-        cost_estimate=COST,
+        cost_estimate=pl.CostEstimate(
+            flops=8 * rows * width * local * both, bytes_accessed=8 * width * local * both, transcendentals=0
+        ),
         compiler_params=pltpu.CompilerParams(vmem_limit_bytes=VMEM_LIMIT),
         name="shrink_rows",
     )(core, *messages, mine, sibling, *carry)
@@ -217,54 +220,62 @@
     )(core, *parts, place, mine, sibling)
 
 
-def base_kernel(steps, blocks, place_ref, tokens_ref, weight_ref, *refs):
-    outs, total = refs[:blocks], refs[blocks]
-    step = pl.program_id(0)
-    weight = jnp.swapaxes(weight_ref[...], 0, 1)
-    columns = total.shape[2] // blocks
-    for j in range(2):
-        product = dot(tokens_ref[...], weight[j])
-
-        @pl.when(step == 0)
-        def _():
-            total[j] = product
-
-        @pl.when(step > 0)
-        def _():
-            total[j] += product
-
-    @pl.when(step == steps - 1)
-    def _():
-        for r, out in enumerate(outs):
-            start = pl.multiple_of((place_ref[0] ^ r) * columns, columns)
-            for j in range(2):
-                out[:, j * columns:(j + 1) * columns] = total[j, :, pl.ds(start, columns)].astype(out.dtype)
-
-
-def base_parts(t, tokens, weight, blocks, steps=4):
+def base_kernel(steps, shifts, count, place_ref, weight_ref, tokens_ref, *refs):
+    arrived, outs, total = refs[:count], refs[count:-1], refs[-1]
+    columns = outs[0].shape[1] // 2
+    rows, width = tokens_ref.shape
+    deep = width // steps
+    read = total.shape[2]
+    chosen = (place_ref[0] ^ shifts[0]) if len(shifts) == 1 else 0
+    total[...] = jnp.zeros(total.shape, F32)
+
+    def body(tokens, weight):
+        turned = jnp.swapaxes(weight[...], 0, 1)
+        for j in range(2):
+            total[j] += dot(tokens[...], turned[j])
+
+    pltpu.emit_pipeline(
+        body,
+        grid=(steps,),
+        in_specs=[
+            pl.BlockSpec((rows, deep), lambda i: (0, i)),
+            pl.BlockSpec((deep, 2, read), lambda i: (i, 0, chosen)),
+        ],
+    )(tokens_ref, weight_ref)
+    for r, out in zip(shifts, outs):
+        start = 0 if len(shifts) == 1 else pl.multiple_of((place_ref[0] ^ r) * columns, columns)
+        for j in range(2):
+            part = total[j, :, pl.ds(start, columns)]
+            for one in arrived:
+                part = part + one[:, j * columns:(j + 1) * columns].astype(F32)
+            out[:, j * columns:(j + 1) * columns] = part.astype(out.dtype)
+
+
+def base_parts(t, tokens, weight, blocks, shifts, steps, arrived=(), dtype=None):
     rows, width = tokens.shape
     columns = weight.shape[2] // blocks
-    types = [BF if r % 2 else F32 for r in range(blocks)]
+    types = [dtype or (BF if r % 2 else F32) for r in shifts]
     if columns % 128:
-        total = jnp.einsum("rd,djn->rjn", tokens, weight, preferred_element_type=F32)
-        cut = [lax.dynamic_slice_in_dim(total, (t ^ r) * columns, columns, 2) for r in range(blocks)]
-        return [c.reshape(rows, 2 * columns).astype(k) for c, k in zip(cut, types)]
-    deep = width // steps
+        cut = [lax.dynamic_slice_in_dim(weight, (t ^ r) * columns, columns, 2) for r in shifts]
+        cut = [dot(tokens, c.reshape(width, 2 * columns)) for c in cut]
+        for one in arrived:
+            cut = [c + one.astype(F32) for c in cut]
+        return [c.astype(k) for c, k in zip(cut, types)]
+    read = columns if len(shifts) == 1 else columns * blocks
+    vmem = pl.BlockSpec(memory_space=pltpu.VMEM)
+    hbm = pl.BlockSpec(memory_space=pltpu.HBM)
     return pl.pallas_call(
-        functools.partial(base_kernel, steps, blocks),
-        grid=(steps,),
-        in_specs=[
-            pl.BlockSpec(memory_space=pltpu.SMEM),
-            pl.BlockSpec((rows, deep), lambda i: (0, i)),
-            pl.BlockSpec((deep, 2, weight.shape[2]), lambda i: (i, 0, 0)),
-        ],
-        out_specs=[pl.BlockSpec((rows, 2 * columns), lambda i: (0, 0))] * blocks,
+        functools.partial(base_kernel, steps, shifts, len(arrived)),
+        in_specs=[pl.BlockSpec(memory_space=pltpu.SMEM), hbm, hbm] + [vmem] * len(arrived),
+        out_specs=[vmem] * len(shifts),
+        scratch_shapes=[pltpu.VMEM((2, rows, read), F32)],
         out_shape=[jax.ShapeDtypeStruct((rows, 2 * columns), k) for k in types],
-        scratch_shapes=[pltpu.VMEM((2, rows, weight.shape[2]), F32)],
-        cost_estimate=COST,
-        compiler_params=pltpu.CompilerParams(vmem_limit_bytes=VMEM_LIMIT),
+        cost_estimate=pl.CostEstimate(
+            flops=16 * rows * width * read, bytes_accessed=8 * width * read, transcendentals=0
+        ),
+        compiler_params=pltpu.CompilerParams(vmem_limit_bytes=VMEM_MOST),
         name="base_parts",
-    )(t.reshape(1), tokens, weight)
+    )(t.reshape(1), weight, tokens, *arrived)
 
 
 def finish_kernel(sizes, count, *refs):
@@ -299,11 +310,13 @@
     sizes = tuple(tuple(u.shape[0] for u in group) for group in groups)
     rows, both = bases[0].shape
     updates = [u for group in groups for u in group]
-    vmem = pl.BlockSpec(memory_space=pltpu.VMEM)
+    block = rows // 4
     return pl.pallas_call(
         functools.partial(finish_kernel, sizes, len(bases)),
-        in_specs=[vmem] * (len(bases) + len(spreads) + len(updates)),
-        out_specs=vmem,
+        grid=(4,),
+        in_specs=[pl.BlockSpec((block, x.shape[1]), lambda i: (i, 0)) for x in bases + spreads]
+        + [pl.BlockSpec(u.shape, lambda i: (0, 0)) for u in updates],
+        out_specs=pl.BlockSpec((block, 2, both // 2), lambda i: (i, 0, 0)),
         out_shape=jax.ShapeDtypeStruct((rows, 2, both // 2), BF),
         cost_estimate=COST,
         compiler_params=pltpu.CompilerParams(vmem_limit_bytes=VMEM_LIMIT),
@@ -352,61 +365,71 @@
 
     near = [m for m in range(chips) if bits(m) <= 1]
     far = [m for m in range(chips) if bits(m) > 1]
-    whole, message = round_up(full + 1, 16), round_up(full * 11 // 16, 16)
+    message = round_up(full * 11 // 16, 16)
     rest = round_up(full - message + 2, 16)
-    sizes, first_rows = (whole,) + (message,) * (chips - 1), (0,) * chips
-
-    packed = pack(chip, adapters, slots, tokens, sizes, first_rows, chip_slots)
+    sizes, first_rows = (message,) * chips, (0,) * chips
+
+    t = lax.axis_index("tensor").astype(jnp.int32)
+    first_shift = blocks - 1
+    parts = {first_shift: base_parts(t, tokens, key_value_base_weight, blocks, [first_shift], 2)[0]}
+    came = {}
+    came[(1, first_shift ^ 1)] = exchange(parts[first_shift], "tensor", 1)
+
+    packed = pack(chip, adapters, slots, after(tokens, parts[first_shift]), sizes, first_rows, chip_slots)
     sent, spread = list(packed[:-1]), packed[-1]
     arrived, returned = {0: sent[0]}, {}
     for m in near[1:]:
         arrived[m] = exchange(sent[m], "dp", 2 * m)
 
-    t = lax.axis_index("tensor").astype(jnp.int32)
-    parts = base_parts(t, after(tokens, *sent), key_value_base_weight, blocks)
-    came = {}
+    plain = [r for r in range(blocks - 1) if r % 2 or r == 0]
+    late_tokens = after(tokens, *sent)
+    parts.update(zip(plain, base_parts(t, late_tokens, key_value_base_weight, blocks, plain, 4)))
 
     def arrived_for(r):
         return [came[key] for key in sorted(came) if key[1] == r]
 
-    carry = shrink(core, [after(sent[0], parts[0])], adapter_down_weight, down_sibling, flag_lane)
     up_sibling = exchange(after(adapter_up_weight, down_sibling), "dp", 1)
-    near_done = [arrived[m] for m in near[1:]] + [carry[0]]
-    for r in sorted(range(1, blocks), key=lambda r: (r & -r, -r)):
+    near_done = [arrived[m] for m in near[1:]]
+    for r in sorted(range(1, blocks - 1), key=lambda r: (r & -r, -r)):
         low = r & -r
-        part = parts[r]
-        for one in arrived_for(r):
-            part = part + one.astype(F32)
-        if r == 1:
-            part = after(part, *near_done)
-        came[(low, r ^ low)] = exchange(part.astype(BF), "tensor", low)
+        if r % 2:
+            part = after(parts[r], came[(1, first_shift ^ 1)]) if r == 1 else parts[r]
+        else:
+            part = base_parts(t, late_tokens, key_value_base_weight, blocks, [r], 2, arrived_for(r), BF)[0]
+        came[(low, r ^ low)] = exchange(part, "tensor", low)
+    carry = shrink(core, [after(sent[0], parts[0], part)], adapter_down_weight, down_sibling, flag_lane)
     for m in far:
-        arrived[m] = exchange(after(sent[m], *near_done), "dp", 2 * m)
+        arrived[m] = exchange(after(sent[m], *near_done, carry[0]), "dp", 2 * m)
 
     flags = []
     for part in (near, far):
         if not part:
             continue
         group = [arrived[m] for m in part if m]
+        if part is far:
+            group[0] = after(group[0], base)
         share, place, flag = shrink(
             core, group, adapter_down_weight, after(down_sibling, up_sibling), flag_lane, carry if part is near else ()
         )
         flags.append(flag)
-        other = came[(1, 0)] if part is near else came[(blocks // 2, 0)]
-        shares = [after(share, other)] + [exchange(share, "tensor", z) for z in range(1, blocks)]
+        if part is near:
+            base = after(parts[0], share)
+            for one in arrived_for(0):
+                base = base + one.astype(F32)
+        shares = [after(share, came[(1, 0)])] + [exchange(share, "tensor", z) for z in range(1, blocks)]
         grown = grow(core, shares, place, adapter_up_weight, up_sibling, tuple(sizes[m] for m in part))
         for m, update in zip(part, grown):
             returned[m] = update if m == 0 else exchange(update, "dp", 2 * m)
     flag = functools.reduce(jnp.maximum, flags)
     flag = jnp.maximum(flag, exchange(flag, "dp", 1))
-    bases = [parts[0]] + arrived_for(0)
+    bases = [base]
     updates = [returned[m] for m in range(chips)]
 
     def as_is():
         return finish(bases, [spread], [updates])
 
     def second_round():
-        later_sizes, later_rows = (16,) + (rest,) * (chips - 1), (full,) + (message - 1,) * (chips - 1)
+        later_sizes, later_rows = (rest,) * chips, (message - 1,) * chips
         packed = pack(chip, adapters, slots, tokens, later_sizes, later_rows, chip_slots)
         group = [packed[0]] + [exchange(packed[m], "dp", 2 * m) for m in range(1, chips)]
         share, place, _ = shrink(core, group, adapter_down_weight, down_sibling, flag_lane)

time: 97.5 us -> 84.7 us (0.87)
  starting transfers between devices: 25.7 us -> 20.9 us
  waiting for transfers between devices: 20.9 us -> 17.4 us
  Pallas kernels: 45.6 us -> 42.6 us
  other arithmetic: 1.65 us -> 0.21 us
    pallas_call x2 -> x4, Pallas kernels: 14.2 us -> 20.3 us  [the longest x3 18.8 us: base_parts(): pl.pallas_call(functools.partial(base_kernel, steps, shifts, len(arrived)...]
    ppermute x18, starting transfers between devices: 25.7 us -> 20.9 us  [exchange(): return lax.ppermute(array, axis, [(i, i ^ shift) for i in range(size)])]
    pallas_call x3, Pallas kernels: 20.1 us -> 15.4 us  [shrink(): pl.pallas_call(functools.partial(shrink_kernel, len(messages), len(carry)...]
    pallas_call x2, Pallas kernels: 5.28 us -> 1.19 us  [grow(): pl.pallas_call(functools.partial(grow_kernel, len(parts), sizes), in_spec...]
    ppermute x18, waiting for transfers between devices: 20.9 us -> 17.4 us  [exchange(): return lax.ppermute(array, axis, [(i, i ^ shift) for i in range(size)])]
  transfers between devices with their start and end apart: 18 -> 18, of which waited for: 5 -> 4; matrix products, arithmetic and copies ran while one was open for 2% -> 1% of each run, Pallas kernels for 44% -> 49%
where the time goes in v5:
time: 84.7 us; the launch traced here: 84.3 us
  Pallas kernels  42.6 us (50%)
  starting transfers between devices  20.9 us (25%)
  waiting for transfers between devices  17.4 us (21%)
  local copies, waits for them, and re-layouts  2.25 us (3%)
    ppermute x18, starting transfers between devices, exchange(): return lax.ppermute(array, axis, [(i, i ^ shift) for i in range(size)])  20.9 us
    pallas_call x3, Pallas kernels, base_parts(): pl.pallas_call(functools.partial(base_kernel, steps, shifts, len(arrived)...  18.8 us
    ppermute x18, waiting for transfers between devices, exchange(): return lax.ppermute(array, axis, [(i, i ^ shift) for i in range(size)])  17.4 us
    pallas_call x3, Pallas kernels, shrink(): pl.pallas_call(functools.partial(shrink_kernel, len(messages), len(carry)...  15.4 us
    pallas_call x1, Pallas kernels, pack(): pl.pallas_call(functools.partial(pack_kernel, (sizes, first_rows, chip_sl...  5.7 us
    unnamed x22, local copies, waits for them, and re-layouts  1.74 us
  transfers between devices with their start and end apart: 18, of which 4 were waited for; matrix products, arithmetic and copies ran while one was open for 1% of the time, Pallas kernels for 49%

profile of v5, /device:TPU:0, one launch (start us, length us, event | category | flops | bytes accessed | tf_op | source)
XLA Modules:
  0.0 84.3 jit_solution(11332460016837121650)
XLA Ops:
  0.0 0.5 collective-permute-start.11
  0.5 4.2 %base_parts.3 = bf16[512,512]{1,0:T(8,128)(2,1)} custom-call(s32[1]{0:T(128)} %bitcast.4.place_ref, bf16[2048,2,1024]{2,1,0:T(2,128)(2,1)} %weight_ref.5, bf16[512,2048]{1,0:T(8,128)(2,1)} %tokens_ref.4), custom_call_target="tpu_custom_call" | custom-call | flops 4294967296 | bytes 4194304 | tf_op jit(solution)/shard_map/base_parts/pallas_call | solution.py:267
  4.7 2.6 %collective-permute-start.13 = (bf16[512,512]{1,0:T(8,128)(2,1)}, bf16[512,512]{1,0:T(8,128)(2,1)}, u32[]{:S(2)}, u32[]{:S(2)}) collective-permute-start(bf16[512,512]{1,0:T(8,128)(2,1)} %base_parts.3), channel_id=1, source_target_pairs={{0,1},{1,0},{2,3},{3,2},{4,5},{5,4},{6,7},{7,6},{8,9},{9,8},{10,11... | collective-permute-start | bytes 1572872 | tf_op jit(solution)/shard_map/ppermute | solution.py:329
  7.2 5.7 %pack_rows.3 = (bf16[176,2048]{1,0:T(8,128)(2,1)S(1)}, bf16[176,2048]{1,0:T(8,128)(2,1)}, bf16[176,2048]{1,0:T(8,128)(2,1)S(1)}, bf16[176,2048]{1,0:T(8,128)(2,1)S(1)}, bf16[512,1024]{1,0:T(8,128)(2,1)}) custom-call(s32[1]{0:T(128)} %bitcast.1.place_ref, s32[1,512]{1,0:T(1,128)S(1)} %bitcast.6, s32[1,64]{1,0:T(1,128)S(1)} %bitcast.8, ...), custom_call_target="tpu_custom_call" | custom-call | flops 1000 | bytes 1000 | tf_op jit(solution)/shard_map/pack_rows/pallas_call | solution.py:84
  12.9 0.9 %copy-done = bf16[176,2048]{1,0:T(8,128)(2,1)} copy-done((bf16[176,2048]{1,0:T(8,128)(2,1)}, bf16[176,2048]{1,0:T(8,128)(2,1)S(1)}, u32[]{:S(2)}) %copy-start) | copy-done | bytes 720920
  13.8 1.5 %collective-permute-start.9 = (bf16[176,2048]{1,0:T(8,128)(2,1)}, bf16[176,2048]{1,0:T(8,128)(2,1)S(1)}, u32[]{:S(2)}, u32[]{:S(2)}) collective-permute-start(bf16[176,2048]{1,0:T(8,128)(2,1)} %get-tuple-element.113), channel_id=1, source_target_pairs={{0,8},{4,12},{8,0},{12,4},{16,24},{20,28},{24,16},{28,20},{1,9},{5... | collective-permute-start | bytes 2162696 | tf_op jit(solution)/shard_map/ppermute | solution.py:329
  15.3 1.5 %collective-permute-start.10 = (bf16[176,2048]{1,0:T(8,128)(2,1)S(1)}, bf16[176,2048]{1,0:T(8,128)(2,1)S(1)}, u32[]{:S(2)}, u32[]{:S(2)}) collective-permute-start(bf16[176,2048]{1,0:T(8,128)(2,1)S(1)} %get-tuple-element.114), channel_id=1, source_target_pairs={{0,16},{4,20},{8,24},{12,28},{16,0},{20,4},{24,8},{28,12},{1,17},{... | collective-permute-start | bytes 2162696 | tf_op jit(solution)/shard_map/ppermute | solution.py:329
  16.9 9.3 %base_parts.4 = (f32[512,512]{1,0:T(8,128)}, bf16[512,512]{1,0:T(8,128)(2,1)}) custom-call(s32[1]{0:T(128)} %bitcast.4.place_ref, bf16[2048,2,1024]{2,1,0:T(2,128)(2,1)} %weight_ref.5, bf16[512,2048]{1,0:T(8,128)(2,1)} %tokens_ref.4), custom_call_target="tpu_custom_call" | custom-call | flops 17179869184 | bytes 16777216 | tf_op jit(solution)/shard_map/base_parts/pallas_call | solution.py:267
  26.2 5.4 %base_parts.5 = bf16[512,512]{1,0:T(8,128)(2,1)} custom-call(s32[1]{0:T(128)} %bitcast.4.place_ref, bf16[2048,2,1024]{2,1,0:T(2,128)(2,1)} %weight_ref.5, bf16[512,2048]{1,0:T(8,128)(2,1)} %tokens_ref.4, bf16[512,512]{1,0:T(8,128)(2,1)} %collective-permute-done.13.refs_0_), custom_call_target="tpu_custom_call" | custom-call | flops 4294967296 | bytes 4194304 | tf_op jit(solution)/shard_map/base_parts/pallas_call | solution.py:267
  31.6 2.6 %collective-permute-start.16 = (bf16[512,512]{1,0:T(8,128)(2,1)}, bf16[512,512]{1,0:T(8,128)(2,1)S(1)}, u32[]{:S(2)}, u32[]{:S(2)}) collective-permute-start(bf16[512,512]{1,0:T(8,128)(2,1)} %base_parts.5), channel_id=1, source_target_pairs={{0,2},{1,3},{2,0},{3,1},{4,6},{5,7},{6,4},{7,5},{8,10},{9,11},{10,... | collective-permute-start | bytes 1572872 | tf_op jit(solution)/shard_map/ppermute | solution.py:329
  34.2 0.4 collective-permute-start.15
  34.6 5.4 %shrink_rows.5 = (bf16[176,128]{1,0:T(8,128)(2,1)S(1)}, bf16[176,128]{1,0:T(8,128)(2,1)S(1)}, f32[8,128]{1,0:T(8,128)S(1)}) custom-call(s32[1]{0:T(128)} %bitcast.core_ref, bf16[176,2048]{1,0:T(8,128)(2,1)S(1)} %copy-done.1, bf16[8,2048,128]{2,1,0:T(8,128)(2,1)} %refs_1_.3, bf16[8,2048,128]{2,1,0:T(8,128)(2,1)} %collective-permute-done.11.refs_2_.refs_3_), custom_call_target="tpu_custom_call" | custom-call | flops 2952790016 | bytes 16777216 | tf_op jit(solution)/shard_map/shrink_rows/pallas_call | solution.py:157
  40.0 0.6 collective-permute-start.14
  40.6 5.5 %shrink_rows.6 = (bf16[528,128]{1,0:T(8,128)(2,1)S(1)}, bf16[528,128]{1,0:T(8,128)(2,1)S(1)}, f32[8,128]{1,0:T(8,128)S(1)}) custom-call(s32[1]{0:T(128)} %bitcast.core_ref, bf16[176,2048]{1,0:T(8,128)(2,1)S(1)} %collective-permute-done.9.refs_0_, bf16[176,2048]{1,0:T(8,128)(2,1)S(1)} %collective-permute-done.10.refs_1_, bf16[8,2048,128]{2,1,0:T(8,128)(2,1)S(1)} %copy-done.9, ...), custom_call_target="tpu_custom_call" | custom-call | flops 5905580032 | bytes 16777216 | tf_op jit(solution)/shard_map/shrink_rows/pallas_call | solution.py:157
  46.1 1.4 %collective-permute-start.20 = (bf16[528,128]{1,0:T(8,128)(2,1)S(1)}, bf16[528,128]{1,0:T(8,128)(2,1)S(1)}, u32[]{:S(2)}, u32[]{:S(2)}) collective-permute-start(bf16[528,128]{1,0:T(8,128)(2,1)S(1)} %get-tuple-element.134.refs_0_), channel_id=1, source_target_pairs={{0,3},{1,2},{2,1},{3,0},{4,7},{5,6},{6,5},{7,4},{8,11},{9,10},{10,... | collective-permute-start | bytes 405512 | tf_op jit(solution)/shard_map/ppermute | solution.py:329
  47.5 1.7 %collective-permute-start.19 = (bf16[528,128]{1,0:T(8,128)(2,1)S(1)}, bf16[528,128]{1,0:T(8,128)(2,1)S(1)}, u32[]{:S(2)}, u32[]{:S(2)}) collective-permute-start(bf16[528,128]{1,0:T(8,128)(2,1)S(1)} %get-tuple-element.134.refs_0_), channel_id=1, source_target_pairs={{0,2},{1,3},{2,0},{3,1},{4,6},{5,7},{6,4},{7,5},{8,10},{9,11},{10,... | collective-permute-start | bytes 405512 | tf_op jit(solution)/shard_map/ppermute | solution.py:329
  49.2 9.4 %collective-permute-done.16 = bf16[512,512]{1,0:T(8,128)(2,1)S(1)} collective-permute-done((bf16[512,512]{1,0:T(8,128)(2,1)}, bf16[512,512]{1,0:T(8,128)(2,1)S(1)}, u32[]{:S(2)}, u32[]{:S(2)}) %collective-permute-start.16) | collective-permute-done | bytes 524320 | tf_op jit(solution)/shard_map/ppermute | solution.py:329
  58.7 4.2 %collective-permute-done.15 = bf16[512,512]{1,0:T(8,128)(2,1)S(1)} collective-permute-done((bf16[512,512]{1,0:T(8,128)(2,1)S(1)}, bf16[512,512]{1,0:T(8,128)(2,1)S(1)}, u32[]{:S(2)}, u32[]{:S(2)}) %collective-permute-start.15) | collective-permute-done | bytes 524320 | tf_op jit(solution)/shard_map/ppermute | solution.py:329
  63.1 4.5 %shrink_rows.7 = (bf16[176,128]{1,0:T(8,128)(2,1)S(1)}, bf16[176,128]{1,0:T(8,128)(2,1)S(1)}, f32[8,128]{1,0:T(8,128)S(1)}) custom-call(s32[1]{0:T(128)} %bitcast.core_ref, bf16[176,2048]{1,0:T(8,128)(2,1)S(1)} %collective-permute-done.14.refs_0_, bf16[8,2048,128]{2,1,0:T(8,128)(2,1)S(1)} %copy-done.9, ...), custom_call_target="tpu_custom_call" | custom-call | flops 2952790016 | bytes 16777216 | tf_op jit(solution)/shard_map/shrink_rows/pallas_call | solution.py:157
  67.8 1.0 %collective-permute-start.24 = (bf16[176,128]{1,0:T(8,128)(2,1)S(1)}, bf16[176,128]{1,0:T(8,128)(2,1)S(1)}, u32[]{:S(2)}, u32[]{:S(2)}) collective-permute-start(bf16[176,128]{1,0:T(8,128)(2,1)S(1)} %get-tuple-element.140.refs_0_), channel_id=1, source_target_pairs={{0,2},{1,3},{2,0},{3,1},{4,6},{5,7},{6,4},{7,5},{8,10},{9,11},{10,... | collective-permute-start | bytes 135176 | tf_op jit(solution)/shard_map/ppermute | solution.py:329
  68.8 3.4 %collective-permute-start.23 = (bf16[176,128]{1,0:T(8,128)(2,1)S(1)}, bf16[176,128]{1,0:T(8,128)(2,1)S(1)}, u32[]{:S(2)}, u32[]{:S(2)}) collective-permute-start(bf16[176,128]{1,0:T(8,128)(2,1)S(1)} %get-tuple-element.140.refs_0_), channel_id=1, source_target_pairs={{0,1},{1,0},{2,3},{3,2},{4,5},{5,4},{6,7},{7,6},{8,9},{9,8},{10,11... | collective-permute-start | bytes 135176 | tf_op jit(solution)/shard_map/ppermute | solution.py:329
  72.2 0.8 grow_rows.4
  72.9 0.7 collective-permute-start.21
  73.6 0.5 collective-permute-start.22
  74.2 0.4 grow_rows.5
  74.6 2.4 %collective-permute-start.26 = (bf16[176,512]{1,0:T(8,128)(2,1)S(1)}, bf16[176,512]{1,0:T(8,128)(2,1)S(1)}, u32[]{:S(2)}, u32[]{:S(2)}) collective-permute-start(bf16[176,512]{1,0:T(8,128)(2,1)S(1)} %grow_rows.5), channel_id=1, source_target_pairs={{0,24},{4,28},{8,16},{12,20},{16,8},{20,12},{24,0},{28,4},{1,25},{... | collective-permute-start | bytes 540680 | tf_op jit(solution)/shard_map/ppermute | solution.py:329
  77.0 1.2 %collective-permute-done.17 = f32[8,128]{1,0:T(8,128)S(1)} collective-permute-done((f32[8,128]{1,0:T(8,128)S(1)}, f32[8,128]{1,0:T(8,128)S(1)}, u32[]{:S(2)}, u32[]{:S(2)}) %collective-permute-start.17) | collective-permute-done | bytes 4128 | tf_op jit(solution)/shard_map/ppermute | solution.py:329
  78.2 0.5 slice.3
  79.3 2.5 %collective-permute-done.22 = bf16[176,512]{1,0:T(8,128)(2,1)S(1)} collective-permute-done((bf16[176,512]{1,0:T(8,128)(2,1)S(1)}, bf16[176,512]{1,0:T(8,128)(2,1)S(1)}, u32[]{:S(2)}, u32[]{:S(2)}) %collective-permute-start.22) | collective-permute-done | bytes 180256 | tf_op jit(solution)/shard_map/ppermute | solution.py:329
  81.9 1.7 %conditional.1 = (bf16[512,2,256]{2,1,0:T(2,128)(2,1)S(1)}) conditional(s32[]{:T(128)} %bitcast.5, (f32[512,512]{1,0:T(8,128)S(1)}, bf16[512,1024]{1,0:T(8,128)(2,1)S(1)}, bf16[176,512]{1,0:T(8,128)(2,1)S(1)}, bf16[176,512]{1,0:T(8,128)(2,1)S(1)}, bf16[176,512]{1,0:T(8,128)(2,1)S(1)}, /*index=5*/bf16[176,512]{1,0:T(8,128)(2,1)S(1)}) %tuple.41, ...), branch_computations={%region_0.1_spmd, %region_1.2_spmd} | conditional | flops 6442454016 | bytes 23858472 | solution.py:441
  81.9 1.5 %finish_rows.2 = bf16[512,2,256]{2,1,0:T(2,128)(2,1)S(1)} custom-call(f32[512,512]{1,0:T(8,128)S(1)} %get-tuple-element.50.refs_0_, bf16[512,1024]{1,0:T(8,128)(2,1)S(1)} %get-tuple-element.51.refs_1_, bf16[176,512]{1,0:T(8,128)(2,1)S(1)} %get-tuple-element.52.refs_2_, bf16[176,512]{1,0:T(8,128)(2,1)S(1)} %get-tuple-element.53.refs_3_, ...), custom_call_target="tpu_custom_call" | custom-call | flops 1000 | bytes 1000 | tf_op jit(solution)/shard_map/cond/branch_0_fun/finish_rows/pallas_call | solution.py:314
  83.6 0.8 copy-done.6
  (41 shorter events, 0.5 us)
Async XLA Ops:
  0.0 26.2 %collective-permute-start.11 = (bf16[8,2048,128]{2,1,0:T(8,128)(2,1)}, bf16[8,2048,128]{2,1,0:T(8,128)(2,1)}, u32[]{:S(2)}, u32[]{:S(2)}) collective-permute-start(bf16[8,2048,128]{2,1,0:T(8,128)(2,1)} %refs_1_.3), channel_id=1, source_target_pairs={{0,4},{4,0},{8,12},{12,8},{16,20},{20,16},{24,28},{28,24},{1,5},{5... | collective-permute-start | bytes 12582920 | tf_op jit(solution)/shard_map/ppermute | solution.py:329
  0.5 6.8 %copy-start.7 = (s32[512,1]{0,1:T(1,128)S(1)}, s32[512,1]{0,1:T(1,128)}, u32[]{:S(2)}) copy-start(s32[512,1]{0,1:T(1,128)} %param.9) | copy-start | bytes 6148
  0.5 6.8 %copy-start.8 = (s32[64]{0:T(128)S(1)}, s32[64]{0:T(128)}, u32[]{:S(2)}) copy-start(s32[64]{0:T(128)} %param.10) | copy-start | bytes 772
  4.7 21.6 %collective-permute-start.13 = (bf16[512,512]{1,0:T(8,128)(2,1)}, bf16[512,512]{1,0:T(8,128)(2,1)}, u32[]{:S(2)}, u32[]{:S(2)}) collective-permute-start(bf16[512,512]{1,0:T(8,128)(2,1)} %base_parts.3), channel_id=1, source_target_pairs={{0,1},{1,0},{2,3},{3,2},{4,5},{5,4},{6,7},{7,6},{8,9},{9,8},{10,11... | collective-permute-start | bytes 1572872 | tf_op jit(solution)/shard_map/ppermute | solution.py:329
  12.9 0.9 %copy-start = (bf16[176,2048]{1,0:T(8,128)(2,1)}, bf16[176,2048]{1,0:T(8,128)(2,1)S(1)}, u32[]{:S(2)}) copy-start(bf16[176,2048]{1,0:T(8,128)(2,1)S(1)} %get-tuple-element.121.refs_0_) | copy-start | bytes 2162692
  13.8 26.1 %collective-permute-start.9 = (bf16[176,2048]{1,0:T(8,128)(2,1)}, bf16[176,2048]{1,0:T(8,128)(2,1)S(1)}, u32[]{:S(2)}, u32[]{:S(2)}) collective-permute-start(bf16[176,2048]{1,0:T(8,128)(2,1)} %get-tuple-element.113), channel_id=1, source_target_pairs={{0,8},{4,12},{8,0},{12,4},{16,24},{20,28},{24,16},{28,20},{1,9},{5... | collective-permute-start | bytes 2162696 | tf_op jit(solution)/shard_map/ppermute | solution.py:329
  15.3 24.7 %collective-permute-start.10 = (bf16[176,2048]{1,0:T(8,128)(2,1)S(1)}, bf16[176,2048]{1,0:T(8,128)(2,1)S(1)}, u32[]{:S(2)}, u32[]{:S(2)}) collective-permute-start(bf16[176,2048]{1,0:T(8,128)(2,1)S(1)} %get-tuple-element.114), channel_id=1, source_target_pairs={{0,16},{4,20},{8,24},{12,28},{16,0},{20,4},{24,8},{28,12},{1,17},{... | collective-permute-start | bytes 2162696 | tf_op jit(solution)/shard_map/ppermute | solution.py:329
  26.1 8.0 %copy-start.10 = (bf16[512,512]{1,0:T(8,128)(2,1)S(1)}, bf16[512,512]{1,0:T(8,128)(2,1)}, u32[]{:S(2)}) copy-start(bf16[512,512]{1,0:T(8,128)(2,1)} %get-tuple-element.130) | copy-start | bytes 1572868
  26.1 8.5 %copy-start.1 = (bf16[176,2048]{1,0:T(8,128)(2,1)S(1)}, bf16[176,2048]{1,0:T(8,128)(2,1)}, u32[]{:S(2)}) copy-start(bf16[176,2048]{1,0:T(8,128)(2,1)} %copy-done) | copy-start | bytes 2162692
  26.2 14.4 %collective-permute-start.12 = (bf16[8,2,64,256]{3,2,1,0:T(8,128)(2,1)}, bf16[8,2,64,256]{3,2,1,0:T(8,128)(2,1)S(1)}, u32[]{:S(2)}, u32[]{:S(2)}) collective-permute-start(bf16[8,2,64,256]{3,2,1,0:T(8,128)(2,1)} %refs_5_.3), channel_id=1, source_target_pairs={{0,4},{4,0},{8,12},{12,8},{16,20},{20,16},{24,28},{28,24},{1,5},{5... | collective-permute-start | bytes 1572872 | tf_op jit(solution)/shard_map/ppermute | solution.py:329
  31.6 27.1 %collective-permute-start.16 = (bf16[512,512]{1,0:T(8,128)(2,1)}, bf16[512,512]{1,0:T(8,128)(2,1)S(1)}, u32[]{:S(2)}, u32[]{:S(2)}) collective-permute-start(bf16[512,512]{1,0:T(8,128)(2,1)} %base_parts.5), channel_id=1, source_target_pairs={{0,2},{1,3},{2,0},{3,1},{4,6},{5,7},{6,4},{7,5},{8,10},{9,11},{10,... | collective-permute-start | bytes 1572872 | tf_op jit(solution)/shard_map/ppermute | solution.py:329
  34.2 28.7 %collective-permute-start.15 = (bf16[512,512]{1,0:T(8,128)(2,1)S(1)}, bf16[512,512]{1,0:T(8,128)(2,1)S(1)}, u32[]{:S(2)}, u32[]{:S(2)}) collective-permute-start(bf16[512,512]{1,0:T(8,128)(2,1)S(1)} %copy-done.10), channel_id=1, source_target_pairs={{0,1},{1,0},{2,3},{3,2},{4,5},{5,4},{6,7},{7,6},{8,9},{9,8},{10,11... | collective-permute-start | bytes 1572872 | tf_op jit(solution)/shard_map/ppermute | solution.py:329
  34.6 6.0 %copy-start.9 = (bf16[8,2048,128]{2,1,0:T(8,128)(2,1)S(1)}, bf16[8,2048,128]{2,1,0:T(8,128)(2,1)}, u32[]{:S(2)}) copy-start(bf16[8,2048,128]{2,1,0:T(8,128)(2,1)} %refs_1_.3) | copy-start | bytes 12582916
  40.0 23.1 %collective-permute-start.14 = (bf16[176,2048]{1,0:T(8,128)(2,1)S(1)}, bf16[176,2048]{1,0:T(8,128)(2,1)S(1)}, u32[]{:S(2)}, u32[]{:S(2)}) collective-permute-start(bf16[176,2048]{1,0:T(8,128)(2,1)S(1)} %get-tuple-element.126), channel_id=1, source_target_pairs={{0,24},{4,28},{8,16},{12,20},{16,8},{20,12},{24,0},{28,4},{1,25},{... | collective-permute-start | bytes 2162696 | tf_op jit(solution)/shard_map/ppermute | solution.py:329
  40.6 22.3 %copy-start.5 = (f32[512,512]{1,0:T(8,128)S(1)}, f32[512,512]{1,0:T(8,128)}, u32[]{:S(2)}) copy-start(f32[512,512]{1,0:T(8,128)} %get-tuple-element.128) | copy-start | bytes 3145732
  46.1 22.6 %collective-permute-start.20 = (bf16[528,128]{1,0:T(8,128)(2,1)S(1)}, bf16[528,128]{1,0:T(8,128)(2,1)S(1)}, u32[]{:S(2)}, u32[]{:S(2)}) collective-permute-start(bf16[528,128]{1,0:T(8,128)(2,1)S(1)} %get-tuple-element.134.refs_0_), channel_id=1, source_target_pairs={{0,3},{1,2},{2,1},{3,0},{4,7},{5,6},{6,5},{7,4},{8,11},{9,10},{10,... | collective-permute-start | bytes 405512 | tf_op jit(solution)/shard_map/ppermute | solution.py:329
  47.5 24.6 %collective-permute-start.19 = (bf16[528,128]{1,0:T(8,128)(2,1)S(1)}, bf16[528,128]{1,0:T(8,128)(2,1)S(1)}, u32[]{:S(2)}, u32[]{:S(2)}) collective-permute-start(bf16[528,128]{1,0:T(8,128)(2,1)S(1)} %get-tuple-element.134.refs_0_), channel_id=1, source_target_pairs={{0,2},{1,3},{2,0},{3,1},{4,6},{5,7},{6,4},{7,5},{8,10},{9,11},{10,... | collective-permute-start | bytes 405512 | tf_op jit(solution)/shard_map/ppermute | solution.py:329
  58.7 13.5 %collective-permute-start.18 = (bf16[528,128]{1,0:T(8,128)(2,1)S(1)}, bf16[528,128]{1,0:T(8,128)(2,1)S(1)}, u32[]{:S(2)}, u32[]{:S(2)}) collective-permute-start(bf16[528,128]{1,0:T(8,128)(2,1)S(1)} %get-tuple-element.134.refs_0_), channel_id=1, source_target_pairs={{0,1},{1,0},{2,3},{3,2},{4,5},{5,4},{6,7},{7,6},{8,9},{9,8},{10,11... | collective-permute-start | bytes 405512 | tf_op jit(solution)/shard_map/ppermute | solution.py:329
  63.1 9.1 %copy-start.3 = (bf16[8,2,64,256]{3,2,1,0:T(8,128)(2,1)S(1)}, bf16[8,2,64,256]{3,2,1,0:T(8,128)(2,1)}, u32[]{:S(2)}) copy-start(bf16[8,2,64,256]{3,2,1,0:T(8,128)(2,1)} %refs_5_.3) | copy-start | bytes 1572868
  63.1 18.7 %copy-start.2 = (bf16[512,2048]{1,0:T(8,128)(2,1)S(1)}, bf16[512,2048]{1,0:T(8,128)(2,1)}, u32[]{:S(2)}) copy-start(bf16[512,2048]{1,0:T(8,128)(2,1)} %tokens_ref.4) | copy-start | bytes 6291460
  63.1 18.7 %copy-start.4 = (bf16[512,1024]{1,0:T(8,128)(2,1)S(1)}, bf16[512,1024]{1,0:T(8,128)(2,1)}, u32[]{:S(2)}) copy-start(bf16[512,1024]{1,0:T(8,128)(2,1)} %get-tuple-element.133) | copy-start | bytes 3145732
  67.7 6.5 %collective-permute-start.25 = (bf16[176,128]{1,0:T(8,128)(2,1)S(1)}, bf16[176,128]{1,0:T(8,128)(2,1)S(1)}, u32[]{:S(2)}, u32[]{:S(2)}) collective-permute-start(bf16[176,128]{1,0:T(8,128)(2,1)S(1)} %get-tuple-element.140.refs_0_), channel_id=1, source_target_pairs={{0,3},{1,2},{2,1},{3,0},{4,7},{5,6},{6,5},{7,4},{8,11},{9,10},{10,... | collective-permute-start | bytes 135176 | tf_op jit(solution)/shard_map/ppermute | solution.py:329
  67.8 6.4 %collective-permute-start.24 = (bf16[176,128]{1,0:T(8,128)(2,1)S(1)}, bf16[176,128]{1,0:T(8,128)(2,1)S(1)}, u32[]{:S(2)}, u32[]{:S(2)}) collective-permute-start(bf16[176,128]{1,0:T(8,128)(2,1)S(1)} %get-tuple-element.140.refs_0_), channel_id=1, source_target_pairs={{0,2},{1,3},{2,0},{3,1},{4,6},{5,7},{6,4},{7,5},{8,10},{9,11},{10,... | collective-permute-start | bytes 135176 | tf_op jit(solution)/shard_map/ppermute | solution.py:329
  68.8 5.4 %collective-permute-start.23 = (bf16[176,128]{1,0:T(8,128)(2,1)S(1)}, bf16[176,128]{1,0:T(8,128)(2,1)S(1)}, u32[]{:S(2)}, u32[]{:S(2)}) collective-permute-start(bf16[176,128]{1,0:T(8,128)(2,1)S(1)} %get-tuple-element.140.refs_0_), channel_id=1, source_target_pairs={{0,1},{1,0},{2,3},{3,2},{4,5},{5,4},{6,7},{7,6},{8,9},{9,8},{10,11... | collective-permute-start | bytes 135176 | tf_op jit(solution)/shard_map/ppermute | solution.py:329
  72.9 6.4 %collective-permute-start.21 = (bf16[176,512]{1,0:T(8,128)(2,1)S(1)}, bf16[176,512]{1,0:T(8,128)(2,1)S(1)}, u32[]{:S(2)}, u32[]{:S(2)}) collective-permute-start(bf16[176,512]{1,0:T(8,128)(2,1)S(1)} %get-tuple-element.137), channel_id=1, source_target_pairs={{0,8},{4,12},{8,0},{12,4},{16,24},{20,28},{24,16},{28,20},{1,9},{5... | collective-permute-start | bytes 540680 | tf_op jit(solution)/shard_map/ppermute | solution.py:329
  73.6 8.2 %collective-permute-start.22 = (bf16[176,512]{1,0:T(8,128)(2,1)S(1)}, bf16[176,512]{1,0:T(8,128)(2,1)S(1)}, u32[]{:S(2)}, u32[]{:S(2)}) collective-permute-start(bf16[176,512]{1,0:T(8,128)(2,1)S(1)} %get-tuple-element.138), channel_id=1, source_target_pairs={{0,16},{4,20},{8,24},{12,28},{16,0},{20,4},{24,8},{28,12},{1,17},{... | collective-permute-start | bytes 540680 | tf_op jit(solution)/shard_map/ppermute | solution.py:329
  74.6 7.3 %collective-permute-start.26 = (bf16[176,512]{1,0:T(8,128)(2,1)S(1)}, bf16[176,512]{1,0:T(8,128)(2,1)S(1)}, u32[]{:S(2)}, u32[]{:S(2)}) collective-permute-start(bf16[176,512]{1,0:T(8,128)(2,1)S(1)} %grow_rows.5), channel_id=1, source_target_pairs={{0,24},{4,28},{8,16},{12,20},{16,8},{20,12},{24,0},{28,4},{1,25},{... | collective-permute-start | bytes 540680 | tf_op jit(solution)/shard_map/ppermute | solution.py:329
  77.0 1.2 %collective-permute-start.17 = (f32[8,128]{1,0:T(8,128)S(1)}, f32[8,128]{1,0:T(8,128)S(1)}, u32[]{:S(2)}, u32[]{:S(2)}) collective-permute-start(f32[8,128]{1,0:T(8,128)S(1)} %max.6), channel_id=1, source_target_pairs={{0,4},{4,0},{8,12},{12,8},{16,20},{20,16},{24,28},{28,24},{1,5},{5... | collective-permute-start | bytes 12296 | tf_op jit(solution)/shard_map/ppermute | solution.py:329
  83.5 0.8 copy-start.6

commit v6 on v5

--- a/solution.py
+++ b/solution.py
@@ -26,7 +26,7 @@
 def pack_kernel(shape, place_ref, adapter_ref, slot_ref, tokens_ref, *refs):
     sizes, first_rows, chip_slots, flag_lane = shape
     messages = len(sizes)
-    outs, spread_ref, pick = refs[:messages], refs[messages], refs[messages + 1]
+    outs, key_ref, pick = refs[:messages], refs[messages], refs[messages + 1]
     rows, width = tokens_ref.shape
     experts = slot_ref.shape[1]
     offsets = [sum(round_up(s, 128) for s in sizes[:m]) for m in range(messages)]
@@ -51,7 +51,7 @@
             limit = jnp.where(sub == m, F32(first_rows[m] + sizes[m] - 1), limit)
         over = jnp.max(jnp.where((sub < messages) & (counts > limit), 1.0, 0.0), axis=0, keepdims=True)
         key = jnp.broadcast_to(position + shift * 65536, (8, rows))
-        key_column = key.astype(F32).T[:, 0:1].astype(jnp.int32)
+        key_ref[...] = jnp.broadcast_to(key.astype(F32).T[:, 0:1].astype(jnp.int32), key_ref.shape)
         within8 = jnp.broadcast_to(within, (16, rows)).astype(BF)
         for m in range(messages):
             padded = round_up(sizes[m], 128)
@@ -59,9 +59,6 @@
             hit = (target + first_rows[m] == position) & (shift == m) & (target < sizes[m] - 1)
             chosen = hit.astype(F32).astype(BF)
             pick[offsets[m]:offsets[m] + padded, :] = chosen
-            lane_target = lax.broadcasted_iota(jnp.int32, (rows, padded), 1)
-            back = (lane_target == key_column - first_rows[m] - m * 65536) & (lane_target < sizes[m] - 1)
-            spread_ref[:, offsets[m]:offsets[m] + padded] = back.astype(F32).astype(BF)
             places = dot(within8, chosen, ((1,), (1,)))[0:1, :]
             if padded < width:
                 places = jnp.concatenate([places, jnp.zeros((1, width - padded), F32)], axis=1)
@@ -91,8 +88,8 @@
             pl.BlockSpec((rows, block), lambda i: (0, i)),
         ],
         out_specs=[pl.BlockSpec((s, block), lambda i: (0, i)) for s in sizes]
-        + [pl.BlockSpec((rows, spread), lambda i: (0, 0))],
-        out_shape=[jax.ShapeDtypeStruct((s, width), BF) for s in sizes] + [jax.ShapeDtypeStruct((rows, spread), BF)],
+        + [pl.BlockSpec((rows, 128), lambda i: (0, 0))],
+        out_shape=[jax.ShapeDtypeStruct((s, width), BF) for s in sizes] + [jax.ShapeDtypeStruct((rows, 128), jnp.int32)],
         scratch_shapes=[pltpu.VMEM((spread, rows), BF)],
         cost_estimate=COST,
         compiler_params=pltpu.CompilerParams(vmem_limit_bytes=VMEM_LIMIT),
@@ -143,10 +140,10 @@
 
     @pl.when(step == pl.num_programs(0) - 1)
     def _():
-        out[kept:, :] = total[...].astype(BF)
-
-
-def shrink(core, messages, mine, sibling, flag_lane, carry=()):
+        out[kept:, :] = total[...].astype(out.dtype)
+
+
+def shrink(core, messages, mine, sibling, flag_lane, carry=(), dtype=BF):
     local, width, both = mine.shape
     rows = sum(m.shape[0] for m in messages)
     whole = [pl.BlockSpec(m.shape, lambda i: (0, 0)) for m in messages]
@@ -160,7 +157,7 @@
         in_specs=[pl.BlockSpec(memory_space=pltpu.SMEM)] + whole + [pair, pair] + whole_carry,
         out_specs=[keep, keep, pl.BlockSpec((8, 128), lambda i: (0, 0))],
         out_shape=[
-            jax.ShapeDtypeStruct((every, both), BF),
+            jax.ShapeDtypeStruct((every, both), dtype),
             jax.ShapeDtypeStruct((every, both), BF),
             jax.ShapeDtypeStruct((8, 128), F32),
         ],
@@ -220,62 +217,69 @@
     )(core, *parts, place, mine, sibling)
 
 
-def base_kernel(steps, shifts, count, place_ref, weight_ref, tokens_ref, *refs):
-    arrived, outs, total = refs[:count], refs[count:-1], refs[-1]
-    columns = outs[0].shape[1] // 2
-    rows, width = tokens_ref.shape
-    deep = width // steps
-    read = total.shape[2]
-    chosen = (place_ref[0] ^ shifts[0]) if len(shifts) == 1 else 0
-    total[...] = jnp.zeros(total.shape, F32)
-
-    def body(tokens, weight):
-        turned = jnp.swapaxes(weight[...], 0, 1)
-        for j in range(2):
-            total[j] += dot(tokens[...], turned[j])
-
-    pltpu.emit_pipeline(
-        body,
-        grid=(steps,),
-        in_specs=[
-            pl.BlockSpec((rows, deep), lambda i: (0, i)),
-            pl.BlockSpec((deep, 2, read), lambda i: (i, 0, chosen)),
-        ],
-    )(tokens_ref, weight_ref)
-    for r, out in zip(shifts, outs):
-        start = 0 if len(shifts) == 1 else pl.multiple_of((place_ref[0] ^ r) * columns, columns)
-        for j in range(2):
-            part = total[j, :, pl.ds(start, columns)]
-            for one in arrived:
-                part = part + one[:, j * columns:(j + 1) * columns].astype(F32)
-            out[:, j * columns:(j + 1) * columns] = part.astype(out.dtype)
-
-
-def base_parts(t, tokens, weight, blocks, shifts, steps, arrived=(), dtype=None):
+def base_kernel(shifts, place_ref, tokens_ref, weight_ref, *outs):
+    step = pl.program_id(0)
+    weight = jnp.swapaxes(weight_ref[...], 0, 1)
+    columns = weight.shape[2]
+    both = [dot(tokens_ref[...], weight[j]) for j in range(2)]
+    for i, out in enumerate(outs):
+
+        @pl.when(step == i)
+        def _():
+            for j in range(2):
+                out[:, j * columns:(j + 1) * columns] = both[j].astype(out.dtype)
+
+
+def base_parts(t, tokens, weight, blocks, shifts):
     rows, width = tokens.shape
     columns = weight.shape[2] // blocks
-    types = [dtype or (BF if r % 2 else F32) for r in shifts]
+    types = [BF if r % 2 else F32 for r in shifts]
     if columns % 128:
         cut = [lax.dynamic_slice_in_dim(weight, (t ^ r) * columns, columns, 2) for r in shifts]
-        cut = [dot(tokens, c.reshape(width, 2 * columns)) for c in cut]
-        for one in arrived:
-            cut = [c + one.astype(F32) for c in cut]
-        return [c.astype(k) for c, k in zip(cut, types)]
-    read = columns if len(shifts) == 1 else columns * blocks
-    vmem = pl.BlockSpec(memory_space=pltpu.VMEM)
-    hbm = pl.BlockSpec(memory_space=pltpu.HBM)
-    return pl.pallas_call(
-        functools.partial(base_kernel, steps, shifts, len(arrived)),
-        in_specs=[pl.BlockSpec(memory_space=pltpu.SMEM), hbm, hbm] + [vmem] * len(arrived),
-        out_specs=[vmem] * len(shifts),
-        scratch_shapes=[pltpu.VMEM((2, rows, read), F32)],
+        return [dot(tokens, c.reshape(width, 2 * columns)).astype(k) for c, k in zip(cut, types)]
+    order = jnp.stack([t ^ r for r in shifts])
+    return pl.pallas_call(
+        functools.partial(base_kernel, shifts),
+        grid_spec=pltpu.PrefetchScalarGridSpec(
+            num_scalar_prefetch=1,
+            grid=(len(shifts),),
+            in_specs=[
+                pl.BlockSpec((rows, width), lambda i, p: (0, 0)),
+                pl.BlockSpec((width, 2, columns), lambda i, p: (0, 0, p[i])),
+            ],
+            out_specs=[pl.BlockSpec((rows, 2 * columns), lambda i, p: (0, 0))] * len(shifts),
+        ),
         out_shape=[jax.ShapeDtypeStruct((rows, 2 * columns), k) for k in types],
         cost_estimate=pl.CostEstimate(
-            flops=16 * rows * width * read, bytes_accessed=8 * width * read, transcendentals=0
+            flops=16 * len(shifts) * rows * width * columns, bytes_accessed=8 * width * columns, transcendentals=0
         ),
         compiler_params=pltpu.CompilerParams(vmem_limit_bytes=VMEM_MOST),
         name="base_parts",
-    )(t.reshape(1), weight, tokens, *arrived)
+    )(order, tokens, weight)
+
+
+def spread_kernel(sizes, first_rows, key_ref, out):
+    start = 0
+    for m, size in enumerate(sizes):
+        padded = round_up(size, 128)
+        lane = lax.broadcasted_iota(jnp.int32, (key_ref.shape[0], padded), 1)
+        hit = (lane == key_ref[:, 0:1] - first_rows[m] - m * 65536) & (lane < size - 1)
+        out[:, start:start + padded] = hit.astype(F32).astype(BF)
+        start += padded
+
+
+def spread_of(key, sizes, first_rows):
+    vmem = pl.BlockSpec(memory_space=pltpu.VMEM)
+    total = sum(round_up(size, 128) for size in sizes)
+    return pl.pallas_call(
+        functools.partial(spread_kernel, sizes, first_rows),
+        in_specs=[vmem],
+        out_specs=vmem,
+        out_shape=jax.ShapeDtypeStruct((key.shape[0], total), BF),
+        cost_estimate=COST,
+        compiler_params=pltpu.CompilerParams(vmem_limit_bytes=VMEM_LIMIT),
+        name="spread_rows",
+    )(key)
 
 
 def finish_kernel(sizes, count, *refs):
@@ -369,64 +373,69 @@
     rest = round_up(full - message + 2, 16)
     sizes, first_rows = (message,) * chips, (0,) * chips
 
-    t = lax.axis_index("tensor").astype(jnp.int32)
-    first_shift = blocks - 1
-    parts = {first_shift: base_parts(t, tokens, key_value_base_weight, blocks, [first_shift], 2)[0]}
-    came = {}
-    came[(1, first_shift ^ 1)] = exchange(parts[first_shift], "tensor", 1)
-
-    packed = pack(chip, adapters, slots, after(tokens, parts[first_shift]), sizes, first_rows, chip_slots)
-    sent, spread = list(packed[:-1]), packed[-1]
+    packed = pack(chip, adapters, slots, tokens, sizes, first_rows, chip_slots)
+    sent, key = list(packed[:-1]), packed[-1]
     arrived, returned = {0: sent[0]}, {}
     for m in near[1:]:
         arrived[m] = exchange(sent[m], "dp", 2 * m)
 
-    plain = [r for r in range(blocks - 1) if r % 2 or r == 0]
+    t = lax.axis_index("tensor").astype(jnp.int32)
     late_tokens = after(tokens, *sent)
-    parts.update(zip(plain, base_parts(t, late_tokens, key_value_base_weight, blocks, plain, 4)))
+    first_shift = blocks - 1
+    parts = {first_shift: base_parts(t, late_tokens, key_value_base_weight, blocks, [first_shift])[0]}
+    came = {(1, first_shift ^ 1): exchange(parts[first_shift], "tensor", 1)}
+    others = list(range(first_shift - 1, -1, -1))
+    late_tokens = after(tokens, parts[first_shift])
+    parts.update(zip(others, base_parts(t, late_tokens, key_value_base_weight, blocks, others)))
 
     def arrived_for(r):
         return [came[key] for key in sorted(came) if key[1] == r]
 
     up_sibling = exchange(after(adapter_up_weight, down_sibling), "dp", 1)
+    carry = shrink(core, [after(sent[0], parts[0])], adapter_down_weight, down_sibling, flag_lane, dtype=F32)
     near_done = [arrived[m] for m in near[1:]]
-    for r in sorted(range(1, blocks - 1), key=lambda r: (r & -r, -r)):
-        low = r & -r
-        if r % 2:
-            part = after(parts[r], came[(1, first_shift ^ 1)]) if r == 1 else parts[r]
-        else:
-            part = base_parts(t, late_tokens, key_value_base_weight, blocks, [r], 2, arrived_for(r), BF)[0]
-        came[(low, r ^ low)] = exchange(part, "tensor", low)
-    carry = shrink(core, [after(sent[0], parts[0], part)], adapter_down_weight, down_sibling, flag_lane)
     for m in far:
         arrived[m] = exchange(after(sent[m], *near_done, carry[0]), "dp", 2 * m)
-
-    flags = []
+    for r in sorted(range(1, first_shift), key=lambda r: (r & -r, -r)):
+        low = r & -r
+        part = parts[r]
+        for one in arrived_for(r):
+            part = part + after(one, *near_done, carry[0]).astype(F32)
+        if r == 1:
+            part = after(part, came[(1, first_shift ^ 1)])
+        came[(low, r ^ low)] = exchange(part.astype(BF), "tensor", low)
+
+    both_down = after(down_sibling, up_sibling)
+    flags, updates = [], {}
     for part in (near, far):
         if not part:
             continue
         group = [arrived[m] for m in part if m]
-        if part is far:
-            group[0] = after(group[0], base)
-        share, place, flag = shrink(
-            core, group, adapter_down_weight, after(down_sibling, up_sibling), flag_lane, carry if part is near else ()
-        )
-        flags.append(flag)
         if part is near:
+            share, place, flag = shrink(core, group, adapter_down_weight, both_down, flag_lane, carry, F32)
+            step = 1
+            while 2 * step < blocks:
+                share = share + exchange(share.astype(BF), "tensor", step).astype(F32)
+                step *= 2
+            shares = [share, exchange(share.astype(BF), "tensor", step)]
             base = after(parts[0], share)
             for one in arrived_for(0):
                 base = base + one.astype(F32)
-        shares = [after(share, came[(1, 0)])] + [exchange(share, "tensor", z) for z in range(1, blocks)]
+        else:
+            group[0] = after(group[0], base)
+            share, place, flag = shrink(core, group, adapter_down_weight, both_down, flag_lane)
+            shares = [after(share, returned[0])] + [exchange(share, "tensor", z) for z in range(1, blocks)]
+        flags.append(flag)
         grown = grow(core, shares, place, adapter_up_weight, up_sibling, tuple(sizes[m] for m in part))
         for m, update in zip(part, grown):
             returned[m] = update if m == 0 else exchange(update, "dp", 2 * m)
+    spread = spread_of(after(key, base), sizes, first_rows)
     flag = functools.reduce(jnp.maximum, flags)
     flag = jnp.maximum(flag, exchange(flag, "dp", 1))
-    bases = [base]
     updates = [returned[m] for m in range(chips)]
 
     def as_is():
-        return finish(bases, [spread], [updates])
+        return finish([base], [spread], [updates])
 
     def second_round():
         later_sizes, later_rows = (rest,) * chips, (message - 1,) * chips
@@ -436,7 +445,7 @@
         shares = [share] + [exchange(share, "tensor", z) for z in range(1, blocks)]
         grown = grow(core, shares, place, adapter_up_weight, up_sibling, later_sizes)
         back = [grown[0]] + [exchange(grown[m], "dp", 2 * m) for m in range(1, chips)]
-        return finish(bases, [spread, packed[-1]], [updates, back])
+        return finish([base], [spread, spread_of(packed[-1], later_sizes, later_rows)], [updates, back])
 
     return lax.cond(flag[0, 0] > 0.0, second_round, as_is)
 

time: 84.7 us -> 91.4 us (1.079)
  waiting for transfers between devices: 17.4 us -> 26 us
  Pallas kernels: 42.6 us -> 37.5 us
  other arithmetic: 0.21 us -> 2.11 us
  local copies, waits for them, and re-layouts: 2.25 us -> 3.36 us
    ppermute x18 -> x17, waiting for transfers between devices: 17.4 us -> 26 us  [exchange(): return lax.ppermute(array, axis, [(i, i ^ shift) for i in range(size)])]
    pallas_call x3, Pallas kernels: 18.8 us -> 14 us  [the longest x2 13.7 us: base_parts(): pl.pallas_call(functools.partial(base_kernel, shifts), grid_spec=pltpu.Pr...]
    convert_element_type x0 -> x3, other arithmetic: none -> 1.27 us  [the longest x1 1.21 us: per_device(): came[low, r ^ low] = exchange(part.astype(BF), 'tensor', low)]
    unnamed x22 -> x20, local copies, waits for them, and re-layouts: 1.74 us -> 2.85 us
    ppermute x18 -> x17, starting transfers between devices: 20.9 us -> 20.9 us  [exchange(): return lax.ppermute(array, axis, [(i, i ^ shift) for i in range(size)])]
  transfers between devices with their start and end apart: 18 -> 17, of which waited for: 4 -> 7; matrix products, arithmetic and copies ran while one was open for 1% -> 3% of each run, Pallas kernels for 49% -> 40%
where the time goes in v6:
time: 91.4 us; the launch traced here: 91 us
  Pallas kernels  37.5 us (41%)
  waiting for transfers between devices  26 us (28%)
  starting transfers between devices  20.9 us (23%)
  local copies, waits for them, and re-layouts  3.36 us (4%)
  other arithmetic  2.11 us (2%)
    ppermute x17, waiting for transfers between devices, exchange(): return lax.ppermute(array, axis, [(i, i ^ shift) for i in range(size)])  26 us
    ppermute x17, starting transfers between devices, exchange(): return lax.ppermute(array, axis, [(i, i ^ shift) for i in range(size)])  20.9 us
    pallas_call x3, Pallas kernels, shrink(): pl.pallas_call(functools.partial(shrink_kernel, len(messages), len(carry)...  15.6 us
    pallas_call x2, Pallas kernels, base_parts(): pl.pallas_call(functools.partial(base_kernel, shifts), grid_spec=pltpu.Pr...  13.7 us
    pallas_call x1, Pallas kernels, pack(): pl.pallas_call(functools.partial(pack_kernel, (sizes, first_rows, chip_sl...  5.29 us
    unnamed x20, local copies, waits for them, and re-layouts  2.85 us
  transfers between devices with their start and end apart: 17, of which 7 were waited for; matrix products, arithmetic and copies ran while one was open for 3% of the time, Pallas kernels for 40%

profile of v6, /device:TPU:0, one launch (start us, length us, event | category | flops | bytes accessed | tf_op | source)
XLA Modules:
  0.0 91.0 jit_solution(13691130945808337575)
XLA Ops:
  0.5 5.3 %pack_rows.3 = (bf16[176,2048]{1,0:T(8,128)(2,1)S(1)}, bf16[176,2048]{1,0:T(8,128)(2,1)}, bf16[176,2048]{1,0:T(8,128)(2,1)S(1)}, bf16[176,2048]{1,0:T(8,128)(2,1)S(1)}, s32[512,128]{1,0:T(8,128)S(1)}) custom-call(s32[1]{0:T(128)} %bitcast.1.place_ref, s32[1,512]{1,0:T(1,128)} %bitcast.9, s32[1,64]{1,0:T(1,128)} %bitcast.11, bf16[512,2048]{1,0:T(8,128)(2,1)} %tokens_ref.3), custom_call_target="tpu_custom_call" | custom-call | flops 1000 | bytes 1000 | tf_op jit(solution)/shard_map/pack_rows/pallas_call | solution.py:81
  5.7 0.9 %copy-done = bf16[176,2048]{1,0:T(8,128)(2,1)} copy-done((bf16[176,2048]{1,0:T(8,128)(2,1)}, bf16[176,2048]{1,0:T(8,128)(2,1)S(1)}, u32[]{:S(2)}) %copy-start) | copy-done | bytes 720920
  6.7 2.5 %collective-permute-start.9 = (bf16[176,2048]{1,0:T(8,128)(2,1)}, bf16[176,2048]{1,0:T(8,128)(2,1)S(1)}, u32[]{:S(2)}, u32[]{:S(2)}) collective-permute-start(bf16[176,2048]{1,0:T(8,128)(2,1)} %get-tuple-element.114), channel_id=1, source_target_pairs={{0,8},{4,12},{8,0},{12,4},{16,24},{20,28},{24,16},{28,20},{1,9},{5... | collective-permute-start | bytes 2162696 | tf_op jit(solution)/shard_map/ppermute | solution.py:333
  9.2 1.5 %collective-permute-start.10 = (bf16[176,2048]{1,0:T(8,128)(2,1)S(1)}, bf16[176,2048]{1,0:T(8,128)(2,1)S(1)}, u32[]{:S(2)}, u32[]{:S(2)}) collective-permute-start(bf16[176,2048]{1,0:T(8,128)(2,1)S(1)} %get-tuple-element.115), channel_id=1, source_target_pairs={{0,16},{4,20},{8,24},{12,28},{16,0},{20,4},{24,8},{28,12},{1,17},{... | collective-permute-start | bytes 2162696 | tf_op jit(solution)/shard_map/ppermute | solution.py:333
  10.7 4.6 %base_parts.2 = bf16[512,512]{1,0:T(8,128)(2,1)} custom-call(s32[1]{0:T(128)} %bitcast.7.place_ref, bf16[512,2048]{1,0:T(8,128)(2,1)} %tokens_ref.3, bf16[2048,2,1024]{2,1,0:T(2,128)(2,1)} %weight_ref.3), custom_call_target="tpu_custom_call" | custom-call | flops 4294967296 | bytes 4194304 | tf_op jit(solution)/shard_map/base_parts/pallas_call | solution.py:241
  15.2 1.6 %collective-permute-start.15 = (bf16[512,512]{1,0:T(8,128)(2,1)}, bf16[512,512]{1,0:T(8,128)(2,1)}, u32[]{:S(2)}, u32[]{:S(2)}) collective-permute-start(bf16[512,512]{1,0:T(8,128)(2,1)} %base_parts.2), channel_id=1, source_target_pairs={{0,1},{1,0},{2,3},{3,2},{4,5},{5,4},{6,7},{7,6},{8,9},{9,8},{10,11... | collective-permute-start | bytes 1572872 | tf_op jit(solution)/shard_map/ppermute | solution.py:333
  16.8 0.6 pad_add_fusion.place_ref
  17.4 9.1 %base_parts.3 = (f32[512,512]{1,0:T(8,128)}, bf16[512,512]{1,0:T(8,128)(2,1)}, f32[512,512]{1,0:T(8,128)}) custom-call(s32[3]{0:T(128)} %pad_add_fusion.place_ref, bf16[512,2048]{1,0:T(8,128)(2,1)} %tokens_ref.3, bf16[2048,2,1024]{2,1,0:T(2,128)(2,1)} %weight_ref.3), custom_call_target="tpu_custom_call" | custom-call | flops 12884901888 | bytes 4194304 | tf_op jit(solution)/shard_map/base_parts/pallas_call | solution.py:241
  26.5 2.8 %collective-permute-done.15 = bf16[512,512]{1,0:T(8,128)(2,1)} collective-permute-done((bf16[512,512]{1,0:T(8,128)(2,1)}, bf16[512,512]{1,0:T(8,128)(2,1)}, u32[]{:S(2)}, u32[]{:S(2)}) %collective-permute-start.15) | collective-permute-done | bytes 524320 | tf_op jit(solution)/shard_map/ppermute | solution.py:333
  29.3 1.6 %collective-permute-start.16 = (bf16[512,512]{1,0:T(8,128)(2,1)}, bf16[512,512]{1,0:T(8,128)(2,1)S(1)}, u32[]{:S(2)}, u32[]{:S(2)}) collective-permute-start(bf16[512,512]{1,0:T(8,128)(2,1)} %get-tuple-element.132), channel_id=1, source_target_pairs={{0,1},{1,0},{2,3},{3,2},{4,5},{5,4},{6,7},{7,6},{8,9},{9,8},{10,11... | collective-permute-start | bytes 1572872 | tf_op jit(solution)/shard_map/ppermute | solution.py:333
  30.9 1.1 %copy-done.1 = bf16[176,2048]{1,0:T(8,128)(2,1)S(1)} copy-done((bf16[176,2048]{1,0:T(8,128)(2,1)S(1)}, bf16[176,2048]{1,0:T(8,128)(2,1)}, u32[]{:S(2)}) %copy-start.1) | copy-done | bytes 720920
  32.0 5.6 %shrink_rows.5 = (f32[176,128]{1,0:T(8,128)S(1)}, bf16[176,128]{1,0:T(8,128)(2,1)S(1)}, f32[8,128]{1,0:T(8,128)S(1)}) custom-call(s32[1]{0:T(128)} %bitcast.core_ref, bf16[176,2048]{1,0:T(8,128)(2,1)S(1)} %copy-done.1, bf16[8,2048,128]{2,1,0:T(8,128)(2,1)} %refs_1_.3, bf16[8,2048,128]{2,1,0:T(8,128)(2,1)} %collective-permute-done.11.refs_2_.refs_3_), custom_call_target="tpu_custom_call" | custom-call | flops 2952790016 | bytes 16777216 | tf_op jit(solution)/shard_map/shrink_rows/pallas_call | solution.py:154
  37.7 1.2 %add_convert_fusion = bf16[512,512]{1,0:T(8,128)(2,1)S(1)} fusion(f32[512,512]{1,0:T(8,128)S(1)} %copy-done.5, bf16[512,512]{1,0:T(8,128)(2,1)} %collective-permute-done.15), kind=kLoop, calls=%fused_computation.1 | loop fusion | flops 786432 | bytes 2097152 | tf_op jit(solution)/shard_map/convert_element_type | solution.py:406
  38.9 2.6 %collective-permute-start.17 = (bf16[512,512]{1,0:T(8,128)(2,1)S(1)}, bf16[512,512]{1,0:T(8,128)(2,1)S(1)}, u32[]{:S(2)}, u32[]{:S(2)}) collective-permute-start(bf16[512,512]{1,0:T(8,128)(2,1)S(1)} %add_convert_fusion), channel_id=1, source_target_pairs={{0,2},{1,3},{2,0},{3,1},{4,6},{5,7},{6,4},{7,5},{8,10},{9,11},{10,... | collective-permute-start | bytes 1572872 | tf_op jit(solution)/shard_map/ppermute | solution.py:333
  42.0 5.5 %shrink_rows.6 = (f32[528,128]{1,0:T(8,128)S(1)}, bf16[528,128]{1,0:T(8,128)(2,1)S(1)}, f32[8,128]{1,0:T(8,128)S(1)}) custom-call(s32[1]{0:T(128)} %bitcast.core_ref, bf16[176,2048]{1,0:T(8,128)(2,1)S(1)} %collective-permute-done.9.refs_0_, bf16[176,2048]{1,0:T(8,128)(2,1)S(1)} %collective-permute-done.10.refs_1_, bf16[8,2048,128]{2,1,0:T(8,128)(2,1)S(1)} %copy-done.9, ...), custom_call_target="tpu_custom_call" | custom-call | flops 5905580032 | bytes 16777216 | tf_op jit(solution)/shard_map/shrink_rows/pallas_call | solution.py:154
  47.6 0.5 collective-permute-start.14
  48.1 8.2 %collective-permute-done.14 = bf16[528,128]{1,0:T(8,128)(2,1)S(1)} collective-permute-done((bf16[528,128]{1,0:T(8,128)(2,1)S(1)}, bf16[528,128]{1,0:T(8,128)(2,1)S(1)}, u32[]{:S(2)}, u32[]{:S(2)}) %collective-permute-start.14) | collective-permute-done | bytes 135200 | tf_op jit(solution)/shard_map/ppermute | solution.py:333
  56.4 2.9 %collective-permute-start.19 = (bf16[528,128]{1,0:T(8,128)(2,1)S(1)}, bf16[528,128]{1,0:T(8,128)(2,1)S(1)}, u32[]{:S(2)}, u32[]{:S(2)}) collective-permute-start(bf16[528,128]{1,0:T(8,128)(2,1)S(1)} %get-tuple-element.147), channel_id=1, source_target_pairs={{0,2},{1,3},{2,0},{3,1},{4,6},{5,7},{6,4},{7,5},{8,10},{9,11},{10,... | collective-permute-start | bytes 405512 | tf_op jit(solution)/shard_map/ppermute | solution.py:333
  59.3 9.2 %collective-permute-done.17 = bf16[512,512]{1,0:T(8,128)(2,1)S(1)} collective-permute-done((bf16[512,512]{1,0:T(8,128)(2,1)S(1)}, bf16[512,512]{1,0:T(8,128)(2,1)S(1)}, u32[]{:S(2)}, u32[]{:S(2)}) %collective-permute-start.17) | collective-permute-done | bytes 524320 | tf_op jit(solution)/shard_map/ppermute | solution.py:333
  68.8 4.4 %shrink_rows.7 = (bf16[176,128]{1,0:T(8,128)(2,1)S(1)}, bf16[176,128]{1,0:T(8,128)(2,1)S(1)}, f32[8,128]{1,0:T(8,128)S(1)}) custom-call(s32[1]{0:T(128)} %bitcast.core_ref, bf16[176,2048]{1,0:T(8,128)(2,1)S(1)} %collective-permute-done.13.refs_0_, bf16[8,2048,128]{2,1,0:T(8,128)(2,1)S(1)} %copy-done.9, ...), custom_call_target="tpu_custom_call" | custom-call | flops 2952790016 | bytes 16777216 | tf_op jit(solution)/shard_map/shrink_rows/pallas_call | solution.py:154
  73.3 2.8 %collective-permute-start.24 = (bf16[176,128]{1,0:T(8,128)(2,1)S(1)}, bf16[176,128]{1,0:T(8,128)(2,1)S(1)}, u32[]{:S(2)}, u32[]{:S(2)}) collective-permute-start(bf16[176,128]{1,0:T(8,128)(2,1)S(1)} %get-tuple-element.144.refs_0_), channel_id=1, source_target_pairs={{0,3},{1,2},{2,1},{3,0},{4,7},{5,6},{6,5},{7,4},{8,11},{9,10},{10,... | collective-permute-start | bytes 135176 | tf_op jit(solution)/shard_map/ppermute | solution.py:333
  76.0 1.7 %collective-permute-start.22 = (bf16[176,128]{1,0:T(8,128)(2,1)S(1)}, bf16[176,128]{1,0:T(8,128)(2,1)S(1)}, u32[]{:S(2)}, u32[]{:S(2)}) collective-permute-start(bf16[176,128]{1,0:T(8,128)(2,1)S(1)} %get-tuple-element.144.refs_0_), channel_id=1, source_target_pairs={{0,1},{1,0},{2,3},{3,2},{4,5},{5,4},{6,7},{7,6},{8,9},{9,8},{10,11... | collective-permute-start | bytes 135176 | tf_op jit(solution)/shard_map/ppermute | solution.py:333
  77.7 0.8 grow_rows.4
  78.5 0.6 collective-permute-start.20
  79.6 1.4 %collective-permute-done.23.refs_2_ = bf16[176,128]{1,0:T(8,128)(2,1)S(1)} collective-permute-done((bf16[176,128]{1,0:T(8,128)(2,1)S(1)}, bf16[176,128]{1,0:T(8,128)(2,1)S(1)}, u32[]{:S(2)}, u32[]{:S(2)}) %collective-permute-start.23) | collective-permute-done | bytes 45088 | tf_op jit(solution)/shard_map/ppermute | solution.py:333
  81.4 1.2 %collective-permute-start.25 = (bf16[176,512]{1,0:T(8,128)(2,1)S(1)}, bf16[176,512]{1,0:T(8,128)(2,1)S(1)}, u32[]{:S(2)}, u32[]{:S(2)}) collective-permute-start(bf16[176,512]{1,0:T(8,128)(2,1)S(1)} %grow_rows.5), channel_id=1, source_target_pairs={{0,24},{4,28},{8,16},{12,20},{16,8},{20,12},{24,0},{28,4},{1,25},{... | collective-permute-start | bytes 540680 | tf_op jit(solution)/shard_map/ppermute | solution.py:333
  82.9 0.8 collective-permute-done.18
  83.7 0.5 slice.3
  85.2 3.3 %collective-permute-done.21 = bf16[176,512]{1,0:T(8,128)(2,1)S(1)} collective-permute-done((bf16[176,512]{1,0:T(8,128)(2,1)S(1)}, bf16[176,512]{1,0:T(8,128)(2,1)S(1)}, u32[]{:S(2)}, u32[]{:S(2)}) %collective-permute-start.21) | collective-permute-done | bytes 180256 | tf_op jit(solution)/shard_map/ppermute | solution.py:333
  88.5 1.7 %conditional.1 = (bf16[512,2,256]{2,1,0:T(2,128)(2,1)S(1)}) conditional(s32[]{:T(128)} %bitcast.8, (f32[512,512]{1,0:T(8,128)S(1)}, bf16[512,1024]{1,0:T(8,128)(2,1)S(1)}, bf16[176,512]{1,0:T(8,128)(2,1)S(1)}, bf16[176,512]{1,0:T(8,128)(2,1)S(1)}, bf16[176,512]{1,0:T(8,128)(2,1)S(1)}, /*index=5*/bf16[176,512]{1,0:T(8,128)(2,1)S(1)}) %tuple.35, ...), branch_computations={%region_0.1_spmd, %region_1.2_spmd} | conditional | flops 6442455040 | bytes 23859472 | solution.py:450
  88.5 1.5 %finish_rows.2 = bf16[512,2,256]{2,1,0:T(2,128)(2,1)S(1)} custom-call(f32[512,512]{1,0:T(8,128)S(1)} %get-tuple-element.50.refs_0_, bf16[512,1024]{1,0:T(8,128)(2,1)S(1)} %get-tuple-element.51.refs_1_, bf16[176,512]{1,0:T(8,128)(2,1)S(1)} %get-tuple-element.52.refs_2_, bf16[176,512]{1,0:T(8,128)(2,1)S(1)} %get-tuple-element.53.refs_3_, ...), custom_call_target="tpu_custom_call" | custom-call | flops 1000 | bytes 1000 | tf_op jit(solution)/shard_map/cond/branch_0_fun/finish_rows/pallas_call | solution.py:318
  90.2 0.8 copy-done.6
  (41 shorter events, 2.8 us)
Async XLA Ops:
  0.0 30.9 %collective-permute-start.11 = (bf16[8,2048,128]{2,1,0:T(8,128)(2,1)}, bf16[8,2048,128]{2,1,0:T(8,128)(2,1)}, u32[]{:S(2)}, u32[]{:S(2)}) collective-permute-start(bf16[8,2048,128]{2,1,0:T(8,128)(2,1)} %refs_1_.3), channel_id=1, source_target_pairs={{0,4},{4,0},{8,12},{12,8},{16,20},{20,16},{24,28},{28,24},{1,5},{5... | collective-permute-start | bytes 12582920 | tf_op jit(solution)/shard_map/ppermute | solution.py:333
  5.7 0.9 %copy-start = (bf16[176,2048]{1,0:T(8,128)(2,1)}, bf16[176,2048]{1,0:T(8,128)(2,1)S(1)}, u32[]{:S(2)}) copy-start(bf16[176,2048]{1,0:T(8,128)(2,1)S(1)} %get-tuple-element.123.refs_0_) | copy-start | bytes 2162692
  6.7 31.0 %collective-permute-start.9 = (bf16[176,2048]{1,0:T(8,128)(2,1)}, bf16[176,2048]{1,0:T(8,128)(2,1)S(1)}, u32[]{:S(2)}, u32[]{:S(2)}) collective-permute-start(bf16[176,2048]{1,0:T(8,128)(2,1)} %get-tuple-element.114), channel_id=1, source_target_pairs={{0,8},{4,12},{8,0},{12,4},{16,24},{20,28},{24,16},{28,20},{1,9},{5... | collective-permute-start | bytes 2162696 | tf_op jit(solution)/shard_map/ppermute | solution.py:333
  9.2 28.5 %collective-permute-start.10 = (bf16[176,2048]{1,0:T(8,128)(2,1)S(1)}, bf16[176,2048]{1,0:T(8,128)(2,1)S(1)}, u32[]{:S(2)}, u32[]{:S(2)}) collective-permute-start(bf16[176,2048]{1,0:T(8,128)(2,1)S(1)} %get-tuple-element.115), channel_id=1, source_target_pairs={{0,16},{4,20},{8,24},{12,28},{16,0},{20,4},{24,8},{28,12},{1,17},{... | collective-permute-start | bytes 2162696 | tf_op jit(solution)/shard_map/ppermute | solution.py:333
  15.2 14.1 %collective-permute-start.15 = (bf16[512,512]{1,0:T(8,128)(2,1)}, bf16[512,512]{1,0:T(8,128)(2,1)}, u32[]{:S(2)}, u32[]{:S(2)}) collective-permute-start(bf16[512,512]{1,0:T(8,128)(2,1)} %base_parts.2), channel_id=1, source_target_pairs={{0,1},{1,0},{2,3},{3,2},{4,5},{5,4},{6,7},{7,6},{8,9},{9,8},{10,11... | collective-permute-start | bytes 1572872 | tf_op jit(solution)/shard_map/ppermute | solution.py:333
  29.3 30.0 %collective-permute-start.16 = (bf16[512,512]{1,0:T(8,128)(2,1)}, bf16[512,512]{1,0:T(8,128)(2,1)S(1)}, u32[]{:S(2)}, u32[]{:S(2)}) collective-permute-start(bf16[512,512]{1,0:T(8,128)(2,1)} %get-tuple-element.132), channel_id=1, source_target_pairs={{0,1},{1,0},{2,3},{3,2},{4,5},{5,4},{6,7},{7,6},{8,9},{9,8},{10,11... | collective-permute-start | bytes 1572872 | tf_op jit(solution)/shard_map/ppermute | solution.py:333
  30.9 11.1 %collective-permute-start.12 = (bf16[8,2,64,256]{3,2,1,0:T(8,128)(2,1)}, bf16[8,2,64,256]{3,2,1,0:T(8,128)(2,1)S(1)}, u32[]{:S(2)}, u32[]{:S(2)}) collective-permute-start(bf16[8,2,64,256]{3,2,1,0:T(8,128)(2,1)} %refs_5_.1), channel_id=1, source_target_pairs={{0,4},{4,0},{8,12},{12,8},{16,20},{20,16},{24,28},{28,24},{1,5},{5... | collective-permute-start | bytes 1572872 | tf_op jit(solution)/shard_map/ppermute | solution.py:333
  30.9 1.1 %copy-start.1 = (bf16[176,2048]{1,0:T(8,128)(2,1)S(1)}, bf16[176,2048]{1,0:T(8,128)(2,1)}, u32[]{:S(2)}) copy-start(bf16[176,2048]{1,0:T(8,128)(2,1)} %copy-done) | copy-start | bytes 2162692
  32.0 5.6 %copy-start.5 = (f32[512,512]{1,0:T(8,128)S(1)}, f32[512,512]{1,0:T(8,128)}, u32[]{:S(2)}) copy-start(f32[512,512]{1,0:T(8,128)} %get-tuple-element.133) | copy-start | bytes 3145732
  32.0 10.0 %copy-start.9 = (bf16[8,2048,128]{2,1,0:T(8,128)(2,1)S(1)}, bf16[8,2048,128]{2,1,0:T(8,128)(2,1)}, u32[]{:S(2)}) copy-start(bf16[8,2048,128]{2,1,0:T(8,128)(2,1)} %refs_1_.3) | copy-start | bytes 12582916
  38.9 29.6 %collective-permute-start.17 = (bf16[512,512]{1,0:T(8,128)(2,1)S(1)}, bf16[512,512]{1,0:T(8,128)(2,1)S(1)}, u32[]{:S(2)}, u32[]{:S(2)}) collective-permute-start(bf16[512,512]{1,0:T(8,128)(2,1)S(1)} %add_convert_fusion), channel_id=1, source_target_pairs={{0,2},{1,3},{2,0},{3,1},{4,6},{5,7},{6,4},{7,5},{8,10},{9,11},{10,... | collective-permute-start | bytes 1572872 | tf_op jit(solution)/shard_map/ppermute | solution.py:333
  41.5 27.2 %collective-permute-start.13 = (bf16[176,2048]{1,0:T(8,128)(2,1)S(1)}, bf16[176,2048]{1,0:T(8,128)(2,1)S(1)}, u32[]{:S(2)}, u32[]{:S(2)}) collective-permute-start(bf16[176,2048]{1,0:T(8,128)(2,1)S(1)} %get-tuple-element.128), channel_id=1, source_target_pairs={{0,24},{4,28},{8,16},{12,20},{16,8},{20,12},{24,0},{28,4},{1,25},{... | collective-permute-start | bytes 2162696 | tf_op jit(solution)/shard_map/ppermute | solution.py:333
  42.0 26.5 %copy-start.4 = (f32[512,512]{1,0:T(8,128)S(1)}, f32[512,512]{1,0:T(8,128)}, u32[]{:S(2)}) copy-start(f32[512,512]{1,0:T(8,128)} %get-tuple-element.130) | copy-start | bytes 3145732
  47.6 8.7 %collective-permute-start.14 = (bf16[528,128]{1,0:T(8,128)(2,1)S(1)}, bf16[528,128]{1,0:T(8,128)(2,1)S(1)}, u32[]{:S(2)}, u32[]{:S(2)}) collective-permute-start(bf16[528,128]{1,0:T(8,128)(2,1)S(1)} %convert_element_type.27), channel_id=1, source_target_pairs={{0,1},{1,0},{2,3},{3,2},{4,5},{5,4},{6,7},{7,6},{8,9},{9,8},{10,11... | collective-permute-start | bytes 405512 | tf_op jit(solution)/shard_map/ppermute | solution.py:333
  56.4 21.3 %collective-permute-start.19 = (bf16[528,128]{1,0:T(8,128)(2,1)S(1)}, bf16[528,128]{1,0:T(8,128)(2,1)S(1)}, u32[]{:S(2)}, u32[]{:S(2)}) collective-permute-start(bf16[528,128]{1,0:T(8,128)(2,1)S(1)} %get-tuple-element.147), channel_id=1, source_target_pairs={{0,2},{1,3},{2,0},{3,1},{4,6},{5,7},{6,4},{7,5},{8,10},{9,11},{10,... | collective-permute-start | bytes 405512 | tf_op jit(solution)/shard_map/ppermute | solution.py:333
  68.8 9.0 %copy-start.3 = (bf16[8,2,64,256]{3,2,1,0:T(8,128)(2,1)S(1)}, bf16[8,2,64,256]{3,2,1,0:T(8,128)(2,1)}, u32[]{:S(2)}) copy-start(bf16[8,2,64,256]{3,2,1,0:T(8,128)(2,1)} %refs_5_.1) | copy-start | bytes 1572868
  73.2 15.2 %copy-start.2 = (bf16[512,2048]{1,0:T(8,128)(2,1)S(1)}, bf16[512,2048]{1,0:T(8,128)(2,1)}, u32[]{:S(2)}) copy-start(bf16[512,2048]{1,0:T(8,128)(2,1)} %tokens_ref.3) | copy-start | bytes 6291460
  73.2 15.2 %copy-start.7 = (s32[512,1]{0,1:T(1,128)S(1)}, s32[512,1]{0,1:T(1,128)}, u32[]{:S(2)}) copy-start(s32[512,1]{0,1:T(1,128)} %param.9) | copy-start | bytes 6148
  73.2 15.2 %copy-start.8 = (s32[64]{0:T(128)S(1)}, s32[64]{0:T(128)}, u32[]{:S(2)}) copy-start(s32[64]{0:T(128)} %param.10) | copy-start | bytes 772
  73.3 6.3 %collective-permute-start.24 = (bf16[176,128]{1,0:T(8,128)(2,1)S(1)}, bf16[176,128]{1,0:T(8,128)(2,1)S(1)}, u32[]{:S(2)}, u32[]{:S(2)}) collective-permute-start(bf16[176,128]{1,0:T(8,128)(2,1)S(1)} %get-tuple-element.144.refs_0_), channel_id=1, source_target_pairs={{0,3},{1,2},{2,1},{3,0},{4,7},{5,6},{6,5},{7,4},{8,11},{9,10},{10,... | collective-permute-start | bytes 135176 | tf_op jit(solution)/shard_map/ppermute | solution.py:333
  76.0 4.9 %collective-permute-start.23 = (bf16[176,128]{1,0:T(8,128)(2,1)S(1)}, bf16[176,128]{1,0:T(8,128)(2,1)S(1)}, u32[]{:S(2)}, u32[]{:S(2)}) collective-permute-start(bf16[176,128]{1,0:T(8,128)(2,1)S(1)} %get-tuple-element.144.refs_0_), channel_id=1, source_target_pairs={{0,2},{1,3},{2,0},{3,1},{4,6},{5,7},{6,4},{7,5},{8,10},{9,11},{10,... | collective-permute-start | bytes 135176 | tf_op jit(solution)/shard_map/ppermute | solution.py:333
  76.0 4.9 %collective-permute-start.22 = (bf16[176,128]{1,0:T(8,128)(2,1)S(1)}, bf16[176,128]{1,0:T(8,128)(2,1)S(1)}, u32[]{:S(2)}, u32[]{:S(2)}) collective-permute-start(bf16[176,128]{1,0:T(8,128)(2,1)S(1)} %get-tuple-element.144.refs_0_), channel_id=1, source_target_pairs={{0,1},{1,0},{2,3},{3,2},{4,5},{5,4},{6,7},{7,6},{8,9},{9,8},{10,11... | collective-permute-start | bytes 135176 | tf_op jit(solution)/shard_map/ppermute | solution.py:333
  78.5 6.7 %collective-permute-start.20 = (bf16[176,512]{1,0:T(8,128)(2,1)S(1)}, bf16[176,512]{1,0:T(8,128)(2,1)S(1)}, u32[]{:S(2)}, u32[]{:S(2)}) collective-permute-start(bf16[176,512]{1,0:T(8,128)(2,1)S(1)} %get-tuple-element.141), channel_id=1, source_target_pairs={{0,8},{4,12},{8,0},{12,4},{16,24},{20,28},{24,16},{28,20},{1,9},{5... | collective-permute-start | bytes 540680 | tf_op jit(solution)/shard_map/ppermute | solution.py:333
  79.1 9.4 %collective-permute-start.21 = (bf16[176,512]{1,0:T(8,128)(2,1)S(1)}, bf16[176,512]{1,0:T(8,128)(2,1)S(1)}, u32[]{:S(2)}, u32[]{:S(2)}) collective-permute-start(bf16[176,512]{1,0:T(8,128)(2,1)S(1)} %get-tuple-element.142), channel_id=1, source_target_pairs={{0,16},{4,20},{8,24},{12,28},{16,0},{20,4},{24,8},{28,12},{1,17},{... | collective-permute-start | bytes 540680 | tf_op jit(solution)/shard_map/ppermute | solution.py:333
  81.4 7.1 %collective-permute-start.25 = (bf16[176,512]{1,0:T(8,128)(2,1)S(1)}, bf16[176,512]{1,0:T(8,128)(2,1)S(1)}, u32[]{:S(2)}, u32[]{:S(2)}) collective-permute-start(bf16[176,512]{1,0:T(8,128)(2,1)S(1)} %grow_rows.5), channel_id=1, source_target_pairs={{0,24},{4,28},{8,16},{12,20},{16,8},{20,12},{24,0},{28,4},{1,25},{... | collective-permute-start | bytes 540680 | tf_op jit(solution)/shard_map/ppermute | solution.py:333
  82.5 1.2 %collective-permute-start.18 = (f32[8,128]{1,0:T(8,128)S(1)}, f32[8,128]{1,0:T(8,128)S(1)}, u32[]{:S(2)}, u32[]{:S(2)}) collective-permute-start(f32[8,128]{1,0:T(8,128)S(1)} %max.6), channel_id=1, source_target_pairs={{0,4},{4,0},{8,12},{12,8},{16,20},{20,16},{24,28},{28,24},{1,5},{5... | collective-permute-start | bytes 12296 | tf_op jit(solution)/shard_map/ppermute | solution.py:333
  90.2 0.8 copy-start.6

commit v7 on v6

--- a/solution.py
+++ b/solution.py
@@ -97,11 +97,9 @@
     )(chip, adapters, slots, tokens)
 
 
-def shrink_kernel(count, carried, flag_lane, core_ref, *refs):
+def shrink_kernel(count, flag_lane, core_ref, *refs):
     messages, (mine, sibling) = refs[:count], refs[count:count + 2]
-    carry, refs = refs[count + 2:count + 2 + carried], refs[count + 2 + carried:]
-    out, place_out, flag_out, total, places = refs
-    kept = carry[0].shape[0] if carried else 0
+    out, place_out, flag_out, total, places = refs[count + 2:]
     step = pl.program_id(0)
     local = 2 * pl.num_programs(0)
     sizes = [m.shape[0] for m in messages]
@@ -120,11 +118,7 @@
             last = lax.broadcasted_iota(jnp.int32, (1, 128), 1) == 127
             flag = jnp.maximum(flag, jnp.max(jnp.where(last, block, 0.0), axis=1, keepdims=True))
             start += size
-        place_out[kept:, :] = places[...].astype(BF)
-        if carried:
-            out[:kept, :] = carry[0][...]
-            place_out[:kept, :] = carry[1][...]
-            flag = jnp.maximum(flag, carry[2][0:1, 0:1])
+        place_out[...] = places[...].astype(BF)
         flag_out[...] = jnp.broadcast_to(flag, (8, 128))
         total[...] = jnp.zeros_like(total)
 
@@ -140,25 +134,23 @@
 
     @pl.when(step == pl.num_programs(0) - 1)
     def _():
-        out[kept:, :] = total[...].astype(out.dtype)
-
-
-def shrink(core, messages, mine, sibling, flag_lane, carry=(), dtype=BF):
+        out[...] = total[...].astype(out.dtype)
+
+
+def shrink(core, messages, mine, sibling, flag_lane, dtype=BF):
     local, width, both = mine.shape
     rows = sum(m.shape[0] for m in messages)
     whole = [pl.BlockSpec(m.shape, lambda i: (0, 0)) for m in messages]
     pair = pl.BlockSpec((2, width, both), lambda i: (i, 0, 0))
-    every = rows + (carry[0].shape[0] if carry else 0)
-    keep = pl.BlockSpec((every, both), lambda i: (0, 0))
-    whole_carry = [pl.BlockSpec(c.shape, lambda i: (0, 0)) for c in carry]
-    return pl.pallas_call(
-        functools.partial(shrink_kernel, len(messages), len(carry), flag_lane),
+    keep = pl.BlockSpec((rows, both), lambda i: (0, 0))
+    return pl.pallas_call(
+        functools.partial(shrink_kernel, len(messages), flag_lane),
         grid=(local // 2,),
-        in_specs=[pl.BlockSpec(memory_space=pltpu.SMEM)] + whole + [pair, pair] + whole_carry,
+        in_specs=[pl.BlockSpec(memory_space=pltpu.SMEM)] + whole + [pair, pair],
         out_specs=[keep, keep, pl.BlockSpec((8, 128), lambda i: (0, 0))],
         out_shape=[
-            jax.ShapeDtypeStruct((every, both), dtype),
-            jax.ShapeDtypeStruct((every, both), BF),
+            jax.ShapeDtypeStruct((rows, both), dtype),
+            jax.ShapeDtypeStruct((rows, both), BF),
             jax.ShapeDtypeStruct((8, 128), F32),
         ],
         scratch_shapes=[pltpu.VMEM((rows, both), F32), pltpu.VMEM((rows, both), F32)],
@@ -167,7 +159,7 @@
         ),
         compiler_params=pltpu.CompilerParams(vmem_limit_bytes=VMEM_LIMIT),
         name="shrink_rows",
-    )(core, *messages, mine, sibling, *carry)
+    )(core, *messages, mine, sibling)
 
 
 def grow_kernel(shares, sizes, core_ref, *refs):
@@ -373,46 +365,51 @@
     rest = round_up(full - message + 2, 16)
     sizes, first_rows = (message,) * chips, (0,) * chips
 
-    packed = pack(chip, adapters, slots, tokens, sizes, first_rows, chip_slots)
+    t = lax.axis_index("tensor").astype(jnp.int32)
+    first_shift = blocks - 1
+    parts, came = {}, {}
+
+    def compute(shifts, ready):
+        parts.update(zip(shifts, base_parts(t, ready, key_value_base_weight, blocks, shifts)))
+
+    def arrived_for(r):
+        return [came[key] for key in sorted(came) if key[1] == r]
+
+    def send(r):
+        part = parts[r]
+        for one in arrived_for(r):
+            part = part + one.astype(F32)
+        part = part.astype(BF)
+        came[(r & -r, r ^ (r & -r))] = exchange(part, "tensor", r & -r)
+        return part
+
+    compute([first_shift], tokens)
+    send(first_shift)
+    packed = pack(chip, adapters, slots, after(tokens, parts[first_shift]), sizes, first_rows, chip_slots)
     sent, key = list(packed[:-1]), packed[-1]
     arrived, returned = {0: sent[0]}, {}
     for m in near[1:]:
         arrived[m] = exchange(sent[m], "dp", 2 * m)
-
-    t = lax.axis_index("tensor").astype(jnp.int32)
-    late_tokens = after(tokens, *sent)
-    first_shift = blocks - 1
-    parts = {first_shift: base_parts(t, late_tokens, key_value_base_weight, blocks, [first_shift])[0]}
-    came = {(1, first_shift ^ 1): exchange(parts[first_shift], "tensor", 1)}
-    others = list(range(first_shift - 1, -1, -1))
-    late_tokens = after(tokens, parts[first_shift])
-    parts.update(zip(others, base_parts(t, late_tokens, key_value_base_weight, blocks, others)))
-
-    def arrived_for(r):
-        return [came[key] for key in sorted(came) if key[1] == r]
+    middle = [r for r in range(first_shift - 1, 1, -1)]
+    compute(middle, after(tokens, *sent))
+    for r in sorted(middle, key=lambda r: (r & -r, -r)):
+        last_sent = send(r)
+    compute([1, 0], after(tokens, last_sent))
+    send(1)
 
     up_sibling = exchange(after(adapter_up_weight, down_sibling), "dp", 1)
-    carry = shrink(core, [after(sent[0], parts[0])], adapter_down_weight, down_sibling, flag_lane, dtype=F32)
     near_done = [arrived[m] for m in near[1:]]
     for m in far:
-        arrived[m] = exchange(after(sent[m], *near_done, carry[0]), "dp", 2 * m)
-    for r in sorted(range(1, first_shift), key=lambda r: (r & -r, -r)):
-        low = r & -r
-        part = parts[r]
-        for one in arrived_for(r):
-            part = part + after(one, *near_done, carry[0]).astype(F32)
-        if r == 1:
-            part = after(part, came[(1, first_shift ^ 1)])
-        came[(low, r ^ low)] = exchange(part.astype(BF), "tensor", low)
+        arrived[m] = exchange(after(sent[m], *near_done, parts[0]), "dp", 2 * m)
 
     both_down = after(down_sibling, up_sibling)
     flags, updates = [], {}
     for part in (near, far):
         if not part:
             continue
-        group = [arrived[m] for m in part if m]
+        group = [arrived[m] for m in part]
         if part is near:
-            share, place, flag = shrink(core, group, adapter_down_weight, both_down, flag_lane, carry, F32)
+            share, place, flag = shrink(core, group, adapter_down_weight, both_down, flag_lane, F32)
             step = 1
             while 2 * step < blocks:
                 share = share + exchange(share.astype(BF), "tensor", step).astype(F32)
@@ -422,7 +419,7 @@
             for one in arrived_for(0):
                 base = base + one.astype(F32)
         else:
-            group[0] = after(group[0], base)
+            group[0] = after(group[0], base, shares[-1])
             share, place, flag = shrink(core, group, adapter_down_weight, both_down, flag_lane)
             shares = [after(share, returned[0])] + [exchange(share, "tensor", z) for z in range(1, blocks)]
         flags.append(flag)

time: 91.4 us -> 91.8 us (level)
  waiting for transfers between devices: 26 us -> 28.9 us
  local copies, waits for them, and re-layouts: 3.36 us -> 1.33 us
  Pallas kernels: 37.5 us -> 36 us
  other arithmetic: 2.11 us -> 3.25 us
    pallas_call x3 -> x2, Pallas kernels: 15.6 us -> 11.7 us  [shrink(): pl.pallas_call(functools.partial(shrink_kernel, len(messages), flag_lane)...]
    ppermute x17, waiting for transfers between devices: 26 us -> 28.9 us  [exchange(): return lax.ppermute(array, axis, [(i, i ^ shift) for i in range(size)])]
    pallas_call x2 -> x3, Pallas kernels: 13.7 us -> 15.9 us  [base_parts(): pl.pallas_call(functools.partial(base_kernel, shifts), grid_spec=pltpu.Pr...]
    unnamed x20 -> x14, local copies, waits for them, and re-layouts: 2.85 us -> 0.81 us
    convert_element_type x1, other arithmetic: 1.21 us -> 2.31 us  [send(): part = part.astype(BF)]
  transfers between devices with their start and end apart: 17 -> 17, of which waited for: 7 -> 5; matrix products, arithmetic and copies ran while one was open for 3% -> 4% of each run, Pallas kernels for 40% -> 33%
where the time goes in v7:
time: 91.8 us; the launch traced here: 91.5 us
  Pallas kernels  36 us (39%)
  waiting for transfers between devices  28.9 us (31%)
  starting transfers between devices  21 us (23%)
  other arithmetic  3.25 us (4%)
  local copies, waits for them, and re-layouts  1.33 us (1%)
    ppermute x17, waiting for transfers between devices, exchange(): return lax.ppermute(array, axis, [(i, i ^ shift) for i in range(size)])  28.9 us
    ppermute x17, starting transfers between devices, exchange(): return lax.ppermute(array, axis, [(i, i ^ shift) for i in range(size)])  21 us
    pallas_call x3, Pallas kernels, base_parts(): pl.pallas_call(functools.partial(base_kernel, shifts), grid_spec=pltpu.Pr...  15.9 us
    pallas_call x2, Pallas kernels, shrink(): pl.pallas_call(functools.partial(shrink_kernel, len(messages), flag_lane)...  11.7 us
    pallas_call x1, Pallas kernels, pack(): pl.pallas_call(functools.partial(pack_kernel, (sizes, first_rows, chip_sl...  5.44 us
    convert_element_type x1, other arithmetic, send(): part = part.astype(BF)  2.31 us
  transfers between devices with their start and end apart: 17, of which 5 were waited for; matrix products, arithmetic and copies ran while one was open for 4% of the time, Pallas kernels for 33%

profile of v7, /device:TPU:0, one launch (start us, length us, event | category | flops | bytes accessed | tf_op | source)
XLA Modules:
  0.0 91.5 jit_solution(15724865518313268535)
XLA Ops:
  0.0 0.5 collective-permute-start.11
  0.5 4.5 %base_parts.3 = bf16[512,512]{1,0:T(8,128)(2,1)} custom-call(s32[1]{0:T(128)} %bitcast.4.place_ref, bf16[512,2048]{1,0:T(8,128)(2,1)} %tokens_ref.4, bf16[2048,2,1024]{2,1,0:T(2,128)(2,1)} %weight_ref.5), custom_call_target="tpu_custom_call" | custom-call | flops 4294967296 | bytes 4194304 | tf_op jit(solution)/shard_map/base_parts/pallas_call | solution.py:233
  5.0 2.6 %collective-permute-start.13 = (bf16[512,512]{1,0:T(8,128)(2,1)}, bf16[512,512]{1,0:T(8,128)(2,1)}, u32[]{:S(2)}, u32[]{:S(2)}) collective-permute-start(bf16[512,512]{1,0:T(8,128)(2,1)} %base_parts.3), channel_id=1, source_target_pairs={{0,1},{1,0},{2,3},{3,2},{4,5},{5,4},{6,7},{7,6},{8,9},{9,8},{10,11... | collective-permute-start | bytes 1572872 | tf_op jit(solution)/shard_map/ppermute | solution.py:325
  7.6 5.4 %pack_rows.3 = (bf16[176,2048]{1,0:T(8,128)(2,1)S(1)}, bf16[176,2048]{1,0:T(8,128)(2,1)}, bf16[176,2048]{1,0:T(8,128)(2,1)}, bf16[176,2048]{1,0:T(8,128)(2,1)S(1)}, s32[512,128]{1,0:T(8,128)S(1)}) custom-call(s32[1]{0:T(128)} %bitcast.1.place_ref, s32[1,512]{1,0:T(1,128)S(1)} %bitcast.9, s32[1,64]{1,0:T(1,128)S(1)} %bitcast.11, bf16[512,2048]{1,0:T(8,128)(2,1)} %tokens_ref.4), custom_call_target="tpu_custom_call" | custom-call | flops 1000 | bytes 1000 | tf_op jit(solution)/shard_map/pack_rows/pallas_call | solution.py:81
  13.0 1.5 %collective-permute-start.9 = (bf16[176,2048]{1,0:T(8,128)(2,1)}, bf16[176,2048]{1,0:T(8,128)(2,1)S(1)}, u32[]{:S(2)}, u32[]{:S(2)}) collective-permute-start(bf16[176,2048]{1,0:T(8,128)(2,1)} %get-tuple-element.110), channel_id=1, source_target_pairs={{0,8},{4,12},{8,0},{12,4},{16,24},{20,28},{24,16},{28,20},{1,9},{5... | collective-permute-start | bytes 2162696 | tf_op jit(solution)/shard_map/ppermute | solution.py:325
  14.5 1.5 %collective-permute-start.10 = (bf16[176,2048]{1,0:T(8,128)(2,1)}, bf16[176,2048]{1,0:T(8,128)(2,1)S(1)}, u32[]{:S(2)}, u32[]{:S(2)}) collective-permute-start(bf16[176,2048]{1,0:T(8,128)(2,1)} %get-tuple-element.111), channel_id=1, source_target_pairs={{0,16},{4,20},{8,24},{12,28},{16,0},{20,4},{24,8},{28,12},{1,17},{... | collective-permute-start | bytes 2162696 | tf_op jit(solution)/shard_map/ppermute | solution.py:325
  16.0 0.6 pad_add_fusion.place_ref
  16.7 4.9 %base_parts.4 = f32[512,512]{1,0:T(8,128)} custom-call(s32[1]{0:T(128)} %bitcast.7.place_ref, bf16[512,2048]{1,0:T(8,128)(2,1)} %tokens_ref.4, bf16[2048,2,1024]{2,1,0:T(2,128)(2,1)} %weight_ref.5), custom_call_target="tpu_custom_call" | custom-call | flops 4294967296 | bytes 4194304 | tf_op jit(solution)/shard_map/base_parts/pallas_call | solution.py:233
  21.5 2.3 %add_convert_fusion = bf16[512,512]{1,0:T(8,128)(2,1)} fusion(f32[512,512]{1,0:T(8,128)} %base_parts.4, bf16[512,512]{1,0:T(8,128)(2,1)} %collective-permute-done.13), kind=kLoop, calls=%fused_computation.1 | loop fusion | flops 786432 | bytes 2097152 | tf_op jit(solution)/shard_map/convert_element_type | solution.py:382
  23.8 2.6 %collective-permute-start.17 = (bf16[512,512]{1,0:T(8,128)(2,1)}, bf16[512,512]{1,0:T(8,128)(2,1)S(1)}, u32[]{:S(2)}, u32[]{:S(2)}) collective-permute-start(bf16[512,512]{1,0:T(8,128)(2,1)} %add_convert_fusion), channel_id=1, source_target_pairs={{0,2},{1,3},{2,0},{3,1},{4,6},{5,7},{6,4},{7,5},{8,10},{9,11},{10,... | collective-permute-start | bytes 1572872 | tf_op jit(solution)/shard_map/ppermute | solution.py:325
  26.4 6.6 %base_parts.5 = (bf16[512,512]{1,0:T(8,128)(2,1)}, f32[512,512]{1,0:T(8,128)}) custom-call(s32[2]{0:T(128)} %pad_add_fusion.place_ref, bf16[512,2048]{1,0:T(8,128)(2,1)S(1)} %copy-done, bf16[2048,2,1024]{2,1,0:T(2,128)(2,1)} %weight_ref.5), custom_call_target="tpu_custom_call" | custom-call | flops 8589934592 | bytes 4194304 | tf_op jit(solution)/shard_map/base_parts/pallas_call | solution.py:233
  33.0 0.7 collective-permute-start.16
  33.7 2.4 %collective-permute-start.14 = (bf16[176,2048]{1,0:T(8,128)(2,1)S(1)}, bf16[176,2048]{1,0:T(8,128)(2,1)S(1)}, u32[]{:S(2)}, u32[]{:S(2)}) collective-permute-start(bf16[176,2048]{1,0:T(8,128)(2,1)S(1)} %get-tuple-element.119), channel_id=1, source_target_pairs={{0,24},{4,28},{8,16},{12,20},{16,8},{20,12},{24,0},{28,4},{1,25},{... | collective-permute-start | bytes 2162696 | tf_op jit(solution)/shard_map/ppermute | solution.py:325
  36.1 7.3 %shrink_rows.4 = (f32[528,128]{1,0:T(8,128)S(1)}, bf16[528,128]{1,0:T(8,128)(2,1)S(1)}, f32[8,128]{1,0:T(8,128)S(1)}) custom-call(s32[1]{0:T(128)} %bitcast.core_ref, bf16[176,2048]{1,0:T(8,128)(2,1)S(1)} %get-tuple-element.109.refs_0_, bf16[176,2048]{1,0:T(8,128)(2,1)S(1)} %collective-permute-done.9.refs_1_, ...), custom_call_target="tpu_custom_call" | custom-call | flops 8858370048 | bytes 16777216 | tf_op jit(solution)/shard_map/shrink_rows/pallas_call | solution.py:146
  43.5 0.5 collective-permute-start.15
  44.0 17.4 %collective-permute-done.15 = bf16[528,128]{1,0:T(8,128)(2,1)S(1)} collective-permute-done((bf16[528,128]{1,0:T(8,128)(2,1)S(1)}, bf16[528,128]{1,0:T(8,128)(2,1)S(1)}, u32[]{:S(2)}, u32[]{:S(2)}) %collective-permute-start.15) | collective-permute-done | bytes 135200 | tf_op jit(solution)/shard_map/ppermute | solution.py:325
  61.8 7.7 %collective-permute-done.18.refs_1_ = bf16[528,128]{1,0:T(8,128)(2,1)S(1)} collective-permute-done((bf16[528,128]{1,0:T(8,128)(2,1)S(1)}, bf16[528,128]{1,0:T(8,128)(2,1)S(1)}, u32[]{:S(2)}, u32[]{:S(2)}) %collective-permute-start.18) | collective-permute-done | bytes 135200 | tf_op jit(solution)/shard_map/ppermute | solution.py:325
  69.5 4.4 %shrink_rows.5 = (bf16[176,128]{1,0:T(8,128)(2,1)S(1)}, bf16[176,128]{1,0:T(8,128)(2,1)S(1)}, f32[8,128]{1,0:T(8,128)S(1)}) custom-call(s32[1]{0:T(128)} %bitcast.core_ref, bf16[176,2048]{1,0:T(8,128)(2,1)S(1)} %collective-permute-done.14.refs_0_, bf16[8,2048,128]{2,1,0:T(8,128)(2,1)S(1)} %copy-done.6, ...), custom_call_target="tpu_custom_call" | custom-call | flops 2952790016 | bytes 16777216 | tf_op jit(solution)/shard_map/shrink_rows/pallas_call | solution.py:146
  73.9 1.5 %collective-permute-start.23 = (bf16[176,128]{1,0:T(8,128)(2,1)S(1)}, bf16[176,128]{1,0:T(8,128)(2,1)S(1)}, u32[]{:S(2)}, u32[]{:S(2)}) collective-permute-start(bf16[176,128]{1,0:T(8,128)(2,1)S(1)} %get-tuple-element.132.refs_0_), channel_id=1, source_target_pairs={{0,2},{1,3},{2,0},{3,1},{4,6},{5,7},{6,4},{7,5},{8,10},{9,11},{10,... | collective-permute-start | bytes 135176 | tf_op jit(solution)/shard_map/ppermute | solution.py:325
  75.4 2.9 %collective-permute-start.24 = (bf16[176,128]{1,0:T(8,128)(2,1)S(1)}, bf16[176,128]{1,0:T(8,128)(2,1)S(1)}, u32[]{:S(2)}, u32[]{:S(2)}) collective-permute-start(bf16[176,128]{1,0:T(8,128)(2,1)S(1)} %get-tuple-element.132.refs_0_), channel_id=1, source_target_pairs={{0,3},{1,2},{2,1},{3,0},{4,7},{5,6},{6,5},{7,4},{8,11},{9,10},{10,... | collective-permute-start | bytes 135176 | tf_op jit(solution)/shard_map/ppermute | solution.py:325
  78.3 0.8 grow_rows.4
  79.1 0.6 collective-permute-start.20
  79.7 1.5 %collective-permute-start.21 = (bf16[176,512]{1,0:T(8,128)(2,1)S(1)}, bf16[176,512]{1,0:T(8,128)(2,1)S(1)}, u32[]{:S(2)}, u32[]{:S(2)}) collective-permute-start(bf16[176,512]{1,0:T(8,128)(2,1)S(1)} %get-tuple-element.130), channel_id=1, source_target_pairs={{0,16},{4,20},{8,24},{12,28},{16,0},{20,4},{24,8},{28,12},{1,17},{... | collective-permute-start | bytes 540680 | tf_op jit(solution)/shard_map/ppermute | solution.py:325
  81.4 0.4 grow_rows.5
  81.8 2.1 %collective-permute-start.25 = (bf16[176,512]{1,0:T(8,128)(2,1)S(1)}, bf16[176,512]{1,0:T(8,128)(2,1)S(1)}, u32[]{:S(2)}, u32[]{:S(2)}) collective-permute-start(bf16[176,512]{1,0:T(8,128)(2,1)S(1)} %grow_rows.5), channel_id=1, source_target_pairs={{0,24},{4,28},{8,16},{12,20},{16,8},{20,12},{24,0},{28,4},{1,25},{... | collective-permute-start | bytes 540680 | tf_op jit(solution)/shard_map/ppermute | solution.py:325
  83.9 0.3 spread_rows.3
  84.2 0.8 collective-permute-done.19
  85.1 0.5 slice.3
  86.2 2.8 %collective-permute-done.21 = bf16[176,512]{1,0:T(8,128)(2,1)S(1)} collective-permute-done((bf16[176,512]{1,0:T(8,128)(2,1)S(1)}, bf16[176,512]{1,0:T(8,128)(2,1)S(1)}, u32[]{:S(2)}, u32[]{:S(2)}) %collective-permute-start.21) | collective-permute-done | bytes 180256 | tf_op jit(solution)/shard_map/ppermute | solution.py:325
  89.0 1.7 %conditional.1 = (bf16[512,2,256]{2,1,0:T(2,128)(2,1)S(1)}) conditional(s32[]{:T(128)} %bitcast.8, (f32[512,512]{1,0:T(8,128)S(1)}, bf16[512,1024]{1,0:T(8,128)(2,1)S(1)}, bf16[176,512]{1,0:T(8,128)(2,1)S(1)}, bf16[176,512]{1,0:T(8,128)(2,1)S(1)}, bf16[176,512]{1,0:T(8,128)(2,1)S(1)}, /*index=5*/bf16[176,512]{1,0:T(8,128)(2,1)S(1)}) %tuple.31, ...), branch_computations={%region_0.1_spmd, %region_1.2_spmd} | conditional | flops 6442455040 | bytes 23859472 | solution.py:447
  89.0 1.5 %finish_rows.2 = bf16[512,2,256]{2,1,0:T(2,128)(2,1)S(1)} custom-call(f32[512,512]{1,0:T(8,128)S(1)} %get-tuple-element.50.refs_0_, bf16[512,1024]{1,0:T(8,128)(2,1)S(1)} %get-tuple-element.51.refs_1_, bf16[176,512]{1,0:T(8,128)(2,1)S(1)} %get-tuple-element.52.refs_2_, bf16[176,512]{1,0:T(8,128)(2,1)S(1)} %get-tuple-element.53.refs_3_, ...), custom_call_target="tpu_custom_call" | custom-call | flops 1000 | bytes 1000 | tf_op jit(solution)/shard_map/cond/branch_0_fun/finish_rows/pallas_call | solution.py:310
  90.7 0.8 copy-done.3
  (35 shorter events, 0.7 us)
Async XLA Ops:
  0.0 26.4 %collective-permute-start.11 = (bf16[8,2048,128]{2,1,0:T(8,128)(2,1)}, bf16[8,2048,128]{2,1,0:T(8,128)(2,1)}, u32[]{:S(2)}, u32[]{:S(2)}) collective-permute-start(bf16[8,2048,128]{2,1,0:T(8,128)(2,1)} %refs_1_.1), channel_id=1, source_target_pairs={{0,4},{4,0},{8,12},{12,8},{16,20},{20,16},{24,28},{28,24},{1,5},{5... | collective-permute-start | bytes 12582920 | tf_op jit(solution)/shard_map/ppermute | solution.py:325
  0.5 7.1 %copy-start.4 = (s32[512,1]{0,1:T(1,128)S(1)}, s32[512,1]{0,1:T(1,128)}, u32[]{:S(2)}) copy-start(s32[512,1]{0,1:T(1,128)} %param.9) | copy-start | bytes 6148
  0.5 7.1 %copy-start.5 = (s32[64]{0:T(128)S(1)}, s32[64]{0:T(128)}, u32[]{:S(2)}) copy-start(s32[64]{0:T(128)} %param.10) | copy-start | bytes 772
  5.0 16.5 %collective-permute-start.13 = (bf16[512,512]{1,0:T(8,128)(2,1)}, bf16[512,512]{1,0:T(8,128)(2,1)}, u32[]{:S(2)}, u32[]{:S(2)}) collective-permute-start(bf16[512,512]{1,0:T(8,128)(2,1)} %base_parts.3), channel_id=1, source_target_pairs={{0,1},{1,0},{2,3},{3,2},{4,5},{5,4},{6,7},{7,6},{8,9},{9,8},{10,11... | collective-permute-start | bytes 1572872 | tf_op jit(solution)/shard_map/ppermute | solution.py:325
  13.0 20.7 %collective-permute-start.9 = (bf16[176,2048]{1,0:T(8,128)(2,1)}, bf16[176,2048]{1,0:T(8,128)(2,1)S(1)}, u32[]{:S(2)}, u32[]{:S(2)}) collective-permute-start(bf16[176,2048]{1,0:T(8,128)(2,1)} %get-tuple-element.110), channel_id=1, source_target_pairs={{0,8},{4,12},{8,0},{12,4},{16,24},{20,28},{24,16},{28,20},{1,9},{5... | collective-permute-start | bytes 2162696 | tf_op jit(solution)/shard_map/ppermute | solution.py:325
  14.5 19.2 %collective-permute-start.10 = (bf16[176,2048]{1,0:T(8,128)(2,1)}, bf16[176,2048]{1,0:T(8,128)(2,1)S(1)}, u32[]{:S(2)}, u32[]{:S(2)}) collective-permute-start(bf16[176,2048]{1,0:T(8,128)(2,1)} %get-tuple-element.111), channel_id=1, source_target_pairs={{0,16},{4,20},{8,24},{12,28},{16,0},{20,4},{24,8},{28,12},{1,17},{... | collective-permute-start | bytes 2162696 | tf_op jit(solution)/shard_map/ppermute | solution.py:325
  16.7 9.8 %copy-start.1 = (bf16[8,2,64,256]{3,2,1,0:T(8,128)(2,1)S(1)}, bf16[8,2,64,256]{3,2,1,0:T(8,128)(2,1)}, u32[]{:S(2)}) copy-start(bf16[8,2,64,256]{3,2,1,0:T(8,128)(2,1)} %refs_5_.1) | copy-start | bytes 1572868
  16.7 9.8 %copy-start = (bf16[512,2048]{1,0:T(8,128)(2,1)S(1)}, bf16[512,2048]{1,0:T(8,128)(2,1)}, u32[]{:S(2)}) copy-start(bf16[512,2048]{1,0:T(8,128)(2,1)} %tokens_ref.4) | copy-start | bytes 6291460
  23.8 37.7 %collective-permute-start.17 = (bf16[512,512]{1,0:T(8,128)(2,1)}, bf16[512,512]{1,0:T(8,128)(2,1)S(1)}, u32[]{:S(2)}, u32[]{:S(2)}) collective-permute-start(bf16[512,512]{1,0:T(8,128)(2,1)} %add_convert_fusion), channel_id=1, source_target_pairs={{0,2},{1,3},{2,0},{3,1},{4,6},{5,7},{6,4},{7,5},{8,10},{9,11},{10,... | collective-permute-start | bytes 1572872 | tf_op jit(solution)/shard_map/ppermute | solution.py:325
  26.4 9.7 %collective-permute-start.12 = (bf16[8,2,64,256]{3,2,1,0:T(8,128)(2,1)S(1)}, bf16[8,2,64,256]{3,2,1,0:T(8,128)(2,1)S(1)}, u32[]{:S(2)}, u32[]{:S(2)}) collective-permute-start(bf16[8,2,64,256]{3,2,1,0:T(8,128)(2,1)S(1)} %copy-done.1), channel_id=1, source_target_pairs={{0,4},{4,0},{8,12},{12,8},{16,20},{20,16},{24,28},{28,24},{1,5},{5... | collective-permute-start | bytes 1572872 | tf_op jit(solution)/shard_map/ppermute | solution.py:325
  33.0 28.5 %collective-permute-start.16 = (bf16[512,512]{1,0:T(8,128)(2,1)}, bf16[512,512]{1,0:T(8,128)(2,1)S(1)}, u32[]{:S(2)}, u32[]{:S(2)}) collective-permute-start(bf16[512,512]{1,0:T(8,128)(2,1)} %get-tuple-element.122), channel_id=1, source_target_pairs={{0,1},{1,0},{2,3},{3,2},{4,5},{5,4},{6,7},{7,6},{8,9},{9,8},{10,11... | collective-permute-start | bytes 1572872 | tf_op jit(solution)/shard_map/ppermute | solution.py:325
  33.7 28.1 %collective-permute-start.14 = (bf16[176,2048]{1,0:T(8,128)(2,1)S(1)}, bf16[176,2048]{1,0:T(8,128)(2,1)S(1)}, u32[]{:S(2)}, u32[]{:S(2)}) collective-permute-start(bf16[176,2048]{1,0:T(8,128)(2,1)S(1)} %get-tuple-element.119), channel_id=1, source_target_pairs={{0,24},{4,28},{8,16},{12,20},{16,8},{20,12},{24,0},{28,4},{1,25},{... | collective-permute-start | bytes 2162696 | tf_op jit(solution)/shard_map/ppermute | solution.py:325
  36.1 25.4 %copy-start.2 = (f32[512,512]{1,0:T(8,128)S(1)}, f32[512,512]{1,0:T(8,128)}, u32[]{:S(2)}) copy-start(f32[512,512]{1,0:T(8,128)} %get-tuple-element.121) | copy-start | bytes 3145732
  43.4 26.0 %copy-start.6 = (bf16[8,2048,128]{2,1,0:T(8,128)(2,1)S(1)}, bf16[8,2048,128]{2,1,0:T(8,128)(2,1)}, u32[]{:S(2)}) copy-start(bf16[8,2048,128]{2,1,0:T(8,128)(2,1)} %refs_1_.1) | copy-start | bytes 12582916
  43.5 17.9 %collective-permute-start.15 = (bf16[528,128]{1,0:T(8,128)(2,1)S(1)}, bf16[528,128]{1,0:T(8,128)(2,1)S(1)}, u32[]{:S(2)}, u32[]{:S(2)}) collective-permute-start(bf16[528,128]{1,0:T(8,128)(2,1)S(1)} %convert_element_type.29), channel_id=1, source_target_pairs={{0,1},{1,0},{2,3},{3,2},{4,5},{5,4},{6,7},{7,6},{8,9},{9,8},{10,11... | collective-permute-start | bytes 405512 | tf_op jit(solution)/shard_map/ppermute | solution.py:325
  61.4 8.0 %collective-permute-start.18 = (bf16[528,128]{1,0:T(8,128)(2,1)S(1)}, bf16[528,128]{1,0:T(8,128)(2,1)S(1)}, u32[]{:S(2)}, u32[]{:S(2)}) collective-permute-start(bf16[528,128]{1,0:T(8,128)(2,1)S(1)} %get-tuple-element.135), channel_id=1, source_target_pairs={{0,2},{1,3},{2,0},{3,1},{4,6},{5,7},{6,4},{7,5},{8,10},{9,11},{10,... | collective-permute-start | bytes 405512 | tf_op jit(solution)/shard_map/ppermute | solution.py:325
  73.9 7.3 %collective-permute-start.22 = (bf16[176,128]{1,0:T(8,128)(2,1)S(1)}, bf16[176,128]{1,0:T(8,128)(2,1)S(1)}, u32[]{:S(2)}, u32[]{:S(2)}) collective-permute-start(bf16[176,128]{1,0:T(8,128)(2,1)S(1)} %get-tuple-element.132.refs_0_), channel_id=1, source_target_pairs={{0,1},{1,0},{2,3},{3,2},{4,5},{5,4},{6,7},{7,6},{8,9},{9,8},{10,11... | collective-permute-start | bytes 135176 | tf_op jit(solution)/shard_map/ppermute | solution.py:325
  73.9 7.3 %collective-permute-start.23 = (bf16[176,128]{1,0:T(8,128)(2,1)S(1)}, bf16[176,128]{1,0:T(8,128)(2,1)S(1)}, u32[]{:S(2)}, u32[]{:S(2)}) collective-permute-start(bf16[176,128]{1,0:T(8,128)(2,1)S(1)} %get-tuple-element.132.refs_0_), channel_id=1, source_target_pairs={{0,2},{1,3},{2,0},{3,1},{4,6},{5,7},{6,4},{7,5},{8,10},{9,11},{10,... | collective-permute-start | bytes 135176 | tf_op jit(solution)/shard_map/ppermute | solution.py:325
  75.4 5.9 %collective-permute-start.24 = (bf16[176,128]{1,0:T(8,128)(2,1)S(1)}, bf16[176,128]{1,0:T(8,128)(2,1)S(1)}, u32[]{:S(2)}, u32[]{:S(2)}) collective-permute-start(bf16[176,128]{1,0:T(8,128)(2,1)S(1)} %get-tuple-element.132.refs_0_), channel_id=1, source_target_pairs={{0,3},{1,2},{2,1},{3,0},{4,7},{5,6},{6,5},{7,4},{8,11},{9,10},{10,... | collective-permute-start | bytes 135176 | tf_op jit(solution)/shard_map/ppermute | solution.py:325
  79.1 7.2 %collective-permute-start.20 = (bf16[176,512]{1,0:T(8,128)(2,1)S(1)}, bf16[176,512]{1,0:T(8,128)(2,1)S(1)}, u32[]{:S(2)}, u32[]{:S(2)}) collective-permute-start(bf16[176,512]{1,0:T(8,128)(2,1)S(1)} %get-tuple-element.129), channel_id=1, source_target_pairs={{0,8},{4,12},{8,0},{12,4},{16,24},{20,28},{24,16},{28,20},{1,9},{5... | collective-permute-start | bytes 540680 | tf_op jit(solution)/shard_map/ppermute | solution.py:325
  79.7 9.4 %collective-permute-start.21 = (bf16[176,512]{1,0:T(8,128)(2,1)S(1)}, bf16[176,512]{1,0:T(8,128)(2,1)S(1)}, u32[]{:S(2)}, u32[]{:S(2)}) collective-permute-start(bf16[176,512]{1,0:T(8,128)(2,1)S(1)} %get-tuple-element.130), channel_id=1, source_target_pairs={{0,16},{4,20},{8,24},{12,28},{16,0},{20,4},{24,8},{28,12},{1,17},{... | collective-permute-start | bytes 540680 | tf_op jit(solution)/shard_map/ppermute | solution.py:325
  81.8 7.2 %collective-permute-start.25 = (bf16[176,512]{1,0:T(8,128)(2,1)S(1)}, bf16[176,512]{1,0:T(8,128)(2,1)S(1)}, u32[]{:S(2)}, u32[]{:S(2)}) collective-permute-start(bf16[176,512]{1,0:T(8,128)(2,1)S(1)} %grow_rows.5), channel_id=1, source_target_pairs={{0,24},{4,28},{8,16},{12,20},{16,8},{20,12},{24,0},{28,4},{1,25},{... | collective-permute-start | bytes 540680 | tf_op jit(solution)/shard_map/ppermute | solution.py:325
  83.9 1.2 %collective-permute-start.19 = (f32[8,128]{1,0:T(8,128)S(1)}, f32[8,128]{1,0:T(8,128)S(1)}, u32[]{:S(2)}, u32[]{:S(2)}) collective-permute-start(f32[8,128]{1,0:T(8,128)S(1)} %max.6), channel_id=1, source_target_pairs={{0,4},{4,0},{8,12},{12,8},{16,20},{20,16},{24,28},{28,24},{1,5},{5... | collective-permute-start | bytes 12296 | tf_op jit(solution)/shard_map/ppermute | solution.py:325
  90.7 0.8 copy-start.3

commit v8 on v7

--- a/solution.py
+++ b/solution.py
@@ -229,7 +229,13 @@
     if columns % 128:
         cut = [lax.dynamic_slice_in_dim(weight, (t ^ r) * columns, columns, 2) for r in shifts]
         return [dot(tokens, c.reshape(width, 2 * columns)).astype(k) for c, k in zip(cut, types)]
-    order = jnp.stack([t ^ r for r in shifts])
+
+    def block(i, place):
+        shift = shifts[0]
+        for k, r in enumerate(shifts[1:], 1):
+            shift = jnp.where(i == k, r, shift)
+        return 0, 0, place[0] ^ shift
+
     return pl.pallas_call(
         functools.partial(base_kernel, shifts),
         grid_spec=pltpu.PrefetchScalarGridSpec(
@@ -237,7 +243,7 @@
             grid=(len(shifts),),
             in_specs=[
                 pl.BlockSpec((rows, width), lambda i, p: (0, 0)),
-                pl.BlockSpec((width, 2, columns), lambda i, p: (0, 0, p[i])),
+                pl.BlockSpec((width, 2, columns), block),
             ],
             out_specs=[pl.BlockSpec((rows, 2 * columns), lambda i, p: (0, 0))] * len(shifts),
         ),
@@ -247,7 +253,7 @@
         ),
         compiler_params=pltpu.CompilerParams(vmem_limit_bytes=VMEM_MOST),
         name="base_parts",
-    )(order, tokens, weight)
+    )(t.reshape(1), tokens, weight)
 
 
 def spread_kernel(sizes, first_rows, key_ref, out):
@@ -390,17 +396,15 @@
     arrived, returned = {0: sent[0]}, {}
     for m in near[1:]:
         arrived[m] = exchange(sent[m], "dp", 2 * m)
-    middle = [r for r in range(first_shift - 1, 1, -1)]
+    middle = list(range(1, first_shift))
     compute(middle, after(tokens, *sent))
     for r in sorted(middle, key=lambda r: (r & -r, -r)):
         last_sent = send(r)
-    compute([1, 0], after(tokens, last_sent))
-    send(1)
 
     up_sibling = exchange(after(adapter_up_weight, down_sibling), "dp", 1)
     near_done = [arrived[m] for m in near[1:]]
     for m in far:
-        arrived[m] = exchange(after(sent[m], *near_done, parts[0]), "dp", 2 * m)
+        arrived[m] = exchange(after(sent[m], *near_done, last_sent), "dp", 2 * m)
 
     both_down = after(down_sibling, up_sibling)
     flags, updates = [], {}
@@ -410,6 +414,7 @@
         group = [arrived[m] for m in part]
         if part is near:
             share, place, flag = shrink(core, group, adapter_down_weight, both_down, flag_lane, F32)
+            compute([0], after(tokens, share))
             step = 1
             while 2 * step < blocks:
                 share = share + exchange(share.astype(BF), "tensor", step).astype(F32)

time: 91.8 us -> 85 us (0.926)
  waiting for transfers between devices: 28.9 us -> 16.4 us
  Pallas kernels: 36 us -> 38.5 us
  starting transfers between devices: 21 us -> 23.2 us
    ppermute x17, waiting for transfers between devices: 28.9 us -> 16.4 us  [exchange(): return lax.ppermute(array, axis, [(i, i ^ shift) for i in range(size)])]
    ppermute x17, starting transfers between devices: 21 us -> 23.2 us  [exchange(): return lax.ppermute(array, axis, [(i, i ^ shift) for i in range(size)])]
    pallas_call x2, Pallas kernels: 1.17 us -> 3.26 us  [grow(): pl.pallas_call(functools.partial(grow_kernel, len(parts), sizes), in_spec...]
    add x1, other arithmetic: 0.23 us -> 1.72 us  [per_device(): base = base + one.astype(F32)]
    pallas_call x2, Pallas kernels: 11.7 us -> 12.8 us  [shrink(): pl.pallas_call(functools.partial(shrink_kernel, len(messages), flag_lane)...]
  transfers between devices with their start and end apart: 17 -> 17, of which waited for: 5 -> 6; matrix products, arithmetic and copies ran while one was open for 4% -> 6% of each run, Pallas kernels for 33% -> 37%
where the time goes in v8:
time: 85 us; the launch traced here: 84.5 us
  Pallas kernels  38.5 us (45%)
  starting transfers between devices  23.2 us (27%)
  waiting for transfers between devices  16.4 us (19%)
  other arithmetic  4.14 us (5%)
  local copies, waits for them, and re-layouts  1.33 us (2%)
    ppermute x17, starting transfers between devices, exchange(): return lax.ppermute(array, axis, [(i, i ^ shift) for i in range(size)])  23.2 us
    ppermute x17, waiting for transfers between devices, exchange(): return lax.ppermute(array, axis, [(i, i ^ shift) for i in range(size)])  16.4 us
    pallas_call x3, Pallas kernels, base_parts(): pl.pallas_call(functools.partial(base_kernel, shifts), grid_spec=pltpu.Pr...  15.2 us
    pallas_call x2, Pallas kernels, shrink(): pl.pallas_call(functools.partial(shrink_kernel, len(messages), flag_lane)...  12.8 us
    pallas_call x1, Pallas kernels, pack(): pl.pallas_call(functools.partial(pack_kernel, (sizes, first_rows, chip_sl...  5.44 us
    pallas_call x2, Pallas kernels, grow(): pl.pallas_call(functools.partial(grow_kernel, len(parts), sizes), in_spec...  3.26 us
    convert_element_type x1, other arithmetic, send(): part = part.astype(BF)  2.35 us
    add x1, other arithmetic, per_device(): base = base + one.astype(F32)  1.72 us
  transfers between devices with their start and end apart: 17, of which 6 were waited for; matrix products, arithmetic and copies ran while one was open for 6% of the time, Pallas kernels for 37%

profile of v8, /device:TPU:0, one launch (start us, length us, event | category | flops | bytes accessed | tf_op | source)
XLA Modules:
  0.0 84.5 jit_solution(15183043707425120976)
XLA Ops:
  0.5 4.6 %base_parts.3 = bf16[512,512]{1,0:T(8,128)(2,1)} custom-call(s32[1]{0:T(128)} %bitcast.4.place_ref, bf16[512,2048]{1,0:T(8,128)(2,1)} %tokens_ref.4, bf16[2048,2,1024]{2,1,0:T(2,128)(2,1)} %weight_ref.5), custom_call_target="tpu_custom_call" | custom-call | flops 4294967296 | bytes 4194304 | tf_op jit(solution)/shard_map/base_parts/pallas_call | solution.py:239
  5.0 2.6 %collective-permute-start.13 = (bf16[512,512]{1,0:T(8,128)(2,1)}, bf16[512,512]{1,0:T(8,128)(2,1)}, u32[]{:S(2)}, u32[]{:S(2)}) collective-permute-start(bf16[512,512]{1,0:T(8,128)(2,1)} %base_parts.3), channel_id=1, source_target_pairs={{0,1},{1,0},{2,3},{3,2},{4,5},{5,4},{6,7},{7,6},{8,9},{9,8},{10,11... | collective-permute-start | bytes 1572872 | tf_op jit(solution)/shard_map/ppermute | solution.py:331
  7.6 5.4 %pack_rows.3 = (bf16[176,2048]{1,0:T(8,128)(2,1)S(1)}, bf16[176,2048]{1,0:T(8,128)(2,1)}, bf16[176,2048]{1,0:T(8,128)(2,1)}, bf16[176,2048]{1,0:T(8,128)(2,1)S(1)}, s32[512,128]{1,0:T(8,128)S(1)}) custom-call(s32[1]{0:T(128)} %bitcast.1.place_ref, s32[1,512]{1,0:T(1,128)S(1)} %bitcast.6, s32[1,64]{1,0:T(1,128)S(1)} %bitcast.8, bf16[512,2048]{1,0:T(8,128)(2,1)} %tokens_ref.4), custom_call_target="tpu_custom_call" | custom-call | flops 1000 | bytes 1000 | tf_op jit(solution)/shard_map/pack_rows/pallas_call | solution.py:81
  13.0 1.5 %collective-permute-start.9 = (bf16[176,2048]{1,0:T(8,128)(2,1)}, bf16[176,2048]{1,0:T(8,128)(2,1)S(1)}, u32[]{:S(2)}, u32[]{:S(2)}) collective-permute-start(bf16[176,2048]{1,0:T(8,128)(2,1)} %get-tuple-element.110), channel_id=1, source_target_pairs={{0,8},{4,12},{8,0},{12,4},{16,24},{20,28},{24,16},{28,20},{1,9},{5... | collective-permute-start | bytes 2162696 | tf_op jit(solution)/shard_map/ppermute | solution.py:331
  14.5 1.5 %collective-permute-start.10 = (bf16[176,2048]{1,0:T(8,128)(2,1)}, bf16[176,2048]{1,0:T(8,128)(2,1)S(1)}, u32[]{:S(2)}, u32[]{:S(2)}) collective-permute-start(bf16[176,2048]{1,0:T(8,128)(2,1)} %get-tuple-element.111), channel_id=1, source_target_pairs={{0,16},{4,20},{8,24},{12,28},{16,0},{20,4},{24,8},{28,12},{1,17},{... | collective-permute-start | bytes 2162696 | tf_op jit(solution)/shard_map/ppermute | solution.py:331
  16.1 6.5 %base_parts.4 = (bf16[512,512]{1,0:T(8,128)(2,1)}, f32[512,512]{1,0:T(8,128)}) custom-call(s32[1]{0:T(128)} %bitcast.4.place_ref, bf16[512,2048]{1,0:T(8,128)(2,1)} %tokens_ref.4, bf16[2048,2,1024]{2,1,0:T(2,128)(2,1)} %weight_ref.5), custom_call_target="tpu_custom_call" | custom-call | flops 8589934592 | bytes 4194304 | tf_op jit(solution)/shard_map/base_parts/pallas_call | solution.py:239
  23.0 2.3 %add_convert_fusion = bf16[512,512]{1,0:T(8,128)(2,1)} fusion(f32[512,512]{1,0:T(8,128)} %get-tuple-element.117, bf16[512,512]{1,0:T(8,128)(2,1)} %collective-permute-done.13), kind=kLoop, calls=%fused_computation.1 | loop fusion | flops 786432 | bytes 2097152 | tf_op jit(solution)/shard_map/convert_element_type | solution.py:388
  25.4 2.6 %collective-permute-start.17 = (bf16[512,512]{1,0:T(8,128)(2,1)}, bf16[512,512]{1,0:T(8,128)(2,1)}, u32[]{:S(2)}, u32[]{:S(2)}) collective-permute-start(bf16[512,512]{1,0:T(8,128)(2,1)} %add_convert_fusion), channel_id=1, source_target_pairs={{0,2},{1,3},{2,0},{3,1},{4,6},{5,7},{6,4},{7,5},{8,10},{9,11},{10,... | collective-permute-start | bytes 1572872 | tf_op jit(solution)/shard_map/ppermute | solution.py:331
  28.0 3.5 %collective-permute-done.9.refs_1_ = bf16[176,2048]{1,0:T(8,128)(2,1)S(1)} collective-permute-done((bf16[176,2048]{1,0:T(8,128)(2,1)}, bf16[176,2048]{1,0:T(8,128)(2,1)S(1)}, u32[]{:S(2)}, u32[]{:S(2)}) %collective-permute-start.9) | collective-permute-done | bytes 720928 | tf_op jit(solution)/shard_map/ppermute | solution.py:331
  31.5 1.2 %collective-permute-done.10.refs_2_ = bf16[176,2048]{1,0:T(8,128)(2,1)S(1)} collective-permute-done((bf16[176,2048]{1,0:T(8,128)(2,1)}, bf16[176,2048]{1,0:T(8,128)(2,1)S(1)}, u32[]{:S(2)}, u32[]{:S(2)}) %collective-permute-start.10) | collective-permute-done | bytes 720928 | tf_op jit(solution)/shard_map/ppermute | solution.py:331
  32.7 1.5 %collective-permute-start.14 = (bf16[176,2048]{1,0:T(8,128)(2,1)S(1)}, bf16[176,2048]{1,0:T(8,128)(2,1)S(1)}, u32[]{:S(2)}, u32[]{:S(2)}) collective-permute-start(bf16[176,2048]{1,0:T(8,128)(2,1)S(1)} %get-tuple-element.118), channel_id=1, source_target_pairs={{0,24},{4,28},{8,16},{12,20},{16,8},{20,12},{24,0},{28,4},{1,25},{... | collective-permute-start | bytes 2162696 | tf_op jit(solution)/shard_map/ppermute | solution.py:331
  34.2 7.4 %shrink_rows.4 = (f32[528,128]{1,0:T(8,128)S(1)}, bf16[528,128]{1,0:T(8,128)(2,1)S(1)}, f32[8,128]{1,0:T(8,128)S(1)}) custom-call(s32[1]{0:T(128)} %bitcast.core_ref, bf16[176,2048]{1,0:T(8,128)(2,1)S(1)} %get-tuple-element.109.refs_0_, bf16[176,2048]{1,0:T(8,128)(2,1)S(1)} %collective-permute-done.9.refs_1_, ...), custom_call_target="tpu_custom_call" | custom-call | flops 8858370048 | bytes 16777216 | tf_op jit(solution)/shard_map/shrink_rows/pallas_call | solution.py:146
  41.6 0.5 collective-permute-start.15
  42.2 4.1 %base_parts.5 = f32[512,512]{1,0:T(8,128)} custom-call(s32[1]{0:T(128)} %bitcast.4.place_ref, bf16[512,2048]{1,0:T(8,128)(2,1)S(1)} %copy-done, bf16[2048,2,1024]{2,1,0:T(2,128)(2,1)} %weight_ref.5), custom_call_target="tpu_custom_call" | custom-call | flops 4294967296 | bytes 4194304 | tf_op jit(solution)/shard_map/base_parts/pallas_call | solution.py:239
  46.3 3.6 %collective-permute-done.15 = bf16[528,128]{1,0:T(8,128)(2,1)S(1)} collective-permute-done((bf16[528,128]{1,0:T(8,128)(2,1)S(1)}, bf16[528,128]{1,0:T(8,128)(2,1)S(1)}, u32[]{:S(2)}, u32[]{:S(2)}) %collective-permute-start.15) | collective-permute-done | bytes 135200 | tf_op jit(solution)/shard_map/ppermute | solution.py:331
  50.0 4.0 %collective-permute-start.18 = (bf16[528,128]{1,0:T(8,128)(2,1)S(1)}, bf16[528,128]{1,0:T(8,128)(2,1)S(1)}, u32[]{:S(2)}, u32[]{:S(2)}) collective-permute-start(bf16[528,128]{1,0:T(8,128)(2,1)S(1)} %get-tuple-element.135), channel_id=1, source_target_pairs={{0,2},{1,3},{2,0},{3,1},{4,6},{5,7},{6,4},{7,5},{8,10},{9,11},{10,... | collective-permute-start | bytes 405512 | tf_op jit(solution)/shard_map/ppermute | solution.py:331
  54.0 1.7 %convert_add_fusion = f32[512,512]{1,0:T(8,128)S(1)} fusion(bf16[512,512]{1,0:T(8,128)(2,1)} %collective-permute-done.17, f32[512,512]{1,0:T(8,128)} %base_parts.5, bf16[512,512]{1,0:T(8,128)(2,1)} %collective-permute-done.16), kind=kLoop, calls=%fused_computation | loop fusion | flops 1048576 | bytes 3145728 | tf_op jit(solution)/shard_map/add | solution.py:425
  55.8 4.6 %collective-permute-done.18.refs_1_ = bf16[528,128]{1,0:T(8,128)(2,1)S(1)} collective-permute-done((bf16[528,128]{1,0:T(8,128)(2,1)S(1)}, bf16[528,128]{1,0:T(8,128)(2,1)S(1)}, u32[]{:S(2)}, u32[]{:S(2)}) %collective-permute-start.18) | collective-permute-done | bytes 135200 | tf_op jit(solution)/shard_map/ppermute | solution.py:331
  60.4 5.4 %shrink_rows.5 = (bf16[176,128]{1,0:T(8,128)(2,1)S(1)}, bf16[176,128]{1,0:T(8,128)(2,1)S(1)}, f32[8,128]{1,0:T(8,128)S(1)}) custom-call(s32[1]{0:T(128)} %bitcast.core_ref, bf16[176,2048]{1,0:T(8,128)(2,1)S(1)} %collective-permute-done.14.refs_0_, bf16[8,2048,128]{2,1,0:T(8,128)(2,1)} %refs_1_.1, bf16[8,2048,128]{2,1,0:T(8,128)(2,1)} %collective-permute-done.11.refs_4_.refs_2_), custom_call_target="tpu_custom_call" | custom-call | flops 2952790016 | bytes 16777216 | tf_op jit(solution)/shard_map/shrink_rows/pallas_call | solution.py:146
  65.8 1.7 %collective-permute-start.24 = (bf16[176,128]{1,0:T(8,128)(2,1)S(1)}, bf16[176,128]{1,0:T(8,128)(2,1)S(1)}, u32[]{:S(2)}, u32[]{:S(2)}) collective-permute-start(bf16[176,128]{1,0:T(8,128)(2,1)S(1)} %get-tuple-element.132.refs_0_), channel_id=1, source_target_pairs={{0,3},{1,2},{2,1},{3,0},{4,7},{5,6},{6,5},{7,4},{8,11},{9,10},{10,... | collective-permute-start | bytes 135176 | tf_op jit(solution)/shard_map/ppermute | solution.py:331
  67.5 2.8 %collective-permute-start.22 = (bf16[176,128]{1,0:T(8,128)(2,1)S(1)}, bf16[176,128]{1,0:T(8,128)(2,1)S(1)}, u32[]{:S(2)}, u32[]{:S(2)}) collective-permute-start(bf16[176,128]{1,0:T(8,128)(2,1)S(1)} %get-tuple-element.132.refs_0_), channel_id=1, source_target_pairs={{0,1},{1,0},{2,3},{3,2},{4,5},{5,4},{6,7},{7,6},{8,9},{9,8},{10,11... | collective-permute-start | bytes 135176 | tf_op jit(solution)/shard_map/ppermute | solution.py:331
  70.2 1.8 %grow_rows.4 = (bf16[176,512]{1,0:T(8,128)(2,1)S(1)}, bf16[176,512]{1,0:T(8,128)(2,1)S(1)}, bf16[176,512]{1,0:T(8,128)(2,1)S(1)}) custom-call(s32[1]{0:T(128)} %bitcast.core_ref, f32[528,128]{1,0:T(8,128)S(1)} %get-tuple-element.136.refs_0_, bf16[528,128]{1,0:T(8,128)(2,1)S(1)} %collective-permute-done.18.refs_1_, ...), custom_call_target="tpu_custom_call" | custom-call | flops 1000 | bytes 1000 | tf_op jit(solution)/shard_map/grow_rows/pallas_call | solution.py:201
  72.1 0.6 collective-permute-start.20
  72.6 0.5 collective-permute-start.21
  73.2 1.4 %grow_rows.5 = bf16[176,512]{1,0:T(8,128)(2,1)S(1)} custom-call(s32[1]{0:T(128)} %bitcast.core_ref, bf16[176,128]{1,0:T(8,128)(2,1)S(1)} %get-tuple-element.132.refs_0_, bf16[176,128]{1,0:T(8,128)(2,1)S(1)} %collective-permute-done.22.refs_1_, bf16[176,128]{1,0:T(8,128)(2,1)S(1)} %collective-permute-done.23.refs_2_, ...), custom_call_target="tpu_custom_call" | custom-call | flops 1000 | bytes 1000 | tf_op jit(solution)/shard_map/grow_rows/pallas_call | solution.py:201
  74.6 2.5 %collective-permute-start.25 = (bf16[176,512]{1,0:T(8,128)(2,1)S(1)}, bf16[176,512]{1,0:T(8,128)(2,1)S(1)}, u32[]{:S(2)}, u32[]{:S(2)}) collective-permute-start(bf16[176,512]{1,0:T(8,128)(2,1)S(1)} %grow_rows.5), channel_id=1, source_target_pairs={{0,24},{4,28},{8,16},{12,20},{16,8},{20,12},{24,0},{28,4},{1,25},{... | collective-permute-start | bytes 540680 | tf_op jit(solution)/shard_map/ppermute | solution.py:331
  77.5 0.8 collective-permute-done.19
  78.3 0.5 slice.3
  79.5 2.5 %collective-permute-done.21 = bf16[176,512]{1,0:T(8,128)(2,1)S(1)} collective-permute-done((bf16[176,512]{1,0:T(8,128)(2,1)S(1)}, bf16[176,512]{1,0:T(8,128)(2,1)S(1)}, u32[]{:S(2)}, u32[]{:S(2)}) %collective-permute-start.21) | collective-permute-done | bytes 180256 | tf_op jit(solution)/shard_map/ppermute | solution.py:331
  82.0 1.7 %conditional.1 = (bf16[512,2,256]{2,1,0:T(2,128)(2,1)S(1)}) conditional(s32[]{:T(128)} %bitcast.5, (f32[512,512]{1,0:T(8,128)S(1)}, bf16[512,1024]{1,0:T(8,128)(2,1)S(1)}, bf16[176,512]{1,0:T(8,128)(2,1)S(1)}, bf16[176,512]{1,0:T(8,128)(2,1)S(1)}, bf16[176,512]{1,0:T(8,128)(2,1)S(1)}, /*index=5*/bf16[176,512]{1,0:T(8,128)(2,1)S(1)}) %tuple.31, ...), branch_computations={%region_0.1_spmd, %region_1.2_spmd} | conditional | flops 6442455040 | bytes 23859472 | solution.py:452
  82.0 1.5 %finish_rows.2 = bf16[512,2,256]{2,1,0:T(2,128)(2,1)S(1)} custom-call(f32[512,512]{1,0:T(8,128)S(1)} %get-tuple-element.50.refs_0_, bf16[512,1024]{1,0:T(8,128)(2,1)S(1)} %get-tuple-element.51.refs_1_, bf16[176,512]{1,0:T(8,128)(2,1)S(1)} %get-tuple-element.52.refs_2_, bf16[176,512]{1,0:T(8,128)(2,1)S(1)} %get-tuple-element.53.refs_3_, ...), custom_call_target="tpu_custom_call" | custom-call | flops 1000 | bytes 1000 | tf_op jit(solution)/shard_map/cond/branch_0_fun/finish_rows/pallas_call | solution.py:316
  83.7 0.8 copy-done.3
  (34 shorter events, 1.4 us)
Async XLA Ops:
  0.0 16.1 %collective-permute-start.11 = (bf16[8,2048,128]{2,1,0:T(8,128)(2,1)}, bf16[8,2048,128]{2,1,0:T(8,128)(2,1)}, u32[]{:S(2)}, u32[]{:S(2)}) collective-permute-start(bf16[8,2048,128]{2,1,0:T(8,128)(2,1)} %refs_1_.1), channel_id=1, source_target_pairs={{0,4},{4,0},{8,12},{12,8},{16,20},{20,16},{24,28},{28,24},{1,5},{5... | collective-permute-start | bytes 12582920 | tf_op jit(solution)/shard_map/ppermute | solution.py:331
  0.5 7.1 %copy-start.4 = (s32[512,1]{0,1:T(1,128)S(1)}, s32[512,1]{0,1:T(1,128)}, u32[]{:S(2)}) copy-start(s32[512,1]{0,1:T(1,128)} %param.9) | copy-start | bytes 6148
  0.5 7.1 %copy-start.5 = (s32[64]{0:T(128)S(1)}, s32[64]{0:T(128)}, u32[]{:S(2)}) copy-start(s32[64]{0:T(128)} %param.10) | copy-start | bytes 772
  5.0 18.0 %collective-permute-start.13 = (bf16[512,512]{1,0:T(8,128)(2,1)}, bf16[512,512]{1,0:T(8,128)(2,1)}, u32[]{:S(2)}, u32[]{:S(2)}) collective-permute-start(bf16[512,512]{1,0:T(8,128)(2,1)} %base_parts.3), channel_id=1, source_target_pairs={{0,1},{1,0},{2,3},{3,2},{4,5},{5,4},{6,7},{7,6},{8,9},{9,8},{10,11... | collective-permute-start | bytes 1572872 | tf_op jit(solution)/shard_map/ppermute | solution.py:331
  13.0 18.5 %collective-permute-start.9 = (bf16[176,2048]{1,0:T(8,128)(2,1)}, bf16[176,2048]{1,0:T(8,128)(2,1)S(1)}, u32[]{:S(2)}, u32[]{:S(2)}) collective-permute-start(bf16[176,2048]{1,0:T(8,128)(2,1)} %get-tuple-element.110), channel_id=1, source_target_pairs={{0,8},{4,12},{8,0},{12,4},{16,24},{20,28},{24,16},{28,20},{1,9},{5... | collective-permute-start | bytes 2162696 | tf_op jit(solution)/shard_map/ppermute | solution.py:331
  14.5 18.2 %collective-permute-start.10 = (bf16[176,2048]{1,0:T(8,128)(2,1)}, bf16[176,2048]{1,0:T(8,128)(2,1)S(1)}, u32[]{:S(2)}, u32[]{:S(2)}) collective-permute-start(bf16[176,2048]{1,0:T(8,128)(2,1)} %get-tuple-element.111), channel_id=1, source_target_pairs={{0,16},{4,20},{8,24},{12,28},{16,0},{20,4},{24,8},{28,12},{1,17},{... | collective-permute-start | bytes 2162696 | tf_op jit(solution)/shard_map/ppermute | solution.py:331
  16.1 18.2 %collective-permute-start.12 = (bf16[8,2,64,256]{3,2,1,0:T(8,128)(2,1)}, bf16[8,2,64,256]{3,2,1,0:T(8,128)(2,1)}, u32[]{:S(2)}, u32[]{:S(2)}) collective-permute-start(bf16[8,2,64,256]{3,2,1,0:T(8,128)(2,1)} %refs_5_.1), channel_id=1, source_target_pairs={{0,4},{4,0},{8,12},{12,8},{16,20},{20,16},{24,28},{28,24},{1,5},{5... | collective-permute-start | bytes 1572872 | tf_op jit(solution)/shard_map/ppermute | solution.py:331
  22.6 31.4 %collective-permute-start.16 = (bf16[512,512]{1,0:T(8,128)(2,1)}, bf16[512,512]{1,0:T(8,128)(2,1)}, u32[]{:S(2)}, u32[]{:S(2)}) collective-permute-start(bf16[512,512]{1,0:T(8,128)(2,1)} %get-tuple-element.122), channel_id=1, source_target_pairs={{0,1},{1,0},{2,3},{3,2},{4,5},{5,4},{6,7},{7,6},{8,9},{9,8},{10,11... | collective-permute-start | bytes 1572872 | tf_op jit(solution)/shard_map/ppermute | solution.py:331
  25.4 28.6 %collective-permute-start.17 = (bf16[512,512]{1,0:T(8,128)(2,1)}, bf16[512,512]{1,0:T(8,128)(2,1)}, u32[]{:S(2)}, u32[]{:S(2)}) collective-permute-start(bf16[512,512]{1,0:T(8,128)(2,1)} %add_convert_fusion), channel_id=1, source_target_pairs={{0,2},{1,3},{2,0},{3,1},{4,6},{5,7},{6,4},{7,5},{8,10},{9,11},{10,... | collective-permute-start | bytes 1572872 | tf_op jit(solution)/shard_map/ppermute | solution.py:331
  32.7 23.0 %collective-permute-start.14 = (bf16[176,2048]{1,0:T(8,128)(2,1)S(1)}, bf16[176,2048]{1,0:T(8,128)(2,1)S(1)}, u32[]{:S(2)}, u32[]{:S(2)}) collective-permute-start(bf16[176,2048]{1,0:T(8,128)(2,1)S(1)} %get-tuple-element.118), channel_id=1, source_target_pairs={{0,24},{4,28},{8,16},{12,20},{16,8},{20,12},{24,0},{28,4},{1,25},{... | collective-permute-start | bytes 2162696 | tf_op jit(solution)/shard_map/ppermute | solution.py:331
  34.2 7.9 %copy-start = (bf16[512,2048]{1,0:T(8,128)(2,1)S(1)}, bf16[512,2048]{1,0:T(8,128)(2,1)}, u32[]{:S(2)}) copy-start(bf16[512,2048]{1,0:T(8,128)(2,1)} %tokens_ref.4) | copy-start | bytes 6291460
  41.6 8.3 %collective-permute-start.15 = (bf16[528,128]{1,0:T(8,128)(2,1)S(1)}, bf16[528,128]{1,0:T(8,128)(2,1)S(1)}, u32[]{:S(2)}, u32[]{:S(2)}) collective-permute-start(bf16[528,128]{1,0:T(8,128)(2,1)S(1)} %convert_element_type.29), channel_id=1, source_target_pairs={{0,1},{1,0},{2,3},{3,2},{4,5},{5,4},{6,7},{7,6},{8,9},{9,8},{10,11... | collective-permute-start | bytes 405512 | tf_op jit(solution)/shard_map/ppermute | solution.py:331
  50.0 10.4 %collective-permute-start.18 = (bf16[528,128]{1,0:T(8,128)(2,1)S(1)}, bf16[528,128]{1,0:T(8,128)(2,1)S(1)}, u32[]{:S(2)}, u32[]{:S(2)}) collective-permute-start(bf16[528,128]{1,0:T(8,128)(2,1)S(1)} %get-tuple-element.135), channel_id=1, source_target_pairs={{0,2},{1,3},{2,0},{3,1},{4,6},{5,7},{6,4},{7,5},{8,10},{9,11},{10,... | collective-permute-start | bytes 405512 | tf_op jit(solution)/shard_map/ppermute | solution.py:331
  55.7 14.5 %copy-start.2 = (bf16[8,2,64,256]{3,2,1,0:T(8,128)(2,1)S(1)}, bf16[8,2,64,256]{3,2,1,0:T(8,128)(2,1)}, u32[]{:S(2)}) copy-start(bf16[8,2,64,256]{3,2,1,0:T(8,128)(2,1)} %refs_5_.1) | copy-start | bytes 1572868
  60.4 21.6 %copy-start.6 = (bf16[8,2048,128]{2,1,0:T(8,128)(2,1)S(1)}, bf16[8,2048,128]{2,1,0:T(8,128)(2,1)}, u32[]{:S(2)}) copy-start(bf16[8,2048,128]{2,1,0:T(8,128)(2,1)} %refs_1_.1) | copy-start | bytes 12582916
  65.8 16.2 %copy-start.1 = (bf16[512,2048]{1,0:T(8,128)(2,1)S(1)}, bf16[512,2048]{1,0:T(8,128)(2,1)}, u32[]{:S(2)}) copy-start(bf16[512,2048]{1,0:T(8,128)(2,1)} %tokens_ref.4) | copy-start | bytes 6291460
  65.8 7.4 %collective-permute-start.24 = (bf16[176,128]{1,0:T(8,128)(2,1)S(1)}, bf16[176,128]{1,0:T(8,128)(2,1)S(1)}, u32[]{:S(2)}, u32[]{:S(2)}) collective-permute-start(bf16[176,128]{1,0:T(8,128)(2,1)S(1)} %get-tuple-element.132.refs_0_), channel_id=1, source_target_pairs={{0,3},{1,2},{2,1},{3,0},{4,7},{5,6},{6,5},{7,4},{8,11},{9,10},{10,... | collective-permute-start | bytes 135176 | tf_op jit(solution)/shard_map/ppermute | solution.py:331
  67.5 5.7 %collective-permute-start.23 = (bf16[176,128]{1,0:T(8,128)(2,1)S(1)}, bf16[176,128]{1,0:T(8,128)(2,1)S(1)}, u32[]{:S(2)}, u32[]{:S(2)}) collective-permute-start(bf16[176,128]{1,0:T(8,128)(2,1)S(1)} %get-tuple-element.132.refs_0_), channel_id=1, source_target_pairs={{0,2},{1,3},{2,0},{3,1},{4,6},{5,7},{6,4},{7,5},{8,10},{9,11},{10,... | collective-permute-start | bytes 135176 | tf_op jit(solution)/shard_map/ppermute | solution.py:331
  67.5 5.7 %collective-permute-start.22 = (bf16[176,128]{1,0:T(8,128)(2,1)S(1)}, bf16[176,128]{1,0:T(8,128)(2,1)S(1)}, u32[]{:S(2)}, u32[]{:S(2)}) collective-permute-start(bf16[176,128]{1,0:T(8,128)(2,1)S(1)} %get-tuple-element.132.refs_0_), channel_id=1, source_target_pairs={{0,1},{1,0},{2,3},{3,2},{4,5},{5,4},{6,7},{7,6},{8,9},{9,8},{10,11... | collective-permute-start | bytes 135176 | tf_op jit(solution)/shard_map/ppermute | solution.py:331
  72.1 7.4 %collective-permute-start.20 = (bf16[176,512]{1,0:T(8,128)(2,1)S(1)}, bf16[176,512]{1,0:T(8,128)(2,1)S(1)}, u32[]{:S(2)}, u32[]{:S(2)}) collective-permute-start(bf16[176,512]{1,0:T(8,128)(2,1)S(1)} %get-tuple-element.129), channel_id=1, source_target_pairs={{0,8},{4,12},{8,0},{12,4},{16,24},{20,28},{24,16},{28,20},{1,9},{5... | collective-permute-start | bytes 540680 | tf_op jit(solution)/shard_map/ppermute | solution.py:331
  72.6 9.4 %collective-permute-start.21 = (bf16[176,512]{1,0:T(8,128)(2,1)S(1)}, bf16[176,512]{1,0:T(8,128)(2,1)S(1)}, u32[]{:S(2)}, u32[]{:S(2)}) collective-permute-start(bf16[176,512]{1,0:T(8,128)(2,1)S(1)} %get-tuple-element.130), channel_id=1, source_target_pairs={{0,16},{4,20},{8,24},{12,28},{16,0},{20,4},{24,8},{28,12},{1,17},{... | collective-permute-start | bytes 540680 | tf_op jit(solution)/shard_map/ppermute | solution.py:331
  74.6 7.4 %collective-permute-start.25 = (bf16[176,512]{1,0:T(8,128)(2,1)S(1)}, bf16[176,512]{1,0:T(8,128)(2,1)S(1)}, u32[]{:S(2)}, u32[]{:S(2)}) collective-permute-start(bf16[176,512]{1,0:T(8,128)(2,1)S(1)} %grow_rows.5), channel_id=1, source_target_pairs={{0,24},{4,28},{8,16},{12,20},{16,8},{20,12},{24,0},{28,4},{1,25},{... | collective-permute-start | bytes 540680 | tf_op jit(solution)/shard_map/ppermute | solution.py:331
  77.1 1.2 %collective-permute-start.19 = (f32[8,128]{1,0:T(8,128)S(1)}, f32[8,128]{1,0:T(8,128)S(1)}, u32[]{:S(2)}, u32[]{:S(2)}) collective-permute-start(f32[8,128]{1,0:T(8,128)S(1)} %max.6), channel_id=1, source_target_pairs={{0,4},{4,0},{8,12},{12,8},{16,20},{20,16},{24,28},{28,24},{1,5},{5... | collective-permute-start | bytes 12296 | tf_op jit(solution)/shard_map/ppermute | solution.py:331
  83.7 0.8 copy-start.3

commit v9 on v8

--- a/solution.py
+++ b/solution.py
@@ -155,7 +155,7 @@
         ],
         scratch_shapes=[pltpu.VMEM((rows, both), F32), pltpu.VMEM((rows, both), F32)],
         cost_estimate=pl.CostEstimate(
-            flops=8 * rows * width * local * both, bytes_accessed=8 * width * local * both, transcendentals=0
+            flops=1000, bytes_accessed=1000, transcendentals=0
         ),
         compiler_params=pltpu.CompilerParams(vmem_limit_bytes=VMEM_LIMIT),
         name="shrink_rows",
@@ -404,7 +404,7 @@
     up_sibling = exchange(after(adapter_up_weight, down_sibling), "dp", 1)
     near_done = [arrived[m] for m in near[1:]]
     for m in far:
-        arrived[m] = exchange(after(sent[m], *near_done, last_sent), "dp", 2 * m)
+        arrived[m] = exchange(after(sent[m], last_sent), "dp", 2 * m)
 
     both_down = after(down_sibling, up_sibling)
     flags, updates = [], {}
@@ -424,7 +424,7 @@
             for one in arrived_for(0):
                 base = base + one.astype(F32)
         else:
-            group[0] = after(group[0], base, shares[-1])
+            group[0] = after(group[0], base)
             share, place, flag = shrink(core, group, adapter_down_weight, both_down, flag_lane)
             shares = [after(share, returned[0])] + [exchange(share, "tensor", z) for z in range(1, blocks)]
         flags.append(flag)

time: 85 us -> 89.6 us (1.054)
  waiting for transfers between devices: 16.4 us -> 23.7 us
  starting transfers between devices: 23.2 us -> 20.8 us
    ppermute x17, waiting for transfers between devices: 16.4 us -> 23.7 us  [exchange(): return lax.ppermute(array, axis, [(i, i ^ shift) for i in range(size)])]
    ppermute x17, starting transfers between devices: 23.2 us -> 20.8 us  [exchange(): return lax.ppermute(array, axis, [(i, i ^ shift) for i in range(size)])]
    pallas_call x2, Pallas kernels: 12.8 us -> 11.6 us  [shrink(): pl.pallas_call(functools.partial(shrink_kernel, len(messages), flag_lane)...]
  transfers between devices with their start and end apart: 17 -> 17, of which waited for: 6 -> 5; matrix products, arithmetic and copies ran while one was open for 6% -> 5% of each run, Pallas kernels for 37% -> 41%
where the time goes in v9:
time: 89.6 us; the launch traced here: 89.1 us
  Pallas kernels  38.2 us (43%)
  waiting for transfers between devices  23.7 us (26%)
  starting transfers between devices  20.8 us (23%)
  other arithmetic  4.16 us (5%)
  local copies, waits for them, and re-layouts  1.33 us (1%)
    ppermute x17, waiting for transfers between devices, exchange(): return lax.ppermute(array, axis, [(i, i ^ shift) for i in range(size)])  23.7 us
    ppermute x17, starting transfers between devices, exchange(): return lax.ppermute(array, axis, [(i, i ^ shift) for i in range(size)])  20.8 us
    pallas_call x3, Pallas kernels, base_parts(): pl.pallas_call(functools.partial(base_kernel, shifts), grid_spec=pltpu.Pr...  15.9 us
    pallas_call x2, Pallas kernels, shrink(): pl.pallas_call(functools.partial(shrink_kernel, len(messages), flag_lane)...  11.6 us
    pallas_call x1, Pallas kernels, pack(): pl.pallas_call(functools.partial(pack_kernel, (sizes, first_rows, chip_sl...  5.5 us
    pallas_call x2, Pallas kernels, grow(): pl.pallas_call(functools.partial(grow_kernel, len(parts), sizes), in_spec...  3.25 us
    convert_element_type x1, other arithmetic, send(): part = part.astype(BF)  2.36 us
  transfers between devices with their start and end apart: 17, of which 5 were waited for; matrix products, arithmetic and copies ran while one was open for 5% of the time, Pallas kernels for 41%

profile of v9, /device:TPU:0, one launch (start us, length us, event | category | flops | bytes accessed | tf_op | source)
XLA Modules:
  0.0 89.1 jit_solution(14316929346391149972)
XLA Ops:
  0.5 4.6 %base_parts.3 = bf16[512,512]{1,0:T(8,128)(2,1)} custom-call(s32[1]{0:T(128)} %bitcast.4.place_ref, bf16[512,2048]{1,0:T(8,128)(2,1)} %tokens_ref.4, bf16[2048,2,1024]{2,1,0:T(2,128)(2,1)} %weight_ref.5), custom_call_target="tpu_custom_call" | custom-call | flops 4294967296 | bytes 4194304 | tf_op jit(solution)/shard_map/base_parts/pallas_call | solution.py:239
  5.0 2.6 %collective-permute-start.13 = (bf16[512,512]{1,0:T(8,128)(2,1)}, bf16[512,512]{1,0:T(8,128)(2,1)}, u32[]{:S(2)}, u32[]{:S(2)}) collective-permute-start(bf16[512,512]{1,0:T(8,128)(2,1)} %base_parts.3), channel_id=1, source_target_pairs={{0,1},{1,0},{2,3},{3,2},{4,5},{5,4},{6,7},{7,6},{8,9},{9,8},{10,11... | collective-permute-start | bytes 1572872 | tf_op jit(solution)/shard_map/ppermute | solution.py:331
  7.6 5.5 %pack_rows.3 = (bf16[176,2048]{1,0:T(8,128)(2,1)S(1)}, bf16[176,2048]{1,0:T(8,128)(2,1)}, bf16[176,2048]{1,0:T(8,128)(2,1)}, bf16[176,2048]{1,0:T(8,128)(2,1)S(1)}, s32[512,128]{1,0:T(8,128)S(1)}) custom-call(s32[1]{0:T(128)} %bitcast.1.place_ref, s32[1,512]{1,0:T(1,128)S(1)} %bitcast.6, s32[1,64]{1,0:T(1,128)S(1)} %bitcast.8, bf16[512,2048]{1,0:T(8,128)(2,1)} %tokens_ref.4), custom_call_target="tpu_custom_call" | custom-call | flops 1000 | bytes 1000 | tf_op jit(solution)/shard_map/pack_rows/pallas_call | solution.py:81
  13.1 1.5 %collective-permute-start.9 = (bf16[176,2048]{1,0:T(8,128)(2,1)}, bf16[176,2048]{1,0:T(8,128)(2,1)S(1)}, u32[]{:S(2)}, u32[]{:S(2)}) collective-permute-start(bf16[176,2048]{1,0:T(8,128)(2,1)} %get-tuple-element.110), channel_id=1, source_target_pairs={{0,8},{4,12},{8,0},{12,4},{16,24},{20,28},{24,16},{28,20},{1,9},{5... | collective-permute-start | bytes 2162696 | tf_op jit(solution)/shard_map/ppermute | solution.py:331
  14.6 1.5 %collective-permute-start.10 = (bf16[176,2048]{1,0:T(8,128)(2,1)}, bf16[176,2048]{1,0:T(8,128)(2,1)S(1)}, u32[]{:S(2)}, u32[]{:S(2)}) collective-permute-start(bf16[176,2048]{1,0:T(8,128)(2,1)} %get-tuple-element.111), channel_id=1, source_target_pairs={{0,16},{4,20},{8,24},{12,28},{16,0},{20,4},{24,8},{28,12},{1,17},{... | collective-permute-start | bytes 2162696 | tf_op jit(solution)/shard_map/ppermute | solution.py:331
  16.1 6.5 %base_parts.4 = (bf16[512,512]{1,0:T(8,128)(2,1)}, f32[512,512]{1,0:T(8,128)}) custom-call(s32[1]{0:T(128)} %bitcast.4.place_ref, bf16[512,2048]{1,0:T(8,128)(2,1)} %tokens_ref.4, bf16[2048,2,1024]{2,1,0:T(2,128)(2,1)} %weight_ref.5), custom_call_target="tpu_custom_call" | custom-call | flops 8589934592 | bytes 4194304 | tf_op jit(solution)/shard_map/base_parts/pallas_call | solution.py:239
  22.7 0.5 collective-permute-start.16
  23.1 2.4 %add_convert_fusion = bf16[512,512]{1,0:T(8,128)(2,1)} fusion(f32[512,512]{1,0:T(8,128)} %get-tuple-element.117, bf16[512,512]{1,0:T(8,128)(2,1)} %collective-permute-done.13), kind=kLoop, calls=%fused_computation.1 | loop fusion | flops 786432 | bytes 2097152 | tf_op jit(solution)/shard_map/convert_element_type | solution.py:388
  25.5 2.6 %collective-permute-start.17 = (bf16[512,512]{1,0:T(8,128)(2,1)}, bf16[512,512]{1,0:T(8,128)(2,1)}, u32[]{:S(2)}, u32[]{:S(2)}) collective-permute-start(bf16[512,512]{1,0:T(8,128)(2,1)} %add_convert_fusion), channel_id=1, source_target_pairs={{0,2},{1,3},{2,0},{3,1},{4,6},{5,7},{6,4},{7,5},{8,10},{9,11},{10,... | collective-permute-start | bytes 1572872 | tf_op jit(solution)/shard_map/ppermute | solution.py:331
  28.1 0.5 collective-permute-start.14
  28.6 3.8 %collective-permute-done.9.refs_1_ = bf16[176,2048]{1,0:T(8,128)(2,1)S(1)} collective-permute-done((bf16[176,2048]{1,0:T(8,128)(2,1)}, bf16[176,2048]{1,0:T(8,128)(2,1)S(1)}, u32[]{:S(2)}, u32[]{:S(2)}) %collective-permute-start.9) | collective-permute-done | bytes 720928 | tf_op jit(solution)/shard_map/ppermute | solution.py:331
  32.3 15.9 %collective-permute-done.10.refs_2_ = bf16[176,2048]{1,0:T(8,128)(2,1)S(1)} collective-permute-done((bf16[176,2048]{1,0:T(8,128)(2,1)}, bf16[176,2048]{1,0:T(8,128)(2,1)S(1)}, u32[]{:S(2)}, u32[]{:S(2)}) %collective-permute-start.10) | collective-permute-done | bytes 720928 | tf_op jit(solution)/shard_map/ppermute | solution.py:331
  48.3 7.2 %shrink_rows.4 = (f32[528,128]{1,0:T(8,128)S(1)}, bf16[528,128]{1,0:T(8,128)(2,1)S(1)}, f32[8,128]{1,0:T(8,128)S(1)}) custom-call(s32[1]{0:T(128)} %bitcast.core_ref, bf16[176,2048]{1,0:T(8,128)(2,1)S(1)} %get-tuple-element.109.refs_0_, bf16[176,2048]{1,0:T(8,128)(2,1)S(1)} %collective-permute-done.9.refs_1_, ...), custom_call_target="tpu_custom_call" | custom-call | flops 1000 | bytes 1000 | tf_op jit(solution)/shard_map/shrink_rows/pallas_call | solution.py:146
  55.5 0.5 collective-permute-start.15
  56.0 4.9 %base_parts.5 = f32[512,512]{1,0:T(8,128)} custom-call(s32[1]{0:T(128)} %bitcast.4.place_ref, bf16[512,2048]{1,0:T(8,128)(2,1)} %tokens_ref.4, bf16[2048,2,1024]{2,1,0:T(2,128)(2,1)} %weight_ref.5), custom_call_target="tpu_custom_call" | custom-call | flops 4294967296 | bytes 4194304 | tf_op jit(solution)/shard_map/base_parts/pallas_call | solution.py:239
  60.9 2.6 %collective-permute-start.19 = (bf16[528,128]{1,0:T(8,128)(2,1)S(1)}, bf16[528,128]{1,0:T(8,128)(2,1)S(1)}, u32[]{:S(2)}, u32[]{:S(2)}) collective-permute-start(bf16[528,128]{1,0:T(8,128)(2,1)S(1)} %get-tuple-element.135), channel_id=1, source_target_pairs={{0,2},{1,3},{2,0},{3,1},{4,6},{5,7},{6,4},{7,5},{8,10},{9,11},{10,... | collective-permute-start | bytes 405512 | tf_op jit(solution)/shard_map/ppermute | solution.py:331
  63.6 1.7 %convert_add_fusion = f32[512,512]{1,0:T(8,128)S(1)} fusion(bf16[512,512]{1,0:T(8,128)(2,1)} %collective-permute-done.17, f32[512,512]{1,0:T(8,128)} %base_parts.5, bf16[512,512]{1,0:T(8,128)(2,1)} %collective-permute-done.16), kind=kLoop, calls=%fused_computation | loop fusion | flops 1048576 | bytes 3145728 | tf_op jit(solution)/shard_map/add | solution.py:425
  65.3 4.4 %shrink_rows.5 = (bf16[176,128]{1,0:T(8,128)(2,1)S(1)}, bf16[176,128]{1,0:T(8,128)(2,1)S(1)}, f32[8,128]{1,0:T(8,128)S(1)}) custom-call(s32[1]{0:T(128)} %bitcast.core_ref, bf16[176,2048]{1,0:T(8,128)(2,1)S(1)} %collective-permute-done.14.refs_0_, bf16[8,2048,128]{2,1,0:T(8,128)(2,1)S(1)} %copy-done, ...), custom_call_target="tpu_custom_call" | custom-call | flops 1000 | bytes 1000 | tf_op jit(solution)/shard_map/shrink_rows/pallas_call | solution.py:146
  69.8 1.4 %collective-permute-start.24 = (bf16[176,128]{1,0:T(8,128)(2,1)S(1)}, bf16[176,128]{1,0:T(8,128)(2,1)S(1)}, u32[]{:S(2)}, u32[]{:S(2)}) collective-permute-start(bf16[176,128]{1,0:T(8,128)(2,1)S(1)} %get-tuple-element.132.refs_0_), channel_id=1, source_target_pairs={{0,3},{1,2},{2,1},{3,0},{4,7},{5,6},{6,5},{7,4},{8,11},{9,10},{10,... | collective-permute-start | bytes 135176 | tf_op jit(solution)/shard_map/ppermute | solution.py:331
  71.2 1.7 %collective-permute-start.23 = (bf16[176,128]{1,0:T(8,128)(2,1)S(1)}, bf16[176,128]{1,0:T(8,128)(2,1)S(1)}, u32[]{:S(2)}, u32[]{:S(2)}) collective-permute-start(bf16[176,128]{1,0:T(8,128)(2,1)S(1)} %get-tuple-element.132.refs_0_), channel_id=1, source_target_pairs={{0,2},{1,3},{2,0},{3,1},{4,6},{5,7},{6,4},{7,5},{8,10},{9,11},{10,... | collective-permute-start | bytes 135176 | tf_op jit(solution)/shard_map/ppermute | solution.py:331
  72.9 1.3 %collective-permute-start.22 = (bf16[176,128]{1,0:T(8,128)(2,1)S(1)}, bf16[176,128]{1,0:T(8,128)(2,1)S(1)}, u32[]{:S(2)}, u32[]{:S(2)}) collective-permute-start(bf16[176,128]{1,0:T(8,128)(2,1)S(1)} %get-tuple-element.132.refs_0_), channel_id=1, source_target_pairs={{0,1},{1,0},{2,3},{3,2},{4,5},{5,4},{6,7},{7,6},{8,9},{9,8},{10,11... | collective-permute-start | bytes 135176 | tf_op jit(solution)/shard_map/ppermute | solution.py:331
  74.2 1.8 %grow_rows.4 = (bf16[176,512]{1,0:T(8,128)(2,1)S(1)}, bf16[176,512]{1,0:T(8,128)(2,1)S(1)}, bf16[176,512]{1,0:T(8,128)(2,1)S(1)}) custom-call(s32[1]{0:T(128)} %bitcast.core_ref, f32[528,128]{1,0:T(8,128)S(1)} %get-tuple-element.136.refs_0_, bf16[528,128]{1,0:T(8,128)(2,1)S(1)} %collective-permute-done.19.refs_1_, ...), custom_call_target="tpu_custom_call" | custom-call | flops 1000 | bytes 1000 | tf_op jit(solution)/shard_map/grow_rows/pallas_call | solution.py:201
  76.1 2.6 %collective-permute-start.21 = (bf16[176,512]{1,0:T(8,128)(2,1)S(1)}, bf16[176,512]{1,0:T(8,128)(2,1)S(1)}, u32[]{:S(2)}, u32[]{:S(2)}) collective-permute-start(bf16[176,512]{1,0:T(8,128)(2,1)S(1)} %get-tuple-element.130), channel_id=1, source_target_pairs={{0,16},{4,20},{8,24},{12,28},{16,0},{20,4},{24,8},{28,12},{1,17},{... | collective-permute-start | bytes 540680 | tf_op jit(solution)/shard_map/ppermute | solution.py:331
  78.7 1.4 %grow_rows.5 = bf16[176,512]{1,0:T(8,128)(2,1)S(1)} custom-call(s32[1]{0:T(128)} %bitcast.core_ref, bf16[176,128]{1,0:T(8,128)(2,1)S(1)} %get-tuple-element.132.refs_0_, bf16[176,128]{1,0:T(8,128)(2,1)S(1)} %collective-permute-done.22.refs_1_, bf16[176,128]{1,0:T(8,128)(2,1)S(1)} %collective-permute-done.23.refs_2_, ...), custom_call_target="tpu_custom_call" | custom-call | flops 1000 | bytes 1000 | tf_op jit(solution)/shard_map/grow_rows/pallas_call | solution.py:201
  80.2 1.0 %collective-permute-start.25 = (bf16[176,512]{1,0:T(8,128)(2,1)S(1)}, bf16[176,512]{1,0:T(8,128)(2,1)S(1)}, u32[]{:S(2)}, u32[]{:S(2)}) collective-permute-start(bf16[176,512]{1,0:T(8,128)(2,1)S(1)} %grow_rows.5), channel_id=1, source_target_pairs={{0,24},{4,28},{8,16},{12,20},{16,8},{20,12},{24,0},{28,4},{1,25},{... | collective-permute-start | bytes 540680 | tf_op jit(solution)/shard_map/ppermute | solution.py:331
  81.5 0.8 collective-permute-done.18
  82.3 0.5 slice.3
  83.5 1.2 %collective-permute-done.21 = bf16[176,512]{1,0:T(8,128)(2,1)S(1)} collective-permute-done((bf16[176,512]{1,0:T(8,128)(2,1)S(1)}, bf16[176,512]{1,0:T(8,128)(2,1)S(1)}, u32[]{:S(2)}, u32[]{:S(2)}) %collective-permute-start.21) | collective-permute-done | bytes 180256 | tf_op jit(solution)/shard_map/ppermute | solution.py:331
  84.7 1.9 %collective-permute-done.25 = bf16[176,512]{1,0:T(8,128)(2,1)S(1)} collective-permute-done((bf16[176,512]{1,0:T(8,128)(2,1)S(1)}, bf16[176,512]{1,0:T(8,128)(2,1)S(1)}, u32[]{:S(2)}, u32[]{:S(2)}) %collective-permute-start.25) | collective-permute-done | bytes 180256 | tf_op jit(solution)/shard_map/ppermute | solution.py:331
  86.6 1.7 %conditional.1 = (bf16[512,2,256]{2,1,0:T(2,128)(2,1)S(1)}) conditional(s32[]{:T(128)} %bitcast.5, (f32[512,512]{1,0:T(8,128)S(1)}, bf16[512,1024]{1,0:T(8,128)(2,1)S(1)}, bf16[176,512]{1,0:T(8,128)(2,1)S(1)}, bf16[176,512]{1,0:T(8,128)(2,1)S(1)}, bf16[176,512]{1,0:T(8,128)(2,1)S(1)}, /*index=5*/bf16[176,512]{1,0:T(8,128)(2,1)S(1)}) %tuple.31, ...), branch_computations={%region_0.1_spmd, %region_1.2_spmd} | conditional | flops 5000 | bytes 7083256 | solution.py:452
  86.6 1.5 %finish_rows.2 = bf16[512,2,256]{2,1,0:T(2,128)(2,1)S(1)} custom-call(f32[512,512]{1,0:T(8,128)S(1)} %get-tuple-element.50.refs_0_, bf16[512,1024]{1,0:T(8,128)(2,1)S(1)} %get-tuple-element.51.refs_1_, bf16[176,512]{1,0:T(8,128)(2,1)S(1)} %get-tuple-element.52.refs_2_, bf16[176,512]{1,0:T(8,128)(2,1)S(1)} %get-tuple-element.53.refs_3_, ...), custom_call_target="tpu_custom_call" | custom-call | flops 1000 | bytes 1000 | tf_op jit(solution)/shard_map/cond/branch_0_fun/finish_rows/pallas_call | solution.py:316
  88.3 0.8 copy-done.3
  (32 shorter events, 1.0 us)
Async XLA Ops:
  0.0 16.1 %collective-permute-start.11 = (bf16[8,2048,128]{2,1,0:T(8,128)(2,1)}, bf16[8,2048,128]{2,1,0:T(8,128)(2,1)}, u32[]{:S(2)}, u32[]{:S(2)}) collective-permute-start(bf16[8,2048,128]{2,1,0:T(8,128)(2,1)} %refs_1_.1), channel_id=1, source_target_pairs={{0,4},{4,0},{8,12},{12,8},{16,20},{20,16},{24,28},{28,24},{1,5},{5... | collective-permute-start | bytes 12582920 | tf_op jit(solution)/shard_map/ppermute | solution.py:331
  0.5 7.2 %copy-start.4 = (s32[512,1]{0,1:T(1,128)S(1)}, s32[512,1]{0,1:T(1,128)}, u32[]{:S(2)}) copy-start(s32[512,1]{0,1:T(1,128)} %param.9) | copy-start | bytes 6148
  0.5 7.2 %copy-start.5 = (s32[64]{0:T(128)S(1)}, s32[64]{0:T(128)}, u32[]{:S(2)}) copy-start(s32[64]{0:T(128)} %param.10) | copy-start | bytes 772
  5.0 18.1 %collective-permute-start.13 = (bf16[512,512]{1,0:T(8,128)(2,1)}, bf16[512,512]{1,0:T(8,128)(2,1)}, u32[]{:S(2)}, u32[]{:S(2)}) collective-permute-start(bf16[512,512]{1,0:T(8,128)(2,1)} %base_parts.3), channel_id=1, source_target_pairs={{0,1},{1,0},{2,3},{3,2},{4,5},{5,4},{6,7},{7,6},{8,9},{9,8},{10,11... | collective-permute-start | bytes 1572872 | tf_op jit(solution)/shard_map/ppermute | solution.py:331
  13.1 19.2 %collective-permute-start.9 = (bf16[176,2048]{1,0:T(8,128)(2,1)}, bf16[176,2048]{1,0:T(8,128)(2,1)S(1)}, u32[]{:S(2)}, u32[]{:S(2)}) collective-permute-start(bf16[176,2048]{1,0:T(8,128)(2,1)} %get-tuple-element.110), channel_id=1, source_target_pairs={{0,8},{4,12},{8,0},{12,4},{16,24},{20,28},{24,16},{28,20},{1,9},{5... | collective-permute-start | bytes 2162696 | tf_op jit(solution)/shard_map/ppermute | solution.py:331
  14.6 33.6 %collective-permute-start.10 = (bf16[176,2048]{1,0:T(8,128)(2,1)}, bf16[176,2048]{1,0:T(8,128)(2,1)S(1)}, u32[]{:S(2)}, u32[]{:S(2)}) collective-permute-start(bf16[176,2048]{1,0:T(8,128)(2,1)} %get-tuple-element.111), channel_id=1, source_target_pairs={{0,16},{4,20},{8,24},{12,28},{16,0},{20,4},{24,8},{28,12},{1,17},{... | collective-permute-start | bytes 2162696 | tf_op jit(solution)/shard_map/ppermute | solution.py:331
  16.1 11.9 %collective-permute-start.12 = (bf16[8,2,64,256]{3,2,1,0:T(8,128)(2,1)}, bf16[8,2,64,256]{3,2,1,0:T(8,128)(2,1)}, u32[]{:S(2)}, u32[]{:S(2)}) collective-permute-start(bf16[8,2,64,256]{3,2,1,0:T(8,128)(2,1)} %refs_5_.1), channel_id=1, source_target_pairs={{0,4},{4,0},{8,12},{12,8},{16,20},{20,16},{24,28},{28,24},{1,5},{5... | collective-permute-start | bytes 1572872 | tf_op jit(solution)/shard_map/ppermute | solution.py:331
  22.7 40.9 %collective-permute-start.16 = (bf16[512,512]{1,0:T(8,128)(2,1)}, bf16[512,512]{1,0:T(8,128)(2,1)}, u32[]{:S(2)}, u32[]{:S(2)}) collective-permute-start(bf16[512,512]{1,0:T(8,128)(2,1)} %get-tuple-element.122), channel_id=1, source_target_pairs={{0,1},{1,0},{2,3},{3,2},{4,5},{5,4},{6,7},{7,6},{8,9},{9,8},{10,11... | collective-permute-start | bytes 1572872 | tf_op jit(solution)/shard_map/ppermute | solution.py:331
  25.5 38.1 %collective-permute-start.17 = (bf16[512,512]{1,0:T(8,128)(2,1)}, bf16[512,512]{1,0:T(8,128)(2,1)}, u32[]{:S(2)}, u32[]{:S(2)}) collective-permute-start(bf16[512,512]{1,0:T(8,128)(2,1)} %add_convert_fusion), channel_id=1, source_target_pairs={{0,2},{1,3},{2,0},{3,1},{4,6},{5,7},{6,4},{7,5},{8,10},{9,11},{10,... | collective-permute-start | bytes 1572872 | tf_op jit(solution)/shard_map/ppermute | solution.py:331
  28.1 37.3 %collective-permute-start.14 = (bf16[176,2048]{1,0:T(8,128)(2,1)S(1)}, bf16[176,2048]{1,0:T(8,128)(2,1)S(1)}, u32[]{:S(2)}, u32[]{:S(2)}) collective-permute-start(bf16[176,2048]{1,0:T(8,128)(2,1)S(1)} %get-tuple-element.118), channel_id=1, source_target_pairs={{0,24},{4,28},{8,16},{12,20},{16,8},{20,12},{24,0},{28,4},{1,25},{... | collective-permute-start | bytes 2162696 | tf_op jit(solution)/shard_map/ppermute | solution.py:331
  55.5 5.4 %collective-permute-start.15 = (bf16[528,128]{1,0:T(8,128)(2,1)S(1)}, bf16[528,128]{1,0:T(8,128)(2,1)S(1)}, u32[]{:S(2)}, u32[]{:S(2)}) collective-permute-start(bf16[528,128]{1,0:T(8,128)(2,1)S(1)} %convert_element_type.29), channel_id=1, source_target_pairs={{0,1},{1,0},{2,3},{3,2},{4,5},{5,4},{6,7},{7,6},{8,9},{9,8},{10,11... | collective-permute-start | bytes 405512 | tf_op jit(solution)/shard_map/ppermute | solution.py:331
  56.0 9.3 %copy-start = (bf16[8,2048,128]{2,1,0:T(8,128)(2,1)S(1)}, bf16[8,2048,128]{2,1,0:T(8,128)(2,1)}, u32[]{:S(2)}) copy-start(bf16[8,2048,128]{2,1,0:T(8,128)(2,1)} %refs_1_.1) | copy-start | bytes 12582916
  60.9 13.3 %collective-permute-start.19 = (bf16[528,128]{1,0:T(8,128)(2,1)S(1)}, bf16[528,128]{1,0:T(8,128)(2,1)S(1)}, u32[]{:S(2)}, u32[]{:S(2)}) collective-permute-start(bf16[528,128]{1,0:T(8,128)(2,1)S(1)} %get-tuple-element.135), channel_id=1, source_target_pairs={{0,2},{1,3},{2,0},{3,1},{4,6},{5,7},{6,4},{7,5},{8,10},{9,11},{10,... | collective-permute-start | bytes 405512 | tf_op jit(solution)/shard_map/ppermute | solution.py:331
  65.3 8.9 %copy-start.2 = (bf16[8,2,64,256]{3,2,1,0:T(8,128)(2,1)S(1)}, bf16[8,2,64,256]{3,2,1,0:T(8,128)(2,1)}, u32[]{:S(2)}) copy-start(bf16[8,2,64,256]{3,2,1,0:T(8,128)(2,1)} %refs_5_.1) | copy-start | bytes 1572868
  69.8 16.8 %copy-start.1 = (bf16[512,2048]{1,0:T(8,128)(2,1)S(1)}, bf16[512,2048]{1,0:T(8,128)(2,1)}, u32[]{:S(2)}) copy-start(bf16[512,2048]{1,0:T(8,128)(2,1)} %tokens_ref.4) | copy-start | bytes 6291460
  69.8 8.9 %collective-permute-start.24 = (bf16[176,128]{1,0:T(8,128)(2,1)S(1)}, bf16[176,128]{1,0:T(8,128)(2,1)S(1)}, u32[]{:S(2)}, u32[]{:S(2)}) collective-permute-start(bf16[176,128]{1,0:T(8,128)(2,1)S(1)} %get-tuple-element.132.refs_0_), channel_id=1, source_target_pairs={{0,3},{1,2},{2,1},{3,0},{4,7},{5,6},{6,5},{7,4},{8,11},{9,10},{10,... | collective-permute-start | bytes 135176 | tf_op jit(solution)/shard_map/ppermute | solution.py:331
  71.2 7.5 %collective-permute-start.23 = (bf16[176,128]{1,0:T(8,128)(2,1)S(1)}, bf16[176,128]{1,0:T(8,128)(2,1)S(1)}, u32[]{:S(2)}, u32[]{:S(2)}) collective-permute-start(bf16[176,128]{1,0:T(8,128)(2,1)S(1)} %get-tuple-element.132.refs_0_), channel_id=1, source_target_pairs={{0,2},{1,3},{2,0},{3,1},{4,6},{5,7},{6,4},{7,5},{8,10},{9,11},{10,... | collective-permute-start | bytes 135176 | tf_op jit(solution)/shard_map/ppermute | solution.py:331
  72.9 5.8 %collective-permute-start.22 = (bf16[176,128]{1,0:T(8,128)(2,1)S(1)}, bf16[176,128]{1,0:T(8,128)(2,1)S(1)}, u32[]{:S(2)}, u32[]{:S(2)}) collective-permute-start(bf16[176,128]{1,0:T(8,128)(2,1)S(1)} %get-tuple-element.132.refs_0_), channel_id=1, source_target_pairs={{0,1},{1,0},{2,3},{3,2},{4,5},{5,4},{6,7},{7,6},{8,9},{9,8},{10,11... | collective-permute-start | bytes 135176 | tf_op jit(solution)/shard_map/ppermute | solution.py:331
  76.1 7.4 %collective-permute-start.20 = (bf16[176,512]{1,0:T(8,128)(2,1)S(1)}, bf16[176,512]{1,0:T(8,128)(2,1)S(1)}, u32[]{:S(2)}, u32[]{:S(2)}) collective-permute-start(bf16[176,512]{1,0:T(8,128)(2,1)S(1)} %get-tuple-element.129), channel_id=1, source_target_pairs={{0,8},{4,12},{8,0},{12,4},{16,24},{20,28},{24,16},{28,20},{1,9},{5... | collective-permute-start | bytes 540680 | tf_op jit(solution)/shard_map/ppermute | solution.py:331
  76.1 8.5 %collective-permute-start.21 = (bf16[176,512]{1,0:T(8,128)(2,1)S(1)}, bf16[176,512]{1,0:T(8,128)(2,1)S(1)}, u32[]{:S(2)}, u32[]{:S(2)}) collective-permute-start(bf16[176,512]{1,0:T(8,128)(2,1)S(1)} %get-tuple-element.130), channel_id=1, source_target_pairs={{0,16},{4,20},{8,24},{12,28},{16,0},{20,4},{24,8},{28,12},{1,17},{... | collective-permute-start | bytes 540680 | tf_op jit(solution)/shard_map/ppermute | solution.py:331
  80.2 6.5 %collective-permute-start.25 = (bf16[176,512]{1,0:T(8,128)(2,1)S(1)}, bf16[176,512]{1,0:T(8,128)(2,1)S(1)}, u32[]{:S(2)}, u32[]{:S(2)}) collective-permute-start(bf16[176,512]{1,0:T(8,128)(2,1)S(1)} %grow_rows.5), channel_id=1, source_target_pairs={{0,24},{4,28},{8,16},{12,20},{16,8},{20,12},{24,0},{28,4},{1,25},{... | collective-permute-start | bytes 540680 | tf_op jit(solution)/shard_map/ppermute | solution.py:331
  81.1 1.2 %collective-permute-start.18 = (f32[8,128]{1,0:T(8,128)S(1)}, f32[8,128]{1,0:T(8,128)S(1)}, u32[]{:S(2)}, u32[]{:S(2)}) collective-permute-start(f32[8,128]{1,0:T(8,128)S(1)} %max.6), channel_id=1, source_target_pairs={{0,4},{4,0},{8,12},{12,8},{16,20},{20,16},{24,28},{28,24},{1,5},{5... | collective-permute-start | bytes 12296 | tf_op jit(solution)/shard_map/ppermute | solution.py:331
  88.3 0.8 copy-start.3

commit v10 on v9

--- a/solution.py
+++ b/solution.py
@@ -404,7 +404,7 @@
     up_sibling = exchange(after(adapter_up_weight, down_sibling), "dp", 1)
     near_done = [arrived[m] for m in near[1:]]
     for m in far:
-        arrived[m] = exchange(after(sent[m], last_sent), "dp", 2 * m)
+        arrived[m] = exchange(after(sent[m], *near_done, last_sent), "dp", 2 * m)
 
     both_down = after(down_sibling, up_sibling)
     flags, updates = [], {}

time: 89.6 us -> 79.5 us (0.89)
  waiting for transfers between devices: 23.7 us -> 11.2 us
  starting transfers between devices: 20.8 us -> 23.2 us
    ppermute x17, waiting for transfers between devices: 23.7 us -> 11.2 us  [exchange(): return lax.ppermute(array, axis, [(i, i ^ shift) for i in range(size)])]
    ppermute x17, starting transfers between devices: 20.8 us -> 23.2 us  [exchange(): return lax.ppermute(array, axis, [(i, i ^ shift) for i in range(size)])]
  transfers between devices with their start and end apart: 17 -> 17, of which waited for: 5 -> 5; matrix products, arithmetic and copies ran while one was open for 5% -> 6% of each run, Pallas kernels for 41% -> 46%
where the time goes in v10:
time: 79.5 us; the launch traced here: 79 us
  Pallas kernels  38.1 us (48%)
  starting transfers between devices  23.2 us (29%)
  waiting for transfers between devices  11.2 us (14%)
  other arithmetic  4.16 us (5%)
  local copies, waits for them, and re-layouts  1.33 us (2%)
    ppermute x17, starting transfers between devices, exchange(): return lax.ppermute(array, axis, [(i, i ^ shift) for i in range(size)])  23.2 us
    pallas_call x3, Pallas kernels, base_parts(): pl.pallas_call(functools.partial(base_kernel, shifts), grid_spec=pltpu.Pr...  15.9 us
    pallas_call x2, Pallas kernels, shrink(): pl.pallas_call(functools.partial(shrink_kernel, len(messages), flag_lane)...  11.6 us
    ppermute x17, waiting for transfers between devices, exchange(): return lax.ppermute(array, axis, [(i, i ^ shift) for i in range(size)])  11.2 us
    pallas_call x1, Pallas kernels, pack(): pl.pallas_call(functools.partial(pack_kernel, (sizes, first_rows, chip_sl...  5.5 us
    pallas_call x2, Pallas kernels, grow(): pl.pallas_call(functools.partial(grow_kernel, len(parts), sizes), in_spec...  3.25 us
    convert_element_type x1, other arithmetic, send(): part = part.astype(BF)  2.36 us
    add x1, other arithmetic, per_device(): base = base + one.astype(F32)  1.73 us
  transfers between devices with their start and end apart: 17, of which 5 were waited for; matrix products, arithmetic and copies ran while one was open for 6% of the time, Pallas kernels for 46%

profile of v10, /device:TPU:0, one launch (start us, length us, event | category | flops | bytes accessed | tf_op | source)
XLA Modules:
  0.0 79.0 jit_solution(12263764697237813240)
XLA Ops:
  0.5 4.6 %base_parts.3 = bf16[512,512]{1,0:T(8,128)(2,1)} custom-call(s32[1]{0:T(128)} %bitcast.4.place_ref, bf16[512,2048]{1,0:T(8,128)(2,1)} %tokens_ref.4, bf16[2048,2,1024]{2,1,0:T(2,128)(2,1)} %weight_ref.5), custom_call_target="tpu_custom_call" | custom-call | flops 4294967296 | bytes 4194304 | tf_op jit(solution)/shard_map/base_parts/pallas_call | solution.py:239
  5.0 2.6 %collective-permute-start.13 = (bf16[512,512]{1,0:T(8,128)(2,1)}, bf16[512,512]{1,0:T(8,128)(2,1)}, u32[]{:S(2)}, u32[]{:S(2)}) collective-permute-start(bf16[512,512]{1,0:T(8,128)(2,1)} %base_parts.3), channel_id=1, source_target_pairs={{0,1},{1,0},{2,3},{3,2},{4,5},{5,4},{6,7},{7,6},{8,9},{9,8},{10,11... | collective-permute-start | bytes 1572872 | tf_op jit(solution)/shard_map/ppermute | solution.py:331
  7.6 5.5 %pack_rows.3 = (bf16[176,2048]{1,0:T(8,128)(2,1)S(1)}, bf16[176,2048]{1,0:T(8,128)(2,1)}, bf16[176,2048]{1,0:T(8,128)(2,1)}, bf16[176,2048]{1,0:T(8,128)(2,1)S(1)}, s32[512,128]{1,0:T(8,128)S(1)}) custom-call(s32[1]{0:T(128)} %bitcast.1.place_ref, s32[1,512]{1,0:T(1,128)S(1)} %bitcast.6, s32[1,64]{1,0:T(1,128)S(1)} %bitcast.8, bf16[512,2048]{1,0:T(8,128)(2,1)} %tokens_ref.4), custom_call_target="tpu_custom_call" | custom-call | flops 1000 | bytes 1000 | tf_op jit(solution)/shard_map/pack_rows/pallas_call | solution.py:81
  13.1 1.5 %collective-permute-start.9 = (bf16[176,2048]{1,0:T(8,128)(2,1)}, bf16[176,2048]{1,0:T(8,128)(2,1)S(1)}, u32[]{:S(2)}, u32[]{:S(2)}) collective-permute-start(bf16[176,2048]{1,0:T(8,128)(2,1)} %get-tuple-element.110), channel_id=1, source_target_pairs={{0,8},{4,12},{8,0},{12,4},{16,24},{20,28},{24,16},{28,20},{1,9},{5... | collective-permute-start | bytes 2162696 | tf_op jit(solution)/shard_map/ppermute | solution.py:331
  14.6 1.5 %collective-permute-start.10 = (bf16[176,2048]{1,0:T(8,128)(2,1)}, bf16[176,2048]{1,0:T(8,128)(2,1)S(1)}, u32[]{:S(2)}, u32[]{:S(2)}) collective-permute-start(bf16[176,2048]{1,0:T(8,128)(2,1)} %get-tuple-element.111), channel_id=1, source_target_pairs={{0,16},{4,20},{8,24},{12,28},{16,0},{20,4},{24,8},{28,12},{1,17},{... | collective-permute-start | bytes 2162696 | tf_op jit(solution)/shard_map/ppermute | solution.py:331
  16.1 6.5 %base_parts.4 = (bf16[512,512]{1,0:T(8,128)(2,1)}, f32[512,512]{1,0:T(8,128)}) custom-call(s32[1]{0:T(128)} %bitcast.4.place_ref, bf16[512,2048]{1,0:T(8,128)(2,1)} %tokens_ref.4, bf16[2048,2,1024]{2,1,0:T(2,128)(2,1)} %weight_ref.5), custom_call_target="tpu_custom_call" | custom-call | flops 8589934592 | bytes 4194304 | tf_op jit(solution)/shard_map/base_parts/pallas_call | solution.py:239
  22.7 0.5 collective-permute-start.16
  23.1 2.4 %add_convert_fusion = bf16[512,512]{1,0:T(8,128)(2,1)} fusion(f32[512,512]{1,0:T(8,128)} %get-tuple-element.117, bf16[512,512]{1,0:T(8,128)(2,1)} %collective-permute-done.13), kind=kLoop, calls=%fused_computation.1 | loop fusion | flops 786432 | bytes 2097152 | tf_op jit(solution)/shard_map/convert_element_type | solution.py:388
  25.5 2.6 %collective-permute-start.17 = (bf16[512,512]{1,0:T(8,128)(2,1)}, bf16[512,512]{1,0:T(8,128)(2,1)}, u32[]{:S(2)}, u32[]{:S(2)}) collective-permute-start(bf16[512,512]{1,0:T(8,128)(2,1)} %add_convert_fusion), channel_id=1, source_target_pairs={{0,2},{1,3},{2,0},{3,1},{4,6},{5,7},{6,4},{7,5},{8,10},{9,11},{10,... | collective-permute-start | bytes 1572872 | tf_op jit(solution)/shard_map/ppermute | solution.py:331
  28.1 3.5 %collective-permute-done.9.refs_1_ = bf16[176,2048]{1,0:T(8,128)(2,1)S(1)} collective-permute-done((bf16[176,2048]{1,0:T(8,128)(2,1)}, bf16[176,2048]{1,0:T(8,128)(2,1)S(1)}, u32[]{:S(2)}, u32[]{:S(2)}) %collective-permute-start.9) | collective-permute-done | bytes 720928 | tf_op jit(solution)/shard_map/ppermute | solution.py:331
  31.6 1.2 %collective-permute-done.10.refs_2_ = bf16[176,2048]{1,0:T(8,128)(2,1)S(1)} collective-permute-done((bf16[176,2048]{1,0:T(8,128)(2,1)}, bf16[176,2048]{1,0:T(8,128)(2,1)S(1)}, u32[]{:S(2)}, u32[]{:S(2)}) %collective-permute-start.10) | collective-permute-done | bytes 720928 | tf_op jit(solution)/shard_map/ppermute | solution.py:331
  32.8 1.5 %collective-permute-start.14 = (bf16[176,2048]{1,0:T(8,128)(2,1)S(1)}, bf16[176,2048]{1,0:T(8,128)(2,1)S(1)}, u32[]{:S(2)}, u32[]{:S(2)}) collective-permute-start(bf16[176,2048]{1,0:T(8,128)(2,1)S(1)} %get-tuple-element.118), channel_id=1, source_target_pairs={{0,24},{4,28},{8,16},{12,20},{16,8},{20,12},{24,0},{28,4},{1,25},{... | collective-permute-start | bytes 2162696 | tf_op jit(solution)/shard_map/ppermute | solution.py:331
  34.3 7.2 %shrink_rows.4 = (f32[528,128]{1,0:T(8,128)S(1)}, bf16[528,128]{1,0:T(8,128)(2,1)S(1)}, f32[8,128]{1,0:T(8,128)S(1)}) custom-call(s32[1]{0:T(128)} %bitcast.core_ref, bf16[176,2048]{1,0:T(8,128)(2,1)S(1)} %get-tuple-element.109.refs_0_, bf16[176,2048]{1,0:T(8,128)(2,1)S(1)} %collective-permute-done.9.refs_1_, ...), custom_call_target="tpu_custom_call" | custom-call | flops 1000 | bytes 1000 | tf_op jit(solution)/shard_map/shrink_rows/pallas_call | solution.py:146
  41.5 0.5 collective-permute-start.15
  42.1 4.8 %base_parts.5 = f32[512,512]{1,0:T(8,128)} custom-call(s32[1]{0:T(128)} %bitcast.4.place_ref, bf16[512,2048]{1,0:T(8,128)(2,1)} %tokens_ref.4, bf16[2048,2,1024]{2,1,0:T(2,128)(2,1)} %weight_ref.5), custom_call_target="tpu_custom_call" | custom-call | flops 4294967296 | bytes 4194304 | tf_op jit(solution)/shard_map/base_parts/pallas_call | solution.py:239
  46.9 3.1 %collective-permute-done.15 = bf16[528,128]{1,0:T(8,128)(2,1)S(1)} collective-permute-done((bf16[528,128]{1,0:T(8,128)(2,1)S(1)}, bf16[528,128]{1,0:T(8,128)(2,1)S(1)}, u32[]{:S(2)}, u32[]{:S(2)}) %collective-permute-start.15) | collective-permute-done | bytes 135200 | tf_op jit(solution)/shard_map/ppermute | solution.py:331
  50.0 4.1 %collective-permute-start.19 = (bf16[528,128]{1,0:T(8,128)(2,1)S(1)}, bf16[528,128]{1,0:T(8,128)(2,1)S(1)}, u32[]{:S(2)}, u32[]{:S(2)}) collective-permute-start(bf16[528,128]{1,0:T(8,128)(2,1)S(1)} %get-tuple-element.135), channel_id=1, source_target_pairs={{0,2},{1,3},{2,0},{3,1},{4,6},{5,7},{6,4},{7,5},{8,10},{9,11},{10,... | collective-permute-start | bytes 405512 | tf_op jit(solution)/shard_map/ppermute | solution.py:331
  54.1 1.7 %convert_add_fusion = f32[512,512]{1,0:T(8,128)S(1)} fusion(bf16[512,512]{1,0:T(8,128)(2,1)} %collective-permute-done.17, f32[512,512]{1,0:T(8,128)} %base_parts.5, bf16[512,512]{1,0:T(8,128)(2,1)} %collective-permute-done.16), kind=kLoop, calls=%fused_computation | loop fusion | flops 1048576 | bytes 3145728 | tf_op jit(solution)/shard_map/add | solution.py:425
  55.8 4.4 %shrink_rows.5 = (bf16[176,128]{1,0:T(8,128)(2,1)S(1)}, bf16[176,128]{1,0:T(8,128)(2,1)S(1)}, f32[8,128]{1,0:T(8,128)S(1)}) custom-call(s32[1]{0:T(128)} %bitcast.core_ref, bf16[176,2048]{1,0:T(8,128)(2,1)S(1)} %collective-permute-done.14.refs_0_, bf16[8,2048,128]{2,1,0:T(8,128)(2,1)S(1)} %copy-done, ...), custom_call_target="tpu_custom_call" | custom-call | flops 1000 | bytes 1000 | tf_op jit(solution)/shard_map/shrink_rows/pallas_call | solution.py:146
  60.3 1.6 %collective-permute-start.24 = (bf16[176,128]{1,0:T(8,128)(2,1)S(1)}, bf16[176,128]{1,0:T(8,128)(2,1)S(1)}, u32[]{:S(2)}, u32[]{:S(2)}) collective-permute-start(bf16[176,128]{1,0:T(8,128)(2,1)S(1)} %get-tuple-element.132.refs_0_), channel_id=1, source_target_pairs={{0,3},{1,2},{2,1},{3,0},{4,7},{5,6},{6,5},{7,4},{8,11},{9,10},{10,... | collective-permute-start | bytes 135176 | tf_op jit(solution)/shard_map/ppermute | solution.py:331
  61.9 2.8 %collective-permute-start.22 = (bf16[176,128]{1,0:T(8,128)(2,1)S(1)}, bf16[176,128]{1,0:T(8,128)(2,1)S(1)}, u32[]{:S(2)}, u32[]{:S(2)}) collective-permute-start(bf16[176,128]{1,0:T(8,128)(2,1)S(1)} %get-tuple-element.132.refs_0_), channel_id=1, source_target_pairs={{0,1},{1,0},{2,3},{3,2},{4,5},{5,4},{6,7},{7,6},{8,9},{9,8},{10,11... | collective-permute-start | bytes 135176 | tf_op jit(solution)/shard_map/ppermute | solution.py:331
  64.7 1.8 %grow_rows.4 = (bf16[176,512]{1,0:T(8,128)(2,1)S(1)}, bf16[176,512]{1,0:T(8,128)(2,1)S(1)}, bf16[176,512]{1,0:T(8,128)(2,1)S(1)}) custom-call(s32[1]{0:T(128)} %bitcast.core_ref, f32[528,128]{1,0:T(8,128)S(1)} %get-tuple-element.136.refs_0_, bf16[528,128]{1,0:T(8,128)(2,1)S(1)} %collective-permute-done.19.refs_1_, ...), custom_call_target="tpu_custom_call" | custom-call | flops 1000 | bytes 1000 | tf_op jit(solution)/shard_map/grow_rows/pallas_call | solution.py:201
  66.6 0.6 collective-permute-start.20
  67.2 0.5 collective-permute-start.21
  67.7 1.4 %grow_rows.5 = bf16[176,512]{1,0:T(8,128)(2,1)S(1)} custom-call(s32[1]{0:T(128)} %bitcast.core_ref, bf16[176,128]{1,0:T(8,128)(2,1)S(1)} %get-tuple-element.132.refs_0_, bf16[176,128]{1,0:T(8,128)(2,1)S(1)} %collective-permute-done.22.refs_1_, bf16[176,128]{1,0:T(8,128)(2,1)S(1)} %collective-permute-done.23.refs_2_, ...), custom_call_target="tpu_custom_call" | custom-call | flops 1000 | bytes 1000 | tf_op jit(solution)/shard_map/grow_rows/pallas_call | solution.py:201
  69.1 2.5 %collective-permute-start.25 = (bf16[176,512]{1,0:T(8,128)(2,1)S(1)}, bf16[176,512]{1,0:T(8,128)(2,1)S(1)}, u32[]{:S(2)}, u32[]{:S(2)}) collective-permute-start(bf16[176,512]{1,0:T(8,128)(2,1)S(1)} %grow_rows.5), channel_id=1, source_target_pairs={{0,24},{4,28},{8,16},{12,20},{16,8},{20,12},{24,0},{28,4},{1,25},{... | collective-permute-start | bytes 540680 | tf_op jit(solution)/shard_map/ppermute | solution.py:331
  72.0 0.8 %collective-permute-done.18 = f32[8,128]{1,0:T(8,128)S(1)} collective-permute-done((f32[8,128]{1,0:T(8,128)S(1)}, f32[8,128]{1,0:T(8,128)S(1)}, u32[]{:S(2)}, u32[]{:S(2)}) %collective-permute-start.18) | collective-permute-done | bytes 4128 | tf_op jit(solution)/shard_map/ppermute | solution.py:331
  72.8 0.5 slice.3
  74.0 2.5 %collective-permute-done.21 = bf16[176,512]{1,0:T(8,128)(2,1)S(1)} collective-permute-done((bf16[176,512]{1,0:T(8,128)(2,1)S(1)}, bf16[176,512]{1,0:T(8,128)(2,1)S(1)}, u32[]{:S(2)}, u32[]{:S(2)}) %collective-permute-start.21) | collective-permute-done | bytes 180256 | tf_op jit(solution)/shard_map/ppermute | solution.py:331
  76.5 1.7 %conditional.1 = (bf16[512,2,256]{2,1,0:T(2,128)(2,1)S(1)}) conditional(s32[]{:T(128)} %bitcast.5, (f32[512,512]{1,0:T(8,128)S(1)}, bf16[512,1024]{1,0:T(8,128)(2,1)S(1)}, bf16[176,512]{1,0:T(8,128)(2,1)S(1)}, bf16[176,512]{1,0:T(8,128)(2,1)S(1)}, bf16[176,512]{1,0:T(8,128)(2,1)S(1)}, /*index=5*/bf16[176,512]{1,0:T(8,128)(2,1)S(1)}) %tuple.31, ...), branch_computations={%region_0.1_spmd, %region_1.2_spmd} | conditional | flops 5000 | bytes 7083256 | solution.py:452
  76.5 1.5 %finish_rows.2 = bf16[512,2,256]{2,1,0:T(2,128)(2,1)S(1)} custom-call(f32[512,512]{1,0:T(8,128)S(1)} %get-tuple-element.50.refs_0_, bf16[512,1024]{1,0:T(8,128)(2,1)S(1)} %get-tuple-element.51.refs_1_, bf16[176,512]{1,0:T(8,128)(2,1)S(1)} %get-tuple-element.52.refs_2_, bf16[176,512]{1,0:T(8,128)(2,1)S(1)} %get-tuple-element.53.refs_3_, ...), custom_call_target="tpu_custom_call" | custom-call | flops 1000 | bytes 1000 | tf_op jit(solution)/shard_map/cond/branch_0_fun/finish_rows/pallas_call | solution.py:316
  78.2 0.8 copy-done.3
  (32 shorter events, 0.9 us)
Async XLA Ops:
  0.0 16.1 %collective-permute-start.11 = (bf16[8,2048,128]{2,1,0:T(8,128)(2,1)}, bf16[8,2048,128]{2,1,0:T(8,128)(2,1)}, u32[]{:S(2)}, u32[]{:S(2)}) collective-permute-start(bf16[8,2048,128]{2,1,0:T(8,128)(2,1)} %refs_1_.1), channel_id=1, source_target_pairs={{0,4},{4,0},{8,12},{12,8},{16,20},{20,16},{24,28},{28,24},{1,5},{5... | collective-permute-start | bytes 12582920 | tf_op jit(solution)/shard_map/ppermute | solution.py:331
  0.5 7.2 %copy-start.4 = (s32[512,1]{0,1:T(1,128)S(1)}, s32[512,1]{0,1:T(1,128)}, u32[]{:S(2)}) copy-start(s32[512,1]{0,1:T(1,128)} %param.9) | copy-start | bytes 6148
  0.5 7.2 %copy-start.5 = (s32[64]{0:T(128)S(1)}, s32[64]{0:T(128)}, u32[]{:S(2)}) copy-start(s32[64]{0:T(128)} %param.10) | copy-start | bytes 772
  5.0 18.1 %collective-permute-start.13 = (bf16[512,512]{1,0:T(8,128)(2,1)}, bf16[512,512]{1,0:T(8,128)(2,1)}, u32[]{:S(2)}, u32[]{:S(2)}) collective-permute-start(bf16[512,512]{1,0:T(8,128)(2,1)} %base_parts.3), channel_id=1, source_target_pairs={{0,1},{1,0},{2,3},{3,2},{4,5},{5,4},{6,7},{7,6},{8,9},{9,8},{10,11... | collective-permute-start | bytes 1572872 | tf_op jit(solution)/shard_map/ppermute | solution.py:331
  13.1 18.5 %collective-permute-start.9 = (bf16[176,2048]{1,0:T(8,128)(2,1)}, bf16[176,2048]{1,0:T(8,128)(2,1)S(1)}, u32[]{:S(2)}, u32[]{:S(2)}) collective-permute-start(bf16[176,2048]{1,0:T(8,128)(2,1)} %get-tuple-element.110), channel_id=1, source_target_pairs={{0,8},{4,12},{8,0},{12,4},{16,24},{20,28},{24,16},{28,20},{1,9},{5... | collective-permute-start | bytes 2162696 | tf_op jit(solution)/shard_map/ppermute | solution.py:331
  14.6 18.2 %collective-permute-start.10 = (bf16[176,2048]{1,0:T(8,128)(2,1)}, bf16[176,2048]{1,0:T(8,128)(2,1)S(1)}, u32[]{:S(2)}, u32[]{:S(2)}) collective-permute-start(bf16[176,2048]{1,0:T(8,128)(2,1)} %get-tuple-element.111), channel_id=1, source_target_pairs={{0,16},{4,20},{8,24},{12,28},{16,0},{20,4},{24,8},{28,12},{1,17},{... | collective-permute-start | bytes 2162696 | tf_op jit(solution)/shard_map/ppermute | solution.py:331
  16.1 18.2 %collective-permute-start.12 = (bf16[8,2,64,256]{3,2,1,0:T(8,128)(2,1)}, bf16[8,2,64,256]{3,2,1,0:T(8,128)(2,1)}, u32[]{:S(2)}, u32[]{:S(2)}) collective-permute-start(bf16[8,2,64,256]{3,2,1,0:T(8,128)(2,1)} %refs_5_.1), channel_id=1, source_target_pairs={{0,4},{4,0},{8,12},{12,8},{16,20},{20,16},{24,28},{28,24},{1,5},{5... | collective-permute-start | bytes 1572872 | tf_op jit(solution)/shard_map/ppermute | solution.py:331
  22.7 31.4 %collective-permute-start.16 = (bf16[512,512]{1,0:T(8,128)(2,1)}, bf16[512,512]{1,0:T(8,128)(2,1)}, u32[]{:S(2)}, u32[]{:S(2)}) collective-permute-start(bf16[512,512]{1,0:T(8,128)(2,1)} %get-tuple-element.122), channel_id=1, source_target_pairs={{0,1},{1,0},{2,3},{3,2},{4,5},{5,4},{6,7},{7,6},{8,9},{9,8},{10,11... | collective-permute-start | bytes 1572872 | tf_op jit(solution)/shard_map/ppermute | solution.py:331
  25.5 28.6 %collective-permute-start.17 = (bf16[512,512]{1,0:T(8,128)(2,1)}, bf16[512,512]{1,0:T(8,128)(2,1)}, u32[]{:S(2)}, u32[]{:S(2)}) collective-permute-start(bf16[512,512]{1,0:T(8,128)(2,1)} %add_convert_fusion), channel_id=1, source_target_pairs={{0,2},{1,3},{2,0},{3,1},{4,6},{5,7},{6,4},{7,5},{8,10},{9,11},{10,... | collective-permute-start | bytes 1572872 | tf_op jit(solution)/shard_map/ppermute | solution.py:331
  32.8 23.0 %collective-permute-start.14 = (bf16[176,2048]{1,0:T(8,128)(2,1)S(1)}, bf16[176,2048]{1,0:T(8,128)(2,1)S(1)}, u32[]{:S(2)}, u32[]{:S(2)}) collective-permute-start(bf16[176,2048]{1,0:T(8,128)(2,1)S(1)} %get-tuple-element.118), channel_id=1, source_target_pairs={{0,24},{4,28},{8,16},{12,20},{16,8},{20,12},{24,0},{28,4},{1,25},{... | collective-permute-start | bytes 2162696 | tf_op jit(solution)/shard_map/ppermute | solution.py:331
  41.5 8.4 %collective-permute-start.15 = (bf16[528,128]{1,0:T(8,128)(2,1)S(1)}, bf16[528,128]{1,0:T(8,128)(2,1)S(1)}, u32[]{:S(2)}, u32[]{:S(2)}) collective-permute-start(bf16[528,128]{1,0:T(8,128)(2,1)S(1)} %convert_element_type.29), channel_id=1, source_target_pairs={{0,1},{1,0},{2,3},{3,2},{4,5},{5,4},{6,7},{7,6},{8,9},{9,8},{10,11... | collective-permute-start | bytes 405512 | tf_op jit(solution)/shard_map/ppermute | solution.py:331
  42.1 13.8 %copy-start = (bf16[8,2048,128]{2,1,0:T(8,128)(2,1)S(1)}, bf16[8,2048,128]{2,1,0:T(8,128)(2,1)}, u32[]{:S(2)}) copy-start(bf16[8,2048,128]{2,1,0:T(8,128)(2,1)} %refs_1_.1) | copy-start | bytes 12582916
  50.0 14.7 %collective-permute-start.19 = (bf16[528,128]{1,0:T(8,128)(2,1)S(1)}, bf16[528,128]{1,0:T(8,128)(2,1)S(1)}, u32[]{:S(2)}, u32[]{:S(2)}) collective-permute-start(bf16[528,128]{1,0:T(8,128)(2,1)S(1)} %get-tuple-element.135), channel_id=1, source_target_pairs={{0,2},{1,3},{2,0},{3,1},{4,6},{5,7},{6,4},{7,5},{8,10},{9,11},{10,... | collective-permute-start | bytes 405512 | tf_op jit(solution)/shard_map/ppermute | solution.py:331
  55.8 8.9 %copy-start.2 = (bf16[8,2,64,256]{3,2,1,0:T(8,128)(2,1)S(1)}, bf16[8,2,64,256]{3,2,1,0:T(8,128)(2,1)}, u32[]{:S(2)}) copy-start(bf16[8,2,64,256]{3,2,1,0:T(8,128)(2,1)} %refs_5_.1) | copy-start | bytes 1572868
  60.3 16.2 %copy-start.1 = (bf16[512,2048]{1,0:T(8,128)(2,1)S(1)}, bf16[512,2048]{1,0:T(8,128)(2,1)}, u32[]{:S(2)}) copy-start(bf16[512,2048]{1,0:T(8,128)(2,1)} %tokens_ref.4) | copy-start | bytes 6291460
  60.3 7.4 %collective-permute-start.24 = (bf16[176,128]{1,0:T(8,128)(2,1)S(1)}, bf16[176,128]{1,0:T(8,128)(2,1)S(1)}, u32[]{:S(2)}, u32[]{:S(2)}) collective-permute-start(bf16[176,128]{1,0:T(8,128)(2,1)S(1)} %get-tuple-element.132.refs_0_), channel_id=1, source_target_pairs={{0,3},{1,2},{2,1},{3,0},{4,7},{5,6},{6,5},{7,4},{8,11},{9,10},{10,... | collective-permute-start | bytes 135176 | tf_op jit(solution)/shard_map/ppermute | solution.py:331
  61.9 5.8 %collective-permute-start.23 = (bf16[176,128]{1,0:T(8,128)(2,1)S(1)}, bf16[176,128]{1,0:T(8,128)(2,1)S(1)}, u32[]{:S(2)}, u32[]{:S(2)}) collective-permute-start(bf16[176,128]{1,0:T(8,128)(2,1)S(1)} %get-tuple-element.132.refs_0_), channel_id=1, source_target_pairs={{0,2},{1,3},{2,0},{3,1},{4,6},{5,7},{6,4},{7,5},{8,10},{9,11},{10,... | collective-permute-start | bytes 135176 | tf_op jit(solution)/shard_map/ppermute | solution.py:331
  61.9 5.8 %collective-permute-start.22 = (bf16[176,128]{1,0:T(8,128)(2,1)S(1)}, bf16[176,128]{1,0:T(8,128)(2,1)S(1)}, u32[]{:S(2)}, u32[]{:S(2)}) collective-permute-start(bf16[176,128]{1,0:T(8,128)(2,1)S(1)} %get-tuple-element.132.refs_0_), channel_id=1, source_target_pairs={{0,1},{1,0},{2,3},{3,2},{4,5},{5,4},{6,7},{7,6},{8,9},{9,8},{10,11... | collective-permute-start | bytes 135176 | tf_op jit(solution)/shard_map/ppermute | solution.py:331
  66.6 7.4 %collective-permute-start.20 = (bf16[176,512]{1,0:T(8,128)(2,1)S(1)}, bf16[176,512]{1,0:T(8,128)(2,1)S(1)}, u32[]{:S(2)}, u32[]{:S(2)}) collective-permute-start(bf16[176,512]{1,0:T(8,128)(2,1)S(1)} %get-tuple-element.129), channel_id=1, source_target_pairs={{0,8},{4,12},{8,0},{12,4},{16,24},{20,28},{24,16},{28,20},{1,9},{5... | collective-permute-start | bytes 540680 | tf_op jit(solution)/shard_map/ppermute | solution.py:331
  67.2 9.3 %collective-permute-start.21 = (bf16[176,512]{1,0:T(8,128)(2,1)S(1)}, bf16[176,512]{1,0:T(8,128)(2,1)S(1)}, u32[]{:S(2)}, u32[]{:S(2)}) collective-permute-start(bf16[176,512]{1,0:T(8,128)(2,1)S(1)} %get-tuple-element.130), channel_id=1, source_target_pairs={{0,16},{4,20},{8,24},{12,28},{16,0},{20,4},{24,8},{28,12},{1,17},{... | collective-permute-start | bytes 540680 | tf_op jit(solution)/shard_map/ppermute | solution.py:331
  69.1 7.4 %collective-permute-start.25 = (bf16[176,512]{1,0:T(8,128)(2,1)S(1)}, bf16[176,512]{1,0:T(8,128)(2,1)S(1)}, u32[]{:S(2)}, u32[]{:S(2)}) collective-permute-start(bf16[176,512]{1,0:T(8,128)(2,1)S(1)} %grow_rows.5), channel_id=1, source_target_pairs={{0,24},{4,28},{8,16},{12,20},{16,8},{20,12},{24,0},{28,4},{1,25},{... | collective-permute-start | bytes 540680 | tf_op jit(solution)/shard_map/ppermute | solution.py:331
  71.6 1.2 %collective-permute-start.18 = (f32[8,128]{1,0:T(8,128)S(1)}, f32[8,128]{1,0:T(8,128)S(1)}, u32[]{:S(2)}, u32[]{:S(2)}) collective-permute-start(f32[8,128]{1,0:T(8,128)S(1)} %max.6), channel_id=1, source_target_pairs={{0,4},{4,0},{8,12},{12,8},{16,20},{20,16},{24,28},{28,24},{1,5},{5... | collective-permute-start | bytes 12296 | tf_op jit(solution)/shard_map/ppermute | solution.py:331
  78.2 0.8 %copy-start.3 = (bf16[512,2,256]{2,1,0:T(2,128)(2,1)}, bf16[512,2,256]{2,1,0:T(2,128)(2,1)S(1)}, u32[]{:S(2)}) copy-start(bf16[512,2,256]{2,1,0:T(2,128)(2,1)S(1)} %get-tuple-element.176) | copy-start | bytes 1572868

commit v11 on v10

--- a/solution.py
+++ b/solution.py
@@ -26,10 +26,10 @@
 def pack_kernel(shape, place_ref, adapter_ref, slot_ref, tokens_ref, *refs):
     sizes, first_rows, chip_slots, flag_lane = shape
     messages = len(sizes)
-    outs, key_ref, pick = refs[:messages], refs[messages], refs[messages + 1]
+    outs, key_ref, pick, tail = refs[:messages], *refs[messages:]
     rows, width = tokens_ref.shape
     experts = slot_ref.shape[1]
-    offsets = [sum(round_up(s, 128) for s in sizes[:m]) for m in range(messages)]
+    offsets = [sum(sizes[:m]) for m in range(messages)]
 
     @pl.when(pl.program_id(0) == 0)
     def _():
@@ -56,28 +56,30 @@
         for m in range(messages):
             padded = round_up(sizes[m], 128)
             target = lax.broadcasted_iota(jnp.int32, (padded, rows), 0)
-            hit = (target + first_rows[m] == position) & (shift == m) & (target < sizes[m] - 1)
+            hit = (target == position - first_rows[m]) & (shift == m) & (target < sizes[m] - 1)
             chosen = hit.astype(F32).astype(BF)
-            pick[offsets[m]:offsets[m] + padded, :] = chosen
+            pick[offsets[m]:offsets[m] + sizes[m], :] = chosen[:sizes[m], :]
             places = dot(within8, chosen, ((1,), (1,)))[0:1, :]
             if padded < width:
                 places = jnp.concatenate([places, jnp.zeros((1, width - padded), F32)], axis=1)
             lane = lax.broadcasted_iota(jnp.int32, (1, width), 1)
-            places = jnp.where(lane == flag_lane, over, places)
-            body = dot(chosen, tokens_ref[...])[:sizes[m], :]
-            row = lax.broadcasted_iota(jnp.int32, (sizes[m], 1), 0)
-            outs[m][...] = jnp.where(row == sizes[m] - 1, places, body).astype(BF)
-
-    @pl.when(pl.program_id(0) > 0)
+            tail[m:m + 1, :] = jnp.where(lane == flag_lane, over, places)
+
+    body = dot(pick[...], tokens_ref[...])
+    for m in range(messages):
+        outs[m][...] = body[offsets[m]:offsets[m] + sizes[m], :].astype(BF)
+
+    @pl.when(pl.program_id(0) == 0)
     def _():
         for m in range(messages):
-            outs[m][...] = dot(pick[offsets[m]:offsets[m] + sizes[m], :], tokens_ref[...]).astype(BF)
-
-
-def pack(chip, adapters, slots, tokens, sizes, first_rows, chip_slots, steps=4):
+            end = outs[m][sizes[m] - 16:sizes[m], :].astype(F32)
+            row = lax.broadcasted_iota(jnp.int32, (16, 1), 0)
+            outs[m][sizes[m] - 16:sizes[m], :] = jnp.where(row == 15, tail[m:m + 1, :], end).astype(BF)
+
+
+def pack(chip, adapters, slots, tokens, sizes, first_rows, chip_slots, steps=2):
     rows, width = tokens.shape
     block = width // steps
-    spread = sum(round_up(s, 128) for s in sizes)
     return pl.pallas_call(
         functools.partial(pack_kernel, (sizes, first_rows, chip_slots, block - 1)),
         grid=(steps,),
@@ -90,7 +92,10 @@
         out_specs=[pl.BlockSpec((s, block), lambda i: (0, i)) for s in sizes]
         + [pl.BlockSpec((rows, 128), lambda i: (0, 0))],
         out_shape=[jax.ShapeDtypeStruct((s, width), BF) for s in sizes] + [jax.ShapeDtypeStruct((rows, 128), jnp.int32)],
-        scratch_shapes=[pltpu.VMEM((spread, rows), BF)],
+        scratch_shapes=[
+            pltpu.VMEM((sum(sizes), rows), BF),
+            pltpu.VMEM((round_up(len(sizes), 8), block), F32),
+        ],
         cost_estimate=COST,
         compiler_params=pltpu.CompilerParams(vmem_limit_bytes=VMEM_LIMIT),
         name="pack_rows",
@@ -99,7 +104,8 @@
 
 def shrink_kernel(count, flag_lane, core_ref, *refs):
     messages, (mine, sibling) = refs[:count], refs[count:count + 2]
-    out, place_out, flag_out, total, places = refs[count + 2:]
+    out, send_out, place_out, flag_out, places = refs[count + 2:]
+    total = out
     step = pl.program_id(0)
     local = 2 * pl.num_programs(0)
     sizes = [m.shape[0] for m in messages]
@@ -134,10 +140,10 @@
 
     @pl.when(step == pl.num_programs(0) - 1)
     def _():
-        out[...] = total[...].astype(out.dtype)
-
-
-def shrink(core, messages, mine, sibling, flag_lane, dtype=BF):
+        send_out[...] = total[...].astype(BF)
+
+
+def shrink(core, messages, mine, sibling, flag_lane):
     local, width, both = mine.shape
     rows = sum(m.shape[0] for m in messages)
     whole = [pl.BlockSpec(m.shape, lambda i: (0, 0)) for m in messages]
@@ -147,13 +153,14 @@
         functools.partial(shrink_kernel, len(messages), flag_lane),
         grid=(local // 2,),
         in_specs=[pl.BlockSpec(memory_space=pltpu.SMEM)] + whole + [pair, pair],
-        out_specs=[keep, keep, pl.BlockSpec((8, 128), lambda i: (0, 0))],
+        out_specs=[keep, keep, keep, pl.BlockSpec((8, 128), lambda i: (0, 0))],
         out_shape=[
-            jax.ShapeDtypeStruct((rows, both), dtype),
+            jax.ShapeDtypeStruct((rows, both), F32),
+            jax.ShapeDtypeStruct((rows, both), BF),
             jax.ShapeDtypeStruct((rows, both), BF),
             jax.ShapeDtypeStruct((8, 128), F32),
         ],
-        scratch_shapes=[pltpu.VMEM((rows, both), F32), pltpu.VMEM((rows, both), F32)],
+        scratch_shapes=[pltpu.VMEM((rows, both), F32)],
         cost_estimate=pl.CostEstimate(
             flops=1000, bytes_accessed=1000, transcendentals=0
         ),
@@ -361,7 +368,7 @@
     chip, core = (me // 2).reshape(1), (me % 2).reshape(1)
     adapters = row_adapter_index.reshape(1, row_count)
     slots = adapter_storage_slot.reshape(1, experts)
-    flag_lane = width // 4 - 1
+    flag_lane = width // 2 - 1
 
     down_sibling = exchange(adapter_down_weight, "dp", 1)
 
@@ -413,11 +420,11 @@
             continue
         group = [arrived[m] for m in part]
         if part is near:
-            share, place, flag = shrink(core, group, adapter_down_weight, both_down, flag_lane, F32)
+            share, _, place, flag = shrink(core, group, adapter_down_weight, both_down, flag_lane)
             compute([0], after(tokens, share))
             step = 1
             while 2 * step < blocks:
-                share = share + exchange(share.astype(BF), "tensor", step).astype(F32)
+                share = share + exchange(share if step == 1 else share.astype(BF), "tensor", step).astype(F32)
                 step *= 2
             shares = [share, exchange(share.astype(BF), "tensor", step)]
             base = after(parts[0], share)
@@ -425,29 +432,30 @@
                 base = base + one.astype(F32)
         else:
             group[0] = after(group[0], base)
-            share, place, flag = shrink(core, group, adapter_down_weight, both_down, flag_lane)
-            shares = [after(share, returned[0])] + [exchange(share, "tensor", z) for z in range(1, blocks)]
+            share, rounded, place, flag = shrink(core, group, adapter_down_weight, both_down, flag_lane)
+            shares = [after(share, returned[0])] + [exchange(rounded, "tensor", z) for z in range(1, blocks)]
         flags.append(flag)
         grown = grow(core, shares, place, adapter_up_weight, up_sibling, tuple(sizes[m] for m in part))
         for m, update in zip(part, grown):
             returned[m] = update if m == 0 else exchange(update, "dp", 2 * m)
+    bases = [base]
     spread = spread_of(after(key, base), sizes, first_rows)
     flag = functools.reduce(jnp.maximum, flags)
     flag = jnp.maximum(flag, exchange(flag, "dp", 1))
     updates = [returned[m] for m in range(chips)]
 
     def as_is():
-        return finish([base], [spread], [updates])
+        return finish(bases, [spread], [updates])
 
     def second_round():
         later_sizes, later_rows = (rest,) * chips, (message - 1,) * chips
         packed = pack(chip, adapters, slots, tokens, later_sizes, later_rows, chip_slots)
         group = [packed[0]] + [exchange(packed[m], "dp", 2 * m) for m in range(1, chips)]
-        share, place, _ = shrink(core, group, adapter_down_weight, down_sibling, flag_lane)
-        shares = [share] + [exchange(share, "tensor", z) for z in range(1, blocks)]
+        share, rounded, place, _ = shrink(core, group, adapter_down_weight, down_sibling, flag_lane)
+        shares = [share] + [exchange(rounded, "tensor", z) for z in range(1, blocks)]
         grown = grow(core, shares, place, adapter_up_weight, up_sibling, later_sizes)
         back = [grown[0]] + [exchange(grown[m], "dp", 2 * m) for m in range(1, chips)]
-        return finish([base], [spread, spread_of(packed[-1], later_sizes, later_rows)], [updates, back])
+        return finish(bases, [spread, spread_of(packed[-1], later_sizes, later_rows)], [updates, back])
 
     return lax.cond(flag[0, 0] > 0.0, second_round, as_is)
 

time: 79.5 us -> 81.5 us (1.025)
  waiting for transfers between devices: 11.2 us -> 14.9 us
  starting transfers between devices: 23.2 us -> 21.8 us
    ppermute x17, waiting for transfers between devices: 11.2 us -> 14.9 us  [exchange(): return lax.ppermute(array, axis, [(i, i ^ shift) for i in range(size)])]
    ppermute x17, starting transfers between devices: 23.2 us -> 21.8 us  [exchange(): return lax.ppermute(array, axis, [(i, i ^ shift) for i in range(size)])]
  transfers between devices with their start and end apart: 17 -> 17, of which waited for: 5 -> 5; matrix products, arithmetic and copies ran while one was open for 6% -> 6% of each run, Pallas kernels for 46% -> 45%
where the time goes in v11:
time: 81.5 us; the launch traced here: 81.1 us
  Pallas kernels  38 us (47%)
  starting transfers between devices  21.8 us (27%)
  waiting for transfers between devices  14.9 us (18%)
  other arithmetic  4.14 us (5%)
  local copies, waits for them, and re-layouts  1.33 us (2%)
    ppermute x17, starting transfers between devices, exchange(): return lax.ppermute(array, axis, [(i, i ^ shift) for i in range(size)])  21.8 us
    pallas_call x3, Pallas kernels, base_parts(): pl.pallas_call(functools.partial(base_kernel, shifts), grid_spec=pltpu.Pr...  15.9 us
    ppermute x17, waiting for transfers between devices, exchange(): return lax.ppermute(array, axis, [(i, i ^ shift) for i in range(size)])  14.9 us
    pallas_call x2, Pallas kernels, shrink(): pl.pallas_call(functools.partial(shrink_kernel, len(messages), flag_lane)...  12.3 us
    pallas_call x1, Pallas kernels, pack(): pl.pallas_call(functools.partial(pack_kernel, (sizes, first_rows, chip_sl...  4.7 us
    pallas_call x2, Pallas kernels, grow(): pl.pallas_call(functools.partial(grow_kernel, len(parts), sizes), in_spec...  3.25 us
    convert_element_type x1, other arithmetic, send(): part = part.astype(BF)  2.36 us
    add x1, other arithmetic, per_device(): base = base + one.astype(F32)  1.73 us
  transfers between devices with their start and end apart: 17, of which 5 were waited for; matrix products, arithmetic and copies ran while one was open for 6% of the time, Pallas kernels for 45%

profile of v11, /device:TPU:0, one launch (start us, length us, event | category | flops | bytes accessed | tf_op | source)
XLA Modules:
  0.0 81.1 jit_solution(11804334795331956131)
XLA Ops:
  0.0 0.5 collective-permute-start.11
  0.5 4.6 %base_parts.3 = bf16[512,512]{1,0:T(8,128)(2,1)} custom-call(s32[1]{0:T(128)} %bitcast.4.place_ref, bf16[512,2048]{1,0:T(8,128)(2,1)} %tokens_ref.4, bf16[2048,2,1024]{2,1,0:T(2,128)(2,1)} %weight_ref.5), custom_call_target="tpu_custom_call" | custom-call | flops 4294967296 | bytes 4194304 | tf_op jit(solution)/shard_map/base_parts/pallas_call | solution.py:246
  5.0 2.6 %collective-permute-start.13 = (bf16[512,512]{1,0:T(8,128)(2,1)}, bf16[512,512]{1,0:T(8,128)(2,1)}, u32[]{:S(2)}, u32[]{:S(2)}) collective-permute-start(bf16[512,512]{1,0:T(8,128)(2,1)} %base_parts.3), channel_id=1, source_target_pairs={{0,1},{1,0},{2,3},{3,2},{4,5},{5,4},{6,7},{7,6},{8,9},{9,8},{10,11... | collective-permute-start | bytes 1572872 | tf_op jit(solution)/shard_map/ppermute | solution.py:338
  7.6 4.7 %pack_rows.3 = (bf16[176,2048]{1,0:T(8,128)(2,1)S(1)}, bf16[176,2048]{1,0:T(8,128)(2,1)}, bf16[176,2048]{1,0:T(8,128)(2,1)}, bf16[176,2048]{1,0:T(8,128)(2,1)S(1)}, s32[512,128]{1,0:T(8,128)S(1)}) custom-call(s32[1]{0:T(128)} %bitcast.1.place_ref, s32[1,512]{1,0:T(1,128)S(1)} %bitcast.6, s32[1,64]{1,0:T(1,128)S(1)} %bitcast.8, bf16[512,2048]{1,0:T(8,128)(2,1)} %tokens_ref.4), custom_call_target="tpu_custom_call" | custom-call | flops 1000 | bytes 1000 | tf_op jit(solution)/shard_map/pack_rows/pallas_call | solution.py:83
  12.3 1.5 %collective-permute-start.9 = (bf16[176,2048]{1,0:T(8,128)(2,1)}, bf16[176,2048]{1,0:T(8,128)(2,1)S(1)}, u32[]{:S(2)}, u32[]{:S(2)}) collective-permute-start(bf16[176,2048]{1,0:T(8,128)(2,1)} %get-tuple-element.112), channel_id=1, source_target_pairs={{0,8},{4,12},{8,0},{12,4},{16,24},{20,28},{24,16},{28,20},{1,9},{5... | collective-permute-start | bytes 2162696 | tf_op jit(solution)/shard_map/ppermute | solution.py:338
  13.8 1.5 %collective-permute-start.10 = (bf16[176,2048]{1,0:T(8,128)(2,1)}, bf16[176,2048]{1,0:T(8,128)(2,1)S(1)}, u32[]{:S(2)}, u32[]{:S(2)}) collective-permute-start(bf16[176,2048]{1,0:T(8,128)(2,1)} %get-tuple-element.113), channel_id=1, source_target_pairs={{0,16},{4,20},{8,24},{12,28},{16,0},{20,4},{24,8},{28,12},{1,17},{... | collective-permute-start | bytes 2162696 | tf_op jit(solution)/shard_map/ppermute | solution.py:338
  15.3 6.5 %base_parts.4 = (bf16[512,512]{1,0:T(8,128)(2,1)}, f32[512,512]{1,0:T(8,128)}) custom-call(s32[1]{0:T(128)} %bitcast.4.place_ref, bf16[512,2048]{1,0:T(8,128)(2,1)} %tokens_ref.4, bf16[2048,2,1024]{2,1,0:T(2,128)(2,1)} %weight_ref.5), custom_call_target="tpu_custom_call" | custom-call | flops 8589934592 | bytes 4194304 | tf_op jit(solution)/shard_map/base_parts/pallas_call | solution.py:246
  22.3 2.4 %add_convert_fusion = bf16[512,512]{1,0:T(8,128)(2,1)} fusion(f32[512,512]{1,0:T(8,128)} %get-tuple-element.119, bf16[512,512]{1,0:T(8,128)(2,1)} %collective-permute-done.13), kind=kLoop, calls=%fused_computation.1 | loop fusion | flops 786432 | bytes 2097152 | tf_op jit(solution)/shard_map/convert_element_type | solution.py:395
  24.7 2.6 %collective-permute-start.17 = (bf16[512,512]{1,0:T(8,128)(2,1)}, bf16[512,512]{1,0:T(8,128)(2,1)}, u32[]{:S(2)}, u32[]{:S(2)}) collective-permute-start(bf16[512,512]{1,0:T(8,128)(2,1)} %add_convert_fusion), channel_id=1, source_target_pairs={{0,2},{1,3},{2,0},{3,1},{4,6},{5,7},{6,4},{7,5},{8,10},{9,11},{10,... | collective-permute-start | bytes 1572872 | tf_op jit(solution)/shard_map/ppermute | solution.py:338
  27.3 3.5 %collective-permute-done.9.refs_1_ = bf16[176,2048]{1,0:T(8,128)(2,1)S(1)} collective-permute-done((bf16[176,2048]{1,0:T(8,128)(2,1)}, bf16[176,2048]{1,0:T(8,128)(2,1)S(1)}, u32[]{:S(2)}, u32[]{:S(2)}) %collective-permute-start.9) | collective-permute-done | bytes 720928 | tf_op jit(solution)/shard_map/ppermute | solution.py:338
  30.8 1.2 %collective-permute-done.10.refs_2_ = bf16[176,2048]{1,0:T(8,128)(2,1)S(1)} collective-permute-done((bf16[176,2048]{1,0:T(8,128)(2,1)}, bf16[176,2048]{1,0:T(8,128)(2,1)S(1)}, u32[]{:S(2)}, u32[]{:S(2)}) %collective-permute-start.10) | collective-permute-done | bytes 720928 | tf_op jit(solution)/shard_map/ppermute | solution.py:338
  32.0 1.5 %collective-permute-start.14 = (bf16[176,2048]{1,0:T(8,128)(2,1)S(1)}, bf16[176,2048]{1,0:T(8,128)(2,1)S(1)}, u32[]{:S(2)}, u32[]{:S(2)}) collective-permute-start(bf16[176,2048]{1,0:T(8,128)(2,1)S(1)} %get-tuple-element.120), channel_id=1, source_target_pairs={{0,24},{4,28},{8,16},{12,20},{16,8},{20,12},{24,0},{28,4},{1,25},{... | collective-permute-start | bytes 2162696 | tf_op jit(solution)/shard_map/ppermute | solution.py:338
  33.5 7.9 %shrink_rows.4 = (f32[528,128]{1,0:T(8,128)S(1)}, bf16[528,128]{1,0:T(8,128)(2,1)}, bf16[528,128]{1,0:T(8,128)(2,1)S(1)}, f32[8,128]{1,0:T(8,128)S(1)}) custom-call(s32[1]{0:T(128)} %bitcast.core_ref, bf16[176,2048]{1,0:T(8,128)(2,1)S(1)} %get-tuple-element.111.refs_0_, bf16[176,2048]{1,0:T(8,128)(2,1)S(1)} %collective-permute-done.9.refs_1_, ...), custom_call_target="tpu_custom_call" | custom-call | flops 1000 | bytes 1000 | tf_op jit(solution)/shard_map/shrink_rows/pallas_call | solution.py:152
  41.4 0.4 collective-permute-start.15
  41.8 4.8 %base_parts.5 = f32[512,512]{1,0:T(8,128)} custom-call(s32[1]{0:T(128)} %bitcast.4.place_ref, bf16[512,2048]{1,0:T(8,128)(2,1)} %tokens_ref.4, bf16[2048,2,1024]{2,1,0:T(2,128)(2,1)} %weight_ref.5), custom_call_target="tpu_custom_call" | custom-call | flops 4294967296 | bytes 4194304 | tf_op jit(solution)/shard_map/base_parts/pallas_call | solution.py:246
  46.7 6.8 %collective-permute-done.15 = f32[528,128]{1,0:T(8,128)S(1)} collective-permute-done((f32[528,128]{1,0:T(8,128)S(1)}, f32[528,128]{1,0:T(8,128)S(1)}, u32[]{:S(2)}, u32[]{:S(2)}) %collective-permute-start.15) | collective-permute-done | bytes 270368 | tf_op jit(solution)/shard_map/ppermute | solution.py:338
  53.5 2.7 %collective-permute-start.19 = (bf16[528,128]{1,0:T(8,128)(2,1)S(1)}, bf16[528,128]{1,0:T(8,128)(2,1)S(1)}, u32[]{:S(2)}, u32[]{:S(2)}) collective-permute-start(bf16[528,128]{1,0:T(8,128)(2,1)S(1)} %get-tuple-element.138), channel_id=1, source_target_pairs={{0,2},{1,3},{2,0},{3,1},{4,6},{5,7},{6,4},{7,5},{8,10},{9,11},{10,... | collective-permute-start | bytes 405512 | tf_op jit(solution)/shard_map/ppermute | solution.py:338
  56.2 1.7 %convert_add_fusion = f32[512,512]{1,0:T(8,128)S(1)} fusion(bf16[512,512]{1,0:T(8,128)(2,1)} %collective-permute-done.17, f32[512,512]{1,0:T(8,128)} %base_parts.5, bf16[512,512]{1,0:T(8,128)(2,1)} %collective-permute-done.16), kind=kLoop, calls=%fused_computation | loop fusion | flops 1048576 | bytes 3145728 | tf_op jit(solution)/shard_map/add | solution.py:432
  57.9 4.4 %shrink_rows.5 = (f32[176,128]{1,0:T(8,128)S(1)}, bf16[176,128]{1,0:T(8,128)(2,1)S(1)}, bf16[176,128]{1,0:T(8,128)(2,1)S(1)}, f32[8,128]{1,0:T(8,128)S(1)}) custom-call(s32[1]{0:T(128)} %bitcast.core_ref, bf16[176,2048]{1,0:T(8,128)(2,1)S(1)} %collective-permute-done.14.refs_0_, bf16[8,2048,128]{2,1,0:T(8,128)(2,1)S(1)} %copy-done, ...), custom_call_target="tpu_custom_call" | custom-call | flops 1000 | bytes 1000 | tf_op jit(solution)/shard_map/shrink_rows/pallas_call | solution.py:152
  62.6 1.7 %collective-permute-start.23 = (bf16[176,128]{1,0:T(8,128)(2,1)S(1)}, bf16[176,128]{1,0:T(8,128)(2,1)S(1)}, u32[]{:S(2)}, u32[]{:S(2)}) collective-permute-start(bf16[176,128]{1,0:T(8,128)(2,1)S(1)} %get-tuple-element.135), channel_id=1, source_target_pairs={{0,2},{1,3},{2,0},{3,1},{4,6},{5,7},{6,4},{7,5},{8,10},{9,11},{10,... | collective-permute-start | bytes 135176 | tf_op jit(solution)/shard_map/ppermute | solution.py:338
  64.3 2.5 %collective-permute-start.22 = (bf16[176,128]{1,0:T(8,128)(2,1)S(1)}, bf16[176,128]{1,0:T(8,128)(2,1)S(1)}, u32[]{:S(2)}, u32[]{:S(2)}) collective-permute-start(bf16[176,128]{1,0:T(8,128)(2,1)S(1)} %get-tuple-element.135), channel_id=1, source_target_pairs={{0,1},{1,0},{2,3},{3,2},{4,5},{5,4},{6,7},{7,6},{8,9},{9,8},{10,11... | collective-permute-start | bytes 135176 | tf_op jit(solution)/shard_map/ppermute | solution.py:338
  66.8 1.8 %grow_rows.4 = (bf16[176,512]{1,0:T(8,128)(2,1)S(1)}, bf16[176,512]{1,0:T(8,128)(2,1)S(1)}, bf16[176,512]{1,0:T(8,128)(2,1)S(1)}) custom-call(s32[1]{0:T(128)} %bitcast.core_ref, f32[528,128]{1,0:T(8,128)S(1)} %get-tuple-element.139.refs_0_, bf16[528,128]{1,0:T(8,128)(2,1)S(1)} %collective-permute-done.19.refs_1_, ...), custom_call_target="tpu_custom_call" | custom-call | flops 1000 | bytes 1000 | tf_op jit(solution)/shard_map/grow_rows/pallas_call | solution.py:208
  68.6 0.6 collective-permute-start.20
  69.2 0.5 collective-permute-start.21
  69.7 1.4 %grow_rows.5 = bf16[176,512]{1,0:T(8,128)(2,1)S(1)} custom-call(s32[1]{0:T(128)} %bitcast.core_ref, f32[176,128]{1,0:T(8,128)S(1)} %get-tuple-element.134.refs_0_, bf16[176,128]{1,0:T(8,128)(2,1)S(1)} %collective-permute-done.22.refs_1_, bf16[176,128]{1,0:T(8,128)(2,1)S(1)} %collective-permute-done.23.refs_2_, ...), custom_call_target="tpu_custom_call" | custom-call | flops 1000 | bytes 1000 | tf_op jit(solution)/shard_map/grow_rows/pallas_call | solution.py:208
  71.2 2.5 %collective-permute-start.25 = (bf16[176,512]{1,0:T(8,128)(2,1)S(1)}, bf16[176,512]{1,0:T(8,128)(2,1)S(1)}, u32[]{:S(2)}, u32[]{:S(2)}) collective-permute-start(bf16[176,512]{1,0:T(8,128)(2,1)S(1)} %grow_rows.5), channel_id=1, source_target_pairs={{0,24},{4,28},{8,16},{12,20},{16,8},{20,12},{24,0},{28,4},{1,25},{... | collective-permute-start | bytes 540680 | tf_op jit(solution)/shard_map/ppermute | solution.py:338
  74.1 0.8 %collective-permute-done.18 = f32[8,128]{1,0:T(8,128)S(1)} collective-permute-done((f32[8,128]{1,0:T(8,128)S(1)}, f32[8,128]{1,0:T(8,128)S(1)}, u32[]{:S(2)}, u32[]{:S(2)}) %collective-permute-start.18) | collective-permute-done | bytes 4128 | tf_op jit(solution)/shard_map/ppermute | solution.py:338
  74.9 0.5 slice.3
  76.1 2.5 %collective-permute-done.21 = bf16[176,512]{1,0:T(8,128)(2,1)S(1)} collective-permute-done((bf16[176,512]{1,0:T(8,128)(2,1)S(1)}, bf16[176,512]{1,0:T(8,128)(2,1)S(1)}, u32[]{:S(2)}, u32[]{:S(2)}) %collective-permute-start.21) | collective-permute-done | bytes 180256 | tf_op jit(solution)/shard_map/ppermute | solution.py:338
  78.6 1.7 %conditional.1 = (bf16[512,2,256]{2,1,0:T(2,128)(2,1)S(1)}) conditional(s32[]{:T(128)} %bitcast.5, (f32[512,512]{1,0:T(8,128)S(1)}, bf16[512,1024]{1,0:T(8,128)(2,1)S(1)}, bf16[176,512]{1,0:T(8,128)(2,1)S(1)}, bf16[176,512]{1,0:T(8,128)(2,1)S(1)}, bf16[176,512]{1,0:T(8,128)(2,1)S(1)}, /*index=5*/bf16[176,512]{1,0:T(8,128)(2,1)S(1)}) %tuple.31, ...), branch_computations={%region_0.1_spmd, %region_1.2_spmd} | conditional | flops 5000 | bytes 7083256 | solution.py:460
  78.6 1.5 %finish_rows.2 = bf16[512,2,256]{2,1,0:T(2,128)(2,1)S(1)} custom-call(f32[512,512]{1,0:T(8,128)S(1)} %get-tuple-element.50.refs_0_, bf16[512,1024]{1,0:T(8,128)(2,1)S(1)} %get-tuple-element.51.refs_1_, bf16[176,512]{1,0:T(8,128)(2,1)S(1)} %get-tuple-element.52.refs_2_, bf16[176,512]{1,0:T(8,128)(2,1)S(1)} %get-tuple-element.53.refs_3_, ...), custom_call_target="tpu_custom_call" | custom-call | flops 1000 | bytes 1000 | tf_op jit(solution)/shard_map/cond/branch_0_fun/finish_rows/pallas_call | solution.py:323
  80.3 0.8 copy-done.3
  (31 shorter events, 1.2 us)
Async XLA Ops:
  0.0 15.3 %collective-permute-start.11 = (bf16[8,2048,128]{2,1,0:T(8,128)(2,1)}, bf16[8,2048,128]{2,1,0:T(8,128)(2,1)}, u32[]{:S(2)}, u32[]{:S(2)}) collective-permute-start(bf16[8,2048,128]{2,1,0:T(8,128)(2,1)} %refs_1_.1), channel_id=1, source_target_pairs={{0,4},{4,0},{8,12},{12,8},{16,20},{20,16},{24,28},{28,24},{1,5},{5... | collective-permute-start | bytes 12582920 | tf_op jit(solution)/shard_map/ppermute | solution.py:338
  0.5 7.2 %copy-start.4 = (s32[512,1]{0,1:T(1,128)S(1)}, s32[512,1]{0,1:T(1,128)}, u32[]{:S(2)}) copy-start(s32[512,1]{0,1:T(1,128)} %param.9) | copy-start | bytes 6148
  0.5 7.2 %copy-start.5 = (s32[64]{0:T(128)S(1)}, s32[64]{0:T(128)}, u32[]{:S(2)}) copy-start(s32[64]{0:T(128)} %param.10) | copy-start | bytes 772
  5.0 17.3 %collective-permute-start.13 = (bf16[512,512]{1,0:T(8,128)(2,1)}, bf16[512,512]{1,0:T(8,128)(2,1)}, u32[]{:S(2)}, u32[]{:S(2)}) collective-permute-start(bf16[512,512]{1,0:T(8,128)(2,1)} %base_parts.3), channel_id=1, source_target_pairs={{0,1},{1,0},{2,3},{3,2},{4,5},{5,4},{6,7},{7,6},{8,9},{9,8},{10,11... | collective-permute-start | bytes 1572872 | tf_op jit(solution)/shard_map/ppermute | solution.py:338
  12.3 18.5 %collective-permute-start.9 = (bf16[176,2048]{1,0:T(8,128)(2,1)}, bf16[176,2048]{1,0:T(8,128)(2,1)S(1)}, u32[]{:S(2)}, u32[]{:S(2)}) collective-permute-start(bf16[176,2048]{1,0:T(8,128)(2,1)} %get-tuple-element.112), channel_id=1, source_target_pairs={{0,8},{4,12},{8,0},{12,4},{16,24},{20,28},{24,16},{28,20},{1,9},{5... | collective-permute-start | bytes 2162696 | tf_op jit(solution)/shard_map/ppermute | solution.py:338
  13.8 18.2 %collective-permute-start.10 = (bf16[176,2048]{1,0:T(8,128)(2,1)}, bf16[176,2048]{1,0:T(8,128)(2,1)S(1)}, u32[]{:S(2)}, u32[]{:S(2)}) collective-permute-start(bf16[176,2048]{1,0:T(8,128)(2,1)} %get-tuple-element.113), channel_id=1, source_target_pairs={{0,16},{4,20},{8,24},{12,28},{16,0},{20,4},{24,8},{28,12},{1,17},{... | collective-permute-start | bytes 2162696 | tf_op jit(solution)/shard_map/ppermute | solution.py:338
  15.3 18.2 %collective-permute-start.12 = (bf16[8,2,64,256]{3,2,1,0:T(8,128)(2,1)}, bf16[8,2,64,256]{3,2,1,0:T(8,128)(2,1)}, u32[]{:S(2)}, u32[]{:S(2)}) collective-permute-start(bf16[8,2,64,256]{3,2,1,0:T(8,128)(2,1)} %refs_5_.1), channel_id=1, source_target_pairs={{0,4},{4,0},{8,12},{12,8},{16,20},{20,16},{24,28},{28,24},{1,5},{5... | collective-permute-start | bytes 1572872 | tf_op jit(solution)/shard_map/ppermute | solution.py:338
  21.9 34.3 %collective-permute-start.16 = (bf16[512,512]{1,0:T(8,128)(2,1)}, bf16[512,512]{1,0:T(8,128)(2,1)}, u32[]{:S(2)}, u32[]{:S(2)}) collective-permute-start(bf16[512,512]{1,0:T(8,128)(2,1)} %get-tuple-element.124), channel_id=1, source_target_pairs={{0,1},{1,0},{2,3},{3,2},{4,5},{5,4},{6,7},{7,6},{8,9},{9,8},{10,11... | collective-permute-start | bytes 1572872 | tf_op jit(solution)/shard_map/ppermute | solution.py:338
  24.7 31.5 %collective-permute-start.17 = (bf16[512,512]{1,0:T(8,128)(2,1)}, bf16[512,512]{1,0:T(8,128)(2,1)}, u32[]{:S(2)}, u32[]{:S(2)}) collective-permute-start(bf16[512,512]{1,0:T(8,128)(2,1)} %add_convert_fusion), channel_id=1, source_target_pairs={{0,2},{1,3},{2,0},{3,1},{4,6},{5,7},{6,4},{7,5},{8,10},{9,11},{10,... | collective-permute-start | bytes 1572872 | tf_op jit(solution)/shard_map/ppermute | solution.py:338
  32.0 25.9 %collective-permute-start.14 = (bf16[176,2048]{1,0:T(8,128)(2,1)S(1)}, bf16[176,2048]{1,0:T(8,128)(2,1)S(1)}, u32[]{:S(2)}, u32[]{:S(2)}) collective-permute-start(bf16[176,2048]{1,0:T(8,128)(2,1)S(1)} %get-tuple-element.120), channel_id=1, source_target_pairs={{0,24},{4,28},{8,16},{12,20},{16,8},{20,12},{24,0},{28,4},{1,25},{... | collective-permute-start | bytes 2162696 | tf_op jit(solution)/shard_map/ppermute | solution.py:338
  41.4 12.1 %collective-permute-start.15 = (f32[528,128]{1,0:T(8,128)S(1)}, f32[528,128]{1,0:T(8,128)S(1)}, u32[]{:S(2)}, u32[]{:S(2)}) collective-permute-start(f32[528,128]{1,0:T(8,128)S(1)} %get-tuple-element.121), channel_id=1, source_target_pairs={{0,1},{1,0},{2,3},{3,2},{4,5},{5,4},{6,7},{7,6},{8,9},{9,8},{10,11... | collective-permute-start | bytes 811016 | tf_op jit(solution)/shard_map/ppermute | solution.py:338
  41.8 16.1 %copy-start = (bf16[8,2048,128]{2,1,0:T(8,128)(2,1)S(1)}, bf16[8,2048,128]{2,1,0:T(8,128)(2,1)}, u32[]{:S(2)}) copy-start(bf16[8,2048,128]{2,1,0:T(8,128)(2,1)} %refs_1_.1) | copy-start | bytes 12582916
  53.5 13.3 %collective-permute-start.19 = (bf16[528,128]{1,0:T(8,128)(2,1)S(1)}, bf16[528,128]{1,0:T(8,128)(2,1)S(1)}, u32[]{:S(2)}, u32[]{:S(2)}) collective-permute-start(bf16[528,128]{1,0:T(8,128)(2,1)S(1)} %get-tuple-element.138), channel_id=1, source_target_pairs={{0,2},{1,3},{2,0},{3,1},{4,6},{5,7},{6,4},{7,5},{8,10},{9,11},{10,... | collective-permute-start | bytes 405512 | tf_op jit(solution)/shard_map/ppermute | solution.py:338
  57.9 8.9 %copy-start.2 = (bf16[8,2,64,256]{3,2,1,0:T(8,128)(2,1)S(1)}, bf16[8,2,64,256]{3,2,1,0:T(8,128)(2,1)}, u32[]{:S(2)}) copy-start(bf16[8,2,64,256]{3,2,1,0:T(8,128)(2,1)} %refs_5_.1) | copy-start | bytes 1572868
  62.3 16.2 %copy-start.1 = (bf16[512,2048]{1,0:T(8,128)(2,1)S(1)}, bf16[512,2048]{1,0:T(8,128)(2,1)}, u32[]{:S(2)}) copy-start(bf16[512,2048]{1,0:T(8,128)(2,1)} %tokens_ref.4) | copy-start | bytes 6291460
  62.4 7.4 %collective-permute-start.24 = (bf16[176,128]{1,0:T(8,128)(2,1)S(1)}, bf16[176,128]{1,0:T(8,128)(2,1)S(1)}, u32[]{:S(2)}, u32[]{:S(2)}) collective-permute-start(bf16[176,128]{1,0:T(8,128)(2,1)S(1)} %get-tuple-element.135), channel_id=1, source_target_pairs={{0,3},{1,2},{2,1},{3,0},{4,7},{5,6},{6,5},{7,4},{8,11},{9,10},{10,... | collective-permute-start | bytes 135176 | tf_op jit(solution)/shard_map/ppermute | solution.py:338
  62.6 7.1 %collective-permute-start.23 = (bf16[176,128]{1,0:T(8,128)(2,1)S(1)}, bf16[176,128]{1,0:T(8,128)(2,1)S(1)}, u32[]{:S(2)}, u32[]{:S(2)}) collective-permute-start(bf16[176,128]{1,0:T(8,128)(2,1)S(1)} %get-tuple-element.135), channel_id=1, source_target_pairs={{0,2},{1,3},{2,0},{3,1},{4,6},{5,7},{6,4},{7,5},{8,10},{9,11},{10,... | collective-permute-start | bytes 135176 | tf_op jit(solution)/shard_map/ppermute | solution.py:338
  64.3 5.4 %collective-permute-start.22 = (bf16[176,128]{1,0:T(8,128)(2,1)S(1)}, bf16[176,128]{1,0:T(8,128)(2,1)S(1)}, u32[]{:S(2)}, u32[]{:S(2)}) collective-permute-start(bf16[176,128]{1,0:T(8,128)(2,1)S(1)} %get-tuple-element.135), channel_id=1, source_target_pairs={{0,1},{1,0},{2,3},{3,2},{4,5},{5,4},{6,7},{7,6},{8,9},{9,8},{10,11... | collective-permute-start | bytes 135176 | tf_op jit(solution)/shard_map/ppermute | solution.py:338
  68.6 7.4 %collective-permute-start.20 = (bf16[176,512]{1,0:T(8,128)(2,1)S(1)}, bf16[176,512]{1,0:T(8,128)(2,1)S(1)}, u32[]{:S(2)}, u32[]{:S(2)}) collective-permute-start(bf16[176,512]{1,0:T(8,128)(2,1)S(1)} %get-tuple-element.131), channel_id=1, source_target_pairs={{0,8},{4,12},{8,0},{12,4},{16,24},{20,28},{24,16},{28,20},{1,9},{5... | collective-permute-start | bytes 540680 | tf_op jit(solution)/shard_map/ppermute | solution.py:338
  69.2 9.3 %collective-permute-start.21 = (bf16[176,512]{1,0:T(8,128)(2,1)S(1)}, bf16[176,512]{1,0:T(8,128)(2,1)S(1)}, u32[]{:S(2)}, u32[]{:S(2)}) collective-permute-start(bf16[176,512]{1,0:T(8,128)(2,1)S(1)} %get-tuple-element.132), channel_id=1, source_target_pairs={{0,16},{4,20},{8,24},{12,28},{16,0},{20,4},{24,8},{28,12},{1,17},{... | collective-permute-start | bytes 540680 | tf_op jit(solution)/shard_map/ppermute | solution.py:338
  71.2 7.4 %collective-permute-start.25 = (bf16[176,512]{1,0:T(8,128)(2,1)S(1)}, bf16[176,512]{1,0:T(8,128)(2,1)S(1)}, u32[]{:S(2)}, u32[]{:S(2)}) collective-permute-start(bf16[176,512]{1,0:T(8,128)(2,1)S(1)} %grow_rows.5), channel_id=1, source_target_pairs={{0,24},{4,28},{8,16},{12,20},{16,8},{20,12},{24,0},{28,4},{1,25},{... | collective-permute-start | bytes 540680 | tf_op jit(solution)/shard_map/ppermute | solution.py:338
  73.7 1.2 %collective-permute-start.18 = (f32[8,128]{1,0:T(8,128)S(1)}, f32[8,128]{1,0:T(8,128)S(1)}, u32[]{:S(2)}, u32[]{:S(2)}) collective-permute-start(f32[8,128]{1,0:T(8,128)S(1)} %max.6), channel_id=1, source_target_pairs={{0,4},{4,0},{8,12},{12,8},{16,20},{20,16},{24,28},{28,24},{1,5},{5... | collective-permute-start | bytes 12296 | tf_op jit(solution)/shard_map/ppermute | solution.py:338
  80.3 0.8 copy-start.3

commit v12 on v11

--- a/solution.py
+++ b/solution.py
@@ -102,10 +102,12 @@
     )(chip, adapters, slots, tokens)
 
 
-def shrink_kernel(count, flag_lane, core_ref, *refs):
+def shrink_kernel(count, carried, flag_lane, core_ref, *refs):
     messages, (mine, sibling) = refs[:count], refs[count:count + 2]
-    out, send_out, place_out, flag_out, places = refs[count + 2:]
-    total = out
+    carry, refs = refs[count + 2:count + 2 + carried], refs[count + 2 + carried:]
+    out, send_out, place_out, flag_out, places = refs
+    kept = carry[0].shape[0] if carried else 0
+    total = out.at[kept:, :]
     step = pl.program_id(0)
     local = 2 * pl.num_programs(0)
     sizes = [m.shape[0] for m in messages]
@@ -124,7 +126,11 @@
             last = lax.broadcasted_iota(jnp.int32, (1, 128), 1) == 127
             flag = jnp.maximum(flag, jnp.max(jnp.where(last, block, 0.0), axis=1, keepdims=True))
             start += size
-        place_out[...] = places[...].astype(BF)
+        place_out[kept:, :] = places[...].astype(BF)
+        if carried:
+            out[:kept, :] = carry[0][...]
+            place_out[:kept, :] = carry[1][...]
+            flag = jnp.maximum(flag, carry[2][0:1, 0:1])
         flag_out[...] = jnp.broadcast_to(flag, (8, 128))
         total[...] = jnp.zeros_like(total)
 
@@ -140,24 +146,26 @@
 
     @pl.when(step == pl.num_programs(0) - 1)
     def _():
-        send_out[...] = total[...].astype(BF)
-
-
-def shrink(core, messages, mine, sibling, flag_lane):
+        send_out[...] = out[...].astype(BF)
+
+
+def shrink(core, messages, mine, sibling, flag_lane, carry=()):
     local, width, both = mine.shape
     rows = sum(m.shape[0] for m in messages)
     whole = [pl.BlockSpec(m.shape, lambda i: (0, 0)) for m in messages]
     pair = pl.BlockSpec((2, width, both), lambda i: (i, 0, 0))
-    keep = pl.BlockSpec((rows, both), lambda i: (0, 0))
-    return pl.pallas_call(
-        functools.partial(shrink_kernel, len(messages), flag_lane),
+    every = rows + (carry[0].shape[0] if carry else 0)
+    keep = pl.BlockSpec((every, both), lambda i: (0, 0))
+    kept = [pl.BlockSpec(c.shape, lambda i: (0, 0)) for c in carry]
+    return pl.pallas_call(
+        functools.partial(shrink_kernel, len(messages), len(carry), flag_lane),
         grid=(local // 2,),
-        in_specs=[pl.BlockSpec(memory_space=pltpu.SMEM)] + whole + [pair, pair],
+        in_specs=[pl.BlockSpec(memory_space=pltpu.SMEM)] + whole + [pair, pair] + kept,
         out_specs=[keep, keep, keep, pl.BlockSpec((8, 128), lambda i: (0, 0))],
         out_shape=[
-            jax.ShapeDtypeStruct((rows, both), F32),
-            jax.ShapeDtypeStruct((rows, both), BF),
-            jax.ShapeDtypeStruct((rows, both), BF),
+            jax.ShapeDtypeStruct((every, both), F32),
+            jax.ShapeDtypeStruct((every, both), BF),
+            jax.ShapeDtypeStruct((every, both), BF),
             jax.ShapeDtypeStruct((8, 128), F32),
         ],
         scratch_shapes=[pltpu.VMEM((rows, both), F32)],
@@ -166,7 +174,25 @@
         ),
         compiler_params=pltpu.CompilerParams(vmem_limit_bytes=VMEM_LIMIT),
         name="shrink_rows",
-    )(core, *messages, mine, sibling)
+    )(core, *messages, mine, sibling, *carry)
+
+
+def hold_kernel(source, out):
+    out[...] = source[...]
+
+
+def hold(array):
+    block = pl.BlockSpec((2,) + array.shape[1:], lambda i: (i, 0, 0))
+    return pl.pallas_call(
+        hold_kernel,
+        grid=(array.shape[0] // 2,),
+        in_specs=[block],
+        out_specs=block,
+        out_shape=jax.ShapeDtypeStruct(array.shape, array.dtype),
+        cost_estimate=COST,
+        compiler_params=pltpu.CompilerParams(vmem_limit_bytes=VMEM_LIMIT),
+        name="hold_weights",
+    )(array)
 
 
 def grow_kernel(shares, sizes, core_ref, *refs):
@@ -229,7 +255,7 @@
                 out[:, j * columns:(j + 1) * columns] = both[j].astype(out.dtype)
 
 
-def base_parts(t, tokens, weight, blocks, shifts):
+def base_parts(t, tokens, weight, blocks, shifts, vmem=VMEM_LIMIT):
     rows, width = tokens.shape
     columns = weight.shape[2] // blocks
     types = [BF if r % 2 else F32 for r in shifts]
@@ -258,7 +284,7 @@
         cost_estimate=pl.CostEstimate(
             flops=16 * len(shifts) * rows * width * columns, bytes_accessed=8 * width * columns, transcendentals=0
         ),
-        compiler_params=pltpu.CompilerParams(vmem_limit_bytes=VMEM_MOST),
+        compiler_params=pltpu.CompilerParams(vmem_limit_bytes=vmem),
         name="base_parts",
     )(t.reshape(1), tokens, weight)
 
@@ -382,8 +408,8 @@
     first_shift = blocks - 1
     parts, came = {}, {}
 
-    def compute(shifts, ready):
-        parts.update(zip(shifts, base_parts(t, ready, key_value_base_weight, blocks, shifts)))
+    def compute(shifts, ready, vmem=VMEM_LIMIT):
+        parts.update(zip(shifts, base_parts(t, ready, key_value_base_weight, blocks, shifts, vmem)))
 
     def arrived_for(r):
         return [came[key] for key in sorted(came) if key[1] == r]
@@ -396,31 +422,35 @@
         came[(r & -r, r ^ (r & -r))] = exchange(part, "tensor", r & -r)
         return part
 
-    compute([first_shift], tokens)
-    send(first_shift)
+    odd, even = list(range(first_shift, 0, -2)), list(range(2, first_shift, 2))
+    compute(odd, tokens, VMEM_MOST)
+    for r in odd:
+        send(r)
     packed = pack(chip, adapters, slots, after(tokens, parts[first_shift]), sizes, first_rows, chip_slots)
     sent, key = list(packed[:-1]), packed[-1]
     arrived, returned = {0: sent[0]}, {}
     for m in near[1:]:
         arrived[m] = exchange(sent[m], "dp", 2 * m)
-    middle = list(range(1, first_shift))
-    compute(middle, after(tokens, *sent))
-    for r in sorted(middle, key=lambda r: (r & -r, -r)):
+    compute(even, after(tokens, *sent), VMEM_MOST)
+    for r in sorted(even, key=lambda r: (r & -r, -r)):
         last_sent = send(r)
 
     up_sibling = exchange(after(adapter_up_weight, down_sibling), "dp", 1)
+    held = hold(after(down_sibling, last_sent))
+    carry = shrink(core, [sent[0]], adapter_down_weight, held, flag_lane)
+    carry = (carry[0], carry[2], carry[3])
     near_done = [arrived[m] for m in near[1:]]
     for m in far:
-        arrived[m] = exchange(after(sent[m], *near_done, last_sent), "dp", 2 * m)
-
-    both_down = after(down_sibling, up_sibling)
+        arrived[m] = exchange(after(sent[m], *near_done, carry[0]), "dp", 2 * m)
+
+    both_down = after(held, up_sibling)
     flags, updates = [], {}
     for part in (near, far):
         if not part:
             continue
-        group = [arrived[m] for m in part]
+        group = [arrived[m] for m in part if m]
         if part is near:
-            share, _, place, flag = shrink(core, group, adapter_down_weight, both_down, flag_lane)
+            share, _, place, flag = shrink(core, group, adapter_down_weight, both_down, flag_lane, carry)
             compute([0], after(tokens, share))
             step = 1
             while 2 * step < blocks:

time: 81.5 us -> 75.9 us (0.931)
  Pallas kernels: 38 us -> 33.2 us
  starting transfers between devices: 21.8 us -> 24.8 us
  waiting for transfers between devices: 14.9 us -> 12.5 us
  other arithmetic: 4.14 us -> 2.82 us
    pallas_call x3, Pallas kernels: 15.9 us -> 12.6 us  [base_parts(): pl.pallas_call(functools.partial(base_kernel, shifts), grid_spec=pltpu.Pr...]
    ppermute x17, starting transfers between devices: 21.8 us -> 24.8 us  [exchange(): return lax.ppermute(array, axis, [(i, i ^ shift) for i in range(size)])]
    ppermute x17, waiting for transfers between devices: 14.9 us -> 12.5 us  [exchange(): return lax.ppermute(array, axis, [(i, i ^ shift) for i in range(size)])]
    pallas_call x2, Pallas kernels: 3.25 us -> 1.18 us  [grow(): pl.pallas_call(functools.partial(grow_kernel, len(parts), sizes), in_spec...]
    convert_element_type x1, other arithmetic: 2.36 us -> 1.52 us  [send(): part = part.astype(BF)]
    pallas_call x2 -> x4, Pallas kernels: 12.3 us -> 12.8 us  [the longest x3 9.83 us: shrink(): pl.pallas_call(functools.partial(shrink_kernel, len(messages), len(carry)...]
  transfers between devices with their start and end apart: 17 -> 17, of which waited for: 5 -> 5; matrix products, arithmetic and copies ran while one was open for 6% -> 4% of each run, Pallas kernels for 45% -> 42%
where the time goes in v12:
time: 75.9 us; the launch traced here: 75.6 us
  Pallas kernels  33.2 us (44%)
  starting transfers between devices  24.8 us (33%)
  waiting for transfers between devices  12.5 us (16%)
  other arithmetic  2.82 us (4%)
  local copies, waits for them, and re-layouts  1.34 us (2%)
  between operations  0.81 us (1%)
    ppermute x17, starting transfers between devices, exchange(): return lax.ppermute(array, axis, [(i, i ^ shift) for i in range(size)])  24.8 us
    pallas_call x3, Pallas kernels, base_parts(): pl.pallas_call(functools.partial(base_kernel, shifts), grid_spec=pltpu.Pr...  12.6 us
    ppermute x17, waiting for transfers between devices, exchange(): return lax.ppermute(array, axis, [(i, i ^ shift) for i in range(size)])  12.5 us
    pallas_call x3, Pallas kernels, shrink(): pl.pallas_call(functools.partial(shrink_kernel, len(messages), len(carry)...  9.83 us
    pallas_call x1, Pallas kernels, pack(): pl.pallas_call(functools.partial(pack_kernel, (sizes, first_rows, chip_sl...  4.72 us
    pallas_call x1, Pallas kernels, hold(): pl.pallas_call(hold_kernel, grid=(array.shape[0] // 2,), in_specs=[block]...  2.99 us
  transfers between devices with their start and end apart: 17, of which 5 were waited for; matrix products, arithmetic and copies ran while one was open for 4% of the time, Pallas kernels for 42%

profile of v12, /device:TPU:0, one launch (start us, length us, event | category | flops | bytes accessed | tf_op | source)
XLA Modules:
  0.0 75.6 jit_solution(3063664371164691569)
XLA Ops:
  0.5 6.3 %base_parts.3 = (bf16[512,512]{1,0:T(8,128)(2,1)}, bf16[512,512]{1,0:T(8,128)(2,1)}) custom-call(s32[1]{0:T(128)} %bitcast.4.place_ref, bf16[512,2048]{1,0:T(8,128)(2,1)} %tokens_ref.4, bf16[2048,2,1024]{2,1,0:T(2,128)(2,1)} %weight_ref.5), custom_call_target="tpu_custom_call" | custom-call | flops 8589934592 | bytes 4194304 | tf_op jit(solution)/shard_map/base_parts/pallas_call | solution.py:272
  6.8 2.6 %collective-permute-start.12 = (bf16[512,512]{1,0:T(8,128)(2,1)}, bf16[512,512]{1,0:T(8,128)(2,1)}, u32[]{:S(2)}, u32[]{:S(2)}) collective-permute-start(bf16[512,512]{1,0:T(8,128)(2,1)} %get-tuple-element.114), channel_id=1, source_target_pairs={{0,1},{1,0},{2,3},{3,2},{4,5},{5,4},{6,7},{7,6},{8,9},{9,8},{10,11... | collective-permute-start | bytes 1572872 | tf_op jit(solution)/shard_map/ppermute | solution.py:364
  9.3 4.7 %pack_rows.3 = (bf16[176,2048]{1,0:T(8,128)(2,1)S(1)}, bf16[176,2048]{1,0:T(8,128)(2,1)}, bf16[176,2048]{1,0:T(8,128)(2,1)}, bf16[176,2048]{1,0:T(8,128)(2,1)S(1)}, s32[512,128]{1,0:T(8,128)S(1)}) custom-call(s32[1]{0:T(128)} %bitcast.1.place_ref, s32[1,512]{1,0:T(1,128)S(1)} %bitcast.8, s32[1,64]{1,0:T(1,128)S(1)} %bitcast.10, bf16[512,2048]{1,0:T(8,128)(2,1)} %tokens_ref.4), custom_call_target="tpu_custom_call" | custom-call | flops 1000 | bytes 1000 | tf_op jit(solution)/shard_map/pack_rows/pallas_call | solution.py:83
  14.1 1.5 %collective-permute-start.9 = (bf16[176,2048]{1,0:T(8,128)(2,1)}, bf16[176,2048]{1,0:T(8,128)(2,1)S(1)}, u32[]{:S(2)}, u32[]{:S(2)}) collective-permute-start(bf16[176,2048]{1,0:T(8,128)(2,1)} %get-tuple-element.116), channel_id=1, source_target_pairs={{0,8},{4,12},{8,0},{12,4},{16,24},{20,28},{24,16},{28,20},{1,9},{5... | collective-permute-start | bytes 2162696 | tf_op jit(solution)/shard_map/ppermute | solution.py:364
  15.6 1.5 %collective-permute-start.10 = (bf16[176,2048]{1,0:T(8,128)(2,1)}, bf16[176,2048]{1,0:T(8,128)(2,1)S(1)}, u32[]{:S(2)}, u32[]{:S(2)}) collective-permute-start(bf16[176,2048]{1,0:T(8,128)(2,1)} %get-tuple-element.117), channel_id=1, source_target_pairs={{0,16},{4,20},{8,24},{12,28},{16,0},{20,4},{24,8},{28,12},{1,17},{... | collective-permute-start | bytes 2162696 | tf_op jit(solution)/shard_map/ppermute | solution.py:364
  17.1 0.5 collective-permute-start.16
  17.5 4.7 %base_parts.4 = f32[512,512]{1,0:T(8,128)} custom-call(s32[1]{0:T(128)} %bitcast.4.place_ref, bf16[512,2048]{1,0:T(8,128)(2,1)} %tokens_ref.4, bf16[2048,2,1024]{2,1,0:T(2,128)(2,1)} %weight_ref.5), custom_call_target="tpu_custom_call" | custom-call | flops 4294967296 | bytes 4194304 | tf_op jit(solution)/shard_map/base_parts/pallas_call | solution.py:272
  22.4 1.5 %add_convert_fusion = bf16[512,512]{1,0:T(8,128)(2,1)S(1)} fusion(f32[512,512]{1,0:T(8,128)} %base_parts.4, bf16[512,512]{1,0:T(8,128)(2,1)} %collective-permute-done.12), kind=kLoop, calls=%fused_computation.1 | loop fusion | flops 786432 | bytes 2097152 | tf_op jit(solution)/shard_map/convert_element_type | solution.py:421
  24.0 3.0 %collective-permute-start.17 = (bf16[512,512]{1,0:T(8,128)(2,1)S(1)}, bf16[512,512]{1,0:T(8,128)(2,1)S(1)}, u32[]{:S(2)}, u32[]{:S(2)}) collective-permute-start(bf16[512,512]{1,0:T(8,128)(2,1)S(1)} %add_convert_fusion), channel_id=1, source_target_pairs={{0,2},{1,3},{2,0},{3,1},{4,6},{5,7},{6,4},{7,5},{8,10},{9,11},{10,... | collective-permute-start | bytes 1572872 | tf_op jit(solution)/shard_map/ppermute | solution.py:364
  27.0 3.0 %hold_weights.1.refs_2_.refs_3_ = bf16[8,2048,128]{2,1,0:T(8,128)(2,1)S(1)} custom-call(bf16[8,2048,128]{2,1,0:T(8,128)(2,1)} %collective-permute-done.11.source), custom_call_target="tpu_custom_call" | custom-call | flops 1000 | bytes 1000 | tf_op jit(solution)/shard_map/hold_weights/pallas_call | solution.py:186
  30.0 3.0 %shrink_rows.5 = (f32[176,128]{1,0:T(8,128)S(1)}, bf16[176,128]{1,0:T(8,128)(2,1)}, bf16[176,128]{1,0:T(8,128)(2,1)S(1)}, f32[8,128]{1,0:T(8,128)S(1)}) custom-call(s32[1]{0:T(128)} %bitcast.core_ref, bf16[176,2048]{1,0:T(8,128)(2,1)S(1)} %get-tuple-element.118.refs_0_, bf16[8,2048,128]{2,1,0:T(8,128)(2,1)S(1)} %copy-done, ...), custom_call_target="tpu_custom_call" | custom-call | flops 1000 | bytes 1000 | tf_op jit(solution)/shard_map/shrink_rows/pallas_call | solution.py:160
  33.0 0.8 %collective-permute-done.10.refs_1_ = bf16[176,2048]{1,0:T(8,128)(2,1)S(1)} collective-permute-done((bf16[176,2048]{1,0:T(8,128)(2,1)}, bf16[176,2048]{1,0:T(8,128)(2,1)S(1)}, u32[]{:S(2)}, u32[]{:S(2)}) %collective-permute-start.10) | collective-permute-done | bytes 720928 | tf_op jit(solution)/shard_map/ppermute | solution.py:364
  33.8 1.7 %collective-permute-start.14 = (bf16[176,2048]{1,0:T(8,128)(2,1)S(1)}, bf16[176,2048]{1,0:T(8,128)(2,1)S(1)}, u32[]{:S(2)}, u32[]{:S(2)}) collective-permute-start(bf16[176,2048]{1,0:T(8,128)(2,1)S(1)} %get-tuple-element.128), channel_id=1, source_target_pairs={{0,24},{4,28},{8,16},{12,20},{16,8},{20,12},{24,0},{28,4},{1,25},{... | collective-permute-start | bytes 2162696 | tf_op jit(solution)/shard_map/ppermute | solution.py:364
  35.4 4.5 %shrink_rows.6 = (f32[528,128]{1,0:T(8,128)S(1)}, bf16[528,128]{1,0:T(8,128)(2,1)}, bf16[528,128]{1,0:T(8,128)(2,1)S(1)}, f32[8,128]{1,0:T(8,128)S(1)}) custom-call(s32[1]{0:T(128)} %bitcast.core_ref, bf16[176,2048]{1,0:T(8,128)(2,1)S(1)} %collective-permute-done.9.refs_0_, bf16[176,2048]{1,0:T(8,128)(2,1)S(1)} %collective-permute-done.10.refs_1_, ...), custom_call_target="tpu_custom_call" | custom-call | flops 1000 | bytes 1000 | tf_op jit(solution)/shard_map/shrink_rows/pallas_call | solution.py:160
  39.9 1.6 %collective-permute-start.15 = (f32[528,128]{1,0:T(8,128)S(1)}, f32[528,128]{1,0:T(8,128)S(1)}, u32[]{:S(2)}, u32[]{:S(2)}) collective-permute-start(f32[528,128]{1,0:T(8,128)S(1)} %get-tuple-element.129), channel_id=1, source_target_pairs={{0,1},{1,0},{2,3},{3,2},{4,5},{5,4},{6,7},{7,6},{8,9},{9,8},{10,11... | collective-permute-start | bytes 811016 | tf_op jit(solution)/shard_map/ppermute | solution.py:364
  41.5 1.6 %base_parts.5 = f32[512,512]{1,0:T(8,128)S(1)} custom-call(s32[1]{0:T(128)} %bitcast.4.place_ref, bf16[512,2048]{1,0:T(8,128)(2,1)S(1)} %copy-done.1, bf16[2048,2,1024]{2,1,0:T(2,128)(2,1)S(1)} %bitcast.7), custom_call_target="tpu_custom_call" | custom-call | flops 4294967296 | bytes 4194304 | tf_op jit(solution)/shard_map/base_parts/pallas_call | solution.py:272
  43.2 7.4 %collective-permute-done.15 = f32[528,128]{1,0:T(8,128)S(1)} collective-permute-done((f32[528,128]{1,0:T(8,128)S(1)}, f32[528,128]{1,0:T(8,128)S(1)}, u32[]{:S(2)}, u32[]{:S(2)}) %collective-permute-start.15) | collective-permute-done | bytes 270368 | tf_op jit(solution)/shard_map/ppermute | solution.py:364
  50.6 2.9 %collective-permute-start.19 = (bf16[528,128]{1,0:T(8,128)(2,1)S(1)}, bf16[528,128]{1,0:T(8,128)(2,1)S(1)}, u32[]{:S(2)}, u32[]{:S(2)}) collective-permute-start(bf16[528,128]{1,0:T(8,128)(2,1)S(1)} %get-tuple-element.146), channel_id=1, source_target_pairs={{0,2},{1,3},{2,0},{3,1},{4,6},{5,7},{6,4},{7,5},{8,10},{9,11},{10,... | collective-permute-start | bytes 405512 | tf_op jit(solution)/shard_map/ppermute | solution.py:364
  53.5 1.3 %convert_add_fusion = f32[512,512]{1,0:T(8,128)S(1)} fusion(bf16[512,512]{1,0:T(8,128)(2,1)S(1)} %collective-permute-done.17, f32[512,512]{1,0:T(8,128)S(1)} %base_parts.5, bf16[512,512]{1,0:T(8,128)(2,1)} %collective-permute-done.16), kind=kLoop, calls=%fused_computation | loop fusion | flops 1048576 | bytes 3145728 | tf_op jit(solution)/shard_map/add | solution.py:462
  54.8 2.4 %shrink_rows.7 = (f32[176,128]{1,0:T(8,128)S(1)}, bf16[176,128]{1,0:T(8,128)(2,1)S(1)}, bf16[176,128]{1,0:T(8,128)(2,1)S(1)}, f32[8,128]{1,0:T(8,128)S(1)}) custom-call(s32[1]{0:T(128)} %bitcast.core_ref, bf16[176,2048]{1,0:T(8,128)(2,1)S(1)} %collective-permute-done.14.refs_0_, bf16[8,2048,128]{2,1,0:T(8,128)(2,1)S(1)} %copy-done, ...), custom_call_target="tpu_custom_call" | custom-call | flops 1000 | bytes 1000 | tf_op jit(solution)/shard_map/shrink_rows/pallas_call | solution.py:160
  57.1 2.0 %collective-permute-start.24 = (bf16[176,128]{1,0:T(8,128)(2,1)S(1)}, bf16[176,128]{1,0:T(8,128)(2,1)S(1)}, u32[]{:S(2)}, u32[]{:S(2)}) collective-permute-start(bf16[176,128]{1,0:T(8,128)(2,1)S(1)} %get-tuple-element.143), channel_id=1, source_target_pairs={{0,3},{1,2},{2,1},{3,0},{4,7},{5,6},{6,5},{7,4},{8,11},{9,10},{10,... | collective-permute-start | bytes 135176 | tf_op jit(solution)/shard_map/ppermute | solution.py:364
  59.2 2.0 %collective-permute-start.23 = (bf16[176,128]{1,0:T(8,128)(2,1)S(1)}, bf16[176,128]{1,0:T(8,128)(2,1)S(1)}, u32[]{:S(2)}, u32[]{:S(2)}) collective-permute-start(bf16[176,128]{1,0:T(8,128)(2,1)S(1)} %get-tuple-element.143), channel_id=1, source_target_pairs={{0,2},{1,3},{2,0},{3,1},{4,6},{5,7},{6,4},{7,5},{8,10},{9,11},{10,... | collective-permute-start | bytes 135176 | tf_op jit(solution)/shard_map/ppermute | solution.py:364
  61.6 0.8 %grow_rows.4 = (bf16[176,512]{1,0:T(8,128)(2,1)S(1)}, bf16[176,512]{1,0:T(8,128)(2,1)S(1)}, bf16[176,512]{1,0:T(8,128)(2,1)S(1)}) custom-call(s32[1]{0:T(128)} %bitcast.core_ref, f32[528,128]{1,0:T(8,128)S(1)} %get-tuple-element.147.refs_0_, bf16[528,128]{1,0:T(8,128)(2,1)S(1)} %collective-permute-done.19.refs_1_, ...), custom_call_target="tpu_custom_call" | custom-call | flops 1000 | bytes 1000 | tf_op jit(solution)/shard_map/grow_rows/pallas_call | solution.py:234
  62.4 1.4 %collective-permute-start.20 = (bf16[176,512]{1,0:T(8,128)(2,1)S(1)}, bf16[176,512]{1,0:T(8,128)(2,1)S(1)}, u32[]{:S(2)}, u32[]{:S(2)}) collective-permute-start(bf16[176,512]{1,0:T(8,128)(2,1)S(1)} %get-tuple-element.139), channel_id=1, source_target_pairs={{0,8},{4,12},{8,0},{12,4},{16,24},{20,28},{24,16},{28,20},{1,9},{5... | collective-permute-start | bytes 540680 | tf_op jit(solution)/shard_map/ppermute | solution.py:364
  63.8 1.5 %collective-permute-start.21 = (bf16[176,512]{1,0:T(8,128)(2,1)S(1)}, bf16[176,512]{1,0:T(8,128)(2,1)S(1)}, u32[]{:S(2)}, u32[]{:S(2)}) collective-permute-start(bf16[176,512]{1,0:T(8,128)(2,1)S(1)} %get-tuple-element.140), channel_id=1, source_target_pairs={{0,16},{4,20},{8,24},{12,28},{16,0},{20,4},{24,8},{28,12},{1,17},{... | collective-permute-start | bytes 540680 | tf_op jit(solution)/shard_map/ppermute | solution.py:364
  65.7 1.7 %collective-permute-start.25 = (bf16[176,512]{1,0:T(8,128)(2,1)S(1)}, bf16[176,512]{1,0:T(8,128)(2,1)S(1)}, u32[]{:S(2)}, u32[]{:S(2)}) collective-permute-start(bf16[176,512]{1,0:T(8,128)(2,1)S(1)} %grow_rows.5), channel_id=1, source_target_pairs={{0,24},{4,28},{8,16},{12,20},{16,8},{20,12},{24,0},{28,4},{1,25},{... | collective-permute-start | bytes 540680 | tf_op jit(solution)/shard_map/ppermute | solution.py:364
  67.8 0.8 %collective-permute-done.18 = f32[8,128]{1,0:T(8,128)S(1)} collective-permute-done((f32[8,128]{1,0:T(8,128)S(1)}, f32[8,128]{1,0:T(8,128)S(1)}, u32[]{:S(2)}, u32[]{:S(2)}) %collective-permute-start.18) | collective-permute-done | bytes 4128 | tf_op jit(solution)/shard_map/ppermute | solution.py:364
  68.6 0.5 slice.3
  69.8 3.3 %collective-permute-done.21 = bf16[176,512]{1,0:T(8,128)(2,1)S(1)} collective-permute-done((bf16[176,512]{1,0:T(8,128)(2,1)S(1)}, bf16[176,512]{1,0:T(8,128)(2,1)S(1)}, u32[]{:S(2)}, u32[]{:S(2)}) %collective-permute-start.21) | collective-permute-done | bytes 180256 | tf_op jit(solution)/shard_map/ppermute | solution.py:364
  73.1 1.7 %conditional.1 = (bf16[512,2,256]{2,1,0:T(2,128)(2,1)S(1)}) conditional(s32[]{:T(128)} %bitcast.5, (f32[512,512]{1,0:T(8,128)S(1)}, bf16[512,1024]{1,0:T(8,128)(2,1)S(1)}, bf16[176,512]{1,0:T(8,128)(2,1)S(1)}, bf16[176,512]{1,0:T(8,128)(2,1)S(1)}, bf16[176,512]{1,0:T(8,128)(2,1)S(1)}, /*index=5*/bf16[176,512]{1,0:T(8,128)(2,1)S(1)}) %tuple.33, ...), branch_computations={%region_0.1_spmd, %region_1.2_spmd} | conditional | flops 5000 | bytes 7083256 | solution.py:490
  73.1 1.5 %finish_rows.2 = bf16[512,2,256]{2,1,0:T(2,128)(2,1)S(1)} custom-call(f32[512,512]{1,0:T(8,128)S(1)} %get-tuple-element.50.refs_0_, bf16[512,1024]{1,0:T(8,128)(2,1)S(1)} %get-tuple-element.51.refs_1_, bf16[176,512]{1,0:T(8,128)(2,1)S(1)} %get-tuple-element.52.refs_2_, bf16[176,512]{1,0:T(8,128)(2,1)S(1)} %get-tuple-element.53.refs_3_, ...), custom_call_target="tpu_custom_call" | custom-call | flops 1000 | bytes 1000 | tf_op jit(solution)/shard_map/cond/branch_0_fun/finish_rows/pallas_call | solution.py:349
  74.8 0.8 %copy-done.3 = bf16[512,2,256]{2,1,0:T(2,128)(2,1)} copy-done((bf16[512,2,256]{2,1,0:T(2,128)(2,1)}, bf16[512,2,256]{2,1,0:T(2,128)(2,1)S(1)}, u32[]{:S(2)}) %copy-start.3) | copy-done | bytes 524312
  (38 shorter events, 2.0 us)
Async XLA Ops:
  0.0 17.5 %collective-permute-start.11 = (bf16[8,2048,128]{2,1,0:T(8,128)(2,1)}, bf16[8,2048,128]{2,1,0:T(8,128)(2,1)}, u32[]{:S(2)}, u32[]{:S(2)}) collective-permute-start(bf16[8,2048,128]{2,1,0:T(8,128)(2,1)} %refs_1_.3), channel_id=1, source_target_pairs={{0,4},{4,0},{8,12},{12,8},{16,20},{20,16},{24,28},{28,24},{1,5},{5... | collective-permute-start | bytes 12582920 | tf_op jit(solution)/shard_map/ppermute | solution.py:364
  0.5 8.9 %copy-start.4 = (s32[512,1]{0,1:T(1,128)S(1)}, s32[512,1]{0,1:T(1,128)}, u32[]{:S(2)}) copy-start(s32[512,1]{0,1:T(1,128)} %param.9) | copy-start | bytes 6148
  0.5 8.9 %copy-start.5 = (s32[64]{0:T(128)S(1)}, s32[64]{0:T(128)}, u32[]{:S(2)}) copy-start(s32[64]{0:T(128)} %param.10) | copy-start | bytes 772
  6.8 15.7 %collective-permute-start.12 = (bf16[512,512]{1,0:T(8,128)(2,1)}, bf16[512,512]{1,0:T(8,128)(2,1)}, u32[]{:S(2)}, u32[]{:S(2)}) collective-permute-start(bf16[512,512]{1,0:T(8,128)(2,1)} %get-tuple-element.114), channel_id=1, source_target_pairs={{0,1},{1,0},{2,3},{3,2},{4,5},{5,4},{6,7},{7,6},{8,9},{9,8},{10,11... | collective-permute-start | bytes 1572872 | tf_op jit(solution)/shard_map/ppermute | solution.py:364
  14.1 18.9 %collective-permute-start.9 = (bf16[176,2048]{1,0:T(8,128)(2,1)}, bf16[176,2048]{1,0:T(8,128)(2,1)S(1)}, u32[]{:S(2)}, u32[]{:S(2)}) collective-permute-start(bf16[176,2048]{1,0:T(8,128)(2,1)} %get-tuple-element.116), channel_id=1, source_target_pairs={{0,8},{4,12},{8,0},{12,4},{16,24},{20,28},{24,16},{28,20},{1,9},{5... | collective-permute-start | bytes 2162696 | tf_op jit(solution)/shard_map/ppermute | solution.py:364
  15.6 18.2 %collective-permute-start.10 = (bf16[176,2048]{1,0:T(8,128)(2,1)}, bf16[176,2048]{1,0:T(8,128)(2,1)S(1)}, u32[]{:S(2)}, u32[]{:S(2)}) collective-permute-start(bf16[176,2048]{1,0:T(8,128)(2,1)} %get-tuple-element.117), channel_id=1, source_target_pairs={{0,16},{4,20},{8,24},{12,28},{16,0},{20,4},{24,8},{28,12},{1,17},{... | collective-permute-start | bytes 2162696 | tf_op jit(solution)/shard_map/ppermute | solution.py:364
  17.1 36.4 %collective-permute-start.16 = (bf16[512,512]{1,0:T(8,128)(2,1)}, bf16[512,512]{1,0:T(8,128)(2,1)}, u32[]{:S(2)}, u32[]{:S(2)}) collective-permute-start(bf16[512,512]{1,0:T(8,128)(2,1)} %get-tuple-element.132), channel_id=1, source_target_pairs={{0,1},{1,0},{2,3},{3,2},{4,5},{5,4},{6,7},{7,6},{8,9},{9,8},{10,11... | collective-permute-start | bytes 1572872 | tf_op jit(solution)/shard_map/ppermute | solution.py:364
  17.5 17.9 %collective-permute-start.13 = (bf16[8,2,64,256]{3,2,1,0:T(8,128)(2,1)}, bf16[8,2,64,256]{3,2,1,0:T(8,128)(2,1)S(1)}, u32[]{:S(2)}, u32[]{:S(2)}) collective-permute-start(bf16[8,2,64,256]{3,2,1,0:T(8,128)(2,1)} %refs_5_.1), channel_id=1, source_target_pairs={{0,4},{4,0},{8,12},{12,8},{16,20},{20,16},{24,28},{28,24},{1,5},{5... | collective-permute-start | bytes 1572872 | tf_op jit(solution)/shard_map/ppermute | solution.py:364
  23.9 6.0 %copy-start = (bf16[8,2048,128]{2,1,0:T(8,128)(2,1)S(1)}, bf16[8,2048,128]{2,1,0:T(8,128)(2,1)}, u32[]{:S(2)}) copy-start(bf16[8,2048,128]{2,1,0:T(8,128)(2,1)} %refs_1_.3) | copy-start | bytes 12582916
  24.0 29.5 %collective-permute-start.17 = (bf16[512,512]{1,0:T(8,128)(2,1)S(1)}, bf16[512,512]{1,0:T(8,128)(2,1)S(1)}, u32[]{:S(2)}, u32[]{:S(2)}) collective-permute-start(bf16[512,512]{1,0:T(8,128)(2,1)S(1)} %add_convert_fusion), channel_id=1, source_target_pairs={{0,2},{1,3},{2,0},{3,1},{4,6},{5,7},{6,4},{7,5},{8,10},{9,11},{10,... | collective-permute-start | bytes 1572872 | tf_op jit(solution)/shard_map/ppermute | solution.py:364
  30.0 11.5 %slice-start = ((s8[8388608]{0:T(1024)(128)(4,1)}), s8[4194304]{0:T(1024)(128)(4,1)S(1)}, s32[]{:S(2)}) async-start(s8[8388608]{0:T(1024)(128)(4,1)} %bitcast.6), calls=%async_computation | async-start | bytes 8388608
  33.8 21.0 %collective-permute-start.14 = (bf16[176,2048]{1,0:T(8,128)(2,1)S(1)}, bf16[176,2048]{1,0:T(8,128)(2,1)S(1)}, u32[]{:S(2)}, u32[]{:S(2)}) collective-permute-start(bf16[176,2048]{1,0:T(8,128)(2,1)S(1)} %get-tuple-element.128), channel_id=1, source_target_pairs={{0,24},{4,28},{8,16},{12,20},{16,8},{20,12},{24,0},{28,4},{1,25},{... | collective-permute-start | bytes 2162696 | tf_op jit(solution)/shard_map/ppermute | solution.py:364
  35.4 6.1 %slice-start.1 = ((s8[8388608]{0:T(1024)(128)(4,1)}), s8[4194304]{0:T(1024)(128)(4,1)S(1)}, s32[]{:S(2)}) async-start(s8[8388608]{0:T(1024)(128)(4,1)} %bitcast.6), calls=%async_computation.1 | async-start | bytes 8388608
  35.4 6.1 %copy-start.1 = (bf16[512,2048]{1,0:T(8,128)(2,1)S(1)}, bf16[512,2048]{1,0:T(8,128)(2,1)}, u32[]{:S(2)}) copy-start(bf16[512,2048]{1,0:T(8,128)(2,1)} %tokens_ref.4) | copy-start | bytes 6291460
  39.9 10.6 %collective-permute-start.15 = (f32[528,128]{1,0:T(8,128)S(1)}, f32[528,128]{1,0:T(8,128)S(1)}, u32[]{:S(2)}, u32[]{:S(2)}) collective-permute-start(f32[528,128]{1,0:T(8,128)S(1)} %get-tuple-element.129), channel_id=1, source_target_pairs={{0,1},{1,0},{2,3},{3,2},{4,5},{5,4},{6,7},{7,6},{8,9},{9,8},{10,11... | collective-permute-start | bytes 811016 | tf_op jit(solution)/shard_map/ppermute | solution.py:364
  50.6 11.0 %collective-permute-start.19 = (bf16[528,128]{1,0:T(8,128)(2,1)S(1)}, bf16[528,128]{1,0:T(8,128)(2,1)S(1)}, u32[]{:S(2)}, u32[]{:S(2)}) collective-permute-start(bf16[528,128]{1,0:T(8,128)(2,1)S(1)} %get-tuple-element.146), channel_id=1, source_target_pairs={{0,2},{1,3},{2,0},{3,1},{4,6},{5,7},{6,4},{7,5},{8,10},{9,11},{10,... | collective-permute-start | bytes 405512 | tf_op jit(solution)/shard_map/ppermute | solution.py:364
  54.8 6.8 %copy-start.2 = (bf16[8,2,64,256]{3,2,1,0:T(8,128)(2,1)S(1)}, bf16[8,2,64,256]{3,2,1,0:T(8,128)(2,1)}, u32[]{:S(2)}) copy-start(bf16[8,2,64,256]{3,2,1,0:T(8,128)(2,1)} %refs_5_.1) | copy-start | bytes 1572868
  57.1 8.1 %collective-permute-start.24 = (bf16[176,128]{1,0:T(8,128)(2,1)S(1)}, bf16[176,128]{1,0:T(8,128)(2,1)S(1)}, u32[]{:S(2)}, u32[]{:S(2)}) collective-permute-start(bf16[176,128]{1,0:T(8,128)(2,1)S(1)} %get-tuple-element.143), channel_id=1, source_target_pairs={{0,3},{1,2},{2,1},{3,0},{4,7},{5,6},{6,5},{7,4},{8,11},{9,10},{10,... | collective-permute-start | bytes 135176 | tf_op jit(solution)/shard_map/ppermute | solution.py:364
  59.2 6.1 %collective-permute-start.23 = (bf16[176,128]{1,0:T(8,128)(2,1)S(1)}, bf16[176,128]{1,0:T(8,128)(2,1)S(1)}, u32[]{:S(2)}, u32[]{:S(2)}) collective-permute-start(bf16[176,128]{1,0:T(8,128)(2,1)S(1)} %get-tuple-element.143), channel_id=1, source_target_pairs={{0,2},{1,3},{2,0},{3,1},{4,6},{5,7},{6,4},{7,5},{8,10},{9,11},{10,... | collective-permute-start | bytes 135176 | tf_op jit(solution)/shard_map/ppermute | solution.py:364
  61.2 4.1 %collective-permute-start.22 = (bf16[176,128]{1,0:T(8,128)(2,1)S(1)}, bf16[176,128]{1,0:T(8,128)(2,1)S(1)}, u32[]{:S(2)}, u32[]{:S(2)}) collective-permute-start(bf16[176,128]{1,0:T(8,128)(2,1)S(1)} %get-tuple-element.143), channel_id=1, source_target_pairs={{0,1},{1,0},{2,3},{3,2},{4,5},{5,4},{6,7},{7,6},{8,9},{9,8},{10,11... | collective-permute-start | bytes 135176 | tf_op jit(solution)/shard_map/ppermute | solution.py:364
  62.4 7.4 %collective-permute-start.20 = (bf16[176,512]{1,0:T(8,128)(2,1)S(1)}, bf16[176,512]{1,0:T(8,128)(2,1)S(1)}, u32[]{:S(2)}, u32[]{:S(2)}) collective-permute-start(bf16[176,512]{1,0:T(8,128)(2,1)S(1)} %get-tuple-element.139), channel_id=1, source_target_pairs={{0,8},{4,12},{8,0},{12,4},{16,24},{20,28},{24,16},{28,20},{1,9},{5... | collective-permute-start | bytes 540680 | tf_op jit(solution)/shard_map/ppermute | solution.py:364
  63.8 9.4 %collective-permute-start.21 = (bf16[176,512]{1,0:T(8,128)(2,1)S(1)}, bf16[176,512]{1,0:T(8,128)(2,1)S(1)}, u32[]{:S(2)}, u32[]{:S(2)}) collective-permute-start(bf16[176,512]{1,0:T(8,128)(2,1)S(1)} %get-tuple-element.140), channel_id=1, source_target_pairs={{0,16},{4,20},{8,24},{12,28},{16,0},{20,4},{24,8},{28,12},{1,17},{... | collective-permute-start | bytes 540680 | tf_op jit(solution)/shard_map/ppermute | solution.py:364
  65.7 7.4 %collective-permute-start.25 = (bf16[176,512]{1,0:T(8,128)(2,1)S(1)}, bf16[176,512]{1,0:T(8,128)(2,1)S(1)}, u32[]{:S(2)}, u32[]{:S(2)}) collective-permute-start(bf16[176,512]{1,0:T(8,128)(2,1)S(1)} %grow_rows.5), channel_id=1, source_target_pairs={{0,24},{4,28},{8,16},{12,20},{16,8},{20,12},{24,0},{28,4},{1,25},{... | collective-permute-start | bytes 540680 | tf_op jit(solution)/shard_map/ppermute | solution.py:364
  67.5 1.2 %collective-permute-start.18 = (f32[8,128]{1,0:T(8,128)S(1)}, f32[8,128]{1,0:T(8,128)S(1)}, u32[]{:S(2)}, u32[]{:S(2)}) collective-permute-start(f32[8,128]{1,0:T(8,128)S(1)} %max.6), channel_id=1, source_target_pairs={{0,4},{4,0},{8,12},{12,8},{16,20},{20,16},{24,28},{28,24},{1,5},{5... | collective-permute-start | bytes 12296 | tf_op jit(solution)/shard_map/ppermute | solution.py:364
  74.8 0.8 %copy-start.3 = (bf16[512,2,256]{2,1,0:T(2,128)(2,1)}, bf16[512,2,256]{2,1,0:T(2,128)(2,1)S(1)}, u32[]{:S(2)}) copy-start(bf16[512,2,256]{2,1,0:T(2,128)(2,1)S(1)} %get-tuple-element.189) | copy-start | bytes 1572868

commit v13 on v12

--- a/solution.py
+++ b/solution.py
@@ -109,7 +109,7 @@
     kept = carry[0].shape[0] if carried else 0
     total = out.at[kept:, :]
     step = pl.program_id(0)
-    local = 2 * pl.num_programs(0)
+    local = mine.shape[0] * pl.num_programs(0)
     sizes = [m.shape[0] for m in messages]
 
     @pl.when(step == 0)
@@ -137,12 +137,16 @@
     rows = messages[0][...] if count == 1 else jnp.concatenate([m[...] for m in messages], axis=0)
     place = places[...]
     core = core_ref[0]
-    for weights, side in ((mine, core), (sibling, 1 - core)):
-        product = dot(rows, jnp.concatenate([weights[0], weights[1]], axis=1))
-        first = (side * local + 2 * step + 1).astype(F32)
-        total[...] += jnp.where(place == first, product[:, :128], 0.0) + jnp.where(
-            place == first + 1.0, product[:, 128:], 0.0
-        )
+    each = mine.shape[0]
+    every = [weights[e] for weights in (mine, sibling) for e in range(each)]
+    product = dot(rows, jnp.concatenate(every, axis=1))
+    picked = total[...]
+    for k, side in enumerate((core, 1 - core)):
+        first = (side * local + each * step + 1).astype(F32)
+        for e in range(each):
+            start = 128 * (each * k + e)
+            picked = picked + jnp.where(place == first + e, product[:, start:start + 128], 0.0)
+    total[...] = picked
 
     @pl.when(step == pl.num_programs(0) - 1)
     def _():
@@ -153,13 +157,13 @@
     local, width, both = mine.shape
     rows = sum(m.shape[0] for m in messages)
     whole = [pl.BlockSpec(m.shape, lambda i: (0, 0)) for m in messages]
-    pair = pl.BlockSpec((2, width, both), lambda i: (i, 0, 0))
+    pair = pl.BlockSpec((4, width, both), lambda i: (i, 0, 0))
     every = rows + (carry[0].shape[0] if carry else 0)
     keep = pl.BlockSpec((every, both), lambda i: (0, 0))
     kept = [pl.BlockSpec(c.shape, lambda i: (0, 0)) for c in carry]
     return pl.pallas_call(
         functools.partial(shrink_kernel, len(messages), len(carry), flag_lane),
-        grid=(local // 2,),
+        grid=(local // 4,),
         in_specs=[pl.BlockSpec(memory_space=pltpu.SMEM)] + whole + [pair, pair] + kept,
         out_specs=[keep, keep, keep, pl.BlockSpec((8, 128), lambda i: (0, 0))],
         out_shape=[
@@ -345,10 +349,10 @@
     sizes = tuple(tuple(u.shape[0] for u in group) for group in groups)
     rows, both = bases[0].shape
     updates = [u for group in groups for u in group]
-    block = rows // 4
+    block = rows // 2
     return pl.pallas_call(
         functools.partial(finish_kernel, sizes, len(bases)),
-        grid=(4,),
+        grid=(2,),
         in_specs=[pl.BlockSpec((block, x.shape[1]), lambda i: (i, 0)) for x in bases + spreads]
         + [pl.BlockSpec(u.shape, lambda i: (0, 0)) for u in updates],
         out_specs=pl.BlockSpec((block, 2, both // 2), lambda i: (i, 0, 0)),
@@ -481,8 +485,8 @@
         later_sizes, later_rows = (rest,) * chips, (message - 1,) * chips
         packed = pack(chip, adapters, slots, tokens, later_sizes, later_rows, chip_slots)
         group = [packed[0]] + [exchange(packed[m], "dp", 2 * m) for m in range(1, chips)]
-        share, rounded, place, _ = shrink(core, group, adapter_down_weight, down_sibling, flag_lane)
-        shares = [share] + [exchange(rounded, "tensor", z) for z in range(1, blocks)]
+        share, _, place, _ = shrink(core, group, adapter_down_weight, down_sibling, flag_lane)
+        shares = [share] + [exchange(share, "tensor", z) for z in range(1, blocks)]
         grown = grow(core, shares, place, adapter_up_weight, up_sibling, later_sizes)
         back = [grown[0]] + [exchange(grown[m], "dp", 2 * m) for m in range(1, chips)]
         return finish(bases, [spread, spread_of(packed[-1], later_sizes, later_rows)], [updates, back])

time: 75.9 us -> 75 us (0.988)
  Pallas kernels: 33.2 us -> 31.7 us
    pallas_call x3, Pallas kernels: 9.83 us -> 8.73 us  [shrink(): pl.pallas_call(functools.partial(shrink_kernel, len(messages), len(carry)...]
  transfers between devices with their start and end apart: 17 -> 17, of which waited for: 5 -> 5; matrix products, arithmetic and copies ran while one was open for 4% -> 4% of each run, Pallas kernels for 42% -> 41%
where the time goes in v13:
time: 75 us; the launch traced here: 74.7 us
  Pallas kernels  31.7 us (42%)
  starting transfers between devices  25.3 us (34%)
  waiting for transfers between devices  12.7 us (17%)
  other arithmetic  2.82 us (4%)
  local copies, waits for them, and re-layouts  1.34 us (2%)
  between operations  0.81 us (1%)
    ppermute x17, starting transfers between devices, exchange(): return lax.ppermute(array, axis, [(i, i ^ shift) for i in range(size)])  25.3 us
    ppermute x17, waiting for transfers between devices, exchange(): return lax.ppermute(array, axis, [(i, i ^ shift) for i in range(size)])  12.7 us
    pallas_call x3, Pallas kernels, base_parts(): pl.pallas_call(functools.partial(base_kernel, shifts), grid_spec=pltpu.Pr...  12.6 us
    pallas_call x3, Pallas kernels, shrink(): pl.pallas_call(functools.partial(shrink_kernel, len(messages), len(carry)...  8.73 us
    pallas_call x1, Pallas kernels, pack(): pl.pallas_call(functools.partial(pack_kernel, (sizes, first_rows, chip_sl...  4.72 us
    pallas_call x1, Pallas kernels, hold(): pl.pallas_call(hold_kernel, grid=(array.shape[0] // 2,), in_specs=[block]...  2.99 us
    convert_element_type x1, other arithmetic, send(): part = part.astype(BF)  1.52 us
  transfers between devices with their start and end apart: 17, of which 5 were waited for; matrix products, arithmetic and copies ran while one was open for 4% of the time, Pallas kernels for 41%

profile of v13, /device:TPU:0, one launch (start us, length us, event | category | flops | bytes accessed | tf_op | source)
XLA Modules:
  0.0 74.7 jit_solution(13869035617746158759)
XLA Ops:
  0.5 6.3 %base_parts.3 = (bf16[512,512]{1,0:T(8,128)(2,1)}, bf16[512,512]{1,0:T(8,128)(2,1)}) custom-call(s32[1]{0:T(128)} %bitcast.4.place_ref, bf16[512,2048]{1,0:T(8,128)(2,1)} %tokens_ref.4, bf16[2048,2,1024]{2,1,0:T(2,128)(2,1)} %weight_ref.5), custom_call_target="tpu_custom_call" | custom-call | flops 8589934592 | bytes 4194304 | tf_op jit(solution)/shard_map/base_parts/pallas_call | solution.py:276
  6.8 2.6 %collective-permute-start.12 = (bf16[512,512]{1,0:T(8,128)(2,1)}, bf16[512,512]{1,0:T(8,128)(2,1)}, u32[]{:S(2)}, u32[]{:S(2)}) collective-permute-start(bf16[512,512]{1,0:T(8,128)(2,1)} %get-tuple-element.113), channel_id=1, source_target_pairs={{0,1},{1,0},{2,3},{3,2},{4,5},{5,4},{6,7},{7,6},{8,9},{9,8},{10,11... | collective-permute-start | bytes 1572872 | tf_op jit(solution)/shard_map/ppermute | solution.py:368
  9.3 4.7 %pack_rows.3 = (bf16[176,2048]{1,0:T(8,128)(2,1)S(1)}, bf16[176,2048]{1,0:T(8,128)(2,1)}, bf16[176,2048]{1,0:T(8,128)(2,1)}, bf16[176,2048]{1,0:T(8,128)(2,1)S(1)}, s32[512,128]{1,0:T(8,128)S(1)}) custom-call(s32[1]{0:T(128)} %bitcast.1.place_ref, s32[1,512]{1,0:T(1,128)S(1)} %bitcast.8, s32[1,64]{1,0:T(1,128)S(1)} %bitcast.10, bf16[512,2048]{1,0:T(8,128)(2,1)} %tokens_ref.4), custom_call_target="tpu_custom_call" | custom-call | flops 1000 | bytes 1000 | tf_op jit(solution)/shard_map/pack_rows/pallas_call | solution.py:83
  14.1 1.5 %collective-permute-start.9 = (bf16[176,2048]{1,0:T(8,128)(2,1)}, bf16[176,2048]{1,0:T(8,128)(2,1)S(1)}, u32[]{:S(2)}, u32[]{:S(2)}) collective-permute-start(bf16[176,2048]{1,0:T(8,128)(2,1)} %get-tuple-element.115), channel_id=1, source_target_pairs={{0,8},{4,12},{8,0},{12,4},{16,24},{20,28},{24,16},{28,20},{1,9},{5... | collective-permute-start | bytes 2162696 | tf_op jit(solution)/shard_map/ppermute | solution.py:368
  15.6 1.5 %collective-permute-start.10 = (bf16[176,2048]{1,0:T(8,128)(2,1)}, bf16[176,2048]{1,0:T(8,128)(2,1)S(1)}, u32[]{:S(2)}, u32[]{:S(2)}) collective-permute-start(bf16[176,2048]{1,0:T(8,128)(2,1)} %get-tuple-element.116), channel_id=1, source_target_pairs={{0,16},{4,20},{8,24},{12,28},{16,0},{20,4},{24,8},{28,12},{1,17},{... | collective-permute-start | bytes 2162696 | tf_op jit(solution)/shard_map/ppermute | solution.py:368
  17.5 4.7 %base_parts.4 = f32[512,512]{1,0:T(8,128)} custom-call(s32[1]{0:T(128)} %bitcast.4.place_ref, bf16[512,2048]{1,0:T(8,128)(2,1)} %tokens_ref.4, bf16[2048,2,1024]{2,1,0:T(2,128)(2,1)} %weight_ref.5), custom_call_target="tpu_custom_call" | custom-call | flops 4294967296 | bytes 4194304 | tf_op jit(solution)/shard_map/base_parts/pallas_call | solution.py:276
  22.4 1.5 %add_convert_fusion = bf16[512,512]{1,0:T(8,128)(2,1)S(1)} fusion(f32[512,512]{1,0:T(8,128)} %base_parts.4, bf16[512,512]{1,0:T(8,128)(2,1)} %collective-permute-done.12), kind=kLoop, calls=%fused_computation.1 | loop fusion | flops 786432 | bytes 2097152 | tf_op jit(solution)/shard_map/convert_element_type | solution.py:425
  24.0 3.0 %collective-permute-start.17 = (bf16[512,512]{1,0:T(8,128)(2,1)S(1)}, bf16[512,512]{1,0:T(8,128)(2,1)S(1)}, u32[]{:S(2)}, u32[]{:S(2)}) collective-permute-start(bf16[512,512]{1,0:T(8,128)(2,1)S(1)} %add_convert_fusion), channel_id=1, source_target_pairs={{0,2},{1,3},{2,0},{3,1},{4,6},{5,7},{6,4},{7,5},{8,10},{9,11},{10,... | collective-permute-start | bytes 1572872 | tf_op jit(solution)/shard_map/ppermute | solution.py:368
  27.0 3.0 %hold_weights.1.refs_2_.refs_3_ = bf16[8,2048,128]{2,1,0:T(8,128)(2,1)S(1)} custom-call(bf16[8,2048,128]{2,1,0:T(8,128)(2,1)} %collective-permute-done.11.source), custom_call_target="tpu_custom_call" | custom-call | flops 1000 | bytes 1000 | tf_op jit(solution)/shard_map/hold_weights/pallas_call | solution.py:190
  30.0 2.6 %shrink_rows.5 = (f32[176,128]{1,0:T(8,128)S(1)}, bf16[176,128]{1,0:T(8,128)(2,1)}, bf16[176,128]{1,0:T(8,128)(2,1)S(1)}, f32[8,128]{1,0:T(8,128)S(1)}) custom-call(s32[1]{0:T(128)} %bitcast.core_ref, bf16[176,2048]{1,0:T(8,128)(2,1)S(1)} %get-tuple-element.117.refs_0_, bf16[8,2048,128]{2,1,0:T(8,128)(2,1)S(1)} %copy-done, ...), custom_call_target="tpu_custom_call" | custom-call | flops 1000 | bytes 1000 | tf_op jit(solution)/shard_map/shrink_rows/pallas_call | solution.py:164
  32.6 1.1 %collective-permute-done.10.refs_1_ = bf16[176,2048]{1,0:T(8,128)(2,1)S(1)} collective-permute-done((bf16[176,2048]{1,0:T(8,128)(2,1)}, bf16[176,2048]{1,0:T(8,128)(2,1)S(1)}, u32[]{:S(2)}, u32[]{:S(2)}) %collective-permute-start.10) | collective-permute-done | bytes 720928 | tf_op jit(solution)/shard_map/ppermute | solution.py:368
  33.8 1.5 %collective-permute-start.14 = (bf16[176,2048]{1,0:T(8,128)(2,1)S(1)}, bf16[176,2048]{1,0:T(8,128)(2,1)S(1)}, u32[]{:S(2)}, u32[]{:S(2)}) collective-permute-start(bf16[176,2048]{1,0:T(8,128)(2,1)S(1)} %get-tuple-element.127), channel_id=1, source_target_pairs={{0,24},{4,28},{8,16},{12,20},{16,8},{20,12},{24,0},{28,4},{1,25},{... | collective-permute-start | bytes 2162696 | tf_op jit(solution)/shard_map/ppermute | solution.py:368
  35.3 4.1 %shrink_rows.6 = (f32[528,128]{1,0:T(8,128)S(1)}, bf16[528,128]{1,0:T(8,128)(2,1)}, bf16[528,128]{1,0:T(8,128)(2,1)S(1)}, f32[8,128]{1,0:T(8,128)S(1)}) custom-call(s32[1]{0:T(128)} %bitcast.core_ref, bf16[176,2048]{1,0:T(8,128)(2,1)S(1)} %collective-permute-done.9.refs_0_, bf16[176,2048]{1,0:T(8,128)(2,1)S(1)} %collective-permute-done.10.refs_1_, ...), custom_call_target="tpu_custom_call" | custom-call | flops 1000 | bytes 1000 | tf_op jit(solution)/shard_map/shrink_rows/pallas_call | solution.py:164
  39.4 1.4 %collective-permute-start.15 = (f32[528,128]{1,0:T(8,128)S(1)}, f32[528,128]{1,0:T(8,128)S(1)}, u32[]{:S(2)}, u32[]{:S(2)}) collective-permute-start(f32[528,128]{1,0:T(8,128)S(1)} %get-tuple-element.128), channel_id=1, source_target_pairs={{0,1},{1,0},{2,3},{3,2},{4,5},{5,4},{6,7},{7,6},{8,9},{9,8},{10,11... | collective-permute-start | bytes 811016 | tf_op jit(solution)/shard_map/ppermute | solution.py:368
  40.8 1.6 %base_parts.5 = f32[512,512]{1,0:T(8,128)S(1)} custom-call(s32[1]{0:T(128)} %bitcast.4.place_ref, bf16[512,2048]{1,0:T(8,128)(2,1)S(1)} %copy-done.1, bf16[2048,2,1024]{2,1,0:T(2,128)(2,1)S(1)} %bitcast.7), custom_call_target="tpu_custom_call" | custom-call | flops 4294967296 | bytes 4194304 | tf_op jit(solution)/shard_map/base_parts/pallas_call | solution.py:276
  42.5 7.3 %collective-permute-done.15 = f32[528,128]{1,0:T(8,128)S(1)} collective-permute-done((f32[528,128]{1,0:T(8,128)S(1)}, f32[528,128]{1,0:T(8,128)S(1)}, u32[]{:S(2)}, u32[]{:S(2)}) %collective-permute-start.15) | collective-permute-done | bytes 270368 | tf_op jit(solution)/shard_map/ppermute | solution.py:368
  49.7 3.6 %collective-permute-start.19 = (bf16[528,128]{1,0:T(8,128)(2,1)S(1)}, bf16[528,128]{1,0:T(8,128)(2,1)S(1)}, u32[]{:S(2)}, u32[]{:S(2)}) collective-permute-start(bf16[528,128]{1,0:T(8,128)(2,1)S(1)} %get-tuple-element.145), channel_id=1, source_target_pairs={{0,2},{1,3},{2,0},{3,1},{4,6},{5,7},{6,4},{7,5},{8,10},{9,11},{10,... | collective-permute-start | bytes 405512 | tf_op jit(solution)/shard_map/ppermute | solution.py:368
  53.3 1.3 %convert_add_fusion = f32[512,512]{1,0:T(8,128)S(1)} fusion(bf16[512,512]{1,0:T(8,128)(2,1)S(1)} %collective-permute-done.17, f32[512,512]{1,0:T(8,128)S(1)} %base_parts.5, bf16[512,512]{1,0:T(8,128)(2,1)} %collective-permute-done.16), kind=kLoop, calls=%fused_computation | loop fusion | flops 1048576 | bytes 3145728 | tf_op jit(solution)/shard_map/add | solution.py:466
  54.6 2.0 %shrink_rows.7 = (f32[176,128]{1,0:T(8,128)S(1)}, bf16[176,128]{1,0:T(8,128)(2,1)S(1)}, bf16[176,128]{1,0:T(8,128)(2,1)S(1)}, f32[8,128]{1,0:T(8,128)S(1)}) custom-call(s32[1]{0:T(128)} %bitcast.core_ref, bf16[176,2048]{1,0:T(8,128)(2,1)S(1)} %collective-permute-done.14.refs_0_, bf16[8,2048,128]{2,1,0:T(8,128)(2,1)S(1)} %copy-done, ...), custom_call_target="tpu_custom_call" | custom-call | flops 1000 | bytes 1000 | tf_op jit(solution)/shard_map/shrink_rows/pallas_call | solution.py:164
  56.6 1.8 %collective-permute-start.24 = (bf16[176,128]{1,0:T(8,128)(2,1)S(1)}, bf16[176,128]{1,0:T(8,128)(2,1)S(1)}, u32[]{:S(2)}, u32[]{:S(2)}) collective-permute-start(bf16[176,128]{1,0:T(8,128)(2,1)S(1)} %get-tuple-element.142), channel_id=1, source_target_pairs={{0,3},{1,2},{2,1},{3,0},{4,7},{5,6},{6,5},{7,4},{8,11},{9,10},{10,... | collective-permute-start | bytes 135176 | tf_op jit(solution)/shard_map/ppermute | solution.py:368
  58.4 2.0 %collective-permute-start.23 = (bf16[176,128]{1,0:T(8,128)(2,1)S(1)}, bf16[176,128]{1,0:T(8,128)(2,1)S(1)}, u32[]{:S(2)}, u32[]{:S(2)}) collective-permute-start(bf16[176,128]{1,0:T(8,128)(2,1)S(1)} %get-tuple-element.142), channel_id=1, source_target_pairs={{0,2},{1,3},{2,0},{3,1},{4,6},{5,7},{6,4},{7,5},{8,10},{9,11},{10,... | collective-permute-start | bytes 135176 | tf_op jit(solution)/shard_map/ppermute | solution.py:368
  60.4 0.6 collective-permute-start.22
  61.1 0.8 %grow_rows.4 = (bf16[176,512]{1,0:T(8,128)(2,1)S(1)}, bf16[176,512]{1,0:T(8,128)(2,1)S(1)}, bf16[176,512]{1,0:T(8,128)(2,1)S(1)}) custom-call(s32[1]{0:T(128)} %bitcast.core_ref, f32[528,128]{1,0:T(8,128)S(1)} %get-tuple-element.146.refs_0_, bf16[528,128]{1,0:T(8,128)(2,1)S(1)} %collective-permute-done.19.refs_1_, ...), custom_call_target="tpu_custom_call" | custom-call | flops 1000 | bytes 1000 | tf_op jit(solution)/shard_map/grow_rows/pallas_call | solution.py:238
  61.8 1.6 %collective-permute-start.20 = (bf16[176,512]{1,0:T(8,128)(2,1)S(1)}, bf16[176,512]{1,0:T(8,128)(2,1)S(1)}, u32[]{:S(2)}, u32[]{:S(2)}) collective-permute-start(bf16[176,512]{1,0:T(8,128)(2,1)S(1)} %get-tuple-element.138), channel_id=1, source_target_pairs={{0,8},{4,12},{8,0},{12,4},{16,24},{20,28},{24,16},{28,20},{1,9},{5... | collective-permute-start | bytes 540680 | tf_op jit(solution)/shard_map/ppermute | solution.py:368
  63.4 1.5 %collective-permute-start.21 = (bf16[176,512]{1,0:T(8,128)(2,1)S(1)}, bf16[176,512]{1,0:T(8,128)(2,1)S(1)}, u32[]{:S(2)}, u32[]{:S(2)}) collective-permute-start(bf16[176,512]{1,0:T(8,128)(2,1)S(1)} %get-tuple-element.139), channel_id=1, source_target_pairs={{0,16},{4,20},{8,24},{12,28},{16,0},{20,4},{24,8},{28,12},{1,17},{... | collective-permute-start | bytes 540680 | tf_op jit(solution)/shard_map/ppermute | solution.py:368
  65.4 1.8 %collective-permute-start.25 = (bf16[176,512]{1,0:T(8,128)(2,1)S(1)}, bf16[176,512]{1,0:T(8,128)(2,1)S(1)}, u32[]{:S(2)}, u32[]{:S(2)}) collective-permute-start(bf16[176,512]{1,0:T(8,128)(2,1)S(1)} %grow_rows.5), channel_id=1, source_target_pairs={{0,24},{4,28},{8,16},{12,20},{16,8},{20,12},{24,0},{28,4},{1,25},{... | collective-permute-start | bytes 540680 | tf_op jit(solution)/shard_map/ppermute | solution.py:368
  67.5 0.8 %collective-permute-done.18 = f32[8,128]{1,0:T(8,128)S(1)} collective-permute-done((f32[8,128]{1,0:T(8,128)S(1)}, f32[8,128]{1,0:T(8,128)S(1)}, u32[]{:S(2)}, u32[]{:S(2)}) %collective-permute-start.18) | collective-permute-done | bytes 4128 | tf_op jit(solution)/shard_map/ppermute | solution.py:368
  68.3 0.5 slice.3
  69.5 3.3 %collective-permute-done.21 = bf16[176,512]{1,0:T(8,128)(2,1)S(1)} collective-permute-done((bf16[176,512]{1,0:T(8,128)(2,1)S(1)}, bf16[176,512]{1,0:T(8,128)(2,1)S(1)}, u32[]{:S(2)}, u32[]{:S(2)}) %collective-permute-start.21) | collective-permute-done | bytes 180256 | tf_op jit(solution)/shard_map/ppermute | solution.py:368
  72.8 1.1 %conditional.1 = (bf16[512,2,256]{2,1,0:T(2,128)(2,1)S(1)}) conditional(s32[]{:T(128)} %bitcast.5, (f32[512,512]{1,0:T(8,128)S(1)}, bf16[512,1024]{1,0:T(8,128)(2,1)S(1)}, bf16[176,512]{1,0:T(8,128)(2,1)S(1)}, bf16[176,512]{1,0:T(8,128)(2,1)S(1)}, bf16[176,512]{1,0:T(8,128)(2,1)S(1)}, /*index=5*/bf16[176,512]{1,0:T(8,128)(2,1)S(1)}) %tuple.33, ...), branch_computations={%region_0.1_spmd, %region_1.2_spmd} | conditional | flops 5000 | bytes 8262904 | solution.py:494
  72.8 1.1 %finish_rows.2 = bf16[512,2,256]{2,1,0:T(2,128)(2,1)S(1)} custom-call(f32[512,512]{1,0:T(8,128)S(1)} %get-tuple-element.50.refs_0_, bf16[512,1024]{1,0:T(8,128)(2,1)S(1)} %get-tuple-element.51.refs_1_, bf16[176,512]{1,0:T(8,128)(2,1)S(1)} %get-tuple-element.52.refs_2_, bf16[176,512]{1,0:T(8,128)(2,1)S(1)} %get-tuple-element.53.refs_3_, ...), custom_call_target="tpu_custom_call" | custom-call | flops 1000 | bytes 1000 | tf_op jit(solution)/shard_map/cond/branch_0_fun/finish_rows/pallas_call | solution.py:353
  73.9 0.8 %copy-done.3 = bf16[512,2,256]{2,1,0:T(2,128)(2,1)} copy-done((bf16[512,2,256]{2,1,0:T(2,128)(2,1)}, bf16[512,2,256]{2,1,0:T(2,128)(2,1)S(1)}, u32[]{:S(2)}) %copy-start.3) | copy-done | bytes 524312
  (38 shorter events, 2.0 us)
Async XLA Ops:
  0.0 17.5 %collective-permute-start.11 = (bf16[8,2048,128]{2,1,0:T(8,128)(2,1)}, bf16[8,2048,128]{2,1,0:T(8,128)(2,1)}, u32[]{:S(2)}, u32[]{:S(2)}) collective-permute-start(bf16[8,2048,128]{2,1,0:T(8,128)(2,1)} %refs_1_.3), channel_id=1, source_target_pairs={{0,4},{4,0},{8,12},{12,8},{16,20},{20,16},{24,28},{28,24},{1,5},{5... | collective-permute-start | bytes 12582920 | tf_op jit(solution)/shard_map/ppermute | solution.py:368
  0.5 8.9 %copy-start.4 = (s32[512,1]{0,1:T(1,128)S(1)}, s32[512,1]{0,1:T(1,128)}, u32[]{:S(2)}) copy-start(s32[512,1]{0,1:T(1,128)} %param.9) | copy-start | bytes 6148
  0.5 8.9 %copy-start.5 = (s32[64]{0:T(128)S(1)}, s32[64]{0:T(128)}, u32[]{:S(2)}) copy-start(s32[64]{0:T(128)} %param.10) | copy-start | bytes 772
  6.8 15.7 %collective-permute-start.12 = (bf16[512,512]{1,0:T(8,128)(2,1)}, bf16[512,512]{1,0:T(8,128)(2,1)}, u32[]{:S(2)}, u32[]{:S(2)}) collective-permute-start(bf16[512,512]{1,0:T(8,128)(2,1)} %get-tuple-element.113), channel_id=1, source_target_pairs={{0,1},{1,0},{2,3},{3,2},{4,5},{5,4},{6,7},{7,6},{8,9},{9,8},{10,11... | collective-permute-start | bytes 1572872 | tf_op jit(solution)/shard_map/ppermute | solution.py:368
  14.1 18.6 %collective-permute-start.9 = (bf16[176,2048]{1,0:T(8,128)(2,1)}, bf16[176,2048]{1,0:T(8,128)(2,1)S(1)}, u32[]{:S(2)}, u32[]{:S(2)}) collective-permute-start(bf16[176,2048]{1,0:T(8,128)(2,1)} %get-tuple-element.115), channel_id=1, source_target_pairs={{0,8},{4,12},{8,0},{12,4},{16,24},{20,28},{24,16},{28,20},{1,9},{5... | collective-permute-start | bytes 2162696 | tf_op jit(solution)/shard_map/ppermute | solution.py:368
  15.6 18.2 %collective-permute-start.10 = (bf16[176,2048]{1,0:T(8,128)(2,1)}, bf16[176,2048]{1,0:T(8,128)(2,1)S(1)}, u32[]{:S(2)}, u32[]{:S(2)}) collective-permute-start(bf16[176,2048]{1,0:T(8,128)(2,1)} %get-tuple-element.116), channel_id=1, source_target_pairs={{0,16},{4,20},{8,24},{12,28},{16,0},{20,4},{24,8},{28,12},{1,17},{... | collective-permute-start | bytes 2162696 | tf_op jit(solution)/shard_map/ppermute | solution.py:368
  17.1 36.2 %collective-permute-start.16 = (bf16[512,512]{1,0:T(8,128)(2,1)}, bf16[512,512]{1,0:T(8,128)(2,1)}, u32[]{:S(2)}, u32[]{:S(2)}) collective-permute-start(bf16[512,512]{1,0:T(8,128)(2,1)} %get-tuple-element.131), channel_id=1, source_target_pairs={{0,1},{1,0},{2,3},{3,2},{4,5},{5,4},{6,7},{7,6},{8,9},{9,8},{10,11... | collective-permute-start | bytes 1572872 | tf_op jit(solution)/shard_map/ppermute | solution.py:368
  17.5 17.7 %collective-permute-start.13 = (bf16[8,2,64,256]{3,2,1,0:T(8,128)(2,1)}, bf16[8,2,64,256]{3,2,1,0:T(8,128)(2,1)S(1)}, u32[]{:S(2)}, u32[]{:S(2)}) collective-permute-start(bf16[8,2,64,256]{3,2,1,0:T(8,128)(2,1)} %refs_5_.1), channel_id=1, source_target_pairs={{0,4},{4,0},{8,12},{12,8},{16,20},{20,16},{24,28},{28,24},{1,5},{5... | collective-permute-start | bytes 1572872 | tf_op jit(solution)/shard_map/ppermute | solution.py:368
  23.9 6.0 %copy-start = (bf16[8,2048,128]{2,1,0:T(8,128)(2,1)S(1)}, bf16[8,2048,128]{2,1,0:T(8,128)(2,1)}, u32[]{:S(2)}) copy-start(bf16[8,2048,128]{2,1,0:T(8,128)(2,1)} %refs_1_.3) | copy-start | bytes 12582916
  24.0 29.4 %collective-permute-start.17 = (bf16[512,512]{1,0:T(8,128)(2,1)S(1)}, bf16[512,512]{1,0:T(8,128)(2,1)S(1)}, u32[]{:S(2)}, u32[]{:S(2)}) collective-permute-start(bf16[512,512]{1,0:T(8,128)(2,1)S(1)} %add_convert_fusion), channel_id=1, source_target_pairs={{0,2},{1,3},{2,0},{3,1},{4,6},{5,7},{6,4},{7,5},{8,10},{9,11},{10,... | collective-permute-start | bytes 1572872 | tf_op jit(solution)/shard_map/ppermute | solution.py:368
  30.0 10.8 %slice-start = ((s8[8388608]{0:T(1024)(128)(4,1)}), s8[4194304]{0:T(1024)(128)(4,1)S(1)}, s32[]{:S(2)}) async-start(s8[8388608]{0:T(1024)(128)(4,1)} %bitcast.6), calls=%async_computation | async-start | bytes 8388608
  33.8 20.8 %collective-permute-start.14 = (bf16[176,2048]{1,0:T(8,128)(2,1)S(1)}, bf16[176,2048]{1,0:T(8,128)(2,1)S(1)}, u32[]{:S(2)}, u32[]{:S(2)}) collective-permute-start(bf16[176,2048]{1,0:T(8,128)(2,1)S(1)} %get-tuple-element.127), channel_id=1, source_target_pairs={{0,24},{4,28},{8,16},{12,20},{16,8},{20,12},{24,0},{28,4},{1,25},{... | collective-permute-start | bytes 2162696 | tf_op jit(solution)/shard_map/ppermute | solution.py:368
  35.2 5.5 %slice-start.1 = ((s8[8388608]{0:T(1024)(128)(4,1)}), s8[4194304]{0:T(1024)(128)(4,1)S(1)}, s32[]{:S(2)}) async-start(s8[8388608]{0:T(1024)(128)(4,1)} %bitcast.6), calls=%async_computation.1 | async-start | bytes 8388608
  35.3 5.5 %copy-start.1 = (bf16[512,2048]{1,0:T(8,128)(2,1)S(1)}, bf16[512,2048]{1,0:T(8,128)(2,1)}, u32[]{:S(2)}) copy-start(bf16[512,2048]{1,0:T(8,128)(2,1)} %tokens_ref.4) | copy-start | bytes 6291460
  39.4 10.3 %collective-permute-start.15 = (f32[528,128]{1,0:T(8,128)S(1)}, f32[528,128]{1,0:T(8,128)S(1)}, u32[]{:S(2)}, u32[]{:S(2)}) collective-permute-start(f32[528,128]{1,0:T(8,128)S(1)} %get-tuple-element.128), channel_id=1, source_target_pairs={{0,1},{1,0},{2,3},{3,2},{4,5},{5,4},{6,7},{7,6},{8,9},{9,8},{10,11... | collective-permute-start | bytes 811016 | tf_op jit(solution)/shard_map/ppermute | solution.py:368
  49.7 11.3 %collective-permute-start.19 = (bf16[528,128]{1,0:T(8,128)(2,1)S(1)}, bf16[528,128]{1,0:T(8,128)(2,1)S(1)}, u32[]{:S(2)}, u32[]{:S(2)}) collective-permute-start(bf16[528,128]{1,0:T(8,128)(2,1)S(1)} %get-tuple-element.145), channel_id=1, source_target_pairs={{0,2},{1,3},{2,0},{3,1},{4,6},{5,7},{6,4},{7,5},{8,10},{9,11},{10,... | collective-permute-start | bytes 405512 | tf_op jit(solution)/shard_map/ppermute | solution.py:368
  54.6 6.5 %copy-start.2 = (bf16[8,2,64,256]{3,2,1,0:T(8,128)(2,1)S(1)}, bf16[8,2,64,256]{3,2,1,0:T(8,128)(2,1)}, u32[]{:S(2)}) copy-start(bf16[8,2,64,256]{3,2,1,0:T(8,128)(2,1)} %refs_5_.1) | copy-start | bytes 1572868
  56.6 8.3 %collective-permute-start.24 = (bf16[176,128]{1,0:T(8,128)(2,1)S(1)}, bf16[176,128]{1,0:T(8,128)(2,1)S(1)}, u32[]{:S(2)}, u32[]{:S(2)}) collective-permute-start(bf16[176,128]{1,0:T(8,128)(2,1)S(1)} %get-tuple-element.142), channel_id=1, source_target_pairs={{0,3},{1,2},{2,1},{3,0},{4,7},{5,6},{6,5},{7,4},{8,11},{9,10},{10,... | collective-permute-start | bytes 135176 | tf_op jit(solution)/shard_map/ppermute | solution.py:368
  58.4 6.5 %collective-permute-start.23 = (bf16[176,128]{1,0:T(8,128)(2,1)S(1)}, bf16[176,128]{1,0:T(8,128)(2,1)S(1)}, u32[]{:S(2)}, u32[]{:S(2)}) collective-permute-start(bf16[176,128]{1,0:T(8,128)(2,1)S(1)} %get-tuple-element.142), channel_id=1, source_target_pairs={{0,2},{1,3},{2,0},{3,1},{4,6},{5,7},{6,4},{7,5},{8,10},{9,11},{10,... | collective-permute-start | bytes 135176 | tf_op jit(solution)/shard_map/ppermute | solution.py:368
  60.4 4.5 %collective-permute-start.22 = (bf16[176,128]{1,0:T(8,128)(2,1)S(1)}, bf16[176,128]{1,0:T(8,128)(2,1)S(1)}, u32[]{:S(2)}, u32[]{:S(2)}) collective-permute-start(bf16[176,128]{1,0:T(8,128)(2,1)S(1)} %get-tuple-element.142), channel_id=1, source_target_pairs={{0,1},{1,0},{2,3},{3,2},{4,5},{5,4},{6,7},{7,6},{8,9},{9,8},{10,11... | collective-permute-start | bytes 135176 | tf_op jit(solution)/shard_map/ppermute | solution.py:368
  61.8 7.6 %collective-permute-start.20 = (bf16[176,512]{1,0:T(8,128)(2,1)S(1)}, bf16[176,512]{1,0:T(8,128)(2,1)S(1)}, u32[]{:S(2)}, u32[]{:S(2)}) collective-permute-start(bf16[176,512]{1,0:T(8,128)(2,1)S(1)} %get-tuple-element.138), channel_id=1, source_target_pairs={{0,8},{4,12},{8,0},{12,4},{16,24},{20,28},{24,16},{28,20},{1,9},{5... | collective-permute-start | bytes 540680 | tf_op jit(solution)/shard_map/ppermute | solution.py:368
  63.4 9.4 %collective-permute-start.21 = (bf16[176,512]{1,0:T(8,128)(2,1)S(1)}, bf16[176,512]{1,0:T(8,128)(2,1)S(1)}, u32[]{:S(2)}, u32[]{:S(2)}) collective-permute-start(bf16[176,512]{1,0:T(8,128)(2,1)S(1)} %get-tuple-element.139), channel_id=1, source_target_pairs={{0,16},{4,20},{8,24},{12,28},{16,0},{20,4},{24,8},{28,12},{1,17},{... | collective-permute-start | bytes 540680 | tf_op jit(solution)/shard_map/ppermute | solution.py:368
  65.4 7.4 %collective-permute-start.25 = (bf16[176,512]{1,0:T(8,128)(2,1)S(1)}, bf16[176,512]{1,0:T(8,128)(2,1)S(1)}, u32[]{:S(2)}, u32[]{:S(2)}) collective-permute-start(bf16[176,512]{1,0:T(8,128)(2,1)S(1)} %grow_rows.5), channel_id=1, source_target_pairs={{0,24},{4,28},{8,16},{12,20},{16,8},{20,12},{24,0},{28,4},{1,25},{... | collective-permute-start | bytes 540680 | tf_op jit(solution)/shard_map/ppermute | solution.py:368
  67.1 1.2 %collective-permute-start.18 = (f32[8,128]{1,0:T(8,128)S(1)}, f32[8,128]{1,0:T(8,128)S(1)}, u32[]{:S(2)}, u32[]{:S(2)}) collective-permute-start(f32[8,128]{1,0:T(8,128)S(1)} %max.6), channel_id=1, source_target_pairs={{0,4},{4,0},{8,12},{12,8},{16,20},{20,16},{24,28},{28,24},{1,5},{5... | collective-permute-start | bytes 12296 | tf_op jit(solution)/shard_map/ppermute | solution.py:368
  73.9 0.8 %copy-start.3 = (bf16[512,2,256]{2,1,0:T(2,128)(2,1)}, bf16[512,2,256]{2,1,0:T(2,128)(2,1)S(1)}, u32[]{:S(2)}) copy-start(bf16[512,2,256]{2,1,0:T(2,128)(2,1)S(1)} %get-tuple-element.188) | copy-start | bytes 1572868

commit v14 on v13

--- a/solution.py
+++ b/solution.py
@@ -56,8 +56,9 @@
         for m in range(messages):
             padded = round_up(sizes[m], 128)
             target = lax.broadcasted_iota(jnp.int32, (padded, rows), 0)
-            hit = (target == position - first_rows[m]) & (shift == m) & (target < sizes[m] - 1)
-            chosen = hit.astype(F32).astype(BF)
+            wanted = position - first_rows[m]
+            wanted = jnp.where((shift == m) & (wanted < sizes[m] - 1), wanted, -1)
+            chosen = jnp.where(target == wanted, 1.0, 0.0).astype(BF)
             pick[offsets[m]:offsets[m] + sizes[m], :] = chosen[:sizes[m], :]
             places = dot(within8, chosen, ((1,), (1,)))[0:1, :]
             if padded < width:

time: 75 us -> 75 us (level)
  no operation moved by 1% of the time
where the time goes in v14:
time: 75 us; the launch traced here: 74.7 us
  Pallas kernels  31.9 us (43%)
  starting transfers between devices  25 us (33%)
  waiting for transfers between devices  12.7 us (17%)
  other arithmetic  2.82 us (4%)
  local copies, waits for them, and re-layouts  1.34 us (2%)
  between operations  0.81 us (1%)
    ppermute x17, starting transfers between devices, exchange(): return lax.ppermute(array, axis, [(i, i ^ shift) for i in range(size)])  25 us
    ppermute x17, waiting for transfers between devices, exchange(): return lax.ppermute(array, axis, [(i, i ^ shift) for i in range(size)])  12.7 us
    pallas_call x3, Pallas kernels, base_parts(): pl.pallas_call(functools.partial(base_kernel, shifts), grid_spec=pltpu.Pr...  12.6 us
    pallas_call x3, Pallas kernels, shrink(): pl.pallas_call(functools.partial(shrink_kernel, len(messages), len(carry)...  8.73 us
    pallas_call x1, Pallas kernels, pack(): pl.pallas_call(functools.partial(pack_kernel, (sizes, first_rows, chip_sl...  4.92 us
    pallas_call x1, Pallas kernels, hold(): pl.pallas_call(hold_kernel, grid=(array.shape[0] // 2,), in_specs=[block]...  2.99 us
    convert_element_type x1, other arithmetic, send(): part = part.astype(BF)  1.52 us
  transfers between devices with their start and end apart: 17, of which 5 were waited for; matrix products, arithmetic and copies ran while one was open for 4% of the time, Pallas kernels for 41%

profile of v14, /device:TPU:0, one launch (start us, length us, event | category | flops | bytes accessed | tf_op | source)
XLA Modules:
  0.0 74.7 jit_solution(6839159703136819173)
XLA Ops:
  0.0 0.5 collective-permute-start.11
  0.5 6.3 %base_parts.3 = (bf16[512,512]{1,0:T(8,128)(2,1)}, bf16[512,512]{1,0:T(8,128)(2,1)}) custom-call(s32[1]{0:T(128)} %bitcast.4.place_ref, bf16[512,2048]{1,0:T(8,128)(2,1)} %tokens_ref.4, bf16[2048,2,1024]{2,1,0:T(2,128)(2,1)} %weight_ref.5), custom_call_target="tpu_custom_call" | custom-call | flops 8589934592 | bytes 4194304 | tf_op jit(solution)/shard_map/base_parts/pallas_call | solution.py:277
  6.8 2.6 %collective-permute-start.12 = (bf16[512,512]{1,0:T(8,128)(2,1)}, bf16[512,512]{1,0:T(8,128)(2,1)}, u32[]{:S(2)}, u32[]{:S(2)}) collective-permute-start(bf16[512,512]{1,0:T(8,128)(2,1)} %get-tuple-element.113), channel_id=1, source_target_pairs={{0,1},{1,0},{2,3},{3,2},{4,5},{5,4},{6,7},{7,6},{8,9},{9,8},{10,11... | collective-permute-start | bytes 1572872 | tf_op jit(solution)/shard_map/ppermute | solution.py:369
  9.3 4.9 %pack_rows.3 = (bf16[176,2048]{1,0:T(8,128)(2,1)S(1)}, bf16[176,2048]{1,0:T(8,128)(2,1)}, bf16[176,2048]{1,0:T(8,128)(2,1)}, bf16[176,2048]{1,0:T(8,128)(2,1)S(1)}, s32[512,128]{1,0:T(8,128)S(1)}) custom-call(s32[1]{0:T(128)} %bitcast.1.place_ref, s32[1,512]{1,0:T(1,128)S(1)} %bitcast.8, s32[1,64]{1,0:T(1,128)S(1)} %bitcast.10, bf16[512,2048]{1,0:T(8,128)(2,1)} %tokens_ref.4), custom_call_target="tpu_custom_call" | custom-call | flops 1000 | bytes 1000 | tf_op jit(solution)/shard_map/pack_rows/pallas_call | solution.py:84
  14.3 1.5 %collective-permute-start.9 = (bf16[176,2048]{1,0:T(8,128)(2,1)}, bf16[176,2048]{1,0:T(8,128)(2,1)S(1)}, u32[]{:S(2)}, u32[]{:S(2)}) collective-permute-start(bf16[176,2048]{1,0:T(8,128)(2,1)} %get-tuple-element.115), channel_id=1, source_target_pairs={{0,8},{4,12},{8,0},{12,4},{16,24},{20,28},{24,16},{28,20},{1,9},{5... | collective-permute-start | bytes 2162696 | tf_op jit(solution)/shard_map/ppermute | solution.py:369
  15.8 1.5 %collective-permute-start.10 = (bf16[176,2048]{1,0:T(8,128)(2,1)}, bf16[176,2048]{1,0:T(8,128)(2,1)S(1)}, u32[]{:S(2)}, u32[]{:S(2)}) collective-permute-start(bf16[176,2048]{1,0:T(8,128)(2,1)} %get-tuple-element.116), channel_id=1, source_target_pairs={{0,16},{4,20},{8,24},{12,28},{16,0},{20,4},{24,8},{28,12},{1,17},{... | collective-permute-start | bytes 2162696 | tf_op jit(solution)/shard_map/ppermute | solution.py:369
  17.7 4.7 %base_parts.4 = f32[512,512]{1,0:T(8,128)} custom-call(s32[1]{0:T(128)} %bitcast.4.place_ref, bf16[512,2048]{1,0:T(8,128)(2,1)} %tokens_ref.4, bf16[2048,2,1024]{2,1,0:T(2,128)(2,1)} %weight_ref.5), custom_call_target="tpu_custom_call" | custom-call | flops 4294967296 | bytes 4194304 | tf_op jit(solution)/shard_map/base_parts/pallas_call | solution.py:277
  22.4 1.5 %add_convert_fusion = bf16[512,512]{1,0:T(8,128)(2,1)S(1)} fusion(f32[512,512]{1,0:T(8,128)} %base_parts.4, bf16[512,512]{1,0:T(8,128)(2,1)} %collective-permute-done.12), kind=kLoop, calls=%fused_computation.1 | loop fusion | flops 786432 | bytes 2097152 | tf_op jit(solution)/shard_map/convert_element_type | solution.py:426
  24.0 3.0 %collective-permute-start.17 = (bf16[512,512]{1,0:T(8,128)(2,1)S(1)}, bf16[512,512]{1,0:T(8,128)(2,1)S(1)}, u32[]{:S(2)}, u32[]{:S(2)}) collective-permute-start(bf16[512,512]{1,0:T(8,128)(2,1)S(1)} %add_convert_fusion), channel_id=1, source_target_pairs={{0,2},{1,3},{2,0},{3,1},{4,6},{5,7},{6,4},{7,5},{8,10},{9,11},{10,... | collective-permute-start | bytes 1572872 | tf_op jit(solution)/shard_map/ppermute | solution.py:369
  27.0 3.0 %hold_weights.1.refs_2_.refs_3_ = bf16[8,2048,128]{2,1,0:T(8,128)(2,1)S(1)} custom-call(bf16[8,2048,128]{2,1,0:T(8,128)(2,1)} %collective-permute-done.11.source), custom_call_target="tpu_custom_call" | custom-call | flops 1000 | bytes 1000 | tf_op jit(solution)/shard_map/hold_weights/pallas_call | solution.py:191
  30.0 2.6 %shrink_rows.5 = (f32[176,128]{1,0:T(8,128)S(1)}, bf16[176,128]{1,0:T(8,128)(2,1)}, bf16[176,128]{1,0:T(8,128)(2,1)S(1)}, f32[8,128]{1,0:T(8,128)S(1)}) custom-call(s32[1]{0:T(128)} %bitcast.core_ref, bf16[176,2048]{1,0:T(8,128)(2,1)S(1)} %get-tuple-element.117.refs_0_, bf16[8,2048,128]{2,1,0:T(8,128)(2,1)S(1)} %copy-done, ...), custom_call_target="tpu_custom_call" | custom-call | flops 1000 | bytes 1000 | tf_op jit(solution)/shard_map/shrink_rows/pallas_call | solution.py:165
  32.7 1.2 %collective-permute-done.10.refs_1_ = bf16[176,2048]{1,0:T(8,128)(2,1)S(1)} collective-permute-done((bf16[176,2048]{1,0:T(8,128)(2,1)}, bf16[176,2048]{1,0:T(8,128)(2,1)S(1)}, u32[]{:S(2)}, u32[]{:S(2)}) %collective-permute-start.10) | collective-permute-done | bytes 720928 | tf_op jit(solution)/shard_map/ppermute | solution.py:369
  34.0 1.5 %collective-permute-start.14 = (bf16[176,2048]{1,0:T(8,128)(2,1)S(1)}, bf16[176,2048]{1,0:T(8,128)(2,1)S(1)}, u32[]{:S(2)}, u32[]{:S(2)}) collective-permute-start(bf16[176,2048]{1,0:T(8,128)(2,1)S(1)} %get-tuple-element.127), channel_id=1, source_target_pairs={{0,24},{4,28},{8,16},{12,20},{16,8},{20,12},{24,0},{28,4},{1,25},{... | collective-permute-start | bytes 2162696 | tf_op jit(solution)/shard_map/ppermute | solution.py:369
  35.5 4.1 %shrink_rows.6 = (f32[528,128]{1,0:T(8,128)S(1)}, bf16[528,128]{1,0:T(8,128)(2,1)}, bf16[528,128]{1,0:T(8,128)(2,1)S(1)}, f32[8,128]{1,0:T(8,128)S(1)}) custom-call(s32[1]{0:T(128)} %bitcast.core_ref, bf16[176,2048]{1,0:T(8,128)(2,1)S(1)} %collective-permute-done.9.refs_0_, bf16[176,2048]{1,0:T(8,128)(2,1)S(1)} %collective-permute-done.10.refs_1_, ...), custom_call_target="tpu_custom_call" | custom-call | flops 1000 | bytes 1000 | tf_op jit(solution)/shard_map/shrink_rows/pallas_call | solution.py:165
  39.6 1.2 %collective-permute-start.15 = (f32[528,128]{1,0:T(8,128)S(1)}, f32[528,128]{1,0:T(8,128)S(1)}, u32[]{:S(2)}, u32[]{:S(2)}) collective-permute-start(f32[528,128]{1,0:T(8,128)S(1)} %get-tuple-element.128), channel_id=1, source_target_pairs={{0,1},{1,0},{2,3},{3,2},{4,5},{5,4},{6,7},{7,6},{8,9},{9,8},{10,11... | collective-permute-start | bytes 811016 | tf_op jit(solution)/shard_map/ppermute | solution.py:369
  40.8 1.6 %base_parts.5 = f32[512,512]{1,0:T(8,128)S(1)} custom-call(s32[1]{0:T(128)} %bitcast.4.place_ref, bf16[512,2048]{1,0:T(8,128)(2,1)S(1)} %copy-done.1, bf16[2048,2,1024]{2,1,0:T(2,128)(2,1)S(1)} %bitcast.7), custom_call_target="tpu_custom_call" | custom-call | flops 4294967296 | bytes 4194304 | tf_op jit(solution)/shard_map/base_parts/pallas_call | solution.py:277
  42.5 7.3 %collective-permute-done.15 = f32[528,128]{1,0:T(8,128)S(1)} collective-permute-done((f32[528,128]{1,0:T(8,128)S(1)}, f32[528,128]{1,0:T(8,128)S(1)}, u32[]{:S(2)}, u32[]{:S(2)}) %collective-permute-start.15) | collective-permute-done | bytes 270368 | tf_op jit(solution)/shard_map/ppermute | solution.py:369
  49.7 3.8 %collective-permute-start.19 = (bf16[528,128]{1,0:T(8,128)(2,1)S(1)}, bf16[528,128]{1,0:T(8,128)(2,1)S(1)}, u32[]{:S(2)}, u32[]{:S(2)}) collective-permute-start(bf16[528,128]{1,0:T(8,128)(2,1)S(1)} %get-tuple-element.145), channel_id=1, source_target_pairs={{0,2},{1,3},{2,0},{3,1},{4,6},{5,7},{6,4},{7,5},{8,10},{9,11},{10,... | collective-permute-start | bytes 405512 | tf_op jit(solution)/shard_map/ppermute | solution.py:369
  53.6 1.3 %convert_add_fusion = f32[512,512]{1,0:T(8,128)S(1)} fusion(bf16[512,512]{1,0:T(8,128)(2,1)S(1)} %collective-permute-done.17, f32[512,512]{1,0:T(8,128)S(1)} %base_parts.5, bf16[512,512]{1,0:T(8,128)(2,1)} %collective-permute-done.16), kind=kLoop, calls=%fused_computation | loop fusion | flops 1048576 | bytes 3145728 | tf_op jit(solution)/shard_map/add | solution.py:467
  54.8 2.0 %shrink_rows.7 = (f32[176,128]{1,0:T(8,128)S(1)}, bf16[176,128]{1,0:T(8,128)(2,1)S(1)}, bf16[176,128]{1,0:T(8,128)(2,1)S(1)}, f32[8,128]{1,0:T(8,128)S(1)}) custom-call(s32[1]{0:T(128)} %bitcast.core_ref, bf16[176,2048]{1,0:T(8,128)(2,1)S(1)} %collective-permute-done.14.refs_0_, bf16[8,2048,128]{2,1,0:T(8,128)(2,1)S(1)} %copy-done, ...), custom_call_target="tpu_custom_call" | custom-call | flops 1000 | bytes 1000 | tf_op jit(solution)/shard_map/shrink_rows/pallas_call | solution.py:165
  56.8 2.0 %collective-permute-start.24 = (bf16[176,128]{1,0:T(8,128)(2,1)S(1)}, bf16[176,128]{1,0:T(8,128)(2,1)S(1)}, u32[]{:S(2)}, u32[]{:S(2)}) collective-permute-start(bf16[176,128]{1,0:T(8,128)(2,1)S(1)} %get-tuple-element.142), channel_id=1, source_target_pairs={{0,3},{1,2},{2,1},{3,0},{4,7},{5,6},{6,5},{7,4},{8,11},{9,10},{10,... | collective-permute-start | bytes 135176 | tf_op jit(solution)/shard_map/ppermute | solution.py:369
  58.8 2.0 %collective-permute-start.23 = (bf16[176,128]{1,0:T(8,128)(2,1)S(1)}, bf16[176,128]{1,0:T(8,128)(2,1)S(1)}, u32[]{:S(2)}, u32[]{:S(2)}) collective-permute-start(bf16[176,128]{1,0:T(8,128)(2,1)S(1)} %get-tuple-element.142), channel_id=1, source_target_pairs={{0,2},{1,3},{2,0},{3,1},{4,6},{5,7},{6,4},{7,5},{8,10},{9,11},{10,... | collective-permute-start | bytes 135176 | tf_op jit(solution)/shard_map/ppermute | solution.py:369
  61.3 0.8 %grow_rows.4 = (bf16[176,512]{1,0:T(8,128)(2,1)S(1)}, bf16[176,512]{1,0:T(8,128)(2,1)S(1)}, bf16[176,512]{1,0:T(8,128)(2,1)S(1)}) custom-call(s32[1]{0:T(128)} %bitcast.core_ref, f32[528,128]{1,0:T(8,128)S(1)} %get-tuple-element.146.refs_0_, bf16[528,128]{1,0:T(8,128)(2,1)S(1)} %collective-permute-done.19.refs_1_, ...), custom_call_target="tpu_custom_call" | custom-call | flops 1000 | bytes 1000 | tf_op jit(solution)/shard_map/grow_rows/pallas_call | solution.py:239
  62.1 1.3 %collective-permute-start.20 = (bf16[176,512]{1,0:T(8,128)(2,1)S(1)}, bf16[176,512]{1,0:T(8,128)(2,1)S(1)}, u32[]{:S(2)}, u32[]{:S(2)}) collective-permute-start(bf16[176,512]{1,0:T(8,128)(2,1)S(1)} %get-tuple-element.138), channel_id=1, source_target_pairs={{0,8},{4,12},{8,0},{12,4},{16,24},{20,28},{24,16},{28,20},{1,9},{5... | collective-permute-start | bytes 540680 | tf_op jit(solution)/shard_map/ppermute | solution.py:369
  63.4 1.5 %collective-permute-start.21 = (bf16[176,512]{1,0:T(8,128)(2,1)S(1)}, bf16[176,512]{1,0:T(8,128)(2,1)S(1)}, u32[]{:S(2)}, u32[]{:S(2)}) collective-permute-start(bf16[176,512]{1,0:T(8,128)(2,1)S(1)} %get-tuple-element.139), channel_id=1, source_target_pairs={{0,16},{4,20},{8,24},{12,28},{16,0},{20,4},{24,8},{28,12},{1,17},{... | collective-permute-start | bytes 540680 | tf_op jit(solution)/shard_map/ppermute | solution.py:369
  65.4 1.8 %collective-permute-start.25 = (bf16[176,512]{1,0:T(8,128)(2,1)S(1)}, bf16[176,512]{1,0:T(8,128)(2,1)S(1)}, u32[]{:S(2)}, u32[]{:S(2)}) collective-permute-start(bf16[176,512]{1,0:T(8,128)(2,1)S(1)} %grow_rows.5), channel_id=1, source_target_pairs={{0,24},{4,28},{8,16},{12,20},{16,8},{20,12},{24,0},{28,4},{1,25},{... | collective-permute-start | bytes 540680 | tf_op jit(solution)/shard_map/ppermute | solution.py:369
  67.5 0.8 %collective-permute-done.18 = f32[8,128]{1,0:T(8,128)S(1)} collective-permute-done((f32[8,128]{1,0:T(8,128)S(1)}, f32[8,128]{1,0:T(8,128)S(1)}, u32[]{:S(2)}, u32[]{:S(2)}) %collective-permute-start.18) | collective-permute-done | bytes 4128 | tf_op jit(solution)/shard_map/ppermute | solution.py:369
  68.3 0.5 slice.3
  69.5 3.3 %collective-permute-done.21 = bf16[176,512]{1,0:T(8,128)(2,1)S(1)} collective-permute-done((bf16[176,512]{1,0:T(8,128)(2,1)S(1)}, bf16[176,512]{1,0:T(8,128)(2,1)S(1)}, u32[]{:S(2)}, u32[]{:S(2)}) %collective-permute-start.21) | collective-permute-done | bytes 180256 | tf_op jit(solution)/shard_map/ppermute | solution.py:369
  72.8 1.1 %conditional.1 = (bf16[512,2,256]{2,1,0:T(2,128)(2,1)S(1)}) conditional(s32[]{:T(128)} %bitcast.5, (f32[512,512]{1,0:T(8,128)S(1)}, bf16[512,1024]{1,0:T(8,128)(2,1)S(1)}, bf16[176,512]{1,0:T(8,128)(2,1)S(1)}, bf16[176,512]{1,0:T(8,128)(2,1)S(1)}, bf16[176,512]{1,0:T(8,128)(2,1)S(1)}, /*index=5*/bf16[176,512]{1,0:T(8,128)(2,1)S(1)}) %tuple.33, ...), branch_computations={%region_0.1_spmd, %region_1.2_spmd} | conditional | flops 5000 | bytes 8262904 | solution.py:495
  72.8 1.1 %finish_rows.2 = bf16[512,2,256]{2,1,0:T(2,128)(2,1)S(1)} custom-call(f32[512,512]{1,0:T(8,128)S(1)} %get-tuple-element.50.refs_0_, bf16[512,1024]{1,0:T(8,128)(2,1)S(1)} %get-tuple-element.51.refs_1_, bf16[176,512]{1,0:T(8,128)(2,1)S(1)} %get-tuple-element.52.refs_2_, bf16[176,512]{1,0:T(8,128)(2,1)S(1)} %get-tuple-element.53.refs_3_, ...), custom_call_target="tpu_custom_call" | custom-call | flops 1000 | bytes 1000 | tf_op jit(solution)/shard_map/cond/branch_0_fun/finish_rows/pallas_call | solution.py:354
  73.9 0.8 %copy-done.3 = bf16[512,2,256]{2,1,0:T(2,128)(2,1)} copy-done((bf16[512,2,256]{2,1,0:T(2,128)(2,1)}, bf16[512,2,256]{2,1,0:T(2,128)(2,1)S(1)}, u32[]{:S(2)}) %copy-start.3) | copy-done | bytes 524312
  (38 shorter events, 1.9 us)
Async XLA Ops:
  0.0 17.7 %collective-permute-start.11 = (bf16[8,2048,128]{2,1,0:T(8,128)(2,1)}, bf16[8,2048,128]{2,1,0:T(8,128)(2,1)}, u32[]{:S(2)}, u32[]{:S(2)}) collective-permute-start(bf16[8,2048,128]{2,1,0:T(8,128)(2,1)} %refs_1_.3), channel_id=1, source_target_pairs={{0,4},{4,0},{8,12},{12,8},{16,20},{20,16},{24,28},{28,24},{1,5},{5... | collective-permute-start | bytes 12582920 | tf_op jit(solution)/shard_map/ppermute | solution.py:369
  0.5 8.9 %copy-start.4 = (s32[512,1]{0,1:T(1,128)S(1)}, s32[512,1]{0,1:T(1,128)}, u32[]{:S(2)}) copy-start(s32[512,1]{0,1:T(1,128)} %param.9) | copy-start | bytes 6148
  0.5 8.9 %copy-start.5 = (s32[64]{0:T(128)S(1)}, s32[64]{0:T(128)}, u32[]{:S(2)}) copy-start(s32[64]{0:T(128)} %param.10) | copy-start | bytes 772
  6.8 15.7 %collective-permute-start.12 = (bf16[512,512]{1,0:T(8,128)(2,1)}, bf16[512,512]{1,0:T(8,128)(2,1)}, u32[]{:S(2)}, u32[]{:S(2)}) collective-permute-start(bf16[512,512]{1,0:T(8,128)(2,1)} %get-tuple-element.113), channel_id=1, source_target_pairs={{0,1},{1,0},{2,3},{3,2},{4,5},{5,4},{6,7},{7,6},{8,9},{9,8},{10,11... | collective-permute-start | bytes 1572872 | tf_op jit(solution)/shard_map/ppermute | solution.py:369
  14.3 18.5 %collective-permute-start.9 = (bf16[176,2048]{1,0:T(8,128)(2,1)}, bf16[176,2048]{1,0:T(8,128)(2,1)S(1)}, u32[]{:S(2)}, u32[]{:S(2)}) collective-permute-start(bf16[176,2048]{1,0:T(8,128)(2,1)} %get-tuple-element.115), channel_id=1, source_target_pairs={{0,8},{4,12},{8,0},{12,4},{16,24},{20,28},{24,16},{28,20},{1,9},{5... | collective-permute-start | bytes 2162696 | tf_op jit(solution)/shard_map/ppermute | solution.py:369
  15.8 18.2 %collective-permute-start.10 = (bf16[176,2048]{1,0:T(8,128)(2,1)}, bf16[176,2048]{1,0:T(8,128)(2,1)S(1)}, u32[]{:S(2)}, u32[]{:S(2)}) collective-permute-start(bf16[176,2048]{1,0:T(8,128)(2,1)} %get-tuple-element.116), channel_id=1, source_target_pairs={{0,16},{4,20},{8,24},{12,28},{16,0},{20,4},{24,8},{28,12},{1,17},{... | collective-permute-start | bytes 2162696 | tf_op jit(solution)/shard_map/ppermute | solution.py:369
  17.3 36.3 %collective-permute-start.16 = (bf16[512,512]{1,0:T(8,128)(2,1)}, bf16[512,512]{1,0:T(8,128)(2,1)}, u32[]{:S(2)}, u32[]{:S(2)}) collective-permute-start(bf16[512,512]{1,0:T(8,128)(2,1)} %get-tuple-element.131), channel_id=1, source_target_pairs={{0,1},{1,0},{2,3},{3,2},{4,5},{5,4},{6,7},{7,6},{8,9},{9,8},{10,11... | collective-permute-start | bytes 1572872 | tf_op jit(solution)/shard_map/ppermute | solution.py:369
  17.7 17.7 %collective-permute-start.13 = (bf16[8,2,64,256]{3,2,1,0:T(8,128)(2,1)}, bf16[8,2,64,256]{3,2,1,0:T(8,128)(2,1)S(1)}, u32[]{:S(2)}, u32[]{:S(2)}) collective-permute-start(bf16[8,2,64,256]{3,2,1,0:T(8,128)(2,1)} %refs_5_.1), channel_id=1, source_target_pairs={{0,4},{4,0},{8,12},{12,8},{16,20},{20,16},{24,28},{28,24},{1,5},{5... | collective-permute-start | bytes 1572872 | tf_op jit(solution)/shard_map/ppermute | solution.py:369
  24.0 6.0 %copy-start = (bf16[8,2048,128]{2,1,0:T(8,128)(2,1)S(1)}, bf16[8,2048,128]{2,1,0:T(8,128)(2,1)}, u32[]{:S(2)}) copy-start(bf16[8,2048,128]{2,1,0:T(8,128)(2,1)} %refs_1_.3) | copy-start | bytes 12582916
  24.0 29.6 %collective-permute-start.17 = (bf16[512,512]{1,0:T(8,128)(2,1)S(1)}, bf16[512,512]{1,0:T(8,128)(2,1)S(1)}, u32[]{:S(2)}, u32[]{:S(2)}) collective-permute-start(bf16[512,512]{1,0:T(8,128)(2,1)S(1)} %add_convert_fusion), channel_id=1, source_target_pairs={{0,2},{1,3},{2,0},{3,1},{4,6},{5,7},{6,4},{7,5},{8,10},{9,11},{10,... | collective-permute-start | bytes 1572872 | tf_op jit(solution)/shard_map/ppermute | solution.py:369
  30.0 10.8 %slice-start = ((s8[8388608]{0:T(1024)(128)(4,1)}), s8[4194304]{0:T(1024)(128)(4,1)S(1)}, s32[]{:S(2)}) async-start(s8[8388608]{0:T(1024)(128)(4,1)} %bitcast.6), calls=%async_computation | async-start | bytes 8388608
  34.0 20.9 %collective-permute-start.14 = (bf16[176,2048]{1,0:T(8,128)(2,1)S(1)}, bf16[176,2048]{1,0:T(8,128)(2,1)S(1)}, u32[]{:S(2)}, u32[]{:S(2)}) collective-permute-start(bf16[176,2048]{1,0:T(8,128)(2,1)S(1)} %get-tuple-element.127), channel_id=1, source_target_pairs={{0,24},{4,28},{8,16},{12,20},{16,8},{20,12},{24,0},{28,4},{1,25},{... | collective-permute-start | bytes 2162696 | tf_op jit(solution)/shard_map/ppermute | solution.py:369
  35.4 5.3 %slice-start.1 = ((s8[8388608]{0:T(1024)(128)(4,1)}), s8[4194304]{0:T(1024)(128)(4,1)S(1)}, s32[]{:S(2)}) async-start(s8[8388608]{0:T(1024)(128)(4,1)} %bitcast.6), calls=%async_computation.1 | async-start | bytes 8388608
  35.5 5.3 %copy-start.1 = (bf16[512,2048]{1,0:T(8,128)(2,1)S(1)}, bf16[512,2048]{1,0:T(8,128)(2,1)}, u32[]{:S(2)}) copy-start(bf16[512,2048]{1,0:T(8,128)(2,1)} %tokens_ref.4) | copy-start | bytes 6291460
  39.6 10.1 %collective-permute-start.15 = (f32[528,128]{1,0:T(8,128)S(1)}, f32[528,128]{1,0:T(8,128)S(1)}, u32[]{:S(2)}, u32[]{:S(2)}) collective-permute-start(f32[528,128]{1,0:T(8,128)S(1)} %get-tuple-element.128), channel_id=1, source_target_pairs={{0,1},{1,0},{2,3},{3,2},{4,5},{5,4},{6,7},{7,6},{8,9},{9,8},{10,11... | collective-permute-start | bytes 811016 | tf_op jit(solution)/shard_map/ppermute | solution.py:369
  49.7 11.5 %collective-permute-start.19 = (bf16[528,128]{1,0:T(8,128)(2,1)S(1)}, bf16[528,128]{1,0:T(8,128)(2,1)S(1)}, u32[]{:S(2)}, u32[]{:S(2)}) collective-permute-start(bf16[528,128]{1,0:T(8,128)(2,1)S(1)} %get-tuple-element.145), channel_id=1, source_target_pairs={{0,2},{1,3},{2,0},{3,1},{4,6},{5,7},{6,4},{7,5},{8,10},{9,11},{10,... | collective-permute-start | bytes 405512 | tf_op jit(solution)/shard_map/ppermute | solution.py:369
  54.8 6.5 %copy-start.2 = (bf16[8,2,64,256]{3,2,1,0:T(8,128)(2,1)S(1)}, bf16[8,2,64,256]{3,2,1,0:T(8,128)(2,1)}, u32[]{:S(2)}) copy-start(bf16[8,2,64,256]{3,2,1,0:T(8,128)(2,1)} %refs_5_.1) | copy-start | bytes 1572868
  56.8 8.1 %collective-permute-start.24 = (bf16[176,128]{1,0:T(8,128)(2,1)S(1)}, bf16[176,128]{1,0:T(8,128)(2,1)S(1)}, u32[]{:S(2)}, u32[]{:S(2)}) collective-permute-start(bf16[176,128]{1,0:T(8,128)(2,1)S(1)} %get-tuple-element.142), channel_id=1, source_target_pairs={{0,3},{1,2},{2,1},{3,0},{4,7},{5,6},{6,5},{7,4},{8,11},{9,10},{10,... | collective-permute-start | bytes 135176 | tf_op jit(solution)/shard_map/ppermute | solution.py:369
  58.8 6.1 %collective-permute-start.23 = (bf16[176,128]{1,0:T(8,128)(2,1)S(1)}, bf16[176,128]{1,0:T(8,128)(2,1)S(1)}, u32[]{:S(2)}, u32[]{:S(2)}) collective-permute-start(bf16[176,128]{1,0:T(8,128)(2,1)S(1)} %get-tuple-element.142), channel_id=1, source_target_pairs={{0,2},{1,3},{2,0},{3,1},{4,6},{5,7},{6,4},{7,5},{8,10},{9,11},{10,... | collective-permute-start | bytes 135176 | tf_op jit(solution)/shard_map/ppermute | solution.py:369
  60.8 4.1 %collective-permute-start.22 = (bf16[176,128]{1,0:T(8,128)(2,1)S(1)}, bf16[176,128]{1,0:T(8,128)(2,1)S(1)}, u32[]{:S(2)}, u32[]{:S(2)}) collective-permute-start(bf16[176,128]{1,0:T(8,128)(2,1)S(1)} %get-tuple-element.142), channel_id=1, source_target_pairs={{0,1},{1,0},{2,3},{3,2},{4,5},{5,4},{6,7},{7,6},{8,9},{9,8},{10,11... | collective-permute-start | bytes 135176 | tf_op jit(solution)/shard_map/ppermute | solution.py:369
  62.1 7.4 %collective-permute-start.20 = (bf16[176,512]{1,0:T(8,128)(2,1)S(1)}, bf16[176,512]{1,0:T(8,128)(2,1)S(1)}, u32[]{:S(2)}, u32[]{:S(2)}) collective-permute-start(bf16[176,512]{1,0:T(8,128)(2,1)S(1)} %get-tuple-element.138), channel_id=1, source_target_pairs={{0,8},{4,12},{8,0},{12,4},{16,24},{20,28},{24,16},{28,20},{1,9},{5... | collective-permute-start | bytes 540680 | tf_op jit(solution)/shard_map/ppermute | solution.py:369
  63.4 9.4 %collective-permute-start.21 = (bf16[176,512]{1,0:T(8,128)(2,1)S(1)}, bf16[176,512]{1,0:T(8,128)(2,1)S(1)}, u32[]{:S(2)}, u32[]{:S(2)}) collective-permute-start(bf16[176,512]{1,0:T(8,128)(2,1)S(1)} %get-tuple-element.139), channel_id=1, source_target_pairs={{0,16},{4,20},{8,24},{12,28},{16,0},{20,4},{24,8},{28,12},{1,17},{... | collective-permute-start | bytes 540680 | tf_op jit(solution)/shard_map/ppermute | solution.py:369
  65.4 7.4 %collective-permute-start.25 = (bf16[176,512]{1,0:T(8,128)(2,1)S(1)}, bf16[176,512]{1,0:T(8,128)(2,1)S(1)}, u32[]{:S(2)}, u32[]{:S(2)}) collective-permute-start(bf16[176,512]{1,0:T(8,128)(2,1)S(1)} %grow_rows.5), channel_id=1, source_target_pairs={{0,24},{4,28},{8,16},{12,20},{16,8},{20,12},{24,0},{28,4},{1,25},{... | collective-permute-start | bytes 540680 | tf_op jit(solution)/shard_map/ppermute | solution.py:369
  67.1 1.2 %collective-permute-start.18 = (f32[8,128]{1,0:T(8,128)S(1)}, f32[8,128]{1,0:T(8,128)S(1)}, u32[]{:S(2)}, u32[]{:S(2)}) collective-permute-start(f32[8,128]{1,0:T(8,128)S(1)} %max.6), channel_id=1, source_target_pairs={{0,4},{4,0},{8,12},{12,8},{16,20},{20,16},{24,28},{28,24},{1,5},{5... | collective-permute-start | bytes 12296 | tf_op jit(solution)/shard_map/ppermute | solution.py:369
  73.9 0.8 %copy-start.3 = (bf16[512,2,256]{2,1,0:T(2,128)(2,1)}, bf16[512,2,256]{2,1,0:T(2,128)(2,1)S(1)}, u32[]{:S(2)}) copy-start(bf16[512,2,256]{2,1,0:T(2,128)(2,1)S(1)} %get-tuple-element.188) | copy-start | bytes 1572868
